TPU v7x, 32 devices: a whole 2x2x4 slice. The times are simulated.
32 devices in a mesh: sec: 2 (over core), blk: 16 (over z, y, x).
Axes of the slice: x: 2, y: 2, z: 4, core: 2. Of those that a mesh axis runs over, the one named last changes fastest.
Arguments:
- atm_state: float32 [4, 72, 131072], P(None, None, ('sec', 'blk')), may hold values from -6 to 6
- atm_surface: float32 [4, 131072], P(None, ('sec', 'blk')), may hold values from -6 to 6
- bulk_coef: float32 [4, 131072], P(None, ('sec', 'blk')), may hold values from 0.05 to 0.5
- atm_nbr: int32 [6, 131072], P(None, ('sec', 'blk')), may hold values from 0 to 4607, as said below
- atm_nbr_coef: float32 [6, 131072], P(None, ('sec', 'blk')), may hold values from 0.02 to 0.15
- atm_mix: float32 [72, 72], replicated, may hold values from -0.375 to 0.375
- ocean_state: float32 [4, 80, 131072], P(None, None, ('sec', 'blk')), may hold values from -6 to 6
- ocean_nbr: int32 [6, 131072], P(None, ('sec', 'blk')), may hold values from 0 to 4863, as said below
- ocean_nbr_coef: float32 [6, 131072], P(None, ('sec', 'blk')), may hold values from 0.02 to 0.15
- ocean_mix: float32 [80, 80], replicated, may hold values from -0.3125 to 0.3125
- send_cols: int32 [32, 32, 512], P(('sec', 'blk')), may hold values from 0 to 4095
- remap_slot: int32 [4, 131072], P(None, ('sec', 'blk')), may hold values from 0 to 16383, as said below
- remap_weight: float32 [4, 131072], P(None, ('sec', 'blk')), may hold values from 0.05 to 0.5
Outputs:
- atm_final: float32 [4, 72, 131072], P(None, None, ('sec', 'blk'))
- ocean_final: float32 [4, 80, 131072], P(None, None, ('sec', 'blk'))
- surface_temp: float32 [131072], P(('sec', 'blk'))
Inputs may be any that keep to these rules, and one draw needn't show every extreme that they name: `atm_nbr`: entry [k, i] is the position of column i's k-th neighbour among the device's columns extended by 256 columns on each side from the neighbouring devices along the block order, wrapping around; it lies within 256 positions of the column and is never the column itself. `ocean_nbr`: entry [k, j] is the position of cell j's k-th neighbour among the device's cells extended by 384 cells on each side from the neighbouring devices along the block order, wrapping around; it lies within 384 positions of the cell and is never the cell itself. `remap_slot`: entry p * 512 + c names slot c of the list that atmosphere block p sends to the block of the ocean cell; each ocean block reads some slot from every atmosphere block.
All inputs are finite; a program needn't handle non-finite values.
Results may differ from a plain program's by a relative error of at most 0.0001.
Values sent between devices are 32-bit elements; how exact they have to be, the bound alone decides.
No kernel may reach another device: no remote copies, remote signals or barrier semaphores. Data moves between devices by JAX's collectives and lax.ppermute only.
A program may use at most 256 MiB of HBM per device.

v0:
```python
import jax
import jax.numpy as jnp
from jax import lax
from jax.sharding import PartitionSpec as P

ASTEPS = 4
HA = 256
HO = 384


def extended_2(shard, sides, width):
    for axis, dim in sides:
        count, length = (lax.axis_size(axis), shard.shape[dim])
        up = [(i, (i + 1) % count) for i in range(count)]
        down = [(j, i) for i, j in up]
        last = lax.slice_in_dim(shard, length - width, length, axis=dim)
        leading = lax.slice_in_dim(shard, 0, width, axis=dim)
        before = lax.ppermute(last, axis, up)
        after = lax.ppermute(leading, axis, down)
        shard = jnp.concatenate([before, shard, after], axis=dim)
    return shard


def column_mix(mixing, fields_now):
    return fields_now + jnp.einsum(
        "lm,fmc->flc", mixing, fields_now, precision=lax.Precision.HIGHEST
    )


def lateral(fields_now, extended, neighbors, weights):
    change = jnp.zeros_like(fields_now)
    for which in range(neighbors.shape[0]):
        change = change + weights[which] * (
            jnp.take(extended, neighbors[which], axis=2) - fields_now
        )
    return fields_now + change


def per_device(
    atm_state,
    atm_surface,
    bulk_coef,
    atm_nbr,
    atm_nbr_coef,
    atm_mix,
    ocean_state,
    ocean_nbr,
    ocean_nbr_coef,
    ocean_mix,
    send_cols,
    remap_slot,
    remap_weight,
):
    columns = atm_state.shape[2]
    field_count = atm_state.shape[0]
    fields_now = atm_state
    fluxes = jnp.zeros((field_count, columns), jnp.float32)
    for repeat in range(ASTEPS):
        extended = extended_2(fields_now, ((("sec", "blk"), 2),), HA)
        mixed = lateral(fields_now, extended, atm_nbr, atm_nbr_coef)
        fluxes = bulk_coef * (atm_surface - mixed[:, -1, :])
        mixed = mixed.at[:, -1, :].add(fluxes)
        fields_now = column_mix(atm_mix, mixed)
    picked = send_cols[0]
    peers, slots = picked.shape
    total_slots = peers * slots
    column_ids = picked.reshape(-1)
    outgoing = jnp.take(fluxes, column_ids, axis=1).reshape(field_count, peers, slots)
    incoming = lax.all_to_all(outgoing, ("sec", "blk"), split_axis=1, concat_axis=1, tiled=True)
    received = incoming.reshape(field_count, total_slots)
    ocean_cells = ocean_state.shape[2]
    ocean_flux = jnp.zeros((field_count, ocean_cells), jnp.float32)
    for which in range(remap_slot.shape[0]):
        ocean_flux = ocean_flux + remap_weight[which] * jnp.take(
            received, remap_slot[which], axis=1
        )
    extended = extended_2(ocean_state, ((("sec", "blk"), 2),), HO)
    mixed = lateral(ocean_state, extended, ocean_nbr, ocean_nbr_coef)
    mixed = mixed.at[:, 0, :].add(ocean_flux)
    ocean_final = column_mix(ocean_mix, mixed)
    sea_surface = ocean_final[0, 0, :]
    slot_flat = remap_slot.reshape(-1)
    weighted = jax.ops.segment_sum(
        (remap_weight * sea_surface[None, :]).reshape(-1), slot_flat, total_slots
    )
    weight_sums = jax.ops.segment_sum(remap_weight.reshape(-1), slot_flat, total_slots)
    back_value, back_weight = (
        lax.all_to_all(
            weighted.reshape(peers, slots), ("sec", "blk"), split_axis=0, concat_axis=0, tiled=True
        ),
        lax.all_to_all(
            weight_sums.reshape(peers, slots),
            ("sec", "blk"),
            split_axis=0,
            concat_axis=0,
            tiled=True,
        ),
    )
    gathered_temp = jax.ops.segment_sum(back_value.reshape(-1), column_ids, columns)
    gathered_weight = jax.ops.segment_sum(back_weight.reshape(-1), column_ids, columns)
    surface_temp = (atm_surface[0] + gathered_temp) / (1.0 + gathered_weight)
    return (fields_now, ocean_final, surface_temp)


def solution(mesh):
    placed = (
        P(None, None, ("sec", "blk")),
        P(None, ("sec", "blk")),
        P(None, ("sec", "blk")),
        P(None, ("sec", "blk")),
        P(None, ("sec", "blk")),
        P(),
        P(None, None, ("sec", "blk")),
        P(None, ("sec", "blk")),
        P(None, ("sec", "blk")),
        P(),
        P(("sec", "blk"), None, None),
        P(None, ("sec", "blk")),
        P(None, ("sec", "blk")),
    )
    return jax.shard_map(
        per_device,
        mesh=mesh,
        in_specs=placed,
        out_specs=(P(None, None, ("sec", "blk")), P(None, None, ("sec", "blk")), P(("sec", "blk"))),
        check_vma=False,
    )
```

profile of v0, /device:TPU:0, one launch (start us, length us, event | category | flops | bytes accessed | tf_op | source)
XLA Modules:
  0.0 2073.2 jit_solution(5239879506230904243)
XLA Ops:
  25.2 86.6 %scatter_custom_fusion.2 = f32[16384]{0:T(1024)} fusion(s32[16384]{0:T(1024)S(1)} %bitcast.448, f32[16384]{0:T(1024)} %bitcast.451, f32[]{:T(128)} %constant.163.clone.1), kind=kCustom, calls=%fused_computation.195 | custom fusion | flops 16384 | bytes 66048 | tf_op jit(solution)/shard_map/scatter-add | solution.py:86
  451.2 86.6 %scatter_custom_fusion.3 = f32[4096]{0:T(1024)} fusion(s32[16384]{0:T(1024)S(1)} %bitcast.403, f32[16384]{0:T(1024)} %bitcast.87, f32[]{:T(128)} %constant.164.clone.1), kind=kCustom, calls=%fused_computation.231 | custom fusion | flops 16384 | bytes 16896 | tf_op jit(solution)/shard_map/scatter-add | solution.py:100
  554.0 34.0 %gather_fusion.12 = f32[4096,4,72]{2,1,0:T(4,128)} fusion(f32[4,72,4608]{1,0,2:T(4,128)} %copy.107, s32[4096]{0:T(1024)S(1)} %fusion.90), kind=kCustom, calls=%fused_computation.13.clone | custom fusion | bytes 9453568 | tf_op jit(solution)/shard_map/jit(_take)/gather | solution.py:34
  588.0 33.8 %gather_fusion.11 = f32[4096,4,72]{2,1,0:T(4,128)} fusion(f32[4,72,4608]{1,0,2:T(4,128)} %copy.107, s32[4096]{0:T(1024)S(1)} %fusion.89), kind=kCustom, calls=%fused_computation.12.clone | custom fusion | bytes 9453568 | tf_op jit(solution)/shard_map/jit(_take)/gather | solution.py:34
  621.9 33.9 %gather_fusion.10 = f32[4096,4,72]{2,1,0:T(4,128)} fusion(f32[4,72,4608]{1,0,2:T(4,128)} %copy.107, s32[4096]{0:T(1024)S(1)} %fusion.88), kind=kCustom, calls=%fused_computation.11.clone | custom fusion | bytes 9453568 | tf_op jit(solution)/shard_map/jit(_take)/gather | solution.py:34
  655.7 33.9 %gather_fusion.9 = f32[4096,4,72]{2,1,0:T(4,128)} fusion(f32[4,72,4608]{1,0,2:T(4,128)} %copy.107, s32[4096]{0:T(1024)S(1)} %fusion.87), kind=kCustom, calls=%fused_computation.10.clone | custom fusion | bytes 9453568 | tf_op jit(solution)/shard_map/jit(_take)/gather | solution.py:34
  723.4 34.0 %gather_fusion.7 = f32[4096,4,72]{2,1,0:T(4,128)} fusion(f32[4,72,4608]{1,0,2:T(4,128)} %copy.107, s32[4096]{0:T(1024)S(1)} %fusion.85), kind=kCustom, calls=%fused_computation.8.clone | custom fusion | bytes 9453568 | tf_op jit(solution)/shard_map/jit(_take)/gather | solution.py:34
  862.8 33.9 %gather_fusion.30 = f32[4096,4,80]{2,1,0:T(4,128)} fusion(f32[4,80,4864]{1,0,2:T(4,128)} %pad_maximum_fusion, s32[4096]{0:T(1024)S(1)} %copy-done.35), kind=kCustom, calls=%fused_computation.30.clone | custom fusion | bytes 10502144 | tf_op jit(solution)/shard_map/jit(_take)/gather | solution.py:34
  905.7 33.9 %gather_fusion.29 = f32[4096,4,80]{2,1,0:T(4,128)} fusion(f32[4,80,4864]{1,0,2:T(4,128)} %pad_maximum_fusion, s32[4096]{0:T(1024)S(1)} %copy-done.32), kind=kCustom, calls=%fused_computation.29.clone | custom fusion | bytes 10502144 | tf_op jit(solution)/shard_map/jit(_take)/gather | solution.py:34
  948.5 33.9 %gather_fusion.28 = f32[4096,4,80]{2,1,0:T(4,128)} fusion(f32[4,80,4864]{1,0,2:T(4,128)} %pad_maximum_fusion, s32[4096]{0:T(1024)S(1)} %copy-done.34), kind=kCustom, calls=%fused_computation.28.clone | custom fusion | bytes 10502144 | tf_op jit(solution)/shard_map/jit(_take)/gather | solution.py:34
  991.4 33.9 %gather_fusion.27 = f32[4096,4,80]{2,1,0:T(4,128)} fusion(f32[4,80,4864]{1,0,2:T(4,128)} %pad_maximum_fusion, s32[4096]{0:T(1024)S(1)} %copy-done.30), kind=kCustom, calls=%fused_computation.27.clone | custom fusion | bytes 10502144 | tf_op jit(solution)/shard_map/jit(_take)/gather | solution.py:34
  1034.3 33.9 %gather_fusion.26 = f32[4096,4,80]{2,1,0:T(4,128)} fusion(f32[4,80,4864]{1,0,2:T(4,128)} %pad_maximum_fusion, s32[4096]{0:T(1024)S(1)} %copy-done.33), kind=kCustom, calls=%fused_computation.26.clone | custom fusion | bytes 10502144 | tf_op jit(solution)/shard_map/jit(_take)/gather | solution.py:34
  1077.2 33.9 %gather_fusion.25 = f32[4096,4,80]{2,1,0:T(4,128)} fusion(f32[4,80,4864]{1,0,2:T(4,128)} %pad_maximum_fusion, s32[4096]{0:T(1024)S(1)} %copy-done.31), kind=kCustom, calls=%fused_computation.1.clone | custom fusion | bytes 10502144 | tf_op jit(solution)/shard_map/jit(_take)/gather | solution.py:34
  1168.9 33.9 %gather_fusion.17 = f32[4096,4,72]{2,1,0:T(4,128)} fusion(f32[4,72,4608]{1,0,2:T(4,128)} %copy.121, s32[4096]{0:T(1024)S(1)} %fusion.89), kind=kCustom, calls=%fused_computation.18.clone | custom fusion | bytes 9453568 | tf_op jit(solution)/shard_map/jit(_take)/gather | solution.py:34
  1202.8 33.8 %gather_fusion.16 = f32[4096,4,72]{2,1,0:T(4,128)} fusion(f32[4,72,4608]{1,0,2:T(4,128)} %copy.121, s32[4096]{0:T(1024)S(1)} %fusion.88), kind=kCustom, calls=%fused_computation.17.clone | custom fusion | bytes 9453568 | tf_op jit(solution)/shard_map/jit(_take)/gather | solution.py:34
  1236.7 33.8 %gather_fusion.15 = f32[4096,4,72]{2,1,0:T(4,128)} fusion(f32[4,72,4608]{1,0,2:T(4,128)} %copy.121, s32[4096]{0:T(1024)S(1)} %fusion.87), kind=kCustom, calls=%fused_computation.16.clone | custom fusion | bytes 9453568 | tf_op jit(solution)/shard_map/jit(_take)/gather | solution.py:34
  1270.5 34.0 %gather_fusion.14 = f32[4096,4,72]{2,1,0:T(4,128)} fusion(f32[4,72,4608]{1,0,2:T(4,128)} %copy.121, s32[4096]{0:T(1024)S(1)} %fusion.86), kind=kCustom, calls=%fused_computation.15.clone | custom fusion | bytes 9453568 | tf_op jit(solution)/shard_map/jit(_take)/gather | solution.py:34
  1486.3 33.9 %gather_fusion.23 = f32[4096,4,72]{2,1,0:T(4,128)} fusion(f32[4,72,4608]{1,0,2:T(4,128)} %copy.135, s32[4096]{0:T(1024)S(1)} %fusion.89), kind=kCustom, calls=%fused_computation.24.clone | custom fusion | bytes 9453568 | tf_op jit(solution)/shard_map/jit(_take)/gather | solution.py:34
  1520.2 33.8 %gather_fusion.22 = f32[4096,4,72]{2,1,0:T(4,128)} fusion(f32[4,72,4608]{1,0,2:T(4,128)} %copy.135, s32[4096]{0:T(1024)S(1)} %fusion.88), kind=kCustom, calls=%fused_computation.23.clone | custom fusion | bytes 9453568 | tf_op jit(solution)/shard_map/jit(_take)/gather | solution.py:34
  1554.0 33.8 %gather_fusion.21 = f32[4096,4,72]{2,1,0:T(4,128)} fusion(f32[4,72,4608]{1,0,2:T(4,128)} %copy.135, s32[4096]{0:T(1024)S(1)} %fusion.87), kind=kCustom, calls=%fused_computation.22.clone | custom fusion | bytes 9453568 | tf_op jit(solution)/shard_map/jit(_take)/gather | solution.py:34
  1587.9 34.0 %gather_fusion.20 = f32[4096,4,72]{2,1,0:T(4,128)} fusion(f32[4,72,4608]{1,0,2:T(4,128)} %copy.135, s32[4096]{0:T(1024)S(1)} %fusion.86), kind=kCustom, calls=%fused_computation.21.clone | custom fusion | bytes 9453568 | tf_op jit(solution)/shard_map/jit(_take)/gather | solution.py:34
  1723.7 54.8 %gather_fusion = f32[16384,4]{1,0:T(8,128)} fusion(f32[4,4096]{0,1:T(8,128)S(1)} %copy.158, s32[16384]{0:T(1024)S(1)} %copy-done.17), kind=kCustom, calls=%fused_computation.34 | custom fusion | bytes 589824 | tf_op jit(solution)/shard_map/jit(_take)/gather | solution.py:68
  1882.9 86.6 %scatter_custom_fusion = f32[16384]{0:T(1024)} fusion(s32[16384]{0:T(1024)} %bitcast.449, f32[16384]{0:T(1024)S(1)} %bitcast.450, f32[]{:T(128)} %constant.163.clone.1), kind=kCustom, calls=%fused_computation.197 | custom fusion | flops 16384 | bytes 66048 | tf_op jit(solution)/shard_map/scatter-add | solution.py:83
  1984.5 87.8 %scatter_fusion = f32[4096]{0:T(1024)S(1)} fusion(f32[4096]{0:T(1024)S(1)} %bitcast.370, s32[16384]{0:T(1024)S(1)} %bitcast.404, f32[16384]{0:T(1024)S(1)} %bitcast.405), kind=kCustom, calls=%fused_computation.36 | custom fusion | flops 16384 | bytes 262144 | tf_op jit(solution)/shard_map/scatter-add | solution.py:99
  (282 shorter events, 1024.8 us)
Async XLA Ops:
  0.6 1868.6 %copy-start = (f32[80,80]{1,0:T(8,128)S(1)}, f32[80,80]{1,0:T(8,128)}, u32[]{:S(2)}) copy-start(f32[80,80]{1,0:T(8,128)} %param.38) | copy-start | bytes 76804
  0.7 117.6 %copy-start.23 = (s32[6,4096]{1,0:T(8,128)S(1)}, s32[6,4096]{1,0:T(8,128)}, u32[]{:S(2)}) copy-start(s32[6,4096]{1,0:T(8,128)} %param.32) | copy-start | bytes 294916
  9.2 121.8 %copy-start.12 = (s32[1,32,512]{2,1,0:T(8,128)S(1)}, s32[1,32,512]{2,1,0:T(8,128)}, u32[]{:S(2)}) copy-start(s32[1,32,512]{2,1,0:T(8,128)} %param.39) | copy-start | bytes 196612
  10.6 124.3 %collective-permute-start.1 = (f32[4,72,256]{1,0,2:T(4,128)S(1)}, f32[4,72,256]{1,0,2:T(4,128)S(1)}, u32[]{:S(2)}, u32[]{:S(2)}) collective-permute-start(f32[4,72,256]{1,0,2:T(4,128)S(1)} %get-tuple-element.67), channel_id=1, source_target_pairs={{1,0},{2,1},{3,2},{4,3},{5,4},{6,5},{7,6},{8,7},{9,8},{10,9},{11,1... | collective-permute-start | bytes 884744 | tf_op jit(solution)/shard_map/ppermute | solution.py:19
  17.0 117.9 %collective-permute-start = (f32[4,72,256]{1,0,2:T(4,128)S(1)}, f32[4,72,256]{1,0,2:T(4,128)S(1)}, u32[]{:S(2)}, u32[]{:S(2)}) collective-permute-start(f32[4,72,256]{1,0,2:T(4,128)S(1)} %get-tuple-element.66), channel_id=1, source_target_pairs={{0,1},{1,2},{2,3},{3,4},{4,5},{5,6},{6,7},{7,8},{8,9},{9,10},{10,1... | collective-permute-start | bytes 884744 | tf_op jit(solution)/shard_map/ppermute | solution.py:18
  19.2 518.6 %collective-permute-start.9 = (f32[4,80,384]{2,1,0:T(8,128)}, f32[4,80,384]{2,1,0:T(8,128)S(1)}, u32[]{:S(2)}, u32[]{:S(2)}) collective-permute-start(f32[4,80,384]{2,1,0:T(8,128)} %get-tuple-element.69), channel_id=1, source_target_pairs={{1,0},{2,1},{3,2},{4,3},{5,4},{6,5},{7,6},{8,7},{9,8},{10,9},{11,1... | collective-permute-start | bytes 1474568 | tf_op jit(solution)/shard_map/ppermute | solution.py:19
  24.6 513.6 %collective-permute-start.8 = (f32[4,80,384]{2,1,0:T(8,128)}, f32[4,80,384]{2,1,0:T(8,128)S(1)}, u32[]{:S(2)}, u32[]{:S(2)}) collective-permute-start(f32[4,80,384]{2,1,0:T(8,128)} %get-tuple-element.68), channel_id=1, source_target_pairs={{0,1},{1,2},{2,3},{3,4},{4,5},{5,6},{6,7},{7,8},{8,9},{9,10},{10,1... | collective-permute-start | bytes 1474568 | tf_op jit(solution)/shard_map/ppermute | solution.py:18
  24.6 102.2 %copy-start.42 = (s32[1,32,4,128]{3,1,2,0:T(8,128)}, s32[1,32,4,128]{3,1,2,0:T(8,128)S(1)}, u32[]{:S(2)}) copy-start(s32[1,32,4,128]{3,1,2,0:T(8,128)S(1)} %copy.171) | copy-start | bytes 196612
  111.9 339.4 %all-to-all-start.2 = ((f32[32,1,512]{2,1,0:T(1,128)}), f32[32,1,512]{2,1,0:T(1,128)}, u32[]{:S(2)}, u32[]{:S(2)}) async-start(f32[32,1,512]{2,1,0:T(1,128)} %bitcast.86), calls=%async_computation.2 | async-start | bytes 131072 | tf_op jit(solution)/shard_map/all_to_all | solution.py:91
  436.2 102.3 %collective-permute-start.3 = (f32[4,72,256]{2,1,0:T(8,128)}, f32[4,72,256]{2,1,0:T(8,128)}, u32[]{:S(2)}, u32[]{:S(2)}) collective-permute-start(f32[4,72,256]{2,1,0:T(8,128)} %get-tuple-element.75), channel_id=1, source_target_pairs={{1,0},{2,1},{3,2},{4,3},{5,4},{6,5},{7,6},{8,7},{9,8},{10,9},{11,1... | collective-permute-start | bytes 884744 | tf_op jit(solution)/shard_map/ppermute | solution.py:19
  441.3 97.2 %collective-permute-start.2 = (f32[4,72,256]{2,1,0:T(8,128)S(1)}, f32[4,72,256]{2,1,0:T(8,128)}, u32[]{:S(2)}, u32[]{:S(2)}) collective-permute-start(f32[4,72,256]{2,1,0:T(8,128)S(1)} %get-tuple-element.74), channel_id=1, source_target_pairs={{0,1},{1,2},{2,3},{3,4},{4,5},{5,6},{6,7},{7,8},{8,9},{9,10},{10,1... | collective-permute-start | bytes 884744 | tf_op jit(solution)/shard_map/ppermute | solution.py:18
  450.6 93.4 %copy-start.15 = (s32[4,4,8,128]{3,1,2,0:T(4,128)}, s32[4,4,8,128]{3,1,2,0:T(4,128)S(1)}, u32[]{:S(2)}) copy-start(s32[4,4,8,128]{3,1,2,0:T(4,128)S(1)} %copy.170) | copy-start | bytes 196612
  838.7 281.3 %collective-permute-start.5 = (f32[4,72,256]{2,1,0:T(8,128)S(1)}, f32[4,72,256]{2,1,0:T(8,128)S(1)}, u32[]{:S(2)}, u32[]{:S(2)}) collective-permute-start(f32[4,72,256]{2,1,0:T(8,128)S(1)} %get-tuple-element.73), channel_id=1, source_target_pairs={{1,0},{2,1},{3,2},{4,3},{5,4},{6,5},{7,6},{8,7},{9,8},{10,9},{11,1... | collective-permute-start | bytes 884744 | tf_op jit(solution)/shard_map/ppermute | solution.py:19
  844.1 275.9 %collective-permute-start.4 = (f32[4,72,256]{2,1,0:T(8,128)S(1)}, f32[4,72,256]{2,1,0:T(8,128)S(1)}, u32[]{:S(2)}, u32[]{:S(2)}) collective-permute-start(f32[4,72,256]{2,1,0:T(8,128)S(1)} %get-tuple-element.72), channel_id=1, source_target_pairs={{0,1},{1,2},{2,3},{3,4},{4,5},{5,6},{6,7},{7,8},{8,9},{9,10},{10,1... | collective-permute-start | bytes 884744 | tf_op jit(solution)/shard_map/ppermute | solution.py:18
  1417.5 22.5 %collective-permute-start.7 = (f32[4,72,256]{2,1,0:T(8,128)S(1)}, f32[4,72,256]{2,1,0:T(8,128)S(1)}, u32[]{:S(2)}, u32[]{:S(2)}) collective-permute-start(f32[4,72,256]{2,1,0:T(8,128)S(1)} %get-tuple-element.71), channel_id=1, source_target_pairs={{1,0},{2,1},{3,2},{4,3},{5,4},{6,5},{7,6},{8,7},{9,8},{10,9},{11,1... | collective-permute-start | bytes 884744 | tf_op jit(solution)/shard_map/ppermute | solution.py:19
  1422.9 17.1 collective-permute-start.6
  1784.6 17.3 all-to-all-start
  1821.0 45.1 %copy-start.43 = (f32[1,4096]{1,0:T(1,128)S(1)}, f32[1,4096]{1,0:T(1,128)}, u32[]{:S(2)}) copy-start(f32[1,4096]{1,0:T(1,128)} %get-tuple-element.100) | copy-start | bytes 49156
  1821.0 45.1 %copy-start.44 = (f32[1,4096]{1,0:T(1,128)S(1)}, f32[1,4096]{1,0:T(1,128)}, u32[]{:S(2)}) copy-start(f32[1,4096]{1,0:T(1,128)} %get-tuple-element.101) | copy-start | bytes 49156
  1821.0 45.1 %copy-start.45 = (f32[1,4096]{1,0:T(1,128)S(1)}, f32[1,4096]{1,0:T(1,128)}, u32[]{:S(2)}) copy-start(f32[1,4096]{1,0:T(1,128)} %get-tuple-element.102) | copy-start | bytes 49156
  1821.0 45.1 %copy-start.46 = (f32[1,4096]{1,0:T(1,128)S(1)}, f32[1,4096]{1,0:T(1,128)}, u32[]{:S(2)}) copy-start(f32[1,4096]{1,0:T(1,128)} %get-tuple-element.103) | copy-start | bytes 49156
  1821.0 45.1 %copy-start.47 = (pred[4096]{0:T(1024)(128)(4,1)S(1)}, pred[4096]{0:T(1024)(128)(4,1)}, u32[]{:S(2)}) copy-start(pred[4096]{0:T(1024)(128)(4,1)} %get-tuple-element.120) | copy-start | bytes 12292
  1969.5 15.0 all-to-all-start.1
  1984.5 87.8 %copy-start.39 = (f32[4096]{0:T(1024)S(1)}, f32[4096]{0:T(1024)}, u32[]{:S(2)}) copy-start(f32[4096]{0:T(1024)} %scatter_custom_fusion.3) | copy-start | bytes 49156
  (47 other events, 729.4 us)
where the time goes:
time: 2090 us; the launch traced here: 2070 us
  local copies, waits for them, and re-layouts  1490 us (71%)
  other arithmetic  480 us (23%)
  matrix products  53.3 us (3%)
  starting transfers between devices  43 us (2%)
    gather x60, local copies, waits for them, and re-layouts, lateral(): jnp.take(extended, neighbors[which], axis=2) - fields_now  1280 us
    scatter-add x1, other arithmetic, per_device(): jax.ops.segment_sum(back_value.reshape(-1), column_ids, columns)  87.8 us
    scatter-add x1, other arithmetic, per_device(): jax.ops.segment_sum(remap_weight.reshape(-1), slot_flat, total_slots)  86.6 us
    scatter-add x1, other arithmetic, per_device(): jax.ops.segment_sum(back_weight.reshape(-1), column_ids, columns)  86.6 us
    scatter-add x1, other arithmetic, per_device(): jax.ops.segment_sum((remap_weight * sea_surface[None, :]).reshape(-1), sl...  86.6 us
    add x5, other arithmetic, lateral(): return fields_now + change  67.9 us
    gather x2, local copies, waits for them, and re-layouts, per_device(): jnp.take(fluxes, column_ids, axis=1).reshape(field_count, peers, slots)  60.1 us
    gather x8, local copies, waits for them, and re-layouts, per_device(): jnp.take(received, remap_slot[which], axis=1)  59.1 us
  transfers between devices with their start and end apart: 13, of which 1 were waited for; matrix products, arithmetic and copies ran while one was open for 39% of the time, Pallas kernels for 0%

commit v1 on v0

v1 whole, which is shorter than its diff:
```python
import numpy as np

import jax
import jax.numpy as jnp
from jax import lax
from jax.experimental import pallas as pl
from jax.experimental.pallas import tpu as pltpu
from jax.sharding import PartitionSpec as P

ASTEPS = 4
HA = 256
HO = 384
BLK = 256
WIDE = ASTEPS * HA
BF = jnp.bfloat16
F32 = jnp.float32
VMEM_BYTES = 56 * 1024 * 1024
AXES = ("sec", "blk")


def call(body, outs, *, in_specs=None, out_specs=None, scratch=(), flops=0, moved=0, aliases=None):
    vmem = pl.BlockSpec(memory_space=pltpu.VMEM)
    return pl.pallas_call(
        body,
        out_shape=outs,
        in_specs=in_specs,
        out_specs=jax.tree.map(lambda _: vmem, outs) if out_specs is None else out_specs,
        scratch_shapes=list(scratch),
        input_output_aliases=aliases or {},
        compiler_params=pltpu.CompilerParams(vmem_limit_bytes=VMEM_BYTES),
        cost_estimate=pl.CostEstimate(flops=flops, bytes_accessed=moved, transcendentals=0),
    )


def shape(dims, dtype=F32):
    return jax.ShapeDtypeStruct(dims, dtype)


def halves(x):
    high = x.astype(BF)
    return high, (x - high.astype(F32)).astype(BF)


def stacked(x):
    return jnp.concatenate(halves(x), axis=0)


def mm(a, b):
    return jnp.dot(a, b, preferred_element_type=F32)


def mm_t(a, b):
    return lax.dot_general(a, b, (((1,), (1,)), ((), ())), preferred_element_type=F32)


def product(x2, w2):
    rows = x2.shape[0] // 2
    wide = mm(x2, w2[0])
    return wide[:rows] + wide[rows:] + mm(x2[:rows], w2[1])


def iota(dims, axis):
    return lax.broadcasted_iota(jnp.int32, dims, axis)


def build_band(store, nbr, coef, halo):
    rows = BLK + 2 * halo
    count = nbr.shape[0]
    ids = [nbr[k : k + 1] for k in range(count)]
    cs = [coef[k : k + 1] for k in range(count)]
    rest = 1.0 - sum(cs[1:], cs[0])
    for k in range(count - 1, 0, -1):
        alive = jnp.ones_like(ids[k]) > 0
        for j in range(k):
            same = jnp.logical_and(ids[k] == ids[j], alive)
            cs[j] = cs[j] + jnp.where(same, cs[k], 0.0)
            alive = jnp.logical_and(alive, jnp.logical_not(same))
        ids[k] = jnp.where(alive, ids[k], -1)
    lanes = 128
    step = 16
    for half in range(BLK // lanes):
        at = slice(half * lanes, (half + 1) * lanes)
        wide_ids = [jnp.broadcast_to(i[:, at], (step, lanes)) for i in ids]
        wide_cs = [jnp.broadcast_to(c[:, at], (step, lanes)) for c in cs]
        own = iota((step, lanes), 1) + (half * lanes + halo)
        wide_rest = jnp.broadcast_to(rest[:, at], (step, lanes))
        base = iota((step, lanes), 0)
        for first in range(0, rows, step):
            if first + step <= half * lanes or first >= half * lanes + lanes + 2 * halo:
                zero = jnp.zeros((step, lanes), BF)
                store(first, step, at, zero, zero)
                continue
            here = base + first
            value = jnp.where(here == own, wide_rest, 0.0)
            for i, c in zip(wide_ids, wide_cs):
                value = jnp.where(here == i, c, value)
            store(first, step, at, *halves(value))


def one_hot(ids, rows):
    return jnp.where(iota((rows, ids.shape[1]), 0) == ids, 1.0, 0.0).astype(BF)


def fold_rows(x, height):
    total = x[:height]
    for first in range(height, x.shape[0], height):
        total = total + x[first : first + height]
    return total


def prepare_kernel(fields):
    def body(mix, omix, atm, sea, nbr, coef, bulk, surf, spread, code, y, yo, first, last, gains, vertical):
        la = mix.shape[0]
        columns = atm.shape[1]
        eye = iota((la, la), 0) == iota((la, la), 1)
        step = mix[...] + jnp.where(eye, 1.0, 0.0)

        def dot(a, b):
            return jnp.dot(a, b, precision=lax.Precision.HIGHEST, preferred_element_type=F32)

        def col(r, same):
            return jnp.sum(jnp.where(same, r, 0.0), axis=1, keepdims=True)

        def row(c, same):
            return jnp.sum(jnp.where(same, c, 0.0), axis=0, keepdims=True)

        twice = dot(step, step)
        fourth = dot(twice, twice)
        rows_up = [step[la - 1 : la, :]]
        cols_up = [step[:, la - 1 : la]]
        for _ in range(ASTEPS - 2):
            rows_up.append(jnp.sum(step * col(rows_up[-1], eye), axis=0, keepdims=True))
        for _ in range(ASTEPS - 1):
            cols_up.append(jnp.sum(step * row(cols_up[-1], eye), axis=1, keepdims=True))
        slot = iota((fields * ASTEPS, 128), 0) // fields
        lane = iota((fields * ASTEPS, 128), 1)
        value = jnp.zeros((fields * ASTEPS, 128), F32)
        for s in range(1, ASTEPS + 1):
            column = jnp.where(slot == s - 1, 1.0, 0.0)
            for j in range(1, ASTEPS):
                column = jnp.where(slot == s - 1 + j, rows_up[j - 1][:, la - 1 : la], column)
            value = jnp.where(lane == s - 1, column, value)
        gains[...] = value

        tall = jnp.concatenate([fourth] * fields, axis=0)
        spreaded = dot(tall, spread[...])
        filled = jnp.where(code[...] == 1, spreaded, 0.0)
        for m in range(ASTEPS):
            tall = jnp.concatenate([cols_up[ASTEPS - 1 - m]] * fields, axis=0)
            filled = jnp.where(code[...] == 2 + m, tall, filled)
        vertical[...] = stacked(filled)

        weights = [jnp.broadcast_to(col(r, eye), (la, 128)) for r in rows_up]
        lo = omix.shape[0]
        sea_eye = iota((lo, lo), 0) == iota((lo, lo), 1)
        sea_row = omix[0:1, :] + jnp.where(iota((1, lo), 1) == 0, 1.0, 0.0)
        sea_weight = jnp.broadcast_to(col(sea_row, sea_eye), (lo, 128))
        for start in range(0, columns, 128):
            at = slice(start, start + 128)
            for f in range(fields):
                x = atm[f * la : (f + 1) * la, at]
                y[f : f + 1, at] = x[la - 1 : la]
                for k in range(1, ASTEPS):
                    y[k * fields + f : k * fields + f + 1, at] = jnp.sum(
                        x * weights[k - 1], axis=0, keepdims=True
                    )
            yo[:, at] = jnp.sum(sea[:, at] * sea_weight, axis=0, keepdims=True)
        for target, at in ((first, slice(0, WIDE)), (last, slice(columns - WIDE, columns))):
            target[0:16, :] = y[:, at]
            target[16:22, :] = nbr[:, at].astype(F32)
            target[22:28, :] = coef[:, at]
            target[28:32, :] = bulk[:, at]
            target[32:36, :] = surf[:, at]
            target[36:37, :] = yo[:, at]
            target[37:40, :] = jnp.zeros((3, WIDE), F32)

    return body


def interior_kernel(atm, nbr, coef, band, kept, mid, w, sa, sb, sems):
    blocks = atm.shape[1] // BLK

    def out_copy(b):
        return pltpu.make_async_copy(w.at[b], band.at[b + ASTEPS - 1], sems.at[b])

    def build(b, _):
        at = pl.ds(pl.multiple_of(b * BLK, BLK), BLK)

        def store(first, step, lanes, high, low):
            w[b, 0, first : first + step, lanes] = high
            w[b, 1, first : first + step, lanes] = low

        build_band(store, nbr[:, at] - b * BLK, coef[:, at], HA)
        sa[b] = stacked(atm[:, at])
        out_copy(b).start()
        return 0

    lax.fori_loop(0, blocks, build, 0)

    def advance(source, target, shift):
        def one(b, _):
            x2 = jnp.concatenate([source[b - 1], source[b], source[b + 1]], axis=1)
            target[b - shift] = stacked(product(x2, (w[b, 0], w[b, 1])))
            return 0

        return one

    buffers = (sa, sb)
    for s in range(1, ASTEPS + 1):
        source = buffers[(s - 1) % 2]
        if s == ASTEPS:
            lax.fori_loop(s, blocks - s, advance(source, mid, s), 0)
        else:
            target = buffers[s % 2]
            lax.fori_loop(s, blocks - s, advance(source, target, 0), 0)
            for i, b in enumerate((s, s + 1, blocks - 2 - s, blocks - 1 - s)):
                kept[(s - 1) * 4 + i] = target[b]

    def finish(b, _):
        out_copy(b).wait()
        return 0

    lax.fori_loop(0, blocks, finish, 0)


def surface_kernel(y, before, after, bulk, surf, gains, band_in, band, q, w, sa, sb, bulks, surfs, tmp, sems):
    blocks = y.shape[1] // BLK
    columns = y.shape[1]
    fields = bulk.shape[0]
    total = blocks + 2 * ASTEPS

    def in_copy(b):
        return pltpu.make_async_copy(band_in.at[b], w.at[b], sems.at[b])

    def start(b, _):
        in_copy(b).start()
        return 0

    lax.fori_loop(ASTEPS - 1, ASTEPS - 1 + blocks, start, 0)

    halo_blocks = list(range(ASTEPS)) + list(range(ASTEPS + blocks, total))
    outs = []
    for e in halo_blocks:
        pack = before if e < ASTEPS else after
        local = e if e < ASTEPS else e - ASTEPS - blocks
        at = slice(local * BLK, (local + 1) * BLK)
        sa[e] = stacked(pack[0:16, at])
        bulks[e] = jnp.concatenate([pack[28:32, at]] * ASTEPS, axis=0)
        surfs[e] = jnp.concatenate([pack[32:36, at]] * ASTEPS, axis=0)
        if e in (0, total - 1):
            continue
        origin = local * BLK + (columns - WIDE if e < ASTEPS else 0)

        def store(first, step, lanes, high, low, e=e):
            tmp[0, first : first + step, lanes] = high
            tmp[1, first : first + step, lanes] = low

        build_band(store, pack[16:22, at].astype(jnp.int32) - origin, pack[22:28, at], HA)
        w[e - 1] = tmp[...]
        copy = pltpu.make_async_copy(w.at[e - 1], band.at[e - 1], sems.at[e - 1])
        copy.start()
        outs.append(copy)
    for e in range(ASTEPS, ASTEPS + blocks):
        at = slice((e - ASTEPS) * BLK, (e - ASTEPS + 1) * BLK)
        sa[e] = stacked(y[:, at])
        bulks[e] = jnp.concatenate([bulk[:, at]] * ASTEPS, axis=0)
        surfs[e] = jnp.concatenate([surf[:, at]] * ASTEPS, axis=0)

    slot = iota((fields * ASTEPS, BLK), 0) // fields
    buffers = (sa, sb)
    for s in range(1, ASTEPS + 1):
        source, target = buffers[(s - 1) % 2], buffers[s % 2]
        gain = gains[:, s - 1 : s]
        kept = jnp.where(slot == s - 1, 0.0, 1.0)

        def one(e, s=s, source=source, target=target, gain=gain, kept=kept):
            x2 = jnp.concatenate([source[e - 1], source[e], source[e + 1]], axis=1)
            moved = product(x2, (w[e - 1, 0], w[e - 1, 1]))
            lowest = jnp.concatenate([moved[(s - 1) * fields : s * fields]] * ASTEPS, axis=0)
            flux = bulks[e] * (surfs[e] - lowest)
            value = moved * kept + gain * flux
            if s == ASTEPS:
                q[e - ASTEPS] = value
            else:
                target[e] = stacked(value)

        def own(e, _, s=s, one=one):
            if s == 1:
                in_copy(e - 1).wait()
            one(e)
            return 0

        for e in list(range(s, ASTEPS)) + list(range(ASTEPS + blocks, total - s)):
            one(e)
        lax.fori_loop(ASTEPS, ASTEPS + blocks, own, 0, unroll=2)
    for copy in outs:
        copy.wait()


def send_kernel(q, cols, out, table):
    fields = q.shape[1] // ASTEPS
    peers, slots = cols.shape
    blocks = q.shape[0]
    lanes = out.shape[2]
    parts = slots // lanes
    for b in range(blocks):
        table[b * fields : (b + 1) * fields, :] = q[b, (ASTEPS - 1) * fields :, :]
    rows = stacked(table[...])
    half = blocks * fields
    block_of_row = iota((half, slots), 0) // fields

    def one(p, _):
        ids = cols[pl.ds(p, 1), :]
        got = mm(rows, one_hot(ids & (BLK - 1), BLK))
        got = jnp.where(block_of_row == ids // BLK, got[:half] + got[half:], 0.0)
        got = fold_rows(got, 2 * fields)
        got = got[:fields] + got[fields:]
        out[p] = jnp.concatenate([got[:, i * lanes : (i + 1) * lanes] for i in range(parts)], axis=0)
        return 0

    lax.fori_loop(0, peers, one, 0, unroll=4)


def exchange_kernel(recv, slot, weight, yo, before, after, nbr, coef, omix, flux_out, back, rows, tiles, acc):
    peers, per_peer, lanes = recv.shape
    links, columns = slot.shape
    fields = flux_out.shape[0]
    parts = per_peer // fields
    highs = peers * parts
    table = highs * fields
    rows[...] = stacked(recv[...].reshape(table, lanes))
    acc[...] = jnp.zeros_like(acc)
    side = HO // 128
    own_tiles = columns // 128
    for t in range(own_tiles + 2 * side):
        if t < side:
            line = before[36:37, WIDE - HO + t * 128 : WIDE - HO + (t + 1) * 128]
        elif t < side + own_tiles:
            line = yo[:, (t - side) * 128 : (t - side + 1) * 128]
        else:
            line = after[36:37, (t - side - own_tiles) * 128 : (t - side - own_tiles + 1) * 128]
        tiles[t] = jnp.broadcast_to(line, (8, 128))
    corner = omix[0:1, 0:1] + 1.0
    high_of_row = iota((table, BLK), 0) // fields
    back_rows = iota((2 * highs, BLK), 0)
    inner = back_rows % (2 * parts)
    back_high = (back_rows // (2 * parts)) * parts + inner % parts
    pattern = iota((8, BLK), 0) % (2 * parts) // parts
    window = 1 + 2 * side
    neighbors = nbr.shape[0]

    def surface(j, half):
        t0 = j * (BLK // 128) + half
        at = pl.ds(pl.multiple_of(t0 * 128, 128), 128)
        pad = jnp.zeros((8 - neighbors, 128), jnp.int32)
        ids = jnp.concatenate([nbr[:, at] - t0 * 128, pad], axis=0)
        cs = jnp.concatenate([coef[:, at], pad.astype(F32)], axis=0)
        middle = tiles[t0 + side]
        got = jnp.zeros((8, 128), F32)
        for t in range(window):
            pick = jnp.take_along_axis(tiles[t0 + t], ids & 127, axis=1, mode="promise_in_bounds")
            got = jnp.where(ids // 128 == t, pick, got)
        return middle[0:1] + jnp.sum(cs * (got - middle), axis=0, keepdims=True)

    def one(j, _):
        at = pl.ds(pl.multiple_of(j * BLK, BLK), BLK)
        sea = jnp.concatenate([surface(j, h) for h in range(BLK // 128)], axis=1)
        ids = [slot[r : r + 1, at] for r in range(links)]
        ws = [weight[r : r + 1, at] for r in range(links)]
        hots = [one_hot(i & (lanes - 1), lanes) for i in ids]
        flux = jnp.zeros((2 * fields, BLK), F32)
        for r in range(links):
            got = mm(rows[...], hots[r])
            got = jnp.where(high_of_row == ids[r] // lanes, got[:table] + got[table:], 0.0)
            flux = flux + ws[r] * fold_rows(got, 2 * fields)
        flux = flux[:fields] + flux[fields:]
        flux_out[:, at] = flux
        sea = sea + corner * flux[0:1]
        left = []
        for r in range(links):
            both = jnp.where(pattern == 1, ws[r], ws[r] * sea)
            both = jnp.concatenate([both] * (2 * highs // 8), axis=0)
            left.append(stacked(jnp.where(back_high == ids[r] // lanes, both, 0.0)))
        sums = mm_t(jnp.concatenate(left, axis=1), jnp.concatenate(hots, axis=1))
        acc[...] += sums[: 2 * highs] + sums[2 * highs :]
        return 0

    lax.fori_loop(0, columns // BLK, one, 0)
    back[...] = acc[...].reshape(back.shape)


def settle_kernel(back, cols, surf, out, acc):
    peers, per_peer, lanes = back.shape
    parts = per_peer // 2
    blocks = surf.shape[0]
    acc[...] = jnp.zeros_like(acc)
    block_of_row = iota((blocks, lanes), 0)

    def one(d, _):
        left, hots = [], []
        for h in range(parts):
            ids = cols[pl.ds(d, 1), h * lanes : (h + 1) * lanes]
            mask = block_of_row == ids // BLK
            value = jnp.where(mask, back[d, h : h + 1, :], 0.0)
            scale = jnp.where(mask, back[d, parts + h : parts + h + 1, :], 0.0)
            left.append(stacked(jnp.concatenate([value, scale], axis=0)))
            hots.append(one_hot(ids & (BLK - 1), BLK))
        acc[...] += mm_t(jnp.concatenate(left, axis=1), jnp.concatenate(hots, axis=1))
        return 0

    lax.fori_loop(0, peers, one, 0, unroll=4)
    sums = acc[: 2 * blocks] + acc[2 * blocks :]
    out[...] = (surf[...] + sums[:blocks]) / (1.0 + sums[blocks:])


def edge_kernel(before, after, atm, kept, mid, q, vertical, band, out, w, sides, sa, sb, sems):
    blocks = q.shape[0]
    count = 2 * ASTEPS - 1
    total = blocks + 2 * ASTEPS
    copies = []
    for side in range(2):
        at = slice(0, 2 * BLK) if side == 0 else slice((blocks - 2) * BLK, blocks * BLK)
        copy = pltpu.make_async_copy(atm.at[:, at], sides.at[side], sems.at[2 * count + side])
        copy.start()
        copies.append(copy)
    for side in range(2):
        base = 0 if side == 0 else total - 2 - count
        for i in range(count):
            copy = pltpu.make_async_copy(band.at[base + i], w.at[side * count + i], sems.at[side * count + i])
            copy.start()
            copies.append(copy)
    for i in range(ASTEPS):
        at = slice(i * BLK, (i + 1) * BLK)
        sa[i] = stacked(before[:, at])
        sa[6 + 2 + i] = stacked(after[:, at])
    for copy in copies:
        copy.wait()
    for i in range(2):
        at = slice(i * BLK, (i + 1) * BLK)
        sa[ASTEPS + i] = stacked(sides[0, :, at])
        sa[6 + i] = stacked(sides[1, :, at])
    buffers = (sa, sb)
    for s in range(1, ASTEPS + 1):
        source, target = buffers[(s - 1) % 2], buffers[s % 2]
        last = s == ASTEPS

        def one(i, _, s=s, source=source, target=target, last=last):
            for side in range(2):
                base = 6 * side
                k = s - 1 + i if side == 0 else count + ASTEPS - s + i
                x2 = jnp.concatenate([source[base + i + d] for d in range(3)], axis=1)
                value = stacked(product(x2, (w[k, 0], w[k, 1])))
                target[base + i + (2 * side if not last else 0)] = value
            return 0

        lax.fori_loop(0, ASTEPS, one, 0)
        if not last:
            for i in range(2):
                target[ASTEPS + i] = kept[(s - 1) * 4 + i]
                target[6 + i] = kept[(s - 1) * 4 + 2 + i]
    rows = out.shape[0]
    final = buffers[ASTEPS % 2]

    def mixed(source, shift):
        def one(b, _):
            at = pl.ds(pl.multiple_of(b * BLK, BLK), BLK)
            qh, ql = halves(q[b])
            x2 = source[b - shift]
            high = jnp.concatenate([x2[:rows], qh], axis=0)
            low = jnp.concatenate([x2[rows:], ql], axis=0)
            wide = mm(vertical[...], high)
            out[:, at] = wide[:rows] + wide[rows:] + mm(vertical[:rows], low)
            return 0

        return one

    lax.fori_loop(0, ASTEPS, mixed(final, 0), 0)
    lax.fori_loop(ASTEPS, blocks - ASTEPS, mixed(mid, ASTEPS), 0)
    lax.fori_loop(blocks - ASTEPS, blocks, mixed(final, blocks - ASTEPS - 6), 0)


def ocean_kernel(ocean, before, after, nbr, coef, omix, flux, out, x2, w):
    levels = omix.shape[0]
    fields = flux.shape[0]
    columns = ocean.shape[1]
    blocks = columns // BLK
    eye = iota((levels, levels), 0) == iota((levels, levels), 1)
    step = omix[...] + jnp.where(eye, 1.0, 0.0)
    top = jnp.broadcast_to(step[:, 0:1], (levels, BLK))
    mix2 = stacked(step)

    def part(first, width):
        pieces = []
        for ref, begin, size in ((before, -HO, HO), (ocean, 0, columns), (after, columns, HO)):
            lo, hi = max(first, begin), min(first + width, begin + size)
            if lo < hi:
                pieces.append(ref[:, lo - begin : hi - begin])
        return pieces[0] if len(pieces) == 1 else jnp.concatenate(pieces, axis=1)

    for e in range((columns + 2 * HO) // BLK):
        x2[e] = stacked(part(e * BLK - HO, BLK))

    def one(b, _):
        at = pl.ds(pl.multiple_of(b * BLK, BLK), BLK)

        def store(first, size, lanes, high, low):
            w[0, first : first + size, lanes] = high
            w[1, first : first + size, lanes] = low

        build_band(store, nbr[:, at] - b * BLK, coef[:, at], HO)
        source = jnp.concatenate([x2[b + d] for d in range(1 + 2 * HO // BLK)], axis=1)
        moved = product(source, (w[0], w[1]))
        for f in range(fields):
            rows = slice(f * levels, (f + 1) * levels)
            high, low = halves(moved[rows])
            wide = mm(mix2, high)
            out[rows, at] = (
                wide[:levels] + wide[levels:] + mm(mix2[:levels], low) + top * flux[f : f + 1, at]
            )
        return 0

    lax.fori_loop(0, blocks, one, 0)


def after_all(value, *others):
    return lax.optimization_barrier((value, *others))[0]


def per_device(
    atm_state,
    atm_surface,
    bulk_coef,
    atm_nbr,
    atm_nbr_coef,
    atm_mix,
    ocean_state,
    ocean_nbr,
    ocean_nbr_coef,
    ocean_mix,
    send_cols,
    remap_slot,
    remap_weight,
):
    fields, la, columns = atm_state.shape
    lo, cells = ocean_state.shape[1:]
    blocks = columns // BLK
    rows = fields * la
    states = fields * ASTEPS
    picked = send_cols[0]
    peers, slots = picked.shape
    lanes = min(BLK, slots)
    parts = slots // lanes
    atm = atm_state.reshape(rows, columns)
    ocean = ocean_state.reshape(fields * lo, cells)
    depth = lax.axis_size(AXES)
    up = [(i, (i + 1) % depth) for i in range(depth)]
    down = [(j, i) for i, j in up]
    window = BLK + 2 * HA
    vmem = pl.BlockSpec(memory_space=pltpu.VMEM)
    anywhere = pl.BlockSpec(memory_space=pl.ANY)

    depth_k = rows + states
    r_of, c_of = np.arange(rows)[:, None], np.arange(depth_k)[None, :]
    code = np.where(
        c_of < rows,
        (c_of // la == r_of // la) * 1,
        ((c_of - rows) % fields == r_of // la) * (2 + (c_of - rows) // fields),
    ).astype(np.int32)
    spread = ((c_of % la == np.arange(la)[:, None]) & (c_of < rows)).astype(np.float32)

    y, yo, first, last, gains, vertical = call(
        prepare_kernel(fields),
        (
            shape((states, columns)),
            shape((1, columns)),
            shape((40, WIDE)),
            shape((40, WIDE)),
            shape((states, 128)),
            shape((2 * rows, depth_k), BF),
        ),
        in_specs=[vmem] * 10,
        flops=10**8,
        moved=8 * 10**6,
    )(
        atm_mix,
        ocean_mix,
        atm,
        ocean[:lo],
        atm_nbr,
        atm_nbr_coef,
        bulk_coef,
        atm_surface,
        jnp.asarray(spread),
        jnp.asarray(code),
    )
    pack_before = lax.ppermute(last, AXES, up)
    pack_after = lax.ppermute(first, AXES, down)

    later, later_sea = lax.optimization_barrier((atm, ocean, first, last))[:2]
    atm_before = lax.ppermute(later[:, columns - WIDE :], AXES, up)
    atm_after = lax.ppermute(later[:, :WIDE], AXES, down)
    sea_before = lax.ppermute(later_sea[:, cells - HO :], AXES, up)
    sea_after = lax.ppermute(later_sea[:, :HO], AXES, down)

    band, kept, mid = call(
        interior_kernel,
        (
            shape((blocks + 2 * ASTEPS - 2, 2, window, BLK), BF),
            shape((4 * (ASTEPS - 1), 2 * rows, BLK), BF),
            shape((blocks - 2 * ASTEPS, 2 * rows, BLK), BF),
        ),
        in_specs=[vmem] * 3,
        out_specs=(anywhere, vmem, vmem),
        scratch=[
            pltpu.VMEM((blocks, 2, window, BLK), BF),
            pltpu.VMEM((blocks, 2 * rows, BLK), BF),
            pltpu.VMEM((blocks, 2 * rows, BLK), BF),
            pltpu.SemaphoreType.DMA((blocks,)),
        ],
        flops=15 * 10**9,
        moved=25 * 10**6,
    )(atm, atm_nbr, atm_nbr_coef)

    total = blocks + 2 * ASTEPS
    band, q = call(
        surface_kernel,
        (shape(band.shape, BF), shape((blocks, states, BLK))),
        in_specs=[vmem] * 6 + [anywhere],
        out_specs=(anywhere, vmem),
        scratch=[
            pltpu.VMEM((total - 2, 2, window, BLK), BF),
            pltpu.VMEM((total, 2 * states, BLK), BF),
            pltpu.VMEM((total, 2 * states, BLK), BF),
            pltpu.VMEM((total, states, BLK), F32),
            pltpu.VMEM((total, states, BLK), F32),
            pltpu.VMEM((2, window, BLK), BF),
            pltpu.SemaphoreType.DMA((total - 2,)),
        ],
        aliases={6: 0},
        flops=10 * 10**9,
        moved=15 * 10**6,
    )(y, pack_before, pack_after, bulk_coef, atm_surface, gains, band)

    outgoing = call(
        send_kernel,
        shape((peers, parts * fields, lanes)),
        in_specs=[vmem] * 2,
        scratch=[pltpu.VMEM((blocks * fields, BLK), F32)],
        flops=5 * 10**9,
        moved=10**6,
    )(q, picked)
    received = lax.all_to_all(outgoing, AXES, split_axis=0, concat_axis=0, tiled=True)

    atm_final = call(
        edge_kernel,
        shape((rows, columns)),
        in_specs=[
            vmem,
            vmem,
            anywhere,
            vmem,
            vmem,
            vmem,
            vmem,
            anywhere,
        ],
        scratch=[
            pltpu.VMEM((2 * (2 * ASTEPS - 1), 2, window, BLK), BF),
            pltpu.VMEM((2, rows, 2 * BLK), F32),
            pltpu.VMEM((12, 2 * rows, BLK), BF),
            pltpu.VMEM((12, 2 * rows, BLK), BF),
            pltpu.SemaphoreType.DMA((4 * ASTEPS,)),
        ],
        flops=12 * 10**9,
        moved=25 * 10**6,
    )(atm_before, atm_after, atm, kept, mid, q, vertical, band)

    flux, back = call(
        exchange_kernel,
        (shape((fields, cells)), shape((peers, 2 * parts, lanes))),
        in_specs=[vmem] * 9,
        scratch=[
            pltpu.VMEM((2 * peers * parts * fields, lanes), BF),
            pltpu.VMEM((cells // 128 + 2 * HO // 128, 8, 128), F32),
            pltpu.VMEM((2 * peers * parts, lanes), F32),
        ],
        flops=8 * 10**9,
        moved=10**6,
    )(received, remap_slot, remap_weight, yo, pack_before, pack_after, ocean_nbr, ocean_nbr_coef, ocean_mix)
    returned = lax.all_to_all(back, AXES, split_axis=0, concat_axis=0, tiled=True)

    ocean_final = call(
        ocean_kernel,
        shape((fields * lo, cells)),
        in_specs=[vmem] * 7,
        scratch=[
            pltpu.VMEM(((cells + 2 * HO) // BLK, 2 * fields * lo, BLK), BF),
            pltpu.VMEM((2, BLK + 2 * HO, BLK), BF),
        ],
        flops=12 * 10**9,
        moved=12 * 10**6,
    )(ocean, sea_before, sea_after, ocean_nbr, ocean_nbr_coef, ocean_mix, flux)

    surface_temp = call(
        settle_kernel,
        shape((blocks, BLK)),
        in_specs=[vmem] * 3,
        scratch=[pltpu.VMEM((4 * blocks, BLK), F32)],
        flops=2 * 10**9,
        moved=10**6,
    )(returned, picked, atm_surface[0].reshape(blocks, BLK))

    return (
        atm_final.reshape(fields, la, columns),
        ocean_final.reshape(fields, lo, cells),
        surface_temp.reshape(columns),
    )


def solution(mesh):
    placed = (
        P(None, None, AXES),
        P(None, AXES),
        P(None, AXES),
        P(None, AXES),
        P(None, AXES),
        P(),
        P(None, None, AXES),
        P(None, AXES),
        P(None, AXES),
        P(),
        P(AXES, None, None),
        P(None, AXES),
        P(None, AXES),
    )
    return jax.shard_map(
        per_device,
        mesh=mesh,
        in_specs=placed,
        out_specs=(P(None, None, AXES), P(None, None, AXES), P(AXES)),
        check_vma=False,
    )
```

time: 2090 us -> 218 us (0.10)
  local copies, waits for them, and re-layouts: 1490 us -> 9.8 us
  other arithmetic: 480 us -> 0 us
  Pallas kernels: 0 us -> 152 us
  matrix products: 53.3 us -> 0 us
  waiting for transfers between devices: 8.18 us -> 31.6 us
    gather x70 -> x0, local copies, waits for them, and re-layouts: 1400 us -> none  [the longest x60 1280 us: lateral(): jnp.take(extended, neighbors[which], axis=2) - fields_now]
    scatter-add x4 -> x0, other arithmetic: 348 us -> none  [the longest x1 87.8 us: per_device(): jax.ops.segment_sum(back_value.reshape(-1), column_ids, columns)]
    pallas_call x0 -> x8, Pallas kernels: none -> 152 us  [the longest x1 36.5 us: per_device(): call(interior_kernel, (shape((blocks + 2 * ASTEPS - 2, 2, window, BLK), B...]
    add x11 -> x0, other arithmetic: 70.5 us -> none  [the longest x5 67.9 us: lateral(): return fields_now + change]
    dot_general x5 -> x0, matrix products: 53.3 us -> none  [column_mix(): jnp.einsum('lm,fmc->flc', mixing, fields_now, precision=lax.Precision.HIG...]
    concatenate x5 -> x0, other arithmetic: 48.4 us -> none  [extended_2(): shard = jnp.concatenate([before, shard, after], axis=dim)]
    unnamed x121 -> x7, local copies, waits for them, and re-layouts: 33.2 us -> 2.69 us
    concatenate x3 -> x0, local copies, waits for them, and re-layouts: 29.4 us -> none  [extended_2(): shard = jnp.concatenate([before, shard, after], axis=dim)]
  transfers between devices with their start and end apart: 13 -> 8, of which waited for: 1 -> 1; matrix products, arithmetic and copies ran while one was open for 39% -> 3% of each run, Pallas kernels for 0% -> 42%
where the time goes in v1:
time: 218 us; the launch traced here: 217 us
  Pallas kernels  152 us (70%)
  waiting for transfers between devices  31.6 us (14%)
  starting transfers between devices  23.1 us (11%)
  local copies, waits for them, and re-layouts  9.8 us (4%)
    pallas_call x1, Pallas kernels, per_device(): call(interior_kernel, (shape((blocks + 2 * ASTEPS - 2, 2, window, BLK), B...  36.5 us
    all_to_all x1, waiting for transfers between devices, per_device(): lax.all_to_all(outgoing, AXES, split_axis=0, concat_axis=0, tiled=True)  31.6 us
    pallas_call x1, Pallas kernels, per_device(): call(ocean_kernel, shape((fields * lo, cells)), in_specs=[vmem] * 7, scra...  31.4 us
    pallas_call x1, Pallas kernels, per_device(): call(edge_kernel, shape((rows, columns)), in_specs=[vmem, vmem, anywhere,...  30.4 us
    pallas_call x1, Pallas kernels, per_device(): call(surface_kernel, (shape(band.shape, BF), shape((blocks, states, BLK))...  20.5 us
    pallas_call x1, Pallas kernels, per_device(): call(exchange_kernel, (shape((fields, cells)), shape((peers, 2 * parts, l...  17.6 us
    pallas_call x1, Pallas kernels, per_device(): call(prepare_kernel(fields), (shape((states, columns)), shape((1, columns...  6.29 us
    ppermute x1, starting transfers between devices, per_device(): atm_after = lax.ppermute(later[:, :WIDE], AXES, down)  5.33 us
  transfers between devices with their start and end apart: 8, of which 1 were waited for; matrix products, arithmetic and copies ran while one was open for 3% of the time, Pallas kernels for 42%

profile of v1, /device:TPU:0, one launch (start us, length us, event | category | flops | bytes accessed | tf_op | source)
XLA Modules:
  0.0 217.5 jit_solution(9327532801099833274)
XLA Ops:
  0.6 2.5 %slice_bitcast_fusion.sea = f32[80,4096]{1,0:T(8,128)} fusion(f32[4,80,4096]{2,1,0:T(8,128)} %param.21), kind=kLoop, calls=%fused_computation | loop fusion | bytes 2621440 | tf_op jit(solution)/shard_map/slice | solution.py:588
  3.1 6.3 %shard_map.166 = (f32[16,4096]{1,0:T(8,128)}, f32[1,4096]{1,0:T(1,128)}, f32[40,1024]{1,0:T(8,128)}, f32[40,1024]{1,0:T(8,128)}, f32[16,128]{1,0:T(8,128)}, /*index=5*/bf16[576,304]{1,0:T(8,128)(2,1)}) custom-call(f32[72,72]{1,0:T(8,128)} %mix.1, f32[80,80]{1,0:T(8,128)} %omix.5, f32[288,4096]{1,0:T(8,128)} %bitcast.9, f32[80,4096]{1,0:T(8,128)} %slice_bitcast_fusion.sea, ...), custom_call_target="tpu_custom_call" | custom-call | flops 100000000 | bytes 8000000 | tf_op jit(solution)/shard_map/pallas_call | solution.py:571
  9.4 2.9 %collective-permute-start.2 = (f32[40,1024]{1,0:T(8,128)}, f32[40,1024]{1,0:T(8,128)S(1)}, u32[]{:S(2)}, u32[]{:S(2)}) collective-permute-start(f32[40,1024]{1,0:T(8,128)} %get-tuple-element.19), channel_id=1, source_target_pairs={{0,1},{1,2},{2,3},{3,4},{4,5},{5,6},{6,7},{7,8},{8,9},{9,10},{10,1... | collective-permute-start | bytes 491528 | tf_op jit(solution)/shard_map/ppermute | solution.py:596
  12.3 3.5 %collective-permute-start.3 = (f32[40,1024]{1,0:T(8,128)}, f32[40,1024]{1,0:T(8,128)S(1)}, u32[]{:S(2)}, u32[]{:S(2)}) collective-permute-start(f32[40,1024]{1,0:T(8,128)} %get-tuple-element.18), channel_id=1, source_target_pairs={{1,0},{2,1},{3,2},{4,3},{5,4},{6,5},{7,6},{8,7},{9,8},{10,9},{11,1... | collective-permute-start | bytes 491528 | tf_op jit(solution)/shard_map/ppermute | solution.py:597
  15.8 36.5 %shard_map.167 = (bf16[22,2,768,256]{3,2,1,0:T(8,128)(2,1)}, bf16[12,576,256]{2,1,0:T(8,128)(2,1)}, bf16[8,576,256]{2,1,0:T(8,128)(2,1)}) custom-call(f32[288,4096]{1,0:T(8,128)} %bitcast.10, s32[6,4096]{1,0:T(8,128)} %nbr.5, f32[6,4096]{1,0:T(8,128)} %coef.5), custom_call_target="tpu_custom_call" | custom-call | flops 15000000512 | bytes 25000000 | tf_op jit(solution)/shard_map/pallas_call | solution.py:605
  52.4 0.6 copy-done.1
  53.1 20.5 %shard_map.168 = (bf16[22,2,768,256]{3,2,1,0:T(8,128)(2,1)}, f32[16,16,256]{2,1,0:T(8,128)}) custom-call(f32[16,4096]{1,0:T(8,128)} %get-tuple-element.23.y, f32[40,1024]{1,0:T(8,128)} %copy-done.1, f32[40,1024]{1,0:T(8,128)} %copy-done.2, f32[4,4096]{1,0:T(4,128)} %bulk.3, f32[4,4096]{1,0:T(4,128)} %surf.3, ...), custom_call_target="tpu_custom_call", output_to_operand_aliasing={{0}: (6, {})} | custom-call | flops 10000000000 | bytes 15000000 | tf_op jit(solution)/shard_map/pallas_call | solution.py:625
  73.6 4.2 %shard_map.170 = f32[32,8,256]{2,1,0:T(8,128)} custom-call(f32[16,16,256]{2,1,0:T(8,128)} %get-tuple-element.26.q, s32[32,512]{1,0:T(8,128)} %bitcast.17), custom_call_target="tpu_custom_call" | custom-call | flops 5000000000 | bytes 1000000 | tf_op jit(solution)/shard_map/pallas_call | solution.py:644
  77.8 3.3 %all-to-all-start = ((f32[32,8,256]{2,1,0:T(8,128)}), f32[32,8,256]{2,1,0:T(8,128)}, u32[]{:S(2)}, u32[]{:S(2)}) async-start(f32[32,8,256]{2,1,0:T(8,128)} %shard_map.170), calls=%async_computation | async-start | bytes 524288 | tf_op jit(solution)/shard_map/all_to_all | solution.py:652
  81.2 1.2 fusion
  82.4 1.6 collective-permute-start.4
  84.0 3.8 %collective-permute-start.5 = (f32[320,384]{1,0:T(8,128)S(1)}, f32[320,384]{1,0:T(8,128)}, u32[]{:S(2)}, u32[]{:S(2)}) collective-permute-start(f32[320,384]{1,0:T(8,128)S(1)} %get-tuple-element.33), channel_id=1, source_target_pairs={{1,0},{2,1},{3,2},{4,3},{5,4},{6,5},{7,6},{8,7},{9,8},{10,9},{11,1... | collective-permute-start | bytes 1474568 | tf_op jit(solution)/shard_map/ppermute | solution.py:603
  87.8 1.9 fusion.1
  89.8 5.3 %collective-permute-start.1 = (f32[288,1024]{1,0:T(8,128)S(1)}, f32[288,1024]{1,0:T(8,128)}, u32[]{:S(2)}, u32[]{:S(2)}) collective-permute-start(f32[288,1024]{1,0:T(8,128)S(1)} %get-tuple-element.35), channel_id=1, source_target_pairs={{1,0},{2,1},{3,2},{4,3},{5,4},{6,5},{7,6},{8,7},{9,8},{10,9},{11,1... | collective-permute-start | bytes 3538952 | tf_op jit(solution)/shard_map/ppermute | solution.py:601
  95.1 0.9 slice_reduce_fusion
  96.0 0.6 reshape_squeeze.3.surf
  96.6 31.6 %all-to-all-done.recv = f32[32,8,256]{2,1,0:T(8,128)} async-done(((f32[32,8,256]{2,1,0:T(8,128)}), f32[32,8,256]{2,1,0:T(8,128)}, u32[]{:S(2)}, u32[]{:S(2)}) %all-to-all-start) | async-done | bytes 262176 | tf_op jit(solution)/shard_map/all_to_all | solution.py:652
  128.2 17.6 %shard_map.171 = (f32[4,4096]{1,0:T(4,128)}, f32[32,4,256]{2,1,0:T(4,128)}) custom-call(f32[32,8,256]{2,1,0:T(8,128)} %all-to-all-done.recv, s32[4,4096]{1,0:T(4,128)} %slot.1, f32[4,4096]{1,0:T(4,128)} %weight.1, f32[1,4096]{1,0:T(1,128)} %get-tuple-element.30.yo, f32[40,1024]{1,0:T(8,128)} %copy-done.1, f32[40,1024]{1,0:T(8,128)} %copy-done.2, ...), custom_call_target="tpu_custom_call" | custom-call | flops 8000000000 | bytes 1000000 | tf_op jit(solution)/shard_map/pallas_call | solution.py:678
  145.7 2.6 %all-to-all-start.1 = ((f32[32,4,256]{2,1,0:T(4,128)}), f32[32,4,256]{2,1,0:T(4,128)S(1)}, u32[]{:S(2)}, u32[]{:S(2)}) async-start(f32[32,4,256]{2,1,0:T(4,128)} %get-tuple-element.32), calls=%async_computation.1 | async-start | bytes 262144 | tf_op jit(solution)/shard_map/all_to_all | solution.py:690
  148.3 31.4 %shard_map.172 = f32[320,4096]{1,0:T(8,128)} custom-call(f32[320,4096]{1,0:T(8,128)} %bitcast.14, f32[320,384]{1,0:T(8,128)} %collective-permute-done.4.before, f32[320,384]{1,0:T(8,128)} %collective-permute-done.5.after, s32[6,4096]{1,0:T(8,128)} %nbr.7, f32[6,4096]{1,0:T(8,128)} %coef.7, f32[80,80]{1,0:T(8,128)} %omix.5, f32[4,4096]{1,0:T(4,128)} %get-tuple-element.31.flux), custom_call_target="tpu_custom_call" | custom-call | flops 12000000000 | bytes 12000000 | tf_op jit(solution)/shard_map/pallas_call | solution.py:692
  179.8 0.7 copy-done
  180.4 5.1 %shard_map.173 = f32[16,256]{1,0:T(8,128)} custom-call(f32[32,4,256]{2,1,0:T(4,128)} %copy-done, s32[32,512]{1,0:T(8,128)} %bitcast.18, f32[16,256]{1,0:T(8,128)} %reshape_squeeze.3.surf), custom_call_target="tpu_custom_call" | custom-call | flops 2000000000 | bytes 1000000 | tf_op jit(solution)/shard_map/pallas_call | solution.py:704
  185.6 1.3 copy.19
  186.9 30.4 %shard_map.169 = f32[288,4096]{1,0:T(8,128)} custom-call(f32[288,1024]{1,0:T(8,128)} %collective-permute-done.before, f32[288,1024]{1,0:T(8,128)} %collective-permute-done.1.after, f32[288,4096]{1,0:T(8,128)} %bitcast.12, bf16[12,576,256]{2,1,0:T(8,128)(2,1)} %get-tuple-element.21.kept, bf16[8,576,256]{2,1,0:T(8,128)(2,1)} %get-tuple-element.22.mid, ...), custom_call_target="tpu_custom_call" | custom-call | flops 12000000000 | bytes 25000000 | tf_op jit(solution)/shard_map/pallas_call | solution.py:654
  (12 shorter events, 0.1 us)
Async XLA Ops:
  9.4 42.9 %collective-permute-start.2 = (f32[40,1024]{1,0:T(8,128)}, f32[40,1024]{1,0:T(8,128)S(1)}, u32[]{:S(2)}, u32[]{:S(2)}) collective-permute-start(f32[40,1024]{1,0:T(8,128)} %get-tuple-element.19), channel_id=1, source_target_pairs={{0,1},{1,2},{2,3},{3,4},{4,5},{5,6},{6,7},{7,8},{8,9},{9,10},{10,1... | collective-permute-start | bytes 491528 | tf_op jit(solution)/shard_map/ppermute | solution.py:596
  12.3 40.0 %collective-permute-start.3 = (f32[40,1024]{1,0:T(8,128)}, f32[40,1024]{1,0:T(8,128)S(1)}, u32[]{:S(2)}, u32[]{:S(2)}) collective-permute-start(f32[40,1024]{1,0:T(8,128)} %get-tuple-element.18), channel_id=1, source_target_pairs={{1,0},{2,1},{3,2},{4,3},{5,4},{6,5},{7,6},{8,7},{9,8},{10,9},{11,1... | collective-permute-start | bytes 491528 | tf_op jit(solution)/shard_map/ppermute | solution.py:597
  52.3 0.7 copy-start.1
  52.4 0.7 copy-start.2
  77.8 50.3 %all-to-all-start = ((f32[32,8,256]{2,1,0:T(8,128)}), f32[32,8,256]{2,1,0:T(8,128)}, u32[]{:S(2)}, u32[]{:S(2)}) async-start(f32[32,8,256]{2,1,0:T(8,128)} %shard_map.170), calls=%async_computation | async-start | bytes 524288 | tf_op jit(solution)/shard_map/all_to_all | solution.py:652
  82.4 65.9 %collective-permute-start.4 = (f32[320,384]{1,0:T(8,128)S(1)}, f32[320,384]{1,0:T(8,128)}, u32[]{:S(2)}, u32[]{:S(2)}) collective-permute-start(f32[320,384]{1,0:T(8,128)S(1)} %get-tuple-element.34), channel_id=1, source_target_pairs={{0,1},{1,2},{2,3},{3,4},{4,5},{5,6},{6,7},{7,8},{8,9},{9,10},{10,1... | collective-permute-start | bytes 1474568 | tf_op jit(solution)/shard_map/ppermute | solution.py:602
  84.0 64.3 %collective-permute-start.5 = (f32[320,384]{1,0:T(8,128)S(1)}, f32[320,384]{1,0:T(8,128)}, u32[]{:S(2)}, u32[]{:S(2)}) collective-permute-start(f32[320,384]{1,0:T(8,128)S(1)} %get-tuple-element.33), channel_id=1, source_target_pairs={{1,0},{2,1},{3,2},{4,3},{5,4},{6,5},{7,6},{8,7},{9,8},{10,9},{11,1... | collective-permute-start | bytes 1474568 | tf_op jit(solution)/shard_map/ppermute | solution.py:603
  89.7 97.2 %collective-permute-start = (f32[288,1024]{1,0:T(8,128)S(1)}, f32[288,1024]{1,0:T(8,128)}, u32[]{:S(2)}, u32[]{:S(2)}) collective-permute-start(f32[288,1024]{1,0:T(8,128)S(1)} %get-tuple-element.36), channel_id=1, source_target_pairs={{0,1},{1,2},{2,3},{3,4},{4,5},{5,6},{6,7},{7,8},{8,9},{9,10},{10,1... | collective-permute-start | bytes 3538952 | tf_op jit(solution)/shard_map/ppermute | solution.py:600
  89.8 97.1 %collective-permute-start.1 = (f32[288,1024]{1,0:T(8,128)S(1)}, f32[288,1024]{1,0:T(8,128)}, u32[]{:S(2)}, u32[]{:S(2)}) collective-permute-start(f32[288,1024]{1,0:T(8,128)S(1)} %get-tuple-element.35), channel_id=1, source_target_pairs={{1,0},{2,1},{3,2},{4,3},{5,4},{6,5},{7,6},{8,7},{9,8},{10,9},{11,1... | collective-permute-start | bytes 3538952 | tf_op jit(solution)/shard_map/ppermute | solution.py:601
  145.7 34.0 %all-to-all-start.1 = ((f32[32,4,256]{2,1,0:T(4,128)}), f32[32,4,256]{2,1,0:T(4,128)S(1)}, u32[]{:S(2)}, u32[]{:S(2)}) async-start(f32[32,4,256]{2,1,0:T(4,128)} %get-tuple-element.32), calls=%async_computation.1 | async-start | bytes 262144 | tf_op jit(solution)/shard_map/all_to_all | solution.py:690
  179.8 0.7 copy-start

commit v2 on v1

--- a/solution.py
+++ b/solution.py
@@ -18,7 +18,7 @@
 AXES = ("sec", "blk")
 
 
-def call(body, outs, *, in_specs=None, out_specs=None, scratch=(), flops=0, moved=0, aliases=None):
+def call(body, outs, *, in_specs=None, out_specs=None, scratch=(), flops=10**6, moved=10**4, aliases=None):
     vmem = pl.BlockSpec(memory_space=pltpu.VMEM)
     return pl.pallas_call(
         body,
@@ -177,30 +177,50 @@
     return body
 
 
-def interior_kernel(atm, nbr, coef, band, kept, mid, w, sa, sb, sems):
+def interior_kernel(atm, nbr, coef, band, kept, mid, w, wa, wb, sa, sb, sems):
     blocks = atm.shape[1] // BLK
-
-    def out_copy(b):
-        return pltpu.make_async_copy(w.at[b], band.at[b + ASTEPS - 1], sems.at[b])
-
-    def build(b, _):
+    sent = list(range(ASTEPS)) + list(range(blocks - ASTEPS, blocks))
+
+    def split(b, _):
         at = pl.ds(pl.multiple_of(b * BLK, BLK), BLK)
+        sa[b] = stacked(atm[:, at])
+        return 0
+
+    lax.fori_loop(0, blocks, split, 0, unroll=4)
+
+    def build(b, near):
+        at = pl.ds(pl.multiple_of(b * BLK, BLK), BLK)
 
         def store(first, step, lanes, high, low):
+            near[0, first : first + step, lanes] = high
+            near[1, first : first + step, lanes] = low
             w[b, 0, first : first + step, lanes] = high
             w[b, 1, first : first + step, lanes] = low
 
         build_band(store, nbr[:, at] - b * BLK, coef[:, at], HA)
-        sa[b] = stacked(atm[:, at])
-        out_copy(b).start()
+
+    def window(source, b):
+        return jnp.concatenate([source[b - 1], source[b], source[b + 1]], axis=1)
+
+    build(0, wb)
+    build(1, wa)
+
+    def first(i, _):
+        b = 2 * i + 1
+        build(b + 1, wb)
+        sb[b] = stacked(product(window(sa, b), (wa[0], wa[1])))
+        build(b + 2, wa)
+        sb[b + 1] = stacked(product(window(sa, b + 1), (wb[0], wb[1])))
         return 0
 
-    lax.fori_loop(0, blocks, build, 0)
+    lax.fori_loop(0, (blocks - 2) // 2, first, 0)
+    copies = [pltpu.make_async_copy(w.at[b], band.at[i], sems.at[i]) for i, b in enumerate(sent)]
+    for copy in copies:
+        copy.start()
 
     def advance(source, target, shift):
         def one(b, _):
-            x2 = jnp.concatenate([source[b - 1], source[b], source[b + 1]], axis=1)
-            target[b - shift] = stacked(product(x2, (w[b, 0], w[b, 1])))
+            target[b - shift] = stacked(product(window(source, b), (w[b, 0], w[b, 1])))
             return 0
 
         return one
@@ -209,92 +229,83 @@
     for s in range(1, ASTEPS + 1):
         source = buffers[(s - 1) % 2]
         if s == ASTEPS:
-            lax.fori_loop(s, blocks - s, advance(source, mid, s), 0)
+            lax.fori_loop(s, blocks - s, advance(source, mid, s), 0, unroll=2)
         else:
             target = buffers[s % 2]
-            lax.fori_loop(s, blocks - s, advance(source, target, 0), 0)
+            if s > 1:
+                lax.fori_loop(s, blocks - s, advance(source, target, 0), 0, unroll=2)
             for i, b in enumerate((s, s + 1, blocks - 2 - s, blocks - 1 - s)):
                 kept[(s - 1) * 4 + i] = target[b]
-
-    def finish(b, _):
-        out_copy(b).wait()
-        return 0
-
-    lax.fori_loop(0, blocks, finish, 0)
-
-
-def surface_kernel(y, before, after, bulk, surf, gains, band_in, band, q, w, sa, sb, bulks, surfs, tmp, sems):
-    blocks = y.shape[1] // BLK
+    for copy in copies:
+        copy.wait()
+
+
+def surface_kernel(y, before, after, nbr, coef, bulk, surf, gains, q, xa, xb, ids, cs, bulks, surfs):
     columns = y.shape[1]
     fields = bulk.shape[0]
-    total = blocks + 2 * ASTEPS
-
-    def in_copy(b):
-        return pltpu.make_async_copy(band_in.at[b], w.at[b], sems.at[b])
-
-    def start(b, _):
-        in_copy(b).start()
-        return 0
-
-    lax.fori_loop(ASTEPS - 1, ASTEPS - 1 + blocks, start, 0)
-
-    halo_blocks = list(range(ASTEPS)) + list(range(ASTEPS + blocks, total))
-    outs = []
-    for e in halo_blocks:
-        pack = before if e < ASTEPS else after
-        local = e if e < ASTEPS else e - ASTEPS - blocks
-        at = slice(local * BLK, (local + 1) * BLK)
-        sa[e] = stacked(pack[0:16, at])
-        bulks[e] = jnp.concatenate([pack[28:32, at]] * ASTEPS, axis=0)
-        surfs[e] = jnp.concatenate([pack[32:36, at]] * ASTEPS, axis=0)
-        if e in (0, total - 1):
-            continue
-        origin = local * BLK + (columns - WIDE if e < ASTEPS else 0)
-
-        def store(first, step, lanes, high, low, e=e):
-            tmp[0, first : first + step, lanes] = high
-            tmp[1, first : first + step, lanes] = low
-
-        build_band(store, pack[16:22, at].astype(jnp.int32) - origin, pack[22:28, at], HA)
-        w[e - 1] = tmp[...]
-        copy = pltpu.make_async_copy(w.at[e - 1], band.at[e - 1], sems.at[e - 1])
-        copy.start()
-        outs.append(copy)
-    for e in range(ASTEPS, ASTEPS + blocks):
-        at = slice((e - ASTEPS) * BLK, (e - ASTEPS + 1) * BLK)
-        sa[e] = stacked(y[:, at])
-        bulks[e] = jnp.concatenate([bulk[:, at]] * ASTEPS, axis=0)
-        surfs[e] = jnp.concatenate([surf[:, at]] * ASTEPS, axis=0)
-
-    slot = iota((fields * ASTEPS, BLK), 0) // fields
-    buffers = (sa, sb)
+    count = nbr.shape[0]
+    side = WIDE // 128
+    own = columns // 128
+    total = own + 2 * side
+    reach = HA // 128
+    for t in range(total):
+        if t < side or t >= side + own:
+            pack = before if t < side else after
+            local = t if t < side else t - side - own
+            at = slice(local * 128, (local + 1) * 128)
+            origin = local * 128 + (columns - WIDE if t < side else 0)
+            xa[t] = pack[0:16, at]
+            ids[t] = pack[16:22, at].astype(jnp.int32) - origin
+            cs[t] = pack[22:28, at]
+            bulks[t] = pack[28:32, at]
+            surfs[t] = pack[32:36, at]
+        else:
+            at = slice((t - side) * 128, (t - side + 1) * 128)
+            xa[t] = y[:, at]
+            ids[t] = nbr[:, at] - (t - side) * 128
+            cs[t] = coef[:, at]
+            bulks[t] = bulk[:, at]
+            surfs[t] = surf[:, at]
+
+    rows = fields * ASTEPS
+    slot = iota((rows, 128), 0) // fields
+    buffers = (xa, xb)
     for s in range(1, ASTEPS + 1):
         source, target = buffers[(s - 1) % 2], buffers[s % 2]
-        gain = gains[:, s - 1 : s]
+        gain = jnp.broadcast_to(gains[:, s - 1 : s], (rows, 128))
         kept = jnp.where(slot == s - 1, 0.0, 1.0)
 
-        def one(e, s=s, source=source, target=target, gain=gain, kept=kept):
-            x2 = jnp.concatenate([source[e - 1], source[e], source[e + 1]], axis=1)
-            moved = product(x2, (w[e - 1, 0], w[e - 1, 1]))
-            lowest = jnp.concatenate([moved[(s - 1) * fields : s * fields]] * ASTEPS, axis=0)
-            flux = bulks[e] * (surfs[e] - lowest)
-            value = moved * kept + gain * flux
+        def tile(t, s=s, source=source, gain=gain, kept=kept):
+            middle = source[t]
+            around = [source[t - reach + i] for i in range(2 * reach + 1)]
+            here, weights = ids[t], cs[t]
+            changes = []
+            for first in range(0, rows, 8):
+                change = jnp.zeros((8, 128), F32)
+                for k in range(count):
+                    at = jnp.broadcast_to(here[k : k + 1], (8, 128))
+                    got = jnp.zeros((8, 128), F32)
+                    for i, x in enumerate(around):
+                        pick = jnp.take_along_axis(
+                            x[first : first + 8], at & 127, axis=1, mode="promise_in_bounds"
+                        )
+                        got = jnp.where(at // 128 == i, pick, got)
+                    change = change + weights[k : k + 1] * (got - middle[first : first + 8])
+                changes.append(change)
+            moved = middle + jnp.concatenate(changes, axis=0)
+            flux = bulks[t] * (surfs[t] - moved[(s - 1) * fields : s * fields])
+            return moved * kept + gain * jnp.concatenate([flux] * ASTEPS, axis=0)
+
+        def pair(e, _, s=s, target=target, tile=tile):
+            left, right = tile(2 * e), tile(2 * e + 1)
             if s == ASTEPS:
-                q[e - ASTEPS] = value
+                q[e - ASTEPS] = jnp.concatenate([left, right], axis=1)
             else:
-                target[e] = stacked(value)
-
-        def own(e, _, s=s, one=one):
-            if s == 1:
-                in_copy(e - 1).wait()
-            one(e)
+                target[2 * e] = left
+                target[2 * e + 1] = right
             return 0
 
-        for e in list(range(s, ASTEPS)) + list(range(ASTEPS + blocks, total - s)):
-            one(e)
-        lax.fori_loop(ASTEPS, ASTEPS + blocks, own, 0, unroll=2)
-    for copy in outs:
-        copy.wait()
+        lax.fori_loop(s, total // 2 - s, pair, 0)
 
 
 def send_kernel(q, cols, out, table):
@@ -321,7 +332,7 @@
     lax.fori_loop(0, peers, one, 0, unroll=4)
 
 
-def exchange_kernel(recv, slot, weight, yo, before, after, nbr, coef, omix, flux_out, back, rows, tiles, acc):
+def exchange_kernel(recv, slot, weight, yo, before, after, nbr, coef, omix, flux_out, back, rows, tiles, hots, seas, acc):
     peers, per_peer, lanes = recv.shape
     links, columns = slot.shape
     fields = flux_out.shape[0]
@@ -362,37 +373,54 @@
             got = jnp.where(ids // 128 == t, pick, got)
         return middle[0:1] + jnp.sum(cs * (got - middle), axis=0, keepdims=True)
 
-    def one(j, _):
+    def base(j, _):
         at = pl.ds(pl.multiple_of(j * BLK, BLK), BLK)
-        sea = jnp.concatenate([surface(j, h) for h in range(BLK // 128)], axis=1)
-        ids = [slot[r : r + 1, at] for r in range(links)]
-        ws = [weight[r : r + 1, at] for r in range(links)]
-        hots = [one_hot(i & (lanes - 1), lanes) for i in ids]
+        seas[:, at] = jnp.concatenate([surface(j, h) for h in range(BLK // 128)], axis=1)
+        return 0
+
+    lax.fori_loop(0, columns // BLK, base, 0, unroll=2)
+
+    def arrive(j, _):
+        at = pl.ds(pl.multiple_of(j * BLK, BLK), BLK)
         flux = jnp.zeros((2 * fields, BLK), F32)
         for r in range(links):
-            got = mm(rows[...], hots[r])
-            got = jnp.where(high_of_row == ids[r] // lanes, got[:table] + got[table:], 0.0)
-            flux = flux + ws[r] * fold_rows(got, 2 * fields)
+            ids = slot[r : r + 1, at]
+            hot = one_hot(ids & (lanes - 1), lanes)
+            hots[j, :, r * BLK : (r + 1) * BLK] = hot
+            got = mm(rows[...], hot)
+            got = jnp.where(high_of_row == ids // lanes, got[:table] + got[table:], 0.0)
+            flux = flux + weight[r : r + 1, at] * fold_rows(got, 2 * fields)
         flux = flux[:fields] + flux[fields:]
         flux_out[:, at] = flux
-        sea = sea + corner * flux[0:1]
+        seas[:, at] += corner * flux[0:1]
+        return 0
+
+    lax.fori_loop(0, columns // BLK, arrive, 0, unroll=2)
+
+    def leave(j, _):
+        at = pl.ds(pl.multiple_of(j * BLK, BLK), BLK)
+        sea = seas[:, at]
         left = []
         for r in range(links):
-            both = jnp.where(pattern == 1, ws[r], ws[r] * sea)
-            both = jnp.concatenate([both] * (2 * highs // 8), axis=0)
-            left.append(stacked(jnp.where(back_high == ids[r] // lanes, both, 0.0)))
-        sums = mm_t(jnp.concatenate(left, axis=1), jnp.concatenate(hots, axis=1))
-        acc[...] += sums[: 2 * highs] + sums[2 * highs :]
+            ids, scale = slot[r : r + 1, at], weight[r : r + 1, at]
+            high, low = halves(jnp.where(pattern == 1, scale, scale * sea))
+            mask = back_high == ids // lanes
+            both = [
+                jnp.where(mask, jnp.concatenate([x.astype(F32)] * (2 * highs // 8), axis=0), 0.0).astype(BF)
+                for x in (high, low)
+            ]
+            left.append(jnp.concatenate(both, axis=0))
+        acc[...] += mm_t(jnp.concatenate(left, axis=1), hots[j])
         return 0
 
-    lax.fori_loop(0, columns // BLK, one, 0)
-    back[...] = acc[...].reshape(back.shape)
+    lax.fori_loop(0, columns // BLK, leave, 0, unroll=2)
+    back[...] = (acc[: 2 * highs] + acc[2 * highs :]).reshape(back.shape)
 
 
 def settle_kernel(back, cols, surf, out, acc):
     peers, per_peer, lanes = back.shape
     parts = per_peer // 2
-    blocks = surf.shape[0]
+    blocks = surf.shape[1] // BLK
     acc[...] = jnp.zeros_like(acc)
     block_of_row = iota((blocks, lanes), 0)
 
@@ -410,25 +438,42 @@
 
     lax.fori_loop(0, peers, one, 0, unroll=4)
     sums = acc[: 2 * blocks] + acc[2 * blocks :]
-    out[...] = (surf[...] + sums[:blocks]) / (1.0 + sums[blocks:])
-
-
-def edge_kernel(before, after, atm, kept, mid, q, vertical, band, out, w, sides, sa, sb, sems):
+    base = jnp.concatenate([surf[0:1, b * BLK : (b + 1) * BLK] for b in range(blocks)], axis=0)
+    value = (base + sums[:blocks]) / (1.0 + sums[blocks:])
+    for b in range(blocks):
+        for i in range(BLK // 128):
+            row = b * (BLK // 128) + i
+            out[row : row + 1, :] = value[b : b + 1, i * 128 : (i + 1) * 128]
+
+
+def edge_kernel(before, after, lists_before, lists_after, atm, kept, mid, q, vertical, band, out, w, sides, sa, sb, sems):
     blocks = q.shape[0]
     count = 2 * ASTEPS - 1
-    total = blocks + 2 * ASTEPS
+    halo = ASTEPS - 1
+    columns = blocks * BLK
     copies = []
     for side in range(2):
         at = slice(0, 2 * BLK) if side == 0 else slice((blocks - 2) * BLK, blocks * BLK)
         copy = pltpu.make_async_copy(atm.at[:, at], sides.at[side], sems.at[2 * count + side])
         copy.start()
         copies.append(copy)
-    for side in range(2):
-        base = 0 if side == 0 else total - 2 - count
-        for i in range(count):
-            copy = pltpu.make_async_copy(band.at[base + i], w.at[side * count + i], sems.at[side * count + i])
-            copy.start()
-            copies.append(copy)
+    for i in range(2 * ASTEPS):
+        copy = pltpu.make_async_copy(band.at[i], w.at[halo + i], sems.at[i])
+        copy.start()
+        copies.append(copy)
+    for i in range(halo):
+        for lists, local, origin, k in (
+            (lists_before, i + 1, columns - WIDE, i),
+            (lists_after, i, 0, halo + 2 * ASTEPS + i),
+        ):
+            at = slice(local * BLK, (local + 1) * BLK)
+
+            def store(first, step, lanes, high, low, k=k):
+                w[k, 0, first : first + step, lanes] = high
+                w[k, 1, first : first + step, lanes] = low
+
+            ids = lists[16:22, at].astype(jnp.int32) - (origin + local * BLK)
+            build_band(store, ids, lists[22:28, at], HA)
     for i in range(ASTEPS):
         at = slice(i * BLK, (i + 1) * BLK)
         sa[i] = stacked(before[:, at])
@@ -453,7 +498,7 @@
                 target[base + i + (2 * side if not last else 0)] = value
             return 0
 
-        lax.fori_loop(0, ASTEPS, one, 0)
+        lax.fori_loop(0, ASTEPS, one, 0, unroll=2)
         if not last:
             for i in range(2):
                 target[ASTEPS + i] = kept[(s - 1) * 4 + i]
@@ -474,12 +519,12 @@
 
         return one
 
-    lax.fori_loop(0, ASTEPS, mixed(final, 0), 0)
-    lax.fori_loop(ASTEPS, blocks - ASTEPS, mixed(mid, ASTEPS), 0)
-    lax.fori_loop(blocks - ASTEPS, blocks, mixed(final, blocks - ASTEPS - 6), 0)
-
-
-def ocean_kernel(ocean, before, after, nbr, coef, omix, flux, out, x2, w):
+    lax.fori_loop(0, ASTEPS, mixed(final, 0), 0, unroll=2)
+    lax.fori_loop(ASTEPS, blocks - ASTEPS, mixed(mid, ASTEPS), 0, unroll=2)
+    lax.fori_loop(blocks - ASTEPS, blocks, mixed(final, blocks - ASTEPS - 6), 0, unroll=2)
+
+
+def ocean_kernel(ocean, before, after, nbr, coef, omix, flux, out, x2, wa, wb):
     levels = omix.shape[0]
     fields = flux.shape[0]
     columns = ocean.shape[1]
@@ -500,7 +545,7 @@
     for e in range((columns + 2 * HO) // BLK):
         x2[e] = stacked(part(e * BLK - HO, BLK))
 
-    def one(b, _):
+    def build(b, w):
         at = pl.ds(pl.multiple_of(b * BLK, BLK), BLK)
 
         def store(first, size, lanes, high, low):
@@ -508,6 +553,9 @@
             w[1, first : first + size, lanes] = low
 
         build_band(store, nbr[:, at] - b * BLK, coef[:, at], HO)
+
+    def finish(b, w):
+        at = pl.ds(pl.multiple_of(b * BLK, BLK), BLK)
         source = jnp.concatenate([x2[b + d] for d in range(1 + 2 * HO // BLK)], axis=1)
         moved = product(source, (w[0], w[1]))
         for f in range(fields):
@@ -517,13 +565,18 @@
             out[rows, at] = (
                 wide[:levels] + wide[levels:] + mm(mix2[:levels], low) + top * flux[f : f + 1, at]
             )
+
+    build(0, wa)
+
+    def one(i, _):
+        b = 2 * i
+        build(b + 1, wb)
+        finish(b, wa)
+        build(jnp.minimum(b + 2, blocks - 1), wa)
+        finish(b + 1, wb)
         return 0
 
-    lax.fori_loop(0, blocks, one, 0)
-
-
-def after_all(value, *others):
-    return lax.optimization_barrier((value, *others))[0]
+    lax.fori_loop(0, blocks // 2, one, 0)
 
 
 def per_device(
@@ -579,8 +632,6 @@
             shape((2 * rows, depth_k), BF),
         ),
         in_specs=[vmem] * 10,
-        flops=10**8,
-        moved=8 * 10**6,
     )(
         atm_mix,
         ocean_mix,
@@ -605,7 +656,7 @@
     band, kept, mid = call(
         interior_kernel,
         (
-            shape((blocks + 2 * ASTEPS - 2, 2, window, BLK), BF),
+            shape((2 * ASTEPS, 2, window, BLK), BF),
             shape((4 * (ASTEPS - 1), 2 * rows, BLK), BF),
             shape((blocks - 2 * ASTEPS, 2 * rows, BLK), BF),
         ),
@@ -613,41 +664,36 @@
         out_specs=(anywhere, vmem, vmem),
         scratch=[
             pltpu.VMEM((blocks, 2, window, BLK), BF),
+            pltpu.VMEM((2, window, BLK), BF),
+            pltpu.VMEM((2, window, BLK), BF),
             pltpu.VMEM((blocks, 2 * rows, BLK), BF),
             pltpu.VMEM((blocks, 2 * rows, BLK), BF),
-            pltpu.SemaphoreType.DMA((blocks,)),
+            pltpu.SemaphoreType.DMA((2 * ASTEPS,)),
         ],
-        flops=15 * 10**9,
-        moved=25 * 10**6,
     )(atm, atm_nbr, atm_nbr_coef)
 
-    total = blocks + 2 * ASTEPS
-    band, q = call(
+    tiles = (columns + 2 * WIDE) // 128
+    count = atm_nbr.shape[0]
+    q = call(
         surface_kernel,
-        (shape(band.shape, BF), shape((blocks, states, BLK))),
-        in_specs=[vmem] * 6 + [anywhere],
-        out_specs=(anywhere, vmem),
+        shape((blocks, states, BLK)),
+        in_specs=[vmem] * 8,
         scratch=[
-            pltpu.VMEM((total - 2, 2, window, BLK), BF),
-            pltpu.VMEM((total, 2 * states, BLK), BF),
-            pltpu.VMEM((total, 2 * states, BLK), BF),
-            pltpu.VMEM((total, states, BLK), F32),
-            pltpu.VMEM((total, states, BLK), F32),
-            pltpu.VMEM((2, window, BLK), BF),
-            pltpu.SemaphoreType.DMA((total - 2,)),
+            pltpu.VMEM((tiles, states, 128), F32),
+            pltpu.VMEM((tiles, states, 128), F32),
+            pltpu.VMEM((tiles, count, 128), jnp.int32),
+            pltpu.VMEM((tiles, count, 128), F32),
+            pltpu.VMEM((tiles, fields, 128), F32),
+            pltpu.VMEM((tiles, fields, 128), F32),
         ],
-        aliases={6: 0},
-        flops=10 * 10**9,
-        moved=15 * 10**6,
-    )(y, pack_before, pack_after, bulk_coef, atm_surface, gains, band)
+    )(y, pack_before, pack_after, atm_nbr, atm_nbr_coef, bulk_coef, atm_surface, gains)
+    q, atm_before, atm_after = lax.optimization_barrier((q, atm_before, atm_after))
 
     outgoing = call(
         send_kernel,
         shape((peers, parts * fields, lanes)),
         in_specs=[vmem] * 2,
         scratch=[pltpu.VMEM((blocks * fields, BLK), F32)],
-        flops=5 * 10**9,
-        moved=10**6,
     )(q, picked)
     received = lax.all_to_all(outgoing, AXES, split_axis=0, concat_axis=0, tiled=True)
 
@@ -655,6 +701,8 @@
         edge_kernel,
         shape((rows, columns)),
         in_specs=[
+            vmem,
+            vmem,
             vmem,
             vmem,
             anywhere,
@@ -671,10 +719,9 @@
             pltpu.VMEM((12, 2 * rows, BLK), BF),
             pltpu.SemaphoreType.DMA((4 * ASTEPS,)),
         ],
-        flops=12 * 10**9,
-        moved=25 * 10**6,
-    )(atm_before, atm_after, atm, kept, mid, q, vertical, band)
-
+    )(atm_before, atm_after, pack_before, pack_after, atm, kept, mid, q, vertical, band)
+
+    received, sea_before, sea_after = lax.optimization_barrier((received, sea_before, sea_after))
     flux, back = call(
         exchange_kernel,
         (shape((fields, cells)), shape((peers, 2 * parts, lanes))),
@@ -682,10 +729,10 @@
         scratch=[
             pltpu.VMEM((2 * peers * parts * fields, lanes), BF),
             pltpu.VMEM((cells // 128 + 2 * HO // 128, 8, 128), F32),
-            pltpu.VMEM((2 * peers * parts, lanes), F32),
+            pltpu.VMEM((cells // BLK, lanes, remap_slot.shape[0] * BLK), BF),
+            pltpu.VMEM((1, cells), F32),
+            pltpu.VMEM((4 * peers * parts, lanes), F32),
         ],
-        flops=8 * 10**9,
-        moved=10**6,
     )(received, remap_slot, remap_weight, yo, pack_before, pack_after, ocean_nbr, ocean_nbr_coef, ocean_mix)
     returned = lax.all_to_all(back, AXES, split_axis=0, concat_axis=0, tiled=True)
 
@@ -696,19 +743,16 @@
         scratch=[
             pltpu.VMEM(((cells + 2 * HO) // BLK, 2 * fields * lo, BLK), BF),
             pltpu.VMEM((2, BLK + 2 * HO, BLK), BF),
+            pltpu.VMEM((2, BLK + 2 * HO, BLK), BF),
         ],
-        flops=12 * 10**9,
-        moved=12 * 10**6,
     )(ocean, sea_before, sea_after, ocean_nbr, ocean_nbr_coef, ocean_mix, flux)
 
     surface_temp = call(
         settle_kernel,
-        shape((blocks, BLK)),
+        shape((columns // 128, 128)),
         in_specs=[vmem] * 3,
         scratch=[pltpu.VMEM((4 * blocks, BLK), F32)],
-        flops=2 * 10**9,
-        moved=10**6,
-    )(returned, picked, atm_surface[0].reshape(blocks, BLK))
+    )(returned, picked, atm_surface)
 
     return (
         atm_final.reshape(fields, la, columns),

time: 218 us -> 250 us (1.15)
  waiting for transfers between devices: 31.6 us -> 71.7 us
  Pallas kernels: 152 us -> 143 us
  starting transfers between devices: 23.1 us -> 26.6 us
    ppermute x1, waiting for transfers between devices: 0.01 us -> 48.7 us  [per_device(): pack_before = lax.ppermute(last, AXES, up)]
    all_to_all x1, waiting for transfers between devices: 31.6 us -> 0.01 us  [per_device(): lax.all_to_all(outgoing, AXES, split_axis=0, concat_axis=0, tiled=True)]
    ppermute x1, waiting for transfers between devices: 0.01 us -> 19.1 us  [per_device(): sea_before = lax.ppermute(later_sea[:, cells - HO:], AXES, up)]
    pallas_call x4, Pallas kernels: 92.6 us -> 86.6 us  [the longest x1 30.2 us: per_device(): call(interior_kernel, (shape((2 * ASTEPS, 2, window, BLK), BF), shape((4...]
    pallas_call x1, Pallas kernels: 17.6 us -> 13.3 us  [per_device(): call(exchange_kernel, (shape((fields, cells)), shape((peers, 2 * parts, l...]
    ppermute x1, starting transfers between devices: 2.95 us -> 0.01 us  [per_device(): pack_before = lax.ppermute(last, AXES, up)]
    ppermute x1, starting transfers between devices: 0.06 us -> 2.99 us  [per_device(): atm_before = lax.ppermute(later[:, columns - WIDE:], AXES, up)]
  transfers between devices with their start and end apart: 8 -> 8, of which waited for: 1 -> 4; matrix products, arithmetic and copies ran while one was open for 3% -> 0% of each run, Pallas kernels for 42% -> 46%
where the time goes in v2:
time: 250 us
  Pallas kernels  143 us (57%)
  waiting for transfers between devices  71.7 us (29%)
  starting transfers between devices  26.6 us (11%)
  local copies, waits for them, and re-layouts  8.1 us (3%)
    ppermute x1, waiting for transfers between devices, per_device(): pack_before = lax.ppermute(last, AXES, up)  48.7 us
    pallas_call x1, Pallas kernels, per_device(): call(ocean_kernel, shape((fields * lo, cells)), in_specs=[vmem] * 7, scra...  32.3 us
    pallas_call x1, Pallas kernels, per_device(): call(interior_kernel, (shape((2 * ASTEPS, 2, window, BLK), BF), shape((4...  30.2 us
    pallas_call x1, Pallas kernels, per_device(): call(edge_kernel, shape((rows, columns)), in_specs=[vmem, vmem, vmem, vme...  27.3 us
    pallas_call x1, Pallas kernels, per_device(): call(surface_kernel, shape((blocks, states, BLK)), in_specs=[vmem] * 8, s...  23.9 us
    ppermute x1, waiting for transfers between devices, per_device(): sea_before = lax.ppermute(later_sea[:, cells - HO:], AXES, up)  19.1 us
    pallas_call x1, Pallas kernels, per_device(): call(exchange_kernel, (shape((fields, cells)), shape((peers, 2 * parts, l...  13.3 us
    pallas_call x1, Pallas kernels, per_device(): call(prepare_kernel(fields), (shape((states, columns)), shape((1, columns...  6.43 us
  transfers between devices with their start and end apart: 8, of which 4 were waited for; matrix products, arithmetic and copies ran while one was open for 0% of the time, Pallas kernels for 46%

profile of v2, /device:TPU:0, one launch (start us, length us, event | category | flops | bytes accessed | tf_op | source)
XLA Modules:
  0.0 250.0 jit_solution(16716928598978165070)
XLA Ops:
  0.6 2.5 slice_bitcast_fusion.sea
  3.1 6.4 %shard_map.166 = (f32[16,4096]{1,0:T(8,128)}, f32[1,4096]{1,0:T(1,128)}, f32[40,1024]{1,0:T(8,128)}, f32[40,1024]{1,0:T(8,128)}, f32[16,128]{1,0:T(8,128)}, /*index=5*/bf16[576,304]{1,0:T(8,128)(2,1)}) custom-call(f32[72,72]{1,0:T(8,128)} %mix.1, f32[80,80]{1,0:T(8,128)} %omix.5, f32[288,4096]{1,0:T(8,128)} %bitcast.8, f32[80,4096]{1,0:T(8,128)} %slice_bitcast_fusion.sea, ...), custom_call_target="tpu_custom_call" | custom-call | flops 1000000 | bytes 10000 | tf_op jit(solution)/shard_map/pallas_call | solution.py:624
  9.8 3.0 %collective-permute-start.2 = (f32[288,1024]{1,0:T(8,128)S(1)}, f32[288,1024]{1,0:T(8,128)S(1)}, u32[]{:S(2)}, u32[]{:S(2)}) collective-permute-start(f32[288,1024]{1,0:T(8,128)S(1)} %get-tuple-element.44), channel_id=1, source_target_pairs={{0,1},{1,2},{2,3},{3,4},{4,5},{5,6},{6,7},{7,8},{8,9},{9,10},{10,1... | collective-permute-start | bytes 3538952 | tf_op jit(solution)/shard_map/ppermute | solution.py:651
  12.8 3.5 %collective-permute-start.3 = (f32[288,1024]{1,0:T(8,128)S(1)}, f32[288,1024]{1,0:T(8,128)S(1)}, u32[]{:S(2)}, u32[]{:S(2)}) collective-permute-start(f32[288,1024]{1,0:T(8,128)S(1)} %get-tuple-element.43), channel_id=1, source_target_pairs={{1,0},{2,1},{3,2},{4,3},{5,4},{6,5},{7,6},{8,7},{9,8},{10,9},{11,1... | collective-permute-start | bytes 3538952 | tf_op jit(solution)/shard_map/ppermute | solution.py:652
  16.4 5.3 %collective-permute-start.1 = (f32[40,1024]{1,0:T(8,128)S(1)}, f32[40,1024]{1,0:T(8,128)S(1)}, u32[]{:S(2)}, u32[]{:S(2)}) collective-permute-start(f32[40,1024]{1,0:T(8,128)S(1)} %copy-done.9), channel_id=1, source_target_pairs={{1,0},{2,1},{3,2},{4,3},{5,4},{6,5},{7,6},{8,7},{9,8},{10,9},{11,1... | collective-permute-start | bytes 491528 | tf_op jit(solution)/shard_map/ppermute | solution.py:648
  21.7 48.7 %collective-permute-done.before.lists_before = f32[40,1024]{1,0:T(8,128)S(1)} collective-permute-done((f32[40,1024]{1,0:T(8,128)S(1)}, f32[40,1024]{1,0:T(8,128)S(1)}, u32[]{:S(2)}, u32[]{:S(2)}) %collective-permute-start) | collective-permute-done | bytes 163872 | tf_op jit(solution)/shard_map/ppermute | solution.py:647
  70.4 1.9 collective-permute-done.1.after.lists_after
  73.0 23.9 %shard_map.167.q = f32[16,16,256]{2,1,0:T(8,128)} custom-call(f32[16,4096]{1,0:T(8,128)} %get-tuple-element.22.y, f32[40,1024]{1,0:T(8,128)} %copy-done.1, f32[40,1024]{1,0:T(8,128)} %copy-done.2, s32[6,4096]{1,0:T(8,128)} %nbr.7, f32[6,4096]{1,0:T(8,128)} %coef.7, f32[4,4096]{1,0:T(4,128)} %bulk.3, f32[4,4096]{1,0:T(4,128)} %surf.5, ...), custom_call_target="tpu_custom_call" | custom-call | flops 1000000 | bytes 10000 | tf_op jit(solution)/shard_map/pallas_call | solution.py:677
  96.9 1.0 copy-done.3
  98.0 1.0 copy-done.4
  99.0 4.2 %shard_map.170 = f32[32,8,256]{2,1,0:T(8,128)} custom-call(f32[16,16,256]{2,1,0:T(8,128)} %shard_map.167.q, s32[32,512]{1,0:T(8,128)} %bitcast.16), custom_call_target="tpu_custom_call" | custom-call | flops 1000000 | bytes 10000 | tf_op jit(solution)/shard_map/pallas_call | solution.py:692
  103.2 4.9 %all-to-all-start = ((f32[32,8,256]{2,1,0:T(8,128)}), f32[32,8,256]{2,1,0:T(8,128)S(1)}, u32[]{:S(2)}, u32[]{:S(2)}) async-start(f32[32,8,256]{2,1,0:T(8,128)} %shard_map.170), calls=%async_computation | async-start | bytes 524288 | tf_op jit(solution)/shard_map/all_to_all | solution.py:698
  108.1 1.2 fusion
  109.4 1.8 collective-permute-start.4
  111.2 3.6 %collective-permute-start.5 = (f32[320,384]{1,0:T(8,128)S(1)}, f32[320,384]{1,0:T(8,128)S(1)}, u32[]{:S(2)}, u32[]{:S(2)}) collective-permute-start(f32[320,384]{1,0:T(8,128)S(1)} %get-tuple-element.41), channel_id=1, source_target_pairs={{1,0},{2,1},{3,2},{4,3},{5,4},{6,5},{7,6},{8,7},{9,8},{10,9},{11,1... | collective-permute-start | bytes 1474568 | tf_op jit(solution)/shard_map/ppermute | solution.py:654
  114.8 19.1 %collective-permute-done.4.before = f32[320,384]{1,0:T(8,128)S(1)} collective-permute-done((f32[320,384]{1,0:T(8,128)S(1)}, f32[320,384]{1,0:T(8,128)S(1)}, u32[]{:S(2)}, u32[]{:S(2)}) %collective-permute-start.4) | collective-permute-done | bytes 491552 | tf_op jit(solution)/shard_map/ppermute | solution.py:653
  133.8 2.0 collective-permute-done.5.after
  135.9 0.7 copy-done.5
  136.6 13.3 %shard_map.171 = (f32[4,4096]{1,0:T(4,128)}, f32[32,4,256]{2,1,0:T(4,128)}) custom-call(f32[32,8,256]{2,1,0:T(8,128)} %copy-done.5, s32[4,4096]{1,0:T(4,128)} %slot.1, f32[4,4096]{1,0:T(4,128)} %weight.1, f32[1,4096]{1,0:T(1,128)} %get-tuple-element.38.yo, f32[40,1024]{1,0:T(8,128)} %copy-done.1, f32[40,1024]{1,0:T(8,128)} %copy-done.2, s32[6,4096]{1,0:T(8,128)} %nbr.9, ...), custom_call_target="tpu_custom_call" | custom-call | flops 1000000 | bytes 10000 | tf_op jit(solution)/shard_map/pallas_call | solution.py:725
  149.9 4.4 %all-to-all-start.1 = ((f32[32,4,256]{2,1,0:T(4,128)}), f32[32,4,256]{2,1,0:T(4,128)S(1)}, u32[]{:S(2)}, u32[]{:S(2)}) async-start(f32[32,4,256]{2,1,0:T(4,128)} %get-tuple-element.40), calls=%async_computation.1 | async-start | bytes 262144 | tf_op jit(solution)/shard_map/all_to_all | solution.py:737
  154.3 30.2 %shard_map.168 = (bf16[8,2,768,256]{3,2,1,0:T(8,128)(2,1)}, bf16[12,576,256]{2,1,0:T(8,128)(2,1)}, bf16[8,576,256]{2,1,0:T(8,128)(2,1)}) custom-call(f32[288,4096]{1,0:T(8,128)} %bitcast.9, s32[6,4096]{1,0:T(8,128)} %nbr.7, f32[6,4096]{1,0:T(8,128)} %coef.7), custom_call_target="tpu_custom_call" | custom-call | flops 1000000 | bytes 10000 | tf_op jit(solution)/shard_map/pallas_call | solution.py:656
  184.6 27.3 %shard_map.169 = f32[288,4096]{1,0:T(8,128)} custom-call(f32[288,1024]{1,0:T(8,128)} %copy-done.3, f32[288,1024]{1,0:T(8,128)} %copy-done.4, f32[40,1024]{1,0:T(8,128)} %copy-done.1, f32[40,1024]{1,0:T(8,128)} %copy-done.2, f32[288,4096]{1,0:T(8,128)} %bitcast.10, bf16[12,576,256]{2,1,0:T(8,128)(2,1)} %get-tuple-element.29.kept, ...), custom_call_target="tpu_custom_call" | custom-call | flops 1000000 | bytes 10000 | tf_op jit(solution)/shard_map/pallas_call | solution.py:700
  211.9 32.3 %shard_map.172 = f32[320,4096]{1,0:T(8,128)} custom-call(f32[320,4096]{1,0:T(8,128)} %bitcast.13, f32[320,384]{1,0:T(8,128)} %copy-done.7, f32[320,384]{1,0:T(8,128)} %copy-done.8, s32[6,4096]{1,0:T(8,128)} %nbr.9, f32[6,4096]{1,0:T(8,128)} %coef.9, f32[80,80]{1,0:T(8,128)} %omix.5, f32[4,4096]{1,0:T(4,128)} %get-tuple-element.39.flux), custom_call_target="tpu_custom_call" | custom-call | flops 1000000 | bytes 10000 | tf_op jit(solution)/shard_map/pallas_call | solution.py:739
  244.9 5.1 %shard_map.173 = f32[32,128]{1,0:T(8,128)} custom-call(f32[32,4,256]{2,1,0:T(4,128)} %copy-done.6, s32[32,512]{1,0:T(8,128)} %bitcast.17, f32[4,4096]{1,0:T(4,128)} %surf.5), custom_call_target="tpu_custom_call" | custom-call | flops 1000000 | bytes 10000 | tf_op jit(solution)/shard_map/pallas_call | solution.py:750
  (25 shorter events, 1.6 us)
Async XLA Ops:
  3.1 6.4 %copy-start = (f32[4,72,4096]{2,1,0:T(8,128)S(1)}, f32[4,72,4096]{2,1,0:T(8,128)}, u32[]{:S(2)}) copy-start(f32[4,72,4096]{2,1,0:T(8,128)} %param.15) | copy-start | bytes 14155780
  9.5 6.8 %copy-start.10 = (f32[40,1024]{1,0:T(8,128)S(1)}, f32[40,1024]{1,0:T(8,128)}, u32[]{:S(2)}) copy-start(f32[40,1024]{1,0:T(8,128)} %get-tuple-element.23) | copy-start | bytes 491524
  9.5 6.8 %copy-start.9 = (f32[40,1024]{1,0:T(8,128)S(1)}, f32[40,1024]{1,0:T(8,128)}, u32[]{:S(2)}) copy-start(f32[40,1024]{1,0:T(8,128)} %get-tuple-element.24) | copy-start | bytes 491524
  9.8 87.1 %collective-permute-start.2 = (f32[288,1024]{1,0:T(8,128)S(1)}, f32[288,1024]{1,0:T(8,128)S(1)}, u32[]{:S(2)}, u32[]{:S(2)}) collective-permute-start(f32[288,1024]{1,0:T(8,128)S(1)} %get-tuple-element.44), channel_id=1, source_target_pairs={{0,1},{1,2},{2,3},{3,4},{4,5},{5,6},{6,7},{7,8},{8,9},{9,10},{10,1... | collective-permute-start | bytes 3538952 | tf_op jit(solution)/shard_map/ppermute | solution.py:651
  12.8 84.1 %collective-permute-start.3 = (f32[288,1024]{1,0:T(8,128)S(1)}, f32[288,1024]{1,0:T(8,128)S(1)}, u32[]{:S(2)}, u32[]{:S(2)}) collective-permute-start(f32[288,1024]{1,0:T(8,128)S(1)} %get-tuple-element.43), channel_id=1, source_target_pairs={{1,0},{2,1},{3,2},{4,3},{5,4},{6,5},{7,6},{8,7},{9,8},{10,9},{11,1... | collective-permute-start | bytes 3538952 | tf_op jit(solution)/shard_map/ppermute | solution.py:652
  16.3 54.0 %collective-permute-start = (f32[40,1024]{1,0:T(8,128)S(1)}, f32[40,1024]{1,0:T(8,128)S(1)}, u32[]{:S(2)}, u32[]{:S(2)}) collective-permute-start(f32[40,1024]{1,0:T(8,128)S(1)} %copy-done.10), channel_id=1, source_target_pairs={{0,1},{1,2},{2,3},{3,4},{4,5},{5,6},{6,7},{7,8},{8,9},{9,10},{10,1... | collective-permute-start | bytes 491528 | tf_op jit(solution)/shard_map/ppermute | solution.py:647
  16.4 56.0 %collective-permute-start.1 = (f32[40,1024]{1,0:T(8,128)S(1)}, f32[40,1024]{1,0:T(8,128)S(1)}, u32[]{:S(2)}, u32[]{:S(2)}) collective-permute-start(f32[40,1024]{1,0:T(8,128)S(1)} %copy-done.9), channel_id=1, source_target_pairs={{1,0},{2,1},{3,2},{4,3},{5,4},{6,5},{7,6},{8,7},{9,8},{10,9},{11,1... | collective-permute-start | bytes 491528 | tf_op jit(solution)/shard_map/ppermute | solution.py:648
  70.4 2.0 copy-start.1
  72.3 0.7 copy-start.2
  96.9 1.0 copy-start.3
  98.0 1.0 copy-start.4
  103.2 32.6 %all-to-all-start = ((f32[32,8,256]{2,1,0:T(8,128)}), f32[32,8,256]{2,1,0:T(8,128)S(1)}, u32[]{:S(2)}, u32[]{:S(2)}) async-start(f32[32,8,256]{2,1,0:T(8,128)} %shard_map.170), calls=%async_computation | async-start | bytes 524288 | tf_op jit(solution)/shard_map/all_to_all | solution.py:698
  109.4 24.5 %collective-permute-start.4 = (f32[320,384]{1,0:T(8,128)S(1)}, f32[320,384]{1,0:T(8,128)S(1)}, u32[]{:S(2)}, u32[]{:S(2)}) collective-permute-start(f32[320,384]{1,0:T(8,128)S(1)} %get-tuple-element.42), channel_id=1, source_target_pairs={{0,1},{1,2},{2,3},{3,4},{4,5},{5,6},{6,7},{7,8},{8,9},{9,10},{10,1... | collective-permute-start | bytes 1474568 | tf_op jit(solution)/shard_map/ppermute | solution.py:653
  111.2 24.7 %collective-permute-start.5 = (f32[320,384]{1,0:T(8,128)S(1)}, f32[320,384]{1,0:T(8,128)S(1)}, u32[]{:S(2)}, u32[]{:S(2)}) collective-permute-start(f32[320,384]{1,0:T(8,128)S(1)} %get-tuple-element.41), channel_id=1, source_target_pairs={{1,0},{2,1},{3,2},{4,3},{5,4},{6,5},{7,6},{8,7},{9,8},{10,9},{11,1... | collective-permute-start | bytes 1474568 | tf_op jit(solution)/shard_map/ppermute | solution.py:654
  133.8 78.1 %copy-start.7 = (f32[320,384]{1,0:T(8,128)}, f32[320,384]{1,0:T(8,128)S(1)}, u32[]{:S(2)}) copy-start(f32[320,384]{1,0:T(8,128)S(1)} %collective-permute-done.4.before) | copy-start | bytes 1474564
  135.8 76.1 %copy-start.8 = (f32[320,384]{1,0:T(8,128)}, f32[320,384]{1,0:T(8,128)S(1)}, u32[]{:S(2)}) copy-start(f32[320,384]{1,0:T(8,128)S(1)} %collective-permute-done.5.after) | copy-start | bytes 1474564
  135.9 0.7 copy-start.5
  149.9 94.4 %all-to-all-start.1 = ((f32[32,4,256]{2,1,0:T(4,128)}), f32[32,4,256]{2,1,0:T(4,128)S(1)}, u32[]{:S(2)}, u32[]{:S(2)}) async-start(f32[32,4,256]{2,1,0:T(4,128)} %get-tuple-element.40), calls=%async_computation.1 | async-start | bytes 262144 | tf_op jit(solution)/shard_map/all_to_all | solution.py:737
  244.3 0.6 copy-start.6

commit v3 on v2

--- a/solution.py
+++ b/solution.py
@@ -57,6 +57,16 @@
     rows = x2.shape[0] // 2
     wide = mm(x2, w2[0])
     return wide[:rows] + wide[rows:] + mm(x2[:rows], w2[1])
+
+
+def product_long(x2s, w2):
+    rows = x2s[0].shape[0] // 2
+    highs = [x[:rows] for x in x2s]
+    lows = [x[rows:] for x in x2s]
+    return mm(
+        jnp.concatenate(highs + lows + highs, axis=1),
+        jnp.concatenate([w2[0], w2[0], w2[1]], axis=0),
+    )
 
 
 def iota(dims, axis):
@@ -78,23 +88,34 @@
         ids[k] = jnp.where(alive, ids[k], -1)
     lanes = 128
     step = 16
+    base = iota((step, lanes), 0).astype(F32)
+    parts = [halves(c) for c in cs + [rest]]
+
+    def wide(x, at):
+        return jnp.broadcast_to(x[:, at].astype(F32), (step, lanes)).astype(BF)
+
     for half in range(BLK // lanes):
         at = slice(half * lanes, (half + 1) * lanes)
-        wide_ids = [jnp.broadcast_to(i[:, at], (step, lanes)) for i in ids]
-        wide_cs = [jnp.broadcast_to(c[:, at], (step, lanes)) for c in cs]
-        own = iota((step, lanes), 1) + (half * lanes + halo)
-        wide_rest = jnp.broadcast_to(rest[:, at], (step, lanes))
-        base = iota((step, lanes), 0)
-        for first in range(0, rows, step):
-            if first + step <= half * lanes or first >= half * lanes + lanes + 2 * halo:
-                zero = jnp.zeros((step, lanes), BF)
-                store(first, step, at, zero, zero)
-                continue
-            here = base + first
-            value = jnp.where(here == own, wide_rest, 0.0)
-            for i, c in zip(wide_ids, wide_cs):
-                value = jnp.where(here == i, c, value)
-            store(first, step, at, *halves(value))
+        highs = [wide(p[0], at) for p in parts]
+        lows = [wide(p[1], at) for p in parts]
+        own = (iota((step, lanes), 1) - iota((step, lanes), 0)).astype(F32).astype(BF)
+        zero = jnp.zeros((step, lanes), BF)
+        for tile in range(0, rows, BLK):
+            near = [wide((i - tile).astype(F32), at) for i in ids]
+            for first in range(tile, tile + BLK, step):
+                high, low = zero, zero
+                if half * lanes - step < first < half * lanes + lanes + 2 * halo:
+                    offset = first - halo - half * lanes
+                    if 0 <= offset < lanes:
+                        same = own == jnp.full((step, lanes), offset, BF)
+                        high = jnp.where(same, highs[-1], zero)
+                        low = jnp.where(same, lows[-1], zero)
+                    here = (base + float(first - tile)).astype(BF)
+                    for k in range(count):
+                        same = here == near[k]
+                        high = jnp.where(same, highs[k], high)
+                        low = jnp.where(same, lows[k], low)
+                store(first, step, at, high, low)
 
 
 def one_hot(ids, rows):
@@ -109,9 +130,11 @@
 
 
 def prepare_kernel(fields):
-    def body(mix, omix, atm, sea, nbr, coef, bulk, surf, spread, code, y, yo, first, last, gains, vertical):
+    def body(mix, omix, atm, sea, nbr, coef, bulk, surf, spread, code, y, yo, first, last, gains, vertical, top, sem):
         la = mix.shape[0]
         columns = atm.shape[1]
+        copy = pltpu.make_async_copy(sea.at[: omix.shape[0], :], top, sem)
+        copy.start()
         eye = iota((la, la), 0) == iota((la, la), 1)
         step = mix[...] + jnp.where(eye, 1.0, 0.0)
 
@@ -155,6 +178,7 @@
         sea_eye = iota((lo, lo), 0) == iota((lo, lo), 1)
         sea_row = omix[0:1, :] + jnp.where(iota((1, lo), 1) == 0, 1.0, 0.0)
         sea_weight = jnp.broadcast_to(col(sea_row, sea_eye), (lo, 128))
+        copy.wait()
         for start in range(0, columns, 128):
             at = slice(start, start + 128)
             for f in range(fields):
@@ -164,7 +188,7 @@
                     y[k * fields + f : k * fields + f + 1, at] = jnp.sum(
                         x * weights[k - 1], axis=0, keepdims=True
                     )
-            yo[:, at] = jnp.sum(sea[:, at] * sea_weight, axis=0, keepdims=True)
+            yo[:, at] = jnp.sum(top[:, at] * sea_weight, axis=0, keepdims=True)
         for target, at in ((first, slice(0, WIDE)), (last, slice(columns - WIDE, columns))):
             target[0:16, :] = y[:, at]
             target[16:22, :] = nbr[:, at].astype(F32)
@@ -177,135 +201,141 @@
     return body
 
 
-def interior_kernel(atm, nbr, coef, band, kept, mid, w, wa, wb, sa, sb, sems):
-    blocks = atm.shape[1] // BLK
-    sent = list(range(ASTEPS)) + list(range(blocks - ASTEPS, blocks))
-
-    def split(b, _):
+def band_kernel(nbr, coef, band, w, sems):
+    blocks = nbr.shape[1] // BLK
+
+    def copy(b):
+        return pltpu.make_async_copy(w.at[b], band.at[b], sems.at[b])
+
+    def build(b, _):
         at = pl.ds(pl.multiple_of(b * BLK, BLK), BLK)
-        sa[b] = stacked(atm[:, at])
-        return 0
-
-    lax.fori_loop(0, blocks, split, 0, unroll=4)
-
-    def build(b, near):
-        at = pl.ds(pl.multiple_of(b * BLK, BLK), BLK)
 
         def store(first, step, lanes, high, low):
-            near[0, first : first + step, lanes] = high
-            near[1, first : first + step, lanes] = low
             w[b, 0, first : first + step, lanes] = high
             w[b, 1, first : first + step, lanes] = low
 
         build_band(store, nbr[:, at] - b * BLK, coef[:, at], HA)
-
-    def window(source, b):
-        return jnp.concatenate([source[b - 1], source[b], source[b + 1]], axis=1)
-
-    build(0, wb)
-    build(1, wa)
-
-    def first(i, _):
-        b = 2 * i + 1
-        build(b + 1, wb)
-        sb[b] = stacked(product(window(sa, b), (wa[0], wa[1])))
-        build(b + 2, wa)
-        sb[b + 1] = stacked(product(window(sa, b + 1), (wb[0], wb[1])))
-        return 0
-
-    lax.fori_loop(0, (blocks - 2) // 2, first, 0)
-    copies = [pltpu.make_async_copy(w.at[b], band.at[i], sems.at[i]) for i, b in enumerate(sent)]
-    for copy in copies:
+        copy(b).start()
+        return 0
+
+    lax.fori_loop(0, blocks, build, 0)
+
+    def finish(b, _):
+        copy(b).wait()
+        return 0
+
+    lax.fori_loop(0, blocks, finish, 0)
+
+
+def interior_kernel(
+    atm, y, before, after, bulk, surf, gains, band, q, kept, mid, far, w, sa, sb, za, zb, bulks, surfs, sems
+):
+    rows, columns = atm.shape
+    blocks = columns // BLK
+    fields = bulk.shape[0]
+    states = fields * ASTEPS
+    total = blocks + 2 * ASTEPS
+    halo = ASTEPS - 1
+
+    def arriving(b):
+        return pltpu.make_async_copy(band.at[b], w.at[halo + b], sems.at[b])
+
+    def begin(b, _):
+        arriving(b).start()
+        return 0
+
+    lax.fori_loop(0, blocks, begin, 0)
+
+    leaving = []
+    for e in list(range(ASTEPS)) + list(range(ASTEPS + blocks, total)):
+        pack = before if e < ASTEPS else after
+        local = e if e < ASTEPS else e - ASTEPS - blocks
+        at = slice(local * BLK, (local + 1) * BLK)
+        za[e] = stacked(pack[0:states, at])
+        bulks[e] = pack[28:32, at]
+        surfs[e] = pack[32:36, at]
+        if e in (0, total - 1):
+            continue
+        origin = local * BLK + (columns - WIDE if e < ASTEPS else 0)
+
+        def store(first, step, lanes, high, low, e=e):
+            w[e - 1, 0, first : first + step, lanes] = high
+            w[e - 1, 1, first : first + step, lanes] = low
+
+        build_band(store, pack[16:22, at].astype(jnp.int32) - origin, pack[22:28, at], HA)
+        i = e - 1 if e < ASTEPS else e - 1 - blocks
+        copy = pltpu.make_async_copy(w.at[e - 1], far.at[i], sems.at[blocks + i])
         copy.start()
-
-    def advance(source, target, shift):
-        def one(b, _):
-            target[b - shift] = stacked(product(window(source, b), (w[b, 0], w[b, 1])))
+        leaving.append(copy)
+    for b in range(blocks):
+        at = slice(b * BLK, (b + 1) * BLK)
+        both = stacked(jnp.concatenate([atm[:, at], y[:, at]], axis=0))
+        sa[b] = both
+        height = rows + states
+        za[b + ASTEPS] = jnp.concatenate([both[rows:height], both[height + rows :]], axis=0)
+        bulks[b + ASTEPS] = bulk[:, at]
+        surfs[b + ASTEPS] = surf[:, at]
+
+    def arrived(b, _):
+        arriving(b).wait()
+        return 0
+
+    lax.fori_loop(0, blocks, arrived, 0)
+
+    slot = iota((states, BLK), 0) // fields
+    for s in range(1, ASTEPS + 1):
+        xs, xt = (sa, sb) if s % 2 else (sb, sa)
+        zs, zt = (za, zb) if s % 2 else (zb, za)
+        gain = jnp.broadcast_to(gains[:, s - 1 : s], (states, BLK))
+        keep = jnp.where(slot == s - 1, 0.0, 1.0)
+
+        def advance(moved, e, s=s, gain=gain, keep=keep):
+            flux = bulks[e] * (surfs[e] - moved[(s - 1) * fields : s * fields])
+            return moved * keep + gain * jnp.concatenate([flux] * ASTEPS, axis=0)
+
+        def edge(e, s=s, zs=zs, zt=zt, advance=advance):
+            x2 = jnp.concatenate([zs[e - 1], zs[e], zs[e + 1]], axis=1)
+            value = advance(product(x2, (w[e - 1, 0], w[e - 1, 1])), e)
+            if s == ASTEPS:
+                q[e - ASTEPS] = value
+            else:
+                zt[e] = stacked(value)
+
+        def inner(b, s=s, xs=xs, xt=xt, zt=zt, advance=advance):
+            x2 = jnp.concatenate([xs[b - 1], xs[b], xs[b + 1]], axis=1)
+            moved = product(x2, (w[b + halo, 0], w[b + halo, 1]))
+            value = advance(moved[rows:], b + ASTEPS)
+            if s == ASTEPS:
+                q[b] = value
+                mid[b - ASTEPS] = stacked(moved[:rows])
+            else:
+                high, low = halves(moved[:rows])
+                zh, zl = halves(value)
+                xt[b] = jnp.concatenate([high, zh, low, zl], axis=0)
+                zt[b + ASTEPS] = jnp.concatenate([zh, zl], axis=0)
+
+        def together(i, _, s=s, edge=edge, inner=inner):
+            inner(s + 2 * i)
+            inner(s + 2 * i + 1)
+            edge(s + i)
+            edge(blocks + ASTEPS - s + i)
             return 0
 
-        return one
-
-    buffers = (sa, sb)
-    for s in range(1, ASTEPS + 1):
-        source = buffers[(s - 1) % 2]
-        if s == ASTEPS:
-            lax.fori_loop(s, blocks - s, advance(source, mid, s), 0, unroll=2)
-        else:
-            target = buffers[s % 2]
-            if s > 1:
-                lax.fori_loop(s, blocks - s, advance(source, target, 0), 0, unroll=2)
+        def alone(i, _, s=s, inner=inner):
+            inner(s + 2 * i)
+            inner(s + 2 * i + 1)
+            return 0
+
+        lax.fori_loop(0, ASTEPS, together, 0)
+        if blocks // 2 - s > ASTEPS:
+            lax.fori_loop(ASTEPS, blocks // 2 - s, alone, 0)
+        if s < ASTEPS:
+            height = rows + states
             for i, b in enumerate((s, s + 1, blocks - 2 - s, blocks - 1 - s)):
-                kept[(s - 1) * 4 + i] = target[b]
-    for copy in copies:
+                kept[(s - 1) * 4 + i, :rows] = xt[b, :rows]
+                kept[(s - 1) * 4 + i, rows:] = xt[b, height : height + rows]
+    for copy in leaving:
         copy.wait()
-
-
-def surface_kernel(y, before, after, nbr, coef, bulk, surf, gains, q, xa, xb, ids, cs, bulks, surfs):
-    columns = y.shape[1]
-    fields = bulk.shape[0]
-    count = nbr.shape[0]
-    side = WIDE // 128
-    own = columns // 128
-    total = own + 2 * side
-    reach = HA // 128
-    for t in range(total):
-        if t < side or t >= side + own:
-            pack = before if t < side else after
-            local = t if t < side else t - side - own
-            at = slice(local * 128, (local + 1) * 128)
-            origin = local * 128 + (columns - WIDE if t < side else 0)
-            xa[t] = pack[0:16, at]
-            ids[t] = pack[16:22, at].astype(jnp.int32) - origin
-            cs[t] = pack[22:28, at]
-            bulks[t] = pack[28:32, at]
-            surfs[t] = pack[32:36, at]
-        else:
-            at = slice((t - side) * 128, (t - side + 1) * 128)
-            xa[t] = y[:, at]
-            ids[t] = nbr[:, at] - (t - side) * 128
-            cs[t] = coef[:, at]
-            bulks[t] = bulk[:, at]
-            surfs[t] = surf[:, at]
-
-    rows = fields * ASTEPS
-    slot = iota((rows, 128), 0) // fields
-    buffers = (xa, xb)
-    for s in range(1, ASTEPS + 1):
-        source, target = buffers[(s - 1) % 2], buffers[s % 2]
-        gain = jnp.broadcast_to(gains[:, s - 1 : s], (rows, 128))
-        kept = jnp.where(slot == s - 1, 0.0, 1.0)
-
-        def tile(t, s=s, source=source, gain=gain, kept=kept):
-            middle = source[t]
-            around = [source[t - reach + i] for i in range(2 * reach + 1)]
-            here, weights = ids[t], cs[t]
-            changes = []
-            for first in range(0, rows, 8):
-                change = jnp.zeros((8, 128), F32)
-                for k in range(count):
-                    at = jnp.broadcast_to(here[k : k + 1], (8, 128))
-                    got = jnp.zeros((8, 128), F32)
-                    for i, x in enumerate(around):
-                        pick = jnp.take_along_axis(
-                            x[first : first + 8], at & 127, axis=1, mode="promise_in_bounds"
-                        )
-                        got = jnp.where(at // 128 == i, pick, got)
-                    change = change + weights[k : k + 1] * (got - middle[first : first + 8])
-                changes.append(change)
-            moved = middle + jnp.concatenate(changes, axis=0)
-            flux = bulks[t] * (surfs[t] - moved[(s - 1) * fields : s * fields])
-            return moved * kept + gain * jnp.concatenate([flux] * ASTEPS, axis=0)
-
-        def pair(e, _, s=s, target=target, tile=tile):
-            left, right = tile(2 * e), tile(2 * e + 1)
-            if s == ASTEPS:
-                q[e - ASTEPS] = jnp.concatenate([left, right], axis=1)
-            else:
-                target[2 * e] = left
-                target[2 * e + 1] = right
-            return 0
-
-        lax.fori_loop(s, total // 2 - s, pair, 0)
 
 
 def send_kernel(q, cols, out, table):
@@ -446,34 +476,22 @@
             out[row : row + 1, :] = value[b : b + 1, i * 128 : (i + 1) * 128]
 
 
-def edge_kernel(before, after, lists_before, lists_after, atm, kept, mid, q, vertical, band, out, w, sides, sa, sb, sems):
+def edge_kernel(before, after, atm, kept, mid, q, vertical, band, far, out, w, sides, sa, sb, sems):
     blocks = q.shape[0]
     count = 2 * ASTEPS - 1
     halo = ASTEPS - 1
-    columns = blocks * BLK
     copies = []
     for side in range(2):
         at = slice(0, 2 * BLK) if side == 0 else slice((blocks - 2) * BLK, blocks * BLK)
         copy = pltpu.make_async_copy(atm.at[:, at], sides.at[side], sems.at[2 * count + side])
         copy.start()
         copies.append(copy)
-    for i in range(2 * ASTEPS):
-        copy = pltpu.make_async_copy(band.at[i], w.at[halo + i], sems.at[i])
+    sources = [far.at[i] for i in range(halo)] + [band.at[i] for i in range(ASTEPS)]
+    sources += [band.at[blocks - ASTEPS + i] for i in range(ASTEPS)] + [far.at[halo + i] for i in range(halo)]
+    for i, source in enumerate(sources):
+        copy = pltpu.make_async_copy(source, w.at[i], sems.at[i])
         copy.start()
         copies.append(copy)
-    for i in range(halo):
-        for lists, local, origin, k in (
-            (lists_before, i + 1, columns - WIDE, i),
-            (lists_after, i, 0, halo + 2 * ASTEPS + i),
-        ):
-            at = slice(local * BLK, (local + 1) * BLK)
-
-            def store(first, step, lanes, high, low, k=k):
-                w[k, 0, first : first + step, lanes] = high
-                w[k, 1, first : first + step, lanes] = low
-
-            ids = lists[16:22, at].astype(jnp.int32) - (origin + local * BLK)
-            build_band(store, ids, lists[22:28, at], HA)
     for i in range(ASTEPS):
         at = slice(i * BLK, (i + 1) * BLK)
         sa[i] = stacked(before[:, at])
@@ -493,8 +511,7 @@
             for side in range(2):
                 base = 6 * side
                 k = s - 1 + i if side == 0 else count + ASTEPS - s + i
-                x2 = jnp.concatenate([source[base + i + d] for d in range(3)], axis=1)
-                value = stacked(product(x2, (w[k, 0], w[k, 1])))
+                value = stacked(product_long([source[base + i + d] for d in range(3)], (w[k, 0], w[k, 1])))
                 target[base + i + (2 * side if not last else 0)] = value
             return 0
 
@@ -577,6 +594,10 @@
         return 0
 
     lax.fori_loop(0, blocks // 2, one, 0)
+
+
+def after_all(value, *others):
+    return lax.optimization_barrier((value, *others))[0]
 
 
 def per_device(
@@ -631,12 +652,13 @@
             shape((states, 128)),
             shape((2 * rows, depth_k), BF),
         ),
-        in_specs=[vmem] * 10,
+        in_specs=[vmem] * 3 + [anywhere] + [vmem] * 6,
+        scratch=[pltpu.VMEM((lo, cells), F32), pltpu.SemaphoreType.DMA(())],
     )(
         atm_mix,
         ocean_mix,
         atm,
-        ocean[:lo],
+        ocean,
         atm_nbr,
         atm_nbr_coef,
         bulk_coef,
@@ -653,41 +675,37 @@
     sea_before = lax.ppermute(later_sea[:, cells - HO :], AXES, up)
     sea_after = lax.ppermute(later_sea[:, :HO], AXES, down)
 
-    band, kept, mid = call(
+    band = call(
+        band_kernel,
+        shape((blocks, 2, window, BLK), BF),
+        in_specs=[vmem] * 2,
+        out_specs=anywhere,
+        scratch=[pltpu.VMEM((blocks, 2, window, BLK), BF), pltpu.SemaphoreType.DMA((blocks,))],
+    )(after_all(atm_nbr, y), atm_nbr_coef)
+
+    total = blocks + 2 * ASTEPS
+    halo = ASTEPS - 1
+    q, kept, mid, far = call(
         interior_kernel,
         (
-            shape((2 * ASTEPS, 2, window, BLK), BF),
-            shape((4 * (ASTEPS - 1), 2 * rows, BLK), BF),
+            shape((blocks, states, BLK)),
+            shape((4 * halo, 2 * rows, BLK), BF),
             shape((blocks - 2 * ASTEPS, 2 * rows, BLK), BF),
+            shape((2 * halo, 2, window, BLK), BF),
         ),
-        in_specs=[vmem] * 3,
-        out_specs=(anywhere, vmem, vmem),
+        in_specs=[vmem] * 7 + [anywhere],
+        out_specs=(vmem, vmem, vmem, anywhere),
         scratch=[
-            pltpu.VMEM((blocks, 2, window, BLK), BF),
-            pltpu.VMEM((2, window, BLK), BF),
-            pltpu.VMEM((2, window, BLK), BF),
-            pltpu.VMEM((blocks, 2 * rows, BLK), BF),
-            pltpu.VMEM((blocks, 2 * rows, BLK), BF),
-            pltpu.SemaphoreType.DMA((2 * ASTEPS,)),
+            pltpu.VMEM((total - 2, 2, window, BLK), BF),
+            pltpu.VMEM((blocks, 2 * depth_k, BLK), BF),
+            pltpu.VMEM((blocks, 2 * depth_k, BLK), BF),
+            pltpu.VMEM((total, 2 * states, BLK), BF),
+            pltpu.VMEM((total, 2 * states, BLK), BF),
+            pltpu.VMEM((total, fields, BLK), F32),
+            pltpu.VMEM((total, fields, BLK), F32),
+            pltpu.SemaphoreType.DMA((blocks + 2 * halo,)),
         ],
-    )(atm, atm_nbr, atm_nbr_coef)
-
-    tiles = (columns + 2 * WIDE) // 128
-    count = atm_nbr.shape[0]
-    q = call(
-        surface_kernel,
-        shape((blocks, states, BLK)),
-        in_specs=[vmem] * 8,
-        scratch=[
-            pltpu.VMEM((tiles, states, 128), F32),
-            pltpu.VMEM((tiles, states, 128), F32),
-            pltpu.VMEM((tiles, count, 128), jnp.int32),
-            pltpu.VMEM((tiles, count, 128), F32),
-            pltpu.VMEM((tiles, fields, 128), F32),
-            pltpu.VMEM((tiles, fields, 128), F32),
-        ],
-    )(y, pack_before, pack_after, atm_nbr, atm_nbr_coef, bulk_coef, atm_surface, gains)
-    q, atm_before, atm_after = lax.optimization_barrier((q, atm_before, atm_after))
+    )(atm, y, after_all(pack_before, band), pack_after, bulk_coef, atm_surface, gains, band)
 
     outgoing = call(
         send_kernel,
@@ -700,18 +718,7 @@
     atm_final = call(
         edge_kernel,
         shape((rows, columns)),
-        in_specs=[
-            vmem,
-            vmem,
-            vmem,
-            vmem,
-            anywhere,
-            vmem,
-            vmem,
-            vmem,
-            vmem,
-            anywhere,
-        ],
+        in_specs=[vmem] * 2 + [anywhere] + [vmem] * 4 + [anywhere] * 2,
         scratch=[
             pltpu.VMEM((2 * (2 * ASTEPS - 1), 2, window, BLK), BF),
             pltpu.VMEM((2, rows, 2 * BLK), F32),
@@ -719,9 +726,9 @@
             pltpu.VMEM((12, 2 * rows, BLK), BF),
             pltpu.SemaphoreType.DMA((4 * ASTEPS,)),
         ],
-    )(atm_before, atm_after, pack_before, pack_after, atm, kept, mid, q, vertical, band)
-
-    received, sea_before, sea_after = lax.optimization_barrier((received, sea_before, sea_after))
+    )(after_all(atm_before, outgoing), atm_after, atm, kept, mid, q, vertical, band, far)
+
+    received = after_all(received, atm_final)
     flux, back = call(
         exchange_kernel,
         (shape((fields, cells)), shape((peers, 2 * parts, lanes))),
@@ -745,14 +752,14 @@
             pltpu.VMEM((2, BLK + 2 * HO, BLK), BF),
             pltpu.VMEM((2, BLK + 2 * HO, BLK), BF),
         ],
-    )(ocean, sea_before, sea_after, ocean_nbr, ocean_nbr_coef, ocean_mix, flux)
+    )(ocean, after_all(sea_before, back), sea_after, ocean_nbr, ocean_nbr_coef, ocean_mix, flux)
 
     surface_temp = call(
         settle_kernel,
         shape((columns // 128, 128)),
         in_specs=[vmem] * 3,
         scratch=[pltpu.VMEM((4 * blocks, BLK), F32)],
-    )(returned, picked, atm_surface)
+    )(after_all(returned, ocean_final), picked, atm_surface)
 
     return (
         atm_final.reshape(fields, la, columns),

time: 250 us -> 206 us (0.82)
  waiting for transfers between devices: 71.7 us -> 43.5 us
  Pallas kernels: 143 us -> 131 us
    ppermute x1, waiting for transfers between devices: 19.1 us -> 0.01 us  [per_device(): sea_before = lax.ppermute(later_sea[:, cells - HO:], AXES, up)]
    pallas_call x3, Pallas kernels: 81.5 us -> 70.2 us  [the longest x1 34.7 us: per_device(): call(interior_kernel, (shape((blocks, states, BLK)), shape((4 * halo, 2 *...]
    ppermute x1, waiting for transfers between devices: 48.7 us -> 41.6 us  [per_device(): pack_before = lax.ppermute(last, AXES, up)]
  transfers between devices with their start and end apart: 8 -> 8, of which waited for: 4 -> 2; matrix products, arithmetic and copies ran while one was open for 0% -> 1% of each run, Pallas kernels for 46% -> 58%
where the time goes in v3:
time: 206 us
  Pallas kernels  131 us (64%)
  waiting for transfers between devices  43.5 us (21%)
  starting transfers between devices  24.6 us (12%)
  local copies, waits for them, and re-layouts  6.13 us (3%)
    ppermute x1, waiting for transfers between devices, per_device(): pack_before = lax.ppermute(last, AXES, up)  41.6 us
    pallas_call x1, Pallas kernels, per_device(): call(interior_kernel, (shape((blocks, states, BLK)), shape((4 * halo, 2 *...  34.7 us
    pallas_call x1, Pallas kernels, per_device(): call(ocean_kernel, shape((fields * lo, cells)), in_specs=[vmem] * 7, scra...  31.1 us
    pallas_call x1, Pallas kernels, per_device(): call(edge_kernel, shape((rows, columns)), in_specs=[vmem] * 2 + [anywhere...  28.1 us
    pallas_call x1, Pallas kernels, per_device(): call(exchange_kernel, (shape((fields, cells)), shape((peers, 2 * parts, l...  13.3 us
    pallas_call x1, Pallas kernels, per_device(): call(band_kernel, shape((blocks, 2, window, BLK), BF), in_specs=[vmem] *...  7.42 us
    pallas_call x1, Pallas kernels, per_device(): call(prepare_kernel(fields), (shape((states, columns)), shape((1, columns...  6.52 us
    ppermute x1, starting transfers between devices, per_device(): pack_after = lax.ppermute(first, AXES, down)  5.34 us
  transfers between devices with their start and end apart: 8, of which 2 were waited for; matrix products, arithmetic and copies ran while one was open for 1% of the time, Pallas kernels for 58%

profile of v3, /device:TPU:0, one launch (start us, length us, event | category | flops | bytes accessed | tf_op | source)
XLA Modules:
  0.0 205.6 jit_solution(1000677620003963978)
XLA Ops:
  0.6 0.0 copy-start
  0.6 6.5 %shard_map.166 = (f32[16,4096]{1,0:T(8,128)}, f32[1,4096]{1,0:T(1,128)}, f32[40,1024]{1,0:T(8,128)}, f32[40,1024]{1,0:T(8,128)}, f32[16,128]{1,0:T(8,128)}, /*index=5*/bf16[576,304]{1,0:T(8,128)(2,1)}) custom-call(f32[72,72]{1,0:T(8,128)} %mix.1, f32[80,80]{1,0:T(8,128)} %omix.5, f32[288,4096]{1,0:T(8,128)} %bitcast.6, f32[320,4096]{1,0:T(8,128)} %bitcast.10, ...), custom_call_target="tpu_custom_call" | custom-call | flops 1000000 | bytes 10000 | tf_op jit(solution)/shard_map/pallas_call | solution.py:645
  7.2 1.2 fusion.1
  8.4 2.9 %collective-permute-start = (f32[288,1024]{1,0:T(8,128)}, f32[288,1024]{1,0:T(8,128)S(1)}, u32[]{:S(2)}, u32[]{:S(2)}) collective-permute-start(f32[288,1024]{1,0:T(8,128)} %get-tuple-element.46), channel_id=1, source_target_pairs={{0,1},{1,2},{2,3},{3,4},{4,5},{5,6},{6,7},{7,8},{8,9},{9,10},{10,1... | collective-permute-start | bytes 3538952 | tf_op jit(solution)/shard_map/ppermute | solution.py:673
  11.4 3.4 %collective-permute-start.3 = (f32[288,1024]{1,0:T(8,128)S(1)}, f32[288,1024]{1,0:T(8,128)S(1)}, u32[]{:S(2)}, u32[]{:S(2)}) collective-permute-start(f32[288,1024]{1,0:T(8,128)S(1)} %get-tuple-element.45), channel_id=1, source_target_pairs={{1,0},{2,1},{3,2},{4,3},{5,4},{6,5},{7,6},{8,7},{9,8},{10,9},{11,1... | collective-permute-start | bytes 3538952 | tf_op jit(solution)/shard_map/ppermute | solution.py:674
  14.8 5.3 %collective-permute-start.2 = (f32[40,1024]{1,0:T(8,128)}, f32[40,1024]{1,0:T(8,128)S(1)}, u32[]{:S(2)}, u32[]{:S(2)}) collective-permute-start(f32[40,1024]{1,0:T(8,128)} %get-tuple-element.23), channel_id=1, source_target_pairs={{1,0},{2,1},{3,2},{4,3},{5,4},{6,5},{7,6},{8,7},{9,8},{10,9},{11,1... | collective-permute-start | bytes 491528 | tf_op jit(solution)/shard_map/ppermute | solution.py:670
  20.1 7.4 %shard_map.167.band = bf16[16,2,768,256]{3,2,1,0:T(8,128)(2,1)} custom-call(s32[6,4096]{1,0:T(8,128)} %nbr.4, f32[6,4096]{1,0:T(8,128)} %coef.5), custom_call_target="tpu_custom_call" | custom-call | flops 1000000 | bytes 10000 | tf_op jit(solution)/shard_map/pallas_call | solution.py:678
  27.6 41.6 %collective-permute-done.1.before = f32[40,1024]{1,0:T(8,128)S(1)} collective-permute-done((f32[40,1024]{1,0:T(8,128)}, f32[40,1024]{1,0:T(8,128)S(1)}, u32[]{:S(2)}, u32[]{:S(2)}) %collective-permute-start.1) | collective-permute-done | bytes 163872 | tf_op jit(solution)/shard_map/ppermute | solution.py:669
  69.2 1.8 collective-permute-done.2.after
  71.0 0.7 copy-done.4
  71.7 34.7 %shard_map.168 = (f32[16,16,256]{2,1,0:T(8,128)}, bf16[12,576,256]{2,1,0:T(8,128)(2,1)}, bf16[8,576,256]{2,1,0:T(8,128)(2,1)}, bf16[6,2,768,256]{3,2,1,0:T(8,128)(2,1)}) custom-call(f32[288,4096]{1,0:T(8,128)} %bitcast.7, f32[16,4096]{1,0:T(8,128)} %get-tuple-element.26.y, f32[40,1024]{1,0:T(8,128)} %copy-done.3, f32[40,1024]{1,0:T(8,128)} %copy-done.4, ...), custom_call_target="tpu_custom_call" | custom-call | flops 1000000 | bytes 10000 | tf_op jit(solution)/shard_map/pallas_call | solution.py:688
  106.4 4.2 %shard_map.169 = f32[32,8,256]{2,1,0:T(8,128)} custom-call(f32[16,16,256]{2,1,0:T(8,128)} %get-tuple-element.30.q, s32[32,512]{1,0:T(8,128)} %bitcast.15), custom_call_target="tpu_custom_call" | custom-call | flops 1000000 | bytes 10000 | tf_op jit(solution)/shard_map/pallas_call | solution.py:710
  110.6 5.0 %all-to-all-start = ((f32[32,8,256]{2,1,0:T(8,128)}), f32[32,8,256]{2,1,0:T(8,128)}, u32[]{:S(2)}, u32[]{:S(2)}) async-start(f32[32,8,256]{2,1,0:T(8,128)} %shard_map.169), calls=%async_computation | async-start | bytes 524288 | tf_op jit(solution)/shard_map/all_to_all | solution.py:716
  115.7 2.2 %fusion = (f32[320,384]{1,0:T(8,128)}, f32[320,384]{1,0:T(8,128)}) fusion(f32[320,4096]{1,0:T(8,128)} %bitcast.11), kind=kLoop, calls=%fused_computation | loop fusion | bytes 1966080 | tf_op jit(solution)/shard_map/slice | solution.py:676
  117.8 1.7 collective-permute-start.4
  119.5 3.6 %collective-permute-start.5 = (f32[320,384]{1,0:T(8,128)}, f32[320,384]{1,0:T(8,128)}, u32[]{:S(2)}, u32[]{:S(2)}) collective-permute-start(f32[320,384]{1,0:T(8,128)} %get-tuple-element.43), channel_id=1, source_target_pairs={{1,0},{2,1},{3,2},{4,3},{5,4},{6,5},{7,6},{8,7},{9,8},{10,9},{11,1... | collective-permute-start | bytes 1474568 | tf_op jit(solution)/shard_map/ppermute | solution.py:676
  123.2 1.0 copy-done.1
  124.2 0.4 copy-done.2
  124.6 28.1 %shard_map.170 = f32[288,4096]{1,0:T(8,128)} custom-call(f32[288,1024]{1,0:T(8,128)} %copy-done.1, f32[288,1024]{1,0:T(8,128)} %copy-done.2, f32[288,4096]{1,0:T(8,128)} %bitcast.8, bf16[12,576,256]{2,1,0:T(8,128)(2,1)} %get-tuple-element.32.kept, bf16[8,576,256]{2,1,0:T(8,128)(2,1)} %get-tuple-element.33.mid, f32[16,16,256]{2,1,0:T(8,128)} %get-tuple-element.30.q, ...), custom_call_target="tpu_custom_call" | custom-call | flops 1000000 | bytes 10000 | tf_op jit(solution)/shard_map/pallas_call | solution.py:718
  152.7 13.3 %shard_map.171 = (f32[4,4096]{1,0:T(4,128)}, f32[32,4,256]{2,1,0:T(4,128)}) custom-call(f32[32,8,256]{2,1,0:T(8,128)} %all-to-all-done.recv, s32[4,4096]{1,0:T(4,128)} %slot.1, f32[4,4096]{1,0:T(4,128)} %weight.1, f32[1,4096]{1,0:T(1,128)} %get-tuple-element.38.yo, f32[40,1024]{1,0:T(8,128)} %copy-done.3, f32[40,1024]{1,0:T(8,128)} %copy-done.4, ...), custom_call_target="tpu_custom_call" | custom-call | flops 1000000 | bytes 10000 | tf_op jit(solution)/shard_map/pallas_call | solution.py:732
  166.1 2.6 %all-to-all-start.1 = ((f32[32,4,256]{2,1,0:T(4,128)}), f32[32,4,256]{2,1,0:T(4,128)S(1)}, u32[]{:S(2)}, u32[]{:S(2)}) async-start(f32[32,4,256]{2,1,0:T(4,128)} %get-tuple-element.39), calls=%async_computation.1 | async-start | bytes 262144 | tf_op jit(solution)/shard_map/all_to_all | solution.py:744
  168.7 31.1 %shard_map.172 = f32[320,4096]{1,0:T(8,128)} custom-call(f32[320,4096]{1,0:T(8,128)} %bitcast.12, f32[320,384]{1,0:T(8,128)} %collective-permute-done.4.before, f32[320,384]{1,0:T(8,128)} %collective-permute-done.5.after, s32[6,4096]{1,0:T(8,128)} %nbr.6, f32[6,4096]{1,0:T(8,128)} %coef.7, f32[80,80]{1,0:T(8,128)} %omix.5, f32[4,4096]{1,0:T(4,128)} %get-tuple-element.41.flux), custom_call_target="tpu_custom_call" | custom-call | flops 1000000 | bytes 10000 | tf_op jit(solution)/shard_map/pallas_call | solution.py:746
  199.8 0.6 copy-done.5
  200.4 5.1 %shard_map.173 = f32[32,128]{1,0:T(8,128)} custom-call(f32[32,4,256]{2,1,0:T(4,128)} %copy-done.5, s32[32,512]{1,0:T(8,128)} %bitcast.16, f32[4,4096]{1,0:T(4,128)} %surf.5), custom_call_target="tpu_custom_call" | custom-call | flops 1000000 | bytes 10000 | tf_op jit(solution)/shard_map/pallas_call | solution.py:757
  (14 shorter events, 0.0 us)
Async XLA Ops:
  0.6 6.5 %copy-start = (f32[4,72,4096]{2,1,0:T(8,128)S(1)}, f32[4,72,4096]{2,1,0:T(8,128)}, u32[]{:S(2)}) copy-start(f32[4,72,4096]{2,1,0:T(8,128)} %param.15) | copy-start | bytes 14155780
  8.4 114.8 %collective-permute-start = (f32[288,1024]{1,0:T(8,128)}, f32[288,1024]{1,0:T(8,128)S(1)}, u32[]{:S(2)}, u32[]{:S(2)}) collective-permute-start(f32[288,1024]{1,0:T(8,128)} %get-tuple-element.46), channel_id=1, source_target_pairs={{0,1},{1,2},{2,3},{3,4},{4,5},{5,6},{6,7},{7,8},{8,9},{9,10},{10,1... | collective-permute-start | bytes 3538952 | tf_op jit(solution)/shard_map/ppermute | solution.py:673
  11.4 111.8 %collective-permute-start.3 = (f32[288,1024]{1,0:T(8,128)S(1)}, f32[288,1024]{1,0:T(8,128)S(1)}, u32[]{:S(2)}, u32[]{:S(2)}) collective-permute-start(f32[288,1024]{1,0:T(8,128)S(1)} %get-tuple-element.45), channel_id=1, source_target_pairs={{1,0},{2,1},{3,2},{4,3},{5,4},{6,5},{7,6},{8,7},{9,8},{10,9},{11,1... | collective-permute-start | bytes 3538952 | tf_op jit(solution)/shard_map/ppermute | solution.py:674
  14.8 54.4 %collective-permute-start.1 = (f32[40,1024]{1,0:T(8,128)}, f32[40,1024]{1,0:T(8,128)S(1)}, u32[]{:S(2)}, u32[]{:S(2)}) collective-permute-start(f32[40,1024]{1,0:T(8,128)} %get-tuple-element.24), channel_id=1, source_target_pairs={{0,1},{1,2},{2,3},{3,4},{4,5},{5,6},{6,7},{7,8},{8,9},{9,10},{10,1... | collective-permute-start | bytes 491528 | tf_op jit(solution)/shard_map/ppermute | solution.py:669
  14.8 56.2 %collective-permute-start.2 = (f32[40,1024]{1,0:T(8,128)}, f32[40,1024]{1,0:T(8,128)S(1)}, u32[]{:S(2)}, u32[]{:S(2)}) collective-permute-start(f32[40,1024]{1,0:T(8,128)} %get-tuple-element.23), channel_id=1, source_target_pairs={{1,0},{2,1},{3,2},{4,3},{5,4},{6,5},{7,6},{8,7},{9,8},{10,9},{11,1... | collective-permute-start | bytes 491528 | tf_op jit(solution)/shard_map/ppermute | solution.py:670
  69.2 1.8 copy-start.3
  71.0 0.7 copy-start.4
  110.6 42.1 %all-to-all-start = ((f32[32,8,256]{2,1,0:T(8,128)}), f32[32,8,256]{2,1,0:T(8,128)}, u32[]{:S(2)}, u32[]{:S(2)}) async-start(f32[32,8,256]{2,1,0:T(8,128)} %shard_map.169), calls=%async_computation | async-start | bytes 524288 | tf_op jit(solution)/shard_map/all_to_all | solution.py:716
  117.8 50.8 %collective-permute-start.4 = (f32[320,384]{1,0:T(8,128)}, f32[320,384]{1,0:T(8,128)}, u32[]{:S(2)}, u32[]{:S(2)}) collective-permute-start(f32[320,384]{1,0:T(8,128)} %get-tuple-element.44), channel_id=1, source_target_pairs={{0,1},{1,2},{2,3},{3,4},{4,5},{5,6},{6,7},{7,8},{8,9},{9,10},{10,1... | collective-permute-start | bytes 1474568 | tf_op jit(solution)/shard_map/ppermute | solution.py:675
  119.5 49.1 %collective-permute-start.5 = (f32[320,384]{1,0:T(8,128)}, f32[320,384]{1,0:T(8,128)}, u32[]{:S(2)}, u32[]{:S(2)}) collective-permute-start(f32[320,384]{1,0:T(8,128)} %get-tuple-element.43), channel_id=1, source_target_pairs={{1,0},{2,1},{3,2},{4,3},{5,4},{6,5},{7,6},{8,7},{9,8},{10,9},{11,1... | collective-permute-start | bytes 1474568 | tf_op jit(solution)/shard_map/ppermute | solution.py:676
  123.2 1.0 copy-start.1
  123.2 1.4 copy-start.2
  166.1 33.7 %all-to-all-start.1 = ((f32[32,4,256]{2,1,0:T(4,128)}), f32[32,4,256]{2,1,0:T(4,128)S(1)}, u32[]{:S(2)}, u32[]{:S(2)}) async-start(f32[32,4,256]{2,1,0:T(4,128)} %get-tuple-element.39), calls=%async_computation.1 | async-start | bytes 262144 | tf_op jit(solution)/shard_map/all_to_all | solution.py:744
  199.8 0.6 copy-start.5

commit v4 on v3

--- a/solution.py
+++ b/solution.py
@@ -59,21 +59,34 @@
     return wide[:rows] + wide[rows:] + mm(x2[:rows], w2[1])
 
 
-def product_long(x2s, w2):
+def product_pieces(x2s, w2, result):
     rows = x2s[0].shape[0] // 2
-    highs = [x[:rows] for x in x2s]
-    lows = [x[rows:] for x in x2s]
-    return mm(
-        jnp.concatenate(highs + lows + highs, axis=1),
-        jnp.concatenate([w2[0], w2[0], w2[1]], axis=0),
-    )
+    for t, x2 in enumerate(x2s):
+        at = slice(t * BLK, (t + 1) * BLK)
+        wide = mm(x2, w2.at[0][at])
+        part = wide[:rows] + wide[rows:]
+        result[...] = part if t == 0 else result[...] + part
+        yield
+        result[...] += mm(x2[:rows], w2.at[1][at])
+        yield
+
+
+def interleave(*works):
+    works = list(works)
+    while works:
+        works = [w for w in works if next(w, w) is not w]
 
 
 def iota(dims, axis):
     return lax.broadcasted_iota(jnp.int32, dims, axis)
 
 
-def build_band(store, nbr, coef, halo):
+def build_band(*args):
+    for _ in band_pieces(*args):
+        pass
+
+
+def band_pieces(store, nbr, coef, halo):
     rows = BLK + 2 * halo
     count = nbr.shape[0]
     ids = [nbr[k : k + 1] for k in range(count)]
@@ -116,6 +129,7 @@
                         high = jnp.where(same, highs[k], high)
                         low = jnp.where(same, lows[k], low)
                 store(first, step, at, high, low)
+            yield
 
 
 def one_hot(ids, rows):
@@ -240,11 +254,8 @@
     def arriving(b):
         return pltpu.make_async_copy(band.at[b], w.at[halo + b], sems.at[b])
 
-    def begin(b, _):
+    for b in [0, blocks - 1] + list(range(1, blocks - 1)):
         arriving(b).start()
-        return 0
-
-    lax.fori_loop(0, blocks, begin, 0)
 
     leaving = []
     for e in list(range(ASTEPS)) + list(range(ASTEPS + blocks, total)):
@@ -276,11 +287,8 @@
         bulks[b + ASTEPS] = bulk[:, at]
         surfs[b + ASTEPS] = surf[:, at]
 
-    def arrived(b, _):
-        arriving(b).wait()
-        return 0
-
-    lax.fori_loop(0, blocks, arrived, 0)
+    arriving(0).wait()
+    arriving(blocks - 1).wait()
 
     slot = iota((states, BLK), 0) // fields
     for s in range(1, ASTEPS + 1):
@@ -315,6 +323,9 @@
                 zt[b + ASTEPS] = jnp.concatenate([zh, zl], axis=0)
 
         def together(i, _, s=s, edge=edge, inner=inner):
+            if s == 1:
+                arriving(1 + 2 * i).wait()
+                arriving(2 + 2 * i).wait()
             inner(s + 2 * i)
             inner(s + 2 * i + 1)
             edge(s + i)
@@ -322,6 +333,9 @@
             return 0
 
         def alone(i, _, s=s, inner=inner):
+            if s == 1:
+                arriving(1 + 2 * i).wait()
+                arriving(2 + 2 * i).wait()
             inner(s + 2 * i)
             inner(s + 2 * i + 1)
             return 0
@@ -476,28 +490,59 @@
             out[row : row + 1, :] = value[b : b + 1, i * 128 : (i + 1) * 128]
 
 
-def edge_kernel(before, after, atm, kept, mid, q, vertical, band, far, out, w, sides, sa, sb, sems):
+def edge_kernel(
+    before, after, atm, kept, mid, q, vertical, band, far, out, w, halos, sides, sa, sb, staged, wsems, sems, osems
+):
+    rows = atm.shape[0]
     blocks = q.shape[0]
-    count = 2 * ASTEPS - 1
     halo = ASTEPS - 1
-    copies = []
-    for side in range(2):
-        at = slice(0, 2 * BLK) if side == 0 else slice((blocks - 2) * BLK, blocks * BLK)
-        copy = pltpu.make_async_copy(atm.at[:, at], sides.at[side], sems.at[2 * count + side])
-        copy.start()
-        copies.append(copy)
+    count = halo + ASTEPS
+    arrivals = [
+        pltpu.make_async_copy(before, halos.at[0], sems.at[0]),
+        pltpu.make_async_copy(after, halos.at[1], sems.at[1]),
+        pltpu.make_async_copy(atm.at[:, : 2 * BLK], sides.at[0], sems.at[2]),
+        pltpu.make_async_copy(atm.at[:, (blocks - 2) * BLK :], sides.at[1], sems.at[3]),
+    ]
     sources = [far.at[i] for i in range(halo)] + [band.at[i] for i in range(ASTEPS)]
     sources += [band.at[blocks - ASTEPS + i] for i in range(ASTEPS)] + [far.at[halo + i] for i in range(halo)]
-    for i, source in enumerate(sources):
-        copy = pltpu.make_async_copy(source, w.at[i], sems.at[i])
+    bands = [pltpu.make_async_copy(source, w.at[i], wsems.at[i]) for i, source in enumerate(sources)]
+    needed = [list(range(ASTEPS)) + list(range(count + halo, 2 * count))]
+    needed += [[ASTEPS - 1 + i, count + halo - i] for i in range(1, ASTEPS)]
+    for copy in arrivals:
         copy.start()
-        copies.append(copy)
+    for group in needed:
+        for i in group:
+            bands[i].start()
+
+    def leaving(b):
+        at = pl.ds(pl.multiple_of(b * BLK, BLK), BLK)
+        return pltpu.make_async_copy(staged.at[b], out.at[:, at], osems.at[b])
+
+    def mixed(source, shift):
+        def one(b):
+            qh, ql = halves(q[b])
+            x2 = source[b - shift]
+            high = jnp.concatenate([x2[:rows], qh], axis=0)
+            low = jnp.concatenate([x2[rows:], ql], axis=0)
+            wide = mm(vertical[...], high)
+            staged[b] = wide[:rows] + wide[rows:] + mm(vertical[:rows], low)
+
+        def pair(i, _):
+            one(2 * i)
+            one(2 * i + 1)
+            leaving(2 * i).start()
+            leaving(2 * i + 1).start()
+            return 0
+
+        return pair
+
+    lax.fori_loop(ASTEPS // 2, (blocks - ASTEPS) // 2, mixed(mid, ASTEPS), 0)
+    for copy in arrivals:
+        copy.wait()
     for i in range(ASTEPS):
         at = slice(i * BLK, (i + 1) * BLK)
-        sa[i] = stacked(before[:, at])
-        sa[6 + 2 + i] = stacked(after[:, at])
-    for copy in copies:
-        copy.wait()
+        sa[i] = stacked(halos[0, :, at])
+        sa[6 + 2 + i] = stacked(halos[1, :, at])
     for i in range(2):
         at = slice(i * BLK, (i + 1) * BLK)
         sa[ASTEPS + i] = stacked(sides[0, :, at])
@@ -506,12 +551,15 @@
     for s in range(1, ASTEPS + 1):
         source, target = buffers[(s - 1) % 2], buffers[s % 2]
         last = s == ASTEPS
+        for i in needed[s - 1]:
+            bands[i].wait()
 
         def one(i, _, s=s, source=source, target=target, last=last):
             for side in range(2):
                 base = 6 * side
                 k = s - 1 + i if side == 0 else count + ASTEPS - s + i
-                value = stacked(product_long([source[base + i + d] for d in range(3)], (w[k, 0], w[k, 1])))
+                x2 = jnp.concatenate([source[base + i + d] for d in range(3)], axis=1)
+                value = stacked(product(x2, (w[k, 0], w[k, 1])))
                 target[base + i + (2 * side if not last else 0)] = value
             return 0
 
@@ -520,28 +568,18 @@
             for i in range(2):
                 target[ASTEPS + i] = kept[(s - 1) * 4 + i]
                 target[6 + i] = kept[(s - 1) * 4 + 2 + i]
-    rows = out.shape[0]
     final = buffers[ASTEPS % 2]
-
-    def mixed(source, shift):
-        def one(b, _):
-            at = pl.ds(pl.multiple_of(b * BLK, BLK), BLK)
-            qh, ql = halves(q[b])
-            x2 = source[b - shift]
-            high = jnp.concatenate([x2[:rows], qh], axis=0)
-            low = jnp.concatenate([x2[rows:], ql], axis=0)
-            wide = mm(vertical[...], high)
-            out[:, at] = wide[:rows] + wide[rows:] + mm(vertical[:rows], low)
-            return 0
-
-        return one
-
-    lax.fori_loop(0, ASTEPS, mixed(final, 0), 0, unroll=2)
-    lax.fori_loop(ASTEPS, blocks - ASTEPS, mixed(mid, ASTEPS), 0, unroll=2)
-    lax.fori_loop(blocks - ASTEPS, blocks, mixed(final, blocks - ASTEPS - 6), 0, unroll=2)
-
-
-def ocean_kernel(ocean, before, after, nbr, coef, omix, flux, out, x2, wa, wb):
+    lax.fori_loop(0, ASTEPS // 2, mixed(final, 0), 0)
+    lax.fori_loop((blocks - ASTEPS) // 2, blocks // 2, mixed(final, blocks - ASTEPS - 6), 0)
+
+    def done(b, _):
+        leaving(b).wait()
+        return 0
+
+    lax.fori_loop(0, blocks, done, 0)
+
+
+def ocean_kernel(ocean, before, after, nbr, coef, omix, flux, out, x2, wa, wb, ma, mb, staged, sems):
     levels = omix.shape[0]
     fields = flux.shape[0]
     columns = ocean.shape[1]
@@ -569,31 +607,41 @@
             w[0, first : first + size, lanes] = high
             w[1, first : first + size, lanes] = low
 
-        build_band(store, nbr[:, at] - b * BLK, coef[:, at], HO)
-
-    def finish(b, w):
+        return band_pieces(store, nbr[:, at] - b * BLK, coef[:, at], HO)
+
+    def finish(b, w, moved):
+        yield from product_pieces([x2[b + d] for d in range(1 + 2 * HO // BLK)], w, moved)
         at = pl.ds(pl.multiple_of(b * BLK, BLK), BLK)
-        source = jnp.concatenate([x2[b + d] for d in range(1 + 2 * HO // BLK)], axis=1)
-        moved = product(source, (w[0], w[1]))
         for f in range(fields):
             rows = slice(f * levels, (f + 1) * levels)
             high, low = halves(moved[rows])
             wide = mm(mix2, high)
-            out[rows, at] = (
+            staged[b, rows] = (
                 wide[:levels] + wide[levels:] + mm(mix2[:levels], low) + top * flux[f : f + 1, at]
             )
-
-    build(0, wa)
+            yield
+
+    def leaving(b):
+        at = pl.ds(pl.multiple_of(b * BLK, BLK), BLK)
+        return pltpu.make_async_copy(staged.at[b], out.at[:, at], sems.at[b])
+
+    interleave(build(0, wa))
 
     def one(i, _):
         b = 2 * i
-        build(b + 1, wb)
-        finish(b, wa)
-        build(jnp.minimum(b + 2, blocks - 1), wa)
-        finish(b + 1, wb)
+        interleave(build(b + 1, wb), finish(b, wa, ma))
+        interleave(build(jnp.minimum(b + 2, blocks - 1), wa), finish(b + 1, wb, mb))
+        leaving(b).start()
+        leaving(b + 1).start()
         return 0
 
     lax.fori_loop(0, blocks // 2, one, 0)
+
+    def done(b, _):
+        leaving(b).wait()
+        return 0
+
+    lax.fori_loop(0, blocks, done, 0)
 
 
 def after_all(value, *others):
@@ -669,12 +717,6 @@
     pack_before = lax.ppermute(last, AXES, up)
     pack_after = lax.ppermute(first, AXES, down)
 
-    later, later_sea = lax.optimization_barrier((atm, ocean, first, last))[:2]
-    atm_before = lax.ppermute(later[:, columns - WIDE :], AXES, up)
-    atm_after = lax.ppermute(later[:, :WIDE], AXES, down)
-    sea_before = lax.ppermute(later_sea[:, cells - HO :], AXES, up)
-    sea_after = lax.ppermute(later_sea[:, :HO], AXES, down)
-
     band = call(
         band_kernel,
         shape((blocks, 2, window, BLK), BF),
@@ -682,6 +724,13 @@
         out_specs=anywhere,
         scratch=[pltpu.VMEM((blocks, 2, window, BLK), BF), pltpu.SemaphoreType.DMA((blocks,))],
     )(after_all(atm_nbr, y), atm_nbr_coef)
+
+    pack_before, pack_after = lax.optimization_barrier((pack_before, pack_after, band))[:2]
+    later, later_sea = lax.optimization_barrier((atm, ocean, pack_before, pack_after))[:2]
+    atm_before = lax.ppermute(later[:, columns - WIDE :], AXES, up)
+    atm_after = lax.ppermute(later[:, :WIDE], AXES, down)
+    sea_before = lax.ppermute(later_sea[:, cells - HO :], AXES, up)
+    sea_after = lax.ppermute(later_sea[:, :HO], AXES, down)
 
     total = blocks + 2 * ASTEPS
     halo = ASTEPS - 1
@@ -705,7 +754,7 @@
             pltpu.VMEM((total, fields, BLK), F32),
             pltpu.SemaphoreType.DMA((blocks + 2 * halo,)),
         ],
-    )(atm, y, after_all(pack_before, band), pack_after, bulk_coef, atm_surface, gains, band)
+    )(atm, y, pack_before, pack_after, bulk_coef, atm_surface, gains, band)
 
     outgoing = call(
         send_kernel,
@@ -718,13 +767,18 @@
     atm_final = call(
         edge_kernel,
         shape((rows, columns)),
-        in_specs=[vmem] * 2 + [anywhere] + [vmem] * 4 + [anywhere] * 2,
+        in_specs=[anywhere] * 3 + [vmem] * 4 + [anywhere] * 2,
+        out_specs=anywhere,
         scratch=[
             pltpu.VMEM((2 * (2 * ASTEPS - 1), 2, window, BLK), BF),
+            pltpu.VMEM((2, rows, WIDE), F32),
             pltpu.VMEM((2, rows, 2 * BLK), F32),
             pltpu.VMEM((12, 2 * rows, BLK), BF),
             pltpu.VMEM((12, 2 * rows, BLK), BF),
-            pltpu.SemaphoreType.DMA((4 * ASTEPS,)),
+            pltpu.VMEM((blocks, rows, BLK), F32),
+            pltpu.SemaphoreType.DMA((2 * (2 * ASTEPS - 1),)),
+            pltpu.SemaphoreType.DMA((4,)),
+            pltpu.SemaphoreType.DMA((blocks,)),
         ],
     )(after_all(atm_before, outgoing), atm_after, atm, kept, mid, q, vertical, band, far)
 
@@ -747,10 +801,15 @@
         ocean_kernel,
         shape((fields * lo, cells)),
         in_specs=[vmem] * 7,
+        out_specs=anywhere,
         scratch=[
             pltpu.VMEM(((cells + 2 * HO) // BLK, 2 * fields * lo, BLK), BF),
             pltpu.VMEM((2, BLK + 2 * HO, BLK), BF),
             pltpu.VMEM((2, BLK + 2 * HO, BLK), BF),
+            pltpu.VMEM((fields * lo, BLK), F32),
+            pltpu.VMEM((fields * lo, BLK), F32),
+            pltpu.VMEM((cells // BLK, fields * lo, BLK), F32),
+            pltpu.SemaphoreType.DMA((cells // BLK,)),
         ],
     )(ocean, after_all(sea_before, back), sea_after, ocean_nbr, ocean_nbr_coef, ocean_mix, flux)
 

time: 206 us -> 168 us (0.82)
  waiting for transfers between devices: 43.5 us -> 12.5 us
  Pallas kernels: 131 us -> 123 us
    ppermute x1, waiting for transfers between devices: 41.6 us -> 0.01 us  [per_device(): pack_before = lax.ppermute(last, AXES, up)]
    ppermute x1, waiting for transfers between devices: 0.01 us -> 12.5 us  [per_device(): atm_before = lax.ppermute(later[:, columns - WIDE:], AXES, up)]
    pallas_call x2, Pallas kernels: 59.2 us -> 54.7 us  [the longest x1 29.5 us: per_device(): call(ocean_kernel, shape((fields * lo, cells)), in_specs=[vmem] * 7, out_...]
    pallas_call x1, Pallas kernels: 34.7 us -> 31.7 us  [per_device(): call(interior_kernel, (shape((blocks, states, BLK)), shape((4 * halo, 2 *...]
    ppermute x1, starting transfers between devices: 0.01 us -> 2.99 us  [per_device(): pack_before = lax.ppermute(last, AXES, up)]
    ppermute x1, starting transfers between devices: 2.94 us -> 0.01 us  [per_device(): atm_before = lax.ppermute(later[:, columns - WIDE:], AXES, up)]
    all_to_all x1, starting transfers between devices: 2.57 us -> 5.41 us  [per_device(): lax.all_to_all(back, AXES, split_axis=0, concat_axis=0, tiled=True)]
  transfers between devices with their start and end apart: 8 -> 8, of which waited for: 2 -> 1; matrix products, arithmetic and copies ran while one was open for 1% -> 1% of each run, Pallas kernels for 58% -> 66%
where the time goes in v4:
time: 168 us
  Pallas kernels  123 us (73%)
  starting transfers between devices  25.9 us (15%)
  waiting for transfers between devices  12.5 us (7%)
  local copies, waits for them, and re-layouts  5.5 us (3%)
    pallas_call x1, Pallas kernels, per_device(): call(interior_kernel, (shape((blocks, states, BLK)), shape((4 * halo, 2 *...  31.7 us
    pallas_call x1, Pallas kernels, per_device(): call(ocean_kernel, shape((fields * lo, cells)), in_specs=[vmem] * 7, out_...  29.5 us
    pallas_call x1, Pallas kernels, per_device(): call(edge_kernel, shape((rows, columns)), in_specs=[anywhere] * 3 + [vmem...  25.2 us
    pallas_call x1, Pallas kernels, per_device(): call(exchange_kernel, (shape((fields, cells)), shape((peers, 2 * parts, l...  13.3 us
    ppermute x1, waiting for transfers between devices, per_device(): atm_before = lax.ppermute(later[:, columns - WIDE:], AXES, up)  12.5 us
    pallas_call x1, Pallas kernels, per_device(): call(band_kernel, shape((blocks, 2, window, BLK), BF), in_specs=[vmem] *...  7.48 us
    pallas_call x1, Pallas kernels, per_device(): call(prepare_kernel(fields), (shape((states, columns)), shape((1, columns...  6.43 us
    all_to_all x1, starting transfers between devices, per_device(): lax.all_to_all(back, AXES, split_axis=0, concat_axis=0, tiled=True)  5.41 us
  transfers between devices with their start and end apart: 8, of which 1 were waited for; matrix products, arithmetic and copies ran while one was open for 1% of the time, Pallas kernels for 66%

profile of v4, /device:TPU:0, one launch (start us, length us, event | category | flops | bytes accessed | tf_op | source)
XLA Modules:
  0.0 167.7 jit_solution(2708705833964041775)
XLA Ops:
  0.6 0.0 slice-start
  0.6 6.4 %shard_map.166 = (f32[16,4096]{1,0:T(8,128)}, f32[1,4096]{1,0:T(1,128)}, f32[40,1024]{1,0:T(8,128)}, f32[40,1024]{1,0:T(8,128)}, f32[16,128]{1,0:T(8,128)}, /*index=5*/bf16[576,304]{1,0:T(8,128)(2,1)}) custom-call(f32[72,72]{1,0:T(8,128)} %mix.1, f32[80,80]{1,0:T(8,128)} %omix.5, f32[288,4096]{1,0:T(8,128)} %bitcast.6, f32[320,4096]{1,0:T(8,128)} %bitcast.12, ...), custom_call_target="tpu_custom_call" | custom-call | flops 1000000 | bytes 10000 | tf_op jit(solution)/shard_map/pallas_call | solution.py:693
  7.1 3.0 %collective-permute-start = (f32[40,1024]{1,0:T(8,128)}, f32[40,1024]{1,0:T(8,128)S(1)}, u32[]{:S(2)}, u32[]{:S(2)}) collective-permute-start(f32[40,1024]{1,0:T(8,128)} %get-tuple-element.24), channel_id=1, source_target_pairs={{0,1},{1,2},{2,3},{3,4},{4,5},{5,6},{6,7},{7,8},{8,9},{9,10},{10,1... | collective-permute-start | bytes 491528 | tf_op jit(solution)/shard_map/ppermute | solution.py:717
  10.1 3.5 %collective-permute-start.1 = (f32[40,1024]{1,0:T(8,128)}, f32[40,1024]{1,0:T(8,128)S(1)}, u32[]{:S(2)}, u32[]{:S(2)}) collective-permute-start(f32[40,1024]{1,0:T(8,128)} %get-tuple-element.25), channel_id=1, source_target_pairs={{1,0},{2,1},{3,2},{4,3},{5,4},{6,5},{7,6},{8,7},{9,8},{10,9},{11,1... | collective-permute-start | bytes 491528 | tf_op jit(solution)/shard_map/ppermute | solution.py:718
  13.6 7.5 %shard_map.167.band = bf16[16,2,768,256]{3,2,1,0:T(8,128)(2,1)} custom-call(s32[6,4096]{1,0:T(8,128)} %nbr.4, f32[6,4096]{1,0:T(8,128)} %coef.5), custom_call_target="tpu_custom_call" | custom-call | flops 1000000 | bytes 10000 | tf_op jit(solution)/shard_map/pallas_call | solution.py:720
  21.1 0.0 collective-permute-done.before
  21.1 1.2 fusion.1
  22.4 0.0 collective-permute-start.2
  22.4 5.3 %collective-permute-start.3 = (f32[288,1024]{1,0:T(8,128)S(1)}, f32[288,1024]{1,0:T(8,128)S(1)}, u32[]{:S(2)}, u32[]{:S(2)}) collective-permute-start(f32[288,1024]{1,0:T(8,128)S(1)} %get-tuple-element.47), channel_id=1, source_target_pairs={{1,0},{2,1},{3,2},{4,3},{5,4},{6,5},{7,6},{8,7},{9,8},{10,9},{11,1... | collective-permute-start | bytes 3538952 | tf_op jit(solution)/shard_map/ppermute | solution.py:731
  27.7 31.7 %shard_map.168 = (f32[16,16,256]{2,1,0:T(8,128)}, bf16[12,576,256]{2,1,0:T(8,128)(2,1)}, bf16[8,576,256]{2,1,0:T(8,128)(2,1)}, bf16[6,2,768,256]{3,2,1,0:T(8,128)(2,1)}) custom-call(f32[288,4096]{1,0:T(8,128)} %bitcast.7, f32[16,4096]{1,0:T(8,128)} %get-tuple-element.26.y, f32[40,1024]{1,0:T(8,128)} %copy-done.2, f32[40,1024]{1,0:T(8,128)} %copy-done.3, ...), custom_call_target="tpu_custom_call" | custom-call | flops 1000000 | bytes 10000 | tf_op jit(solution)/shard_map/pallas_call | solution.py:737
  59.4 4.2 %shard_map.169 = f32[32,8,256]{2,1,0:T(8,128)} custom-call(f32[16,16,256]{2,1,0:T(8,128)} %get-tuple-element.32.q, s32[32,512]{1,0:T(8,128)} %bitcast.17), custom_call_target="tpu_custom_call" | custom-call | flops 1000000 | bytes 10000 | tf_op jit(solution)/shard_map/pallas_call | solution.py:759
  63.6 3.3 %all-to-all-start = ((f32[32,8,256]{2,1,0:T(8,128)}), f32[32,8,256]{2,1,0:T(8,128)}, u32[]{:S(2)}, u32[]{:S(2)}) async-start(f32[32,8,256]{2,1,0:T(8,128)} %shard_map.169), calls=%async_computation | async-start | bytes 524288 | tf_op jit(solution)/shard_map/all_to_all | solution.py:765
  67.0 2.2 %fusion = (f32[320,384]{1,0:T(8,128)}, f32[320,384]{1,0:T(8,128)}) fusion(f32[320,4096]{1,0:T(8,128)} %bitcast.13), kind=kLoop, calls=%fused_computation | loop fusion | bytes 1966080 | tf_op jit(solution)/shard_map/slice | solution.py:733
  69.2 1.6 collective-permute-start.4
  70.7 3.8 %collective-permute-start.5 = (f32[320,384]{1,0:T(8,128)}, f32[320,384]{1,0:T(8,128)}, u32[]{:S(2)}, u32[]{:S(2)}) collective-permute-start(f32[320,384]{1,0:T(8,128)} %get-tuple-element.45), channel_id=1, source_target_pairs={{1,0},{2,1},{3,2},{4,3},{5,4},{6,5},{7,6},{8,7},{9,8},{10,9},{11,1... | collective-permute-start | bytes 1474568 | tf_op jit(solution)/shard_map/ppermute | solution.py:733
  74.5 12.5 %collective-permute-done.2.before = f32[288,1024]{1,0:T(8,128)S(1)} collective-permute-done((f32[288,1024]{1,0:T(8,128)}, f32[288,1024]{1,0:T(8,128)S(1)}, u32[]{:S(2)}, u32[]{:S(2)}) %collective-permute-start.2) | collective-permute-done | bytes 1179680 | tf_op jit(solution)/shard_map/ppermute | solution.py:730
  87.0 1.0 copy-done
  88.0 0.4 copy-done.1
  88.4 25.2 %shard_map.170 = f32[288,4096]{1,0:T(8,128)} custom-call(f32[288,1024]{1,0:T(8,128)} %copy-done, f32[288,1024]{1,0:T(8,128)} %copy-done.1, f32[288,4096]{1,0:T(8,128)} %bitcast.8, bf16[12,576,256]{2,1,0:T(8,128)(2,1)} %get-tuple-element.34.kept, bf16[8,576,256]{2,1,0:T(8,128)(2,1)} %get-tuple-element.35.mid, f32[16,16,256]{2,1,0:T(8,128)} %get-tuple-element.32.q, ...), custom_call_target="tpu_custom_call" | custom-call | flops 1000000 | bytes 10000 | tf_op jit(solution)/shard_map/pallas_call | solution.py:767
  113.6 13.3 %shard_map.171 = (f32[4,4096]{1,0:T(4,128)}, f32[32,4,256]{2,1,0:T(4,128)}) custom-call(f32[32,8,256]{2,1,0:T(8,128)} %all-to-all-done.recv, s32[4,4096]{1,0:T(4,128)} %slot.1, f32[4,4096]{1,0:T(4,128)} %weight.1, f32[1,4096]{1,0:T(1,128)} %get-tuple-element.40.yo, f32[40,1024]{1,0:T(8,128)} %copy-done.2, f32[40,1024]{1,0:T(8,128)} %copy-done.3, ...), custom_call_target="tpu_custom_call" | custom-call | flops 1000000 | bytes 10000 | tf_op jit(solution)/shard_map/pallas_call | solution.py:786
  126.9 5.4 %all-to-all-start.1 = ((f32[32,4,256]{2,1,0:T(4,128)}), f32[32,4,256]{2,1,0:T(4,128)S(1)}, u32[]{:S(2)}, u32[]{:S(2)}) async-start(f32[32,4,256]{2,1,0:T(4,128)} %get-tuple-element.41), calls=%async_computation.1 | async-start | bytes 262144 | tf_op jit(solution)/shard_map/all_to_all | solution.py:798
  132.3 29.5 %shard_map.172 = f32[320,4096]{1,0:T(8,128)} custom-call(f32[320,4096]{1,0:T(8,128)} %bitcast.14, f32[320,384]{1,0:T(8,128)} %collective-permute-done.4.before, f32[320,384]{1,0:T(8,128)} %collective-permute-done.5.after, s32[6,4096]{1,0:T(8,128)} %nbr.6, f32[6,4096]{1,0:T(8,128)} %coef.7, f32[80,80]{1,0:T(8,128)} %omix.5, f32[4,4096]{1,0:T(4,128)} %get-tuple-element.43.flux), custom_call_target="tpu_custom_call" | custom-call | flops 1000000 | bytes 10000 | tf_op jit(solution)/shard_map/pallas_call | solution.py:800
  161.9 0.6 copy-done.4
  162.5 5.1 %shard_map.173 = f32[32,128]{1,0:T(8,128)} custom-call(f32[32,4,256]{2,1,0:T(4,128)} %copy-done.4, s32[32,512]{1,0:T(8,128)} %bitcast.18, f32[4,4096]{1,0:T(4,128)} %surf.5), custom_call_target="tpu_custom_call" | custom-call | flops 1000000 | bytes 10000 | tf_op jit(solution)/shard_map/pallas_call | solution.py:816
  (17 shorter events, 0.0 us)
Async XLA Ops:
  0.6 20.5 %slice-start = ((s8[4718592]{0:T(1024)(128)(4,1)}), s8[4194304]{0:T(1024)(128)(4,1)S(1)}, s32[]{:S(2)}) async-start(s8[4718592]{0:T(1024)(128)(4,1)} %bitcast.9), calls=%async_computation.2 | async-start | bytes 8388608
  7.1 14.0 %collective-permute-start = (f32[40,1024]{1,0:T(8,128)}, f32[40,1024]{1,0:T(8,128)S(1)}, u32[]{:S(2)}, u32[]{:S(2)}) collective-permute-start(f32[40,1024]{1,0:T(8,128)} %get-tuple-element.24), channel_id=1, source_target_pairs={{0,1},{1,2},{2,3},{3,4},{4,5},{5,6},{6,7},{7,8},{8,9},{9,10},{10,1... | collective-permute-start | bytes 491528 | tf_op jit(solution)/shard_map/ppermute | solution.py:717
  10.1 11.0 %collective-permute-start.1 = (f32[40,1024]{1,0:T(8,128)}, f32[40,1024]{1,0:T(8,128)S(1)}, u32[]{:S(2)}, u32[]{:S(2)}) collective-permute-start(f32[40,1024]{1,0:T(8,128)} %get-tuple-element.25), channel_id=1, source_target_pairs={{1,0},{2,1},{3,2},{4,3},{5,4},{6,5},{7,6},{8,7},{9,8},{10,9},{11,1... | collective-permute-start | bytes 491528 | tf_op jit(solution)/shard_map/ppermute | solution.py:718
  13.6 7.5 %slice-start.1 = ((s8[4718592]{0:T(1024)(128)(4,1)}), s8[524288]{0:T(1024)(128)(4,1)S(1)}, s32[]{:S(2)}) async-start(s8[4718592]{0:T(1024)(128)(4,1)} %bitcast.9), calls=%async_computation.3 | async-start | bytes 1048576
  21.1 1.3 copy-start.2
  21.1 1.3 copy-start.3
  22.4 64.6 %collective-permute-start.2 = (f32[288,1024]{1,0:T(8,128)}, f32[288,1024]{1,0:T(8,128)S(1)}, u32[]{:S(2)}, u32[]{:S(2)}) collective-permute-start(f32[288,1024]{1,0:T(8,128)} %get-tuple-element.48), channel_id=1, source_target_pairs={{0,1},{1,2},{2,3},{3,4},{4,5},{5,6},{6,7},{7,8},{8,9},{9,10},{10,1... | collective-permute-start | bytes 3538952 | tf_op jit(solution)/shard_map/ppermute | solution.py:730
  22.4 64.6 %collective-permute-start.3 = (f32[288,1024]{1,0:T(8,128)S(1)}, f32[288,1024]{1,0:T(8,128)S(1)}, u32[]{:S(2)}, u32[]{:S(2)}) collective-permute-start(f32[288,1024]{1,0:T(8,128)S(1)} %get-tuple-element.47), channel_id=1, source_target_pairs={{1,0},{2,1},{3,2},{4,3},{5,4},{6,5},{7,6},{8,7},{9,8},{10,9},{11,1... | collective-permute-start | bytes 3538952 | tf_op jit(solution)/shard_map/ppermute | solution.py:731
  63.6 49.9 %all-to-all-start = ((f32[32,8,256]{2,1,0:T(8,128)}), f32[32,8,256]{2,1,0:T(8,128)}, u32[]{:S(2)}, u32[]{:S(2)}) async-start(f32[32,8,256]{2,1,0:T(8,128)} %shard_map.169), calls=%async_computation | async-start | bytes 524288 | tf_op jit(solution)/shard_map/all_to_all | solution.py:765
  69.2 63.2 %collective-permute-start.4 = (f32[320,384]{1,0:T(8,128)}, f32[320,384]{1,0:T(8,128)}, u32[]{:S(2)}, u32[]{:S(2)}) collective-permute-start(f32[320,384]{1,0:T(8,128)} %get-tuple-element.46), channel_id=1, source_target_pairs={{0,1},{1,2},{2,3},{3,4},{4,5},{5,6},{6,7},{7,8},{8,9},{9,10},{10,1... | collective-permute-start | bytes 1474568 | tf_op jit(solution)/shard_map/ppermute | solution.py:732
  70.7 61.6 %collective-permute-start.5 = (f32[320,384]{1,0:T(8,128)}, f32[320,384]{1,0:T(8,128)}, u32[]{:S(2)}, u32[]{:S(2)}) collective-permute-start(f32[320,384]{1,0:T(8,128)} %get-tuple-element.45), channel_id=1, source_target_pairs={{1,0},{2,1},{3,2},{4,3},{5,4},{6,5},{7,6},{8,7},{9,8},{10,9},{11,1... | collective-permute-start | bytes 1474568 | tf_op jit(solution)/shard_map/ppermute | solution.py:733
  87.0 1.0 copy-start
  87.0 1.4 copy-start.1
  126.9 35.0 %all-to-all-start.1 = ((f32[32,4,256]{2,1,0:T(4,128)}), f32[32,4,256]{2,1,0:T(4,128)S(1)}, u32[]{:S(2)}, u32[]{:S(2)}) async-start(f32[32,4,256]{2,1,0:T(4,128)} %get-tuple-element.41), calls=%async_computation.1 | async-start | bytes 262144 | tf_op jit(solution)/shard_map/all_to_all | solution.py:798
  161.9 0.7 copy-start.4

commit v5 on v4

--- a/solution.py
+++ b/solution.py
@@ -59,22 +59,14 @@
     return wide[:rows] + wide[rows:] + mm(x2[:rows], w2[1])
 
 
-def product_pieces(x2s, w2, result):
+def product_chunks(x2s, w2, chunk):
     rows = x2s[0].shape[0] // 2
-    for t, x2 in enumerate(x2s):
-        at = slice(t * BLK, (t + 1) * BLK)
-        wide = mm(x2, w2.at[0][at])
-        part = wide[:rows] + wide[rows:]
-        result[...] = part if t == 0 else result[...] + part
-        yield
-        result[...] += mm(x2[:rows], w2.at[1][at])
-        yield
-
-
-def interleave(*works):
-    works = list(works)
-    while works:
-        works = [w for w in works if next(w, w) is not w]
+    parts = []
+    for first in range(0, rows, chunk):
+        high = jnp.concatenate([x[first : first + chunk] for x in x2s], axis=1)
+        low = jnp.concatenate([x[rows + first : rows + first + chunk] for x in x2s], axis=1)
+        parts.append(product(jnp.concatenate([high, low], axis=0), w2))
+    return jnp.concatenate(parts, axis=0)
 
 
 def iota(dims, axis):
@@ -133,7 +125,10 @@
 
 
 def one_hot(ids, rows):
-    return jnp.where(iota((rows, ids.shape[1]), 0) == ids, 1.0, 0.0).astype(BF)
+    lanes = ids.shape[1]
+    wide = jnp.broadcast_to(ids.astype(F32), (rows, lanes)).astype(BF)
+    here = iota((rows, lanes), 0).astype(F32).astype(BF)
+    return jnp.where(here == wide, jnp.ones((rows, lanes), BF), jnp.zeros((rows, lanes), BF))
 
 
 def fold_rows(x, height):
@@ -215,8 +210,24 @@
     return body
 
 
-def band_kernel(nbr, coef, band, w, sems):
+def band_kernel(nbr, coef, *refs):
+    w, sems, side_sems = refs[-3:]
+    band = refs[0] if len(refs) == 4 else refs[2]
     blocks = nbr.shape[1] // BLK
+    halo = (w.shape[2] - BLK) // 2
+    sides = []
+    if len(refs) > 4:
+        for i, target in enumerate(refs[3:5]):
+            for k, (source, width) in enumerate(zip(refs[:2], (WIDE, HO))):
+                rows, columns = source.shape
+                first = 0 if i == 0 else columns - width
+                copy = pltpu.make_async_copy(
+                    source.at[:, first : first + width],
+                    target.at[:rows, k * WIDE : k * WIDE + width],
+                    side_sems.at[2 * i + k],
+                )
+                copy.start()
+                sides.append(copy)
 
     def copy(b):
         return pltpu.make_async_copy(w.at[b], band.at[b], sems.at[b])
@@ -228,7 +239,7 @@
             w[b, 0, first : first + step, lanes] = high
             w[b, 1, first : first + step, lanes] = low
 
-        build_band(store, nbr[:, at] - b * BLK, coef[:, at], HA)
+        build_band(store, nbr[:, at] - b * BLK, coef[:, at], halo)
         copy(b).start()
         return 0
 
@@ -239,12 +250,16 @@
         return 0
 
     lax.fori_loop(0, blocks, finish, 0)
+    for side in sides:
+        side.wait()
 
 
 def interior_kernel(
-    atm, y, before, after, bulk, surf, gains, band, q, kept, mid, far, w, sa, sb, za, zb, bulks, surfs, sems
+    y, before, after, bulk, surf, gains, atm_in, band, q, kept_out, mid_out, far, w, sa, sb, za, zb, bulks, surfs, atm, kept, mid, sems, csems
 ):
     rows, columns = atm.shape
+    load = pltpu.make_async_copy(atm_in, atm, csems.at[0])
+    load.start()
     blocks = columns // BLK
     fields = bulk.shape[0]
     states = fields * ASTEPS
@@ -278,6 +293,7 @@
         copy = pltpu.make_async_copy(w.at[e - 1], far.at[i], sems.at[blocks + i])
         copy.start()
         leaving.append(copy)
+    load.wait()
     for b in range(blocks):
         at = slice(b * BLK, (b + 1) * BLK)
         both = stacked(jnp.concatenate([atm[:, at], y[:, at]], axis=0))
@@ -348,6 +364,12 @@
             for i, b in enumerate((s, s + 1, blocks - 2 - s, blocks - 1 - s)):
                 kept[(s - 1) * 4 + i, :rows] = xt[b, :rows]
                 kept[(s - 1) * 4 + i, rows:] = xt[b, height : height + rows]
+            at = slice((s - 1) * 4, s * 4)
+            copy = pltpu.make_async_copy(kept.at[at], kept_out.at[at], csems.at[s])
+        else:
+            copy = pltpu.make_async_copy(mid, mid_out, csems.at[s])
+        copy.start()
+        leaving.append(copy)
     for copy in leaving:
         copy.wait()
 
@@ -498,8 +520,8 @@
     halo = ASTEPS - 1
     count = halo + ASTEPS
     arrivals = [
-        pltpu.make_async_copy(before, halos.at[0], sems.at[0]),
-        pltpu.make_async_copy(after, halos.at[1], sems.at[1]),
+        pltpu.make_async_copy(before.at[:rows, :WIDE], halos.at[0], sems.at[0]),
+        pltpu.make_async_copy(after.at[:rows, :WIDE], halos.at[1], sems.at[1]),
         pltpu.make_async_copy(atm.at[:, : 2 * BLK], sides.at[0], sems.at[2]),
         pltpu.make_async_copy(atm.at[:, (blocks - 2) * BLK :], sides.at[1], sems.at[3]),
     ]
@@ -558,8 +580,8 @@
             for side in range(2):
                 base = 6 * side
                 k = s - 1 + i if side == 0 else count + ASTEPS - s + i
-                x2 = jnp.concatenate([source[base + i + d] for d in range(3)], axis=1)
-                value = stacked(product(x2, (w[k, 0], w[k, 1])))
+                window = [source.at[base + i + d] for d in range(3)]
+                value = stacked(product_chunks(window, (w[k, 0], w[k, 1]), rows // 3))
                 target[base + i + (2 * side if not last else 0)] = value
             return 0
 
@@ -579,19 +601,32 @@
     lax.fori_loop(0, blocks, done, 0)
 
 
-def ocean_kernel(ocean, before, after, nbr, coef, omix, flux, out, x2, wa, wb, ma, mb, staged, sems):
+def ocean_kernel(ocean, omix, flux, before, after, band, out, w, x2, sides, staged, wsems, sems, osems):
     levels = omix.shape[0]
     fields = flux.shape[0]
     columns = ocean.shape[1]
     blocks = columns // BLK
+    arrivals = [
+        pltpu.make_async_copy(ref.at[:, WIDE:], sides.at[i], sems.at[i]) for i, ref in enumerate((before, after))
+    ]
+    for copy in arrivals:
+        copy.start()
+
+    def arriving(b):
+        return pltpu.make_async_copy(band.at[b], w.at[b], wsems.at[b])
+
+    for b in range(blocks):
+        arriving(b).start()
     eye = iota((levels, levels), 0) == iota((levels, levels), 1)
     step = omix[...] + jnp.where(eye, 1.0, 0.0)
     top = jnp.broadcast_to(step[:, 0:1], (levels, BLK))
     mix2 = stacked(step)
+    for copy in arrivals:
+        copy.wait()
 
     def part(first, width):
         pieces = []
-        for ref, begin, size in ((before, -HO, HO), (ocean, 0, columns), (after, columns, HO)):
+        for ref, begin, size in ((sides.at[0], -HO, HO), (ocean, 0, columns), (sides.at[1], columns, HO)):
             lo, hi = max(first, begin), min(first + width, begin + size)
             if lo < hi:
                 pieces.append(ref[:, lo - begin : hi - begin])
@@ -600,18 +635,14 @@
     for e in range((columns + 2 * HO) // BLK):
         x2[e] = stacked(part(e * BLK - HO, BLK))
 
-    def build(b, w):
+    def leaving(b):
         at = pl.ds(pl.multiple_of(b * BLK, BLK), BLK)
-
-        def store(first, size, lanes, high, low):
-            w[0, first : first + size, lanes] = high
-            w[1, first : first + size, lanes] = low
-
-        return band_pieces(store, nbr[:, at] - b * BLK, coef[:, at], HO)
-
-    def finish(b, w, moved):
-        yield from product_pieces([x2[b + d] for d in range(1 + 2 * HO // BLK)], w, moved)
+        return pltpu.make_async_copy(staged.at[b], out.at[:, at], osems.at[b])
+
+    def one(b):
         at = pl.ds(pl.multiple_of(b * BLK, BLK), BLK)
+        source = jnp.concatenate([x2[b + d] for d in range(1 + 2 * HO // BLK)], axis=1)
+        moved = product(source, (w[b, 0], w[b, 1]))
         for f in range(fields):
             rows = slice(f * levels, (f + 1) * levels)
             high, low = halves(moved[rows])
@@ -619,23 +650,19 @@
             staged[b, rows] = (
                 wide[:levels] + wide[levels:] + mm(mix2[:levels], low) + top * flux[f : f + 1, at]
             )
-            yield
-
-    def leaving(b):
-        at = pl.ds(pl.multiple_of(b * BLK, BLK), BLK)
-        return pltpu.make_async_copy(staged.at[b], out.at[:, at], sems.at[b])
-
-    interleave(build(0, wa))
-
-    def one(i, _):
-        b = 2 * i
-        interleave(build(b + 1, wb), finish(b, wa, ma))
-        interleave(build(jnp.minimum(b + 2, blocks - 1), wa), finish(b + 1, wb, mb))
-        leaving(b).start()
-        leaving(b + 1).start()
+
+    group = 4
+
+    def some(i, _):
+        for k in range(group):
+            arriving(group * i + k).wait()
+        for k in range(group):
+            one(group * i + k)
+        for k in range(group):
+            leaving(group * i + k).start()
         return 0
 
-    lax.fori_loop(0, blocks // 2, one, 0)
+    lax.fori_loop(0, blocks // group, some, 0)
 
     def done(b, _):
         leaving(b).wait()
@@ -717,20 +744,24 @@
     pack_before = lax.ppermute(last, AXES, up)
     pack_after = lax.ppermute(first, AXES, down)
 
-    band = call(
+    tall = max(rows, fields * lo)
+    band, wide_first, wide_last = call(
         band_kernel,
-        shape((blocks, 2, window, BLK), BF),
-        in_specs=[vmem] * 2,
-        out_specs=anywhere,
-        scratch=[pltpu.VMEM((blocks, 2, window, BLK), BF), pltpu.SemaphoreType.DMA((blocks,))],
-    )(after_all(atm_nbr, y), atm_nbr_coef)
-
-    pack_before, pack_after = lax.optimization_barrier((pack_before, pack_after, band))[:2]
-    later, later_sea = lax.optimization_barrier((atm, ocean, pack_before, pack_after))[:2]
-    atm_before = lax.ppermute(later[:, columns - WIDE :], AXES, up)
-    atm_after = lax.ppermute(later[:, :WIDE], AXES, down)
-    sea_before = lax.ppermute(later_sea[:, cells - HO :], AXES, up)
-    sea_after = lax.ppermute(later_sea[:, :HO], AXES, down)
+        (shape((blocks, 2, window, BLK), BF), shape((tall, WIDE + HO)), shape((tall, WIDE + HO))),
+        in_specs=[vmem] * 2 + [anywhere] * 2,
+        out_specs=(anywhere,) * 3,
+        scratch=[
+            pltpu.VMEM((blocks, 2, window, BLK), BF),
+            pltpu.SemaphoreType.DMA((blocks,)),
+            pltpu.SemaphoreType.DMA((4,)),
+        ],
+    )(after_all(atm_nbr, y), atm_nbr_coef, atm, ocean)
+
+    pack_before, pack_after, wide_first, wide_last = lax.optimization_barrier(
+        (pack_before, pack_after, wide_first, wide_last)
+    )
+    wide_before = lax.ppermute(wide_last, AXES, up)
+    wide_after = lax.ppermute(wide_first, AXES, down)
 
     total = blocks + 2 * ASTEPS
     halo = ASTEPS - 1
@@ -742,8 +773,8 @@
             shape((blocks - 2 * ASTEPS, 2 * rows, BLK), BF),
             shape((2 * halo, 2, window, BLK), BF),
         ),
-        in_specs=[vmem] * 7 + [anywhere],
-        out_specs=(vmem, vmem, vmem, anywhere),
+        in_specs=[vmem] * 6 + [anywhere] * 2,
+        out_specs=(vmem, anywhere, anywhere, anywhere),
         scratch=[
             pltpu.VMEM((total - 2, 2, window, BLK), BF),
             pltpu.VMEM((blocks, 2 * depth_k, BLK), BF),
@@ -752,9 +783,13 @@
             pltpu.VMEM((total, 2 * states, BLK), BF),
             pltpu.VMEM((total, fields, BLK), F32),
             pltpu.VMEM((total, fields, BLK), F32),
+            pltpu.VMEM((rows, columns), F32),
+            pltpu.VMEM((4 * halo, 2 * rows, BLK), BF),
+            pltpu.VMEM((blocks - 2 * ASTEPS, 2 * rows, BLK), BF),
             pltpu.SemaphoreType.DMA((blocks + 2 * halo,)),
+            pltpu.SemaphoreType.DMA((ASTEPS + 1,)),
         ],
-    )(atm, y, pack_before, pack_after, bulk_coef, atm_surface, gains, band)
+    )(y, pack_before, pack_after, bulk_coef, atm_surface, gains, atm, band)
 
     outgoing = call(
         send_kernel,
@@ -763,6 +798,43 @@
         scratch=[pltpu.VMEM((blocks * fields, BLK), F32)],
     )(q, picked)
     received = lax.all_to_all(outgoing, AXES, split_axis=0, concat_axis=0, tiled=True)
+
+    sea_blocks = cells // BLK
+    sea_band = call(
+        band_kernel,
+        shape((sea_blocks, 2, BLK + 2 * HO, BLK), BF),
+        in_specs=[vmem] * 2,
+        out_specs=anywhere,
+        scratch=[
+            pltpu.VMEM((sea_blocks, 2, BLK + 2 * HO, BLK), BF),
+            pltpu.SemaphoreType.DMA((sea_blocks,)),
+            pltpu.SemaphoreType.DMA((4,)),
+        ],
+    )(after_all(ocean_nbr, outgoing), ocean_nbr_coef)
+
+    flux, back = call(
+        exchange_kernel,
+        (shape((fields, cells)), shape((peers, 2 * parts, lanes))),
+        in_specs=[vmem] * 9,
+        scratch=[
+            pltpu.VMEM((2 * peers * parts * fields, lanes), BF),
+            pltpu.VMEM((cells // 128 + 2 * HO // 128, 8, 128), F32),
+            pltpu.VMEM((cells // BLK, lanes, remap_slot.shape[0] * BLK), BF),
+            pltpu.VMEM((1, cells), F32),
+            pltpu.VMEM((4 * peers * parts, lanes), F32),
+        ],
+    )(
+        after_all(received, sea_band),
+        remap_slot,
+        remap_weight,
+        yo,
+        pack_before,
+        pack_after,
+        ocean_nbr,
+        ocean_nbr_coef,
+        ocean_mix,
+    )
+    returned = lax.all_to_all(back, AXES, split_axis=0, concat_axis=0, tiled=True)
 
     atm_final = call(
         edge_kernel,
@@ -780,38 +852,23 @@
             pltpu.SemaphoreType.DMA((4,)),
             pltpu.SemaphoreType.DMA((blocks,)),
         ],
-    )(after_all(atm_before, outgoing), atm_after, atm, kept, mid, q, vertical, band, far)
-
-    received = after_all(received, atm_final)
-    flux, back = call(
-        exchange_kernel,
-        (shape((fields, cells)), shape((peers, 2 * parts, lanes))),
-        in_specs=[vmem] * 9,
-        scratch=[
-            pltpu.VMEM((2 * peers * parts * fields, lanes), BF),
-            pltpu.VMEM((cells // 128 + 2 * HO // 128, 8, 128), F32),
-            pltpu.VMEM((cells // BLK, lanes, remap_slot.shape[0] * BLK), BF),
-            pltpu.VMEM((1, cells), F32),
-            pltpu.VMEM((4 * peers * parts, lanes), F32),
-        ],
-    )(received, remap_slot, remap_weight, yo, pack_before, pack_after, ocean_nbr, ocean_nbr_coef, ocean_mix)
-    returned = lax.all_to_all(back, AXES, split_axis=0, concat_axis=0, tiled=True)
+    )(wide_before, wide_after, atm, kept, mid, after_all(q, back), vertical, band, far)
 
     ocean_final = call(
         ocean_kernel,
         shape((fields * lo, cells)),
-        in_specs=[vmem] * 7,
+        in_specs=[vmem] * 3 + [anywhere] * 3,
         out_specs=anywhere,
         scratch=[
+            pltpu.VMEM((sea_blocks, 2, BLK + 2 * HO, BLK), BF),
             pltpu.VMEM(((cells + 2 * HO) // BLK, 2 * fields * lo, BLK), BF),
-            pltpu.VMEM((2, BLK + 2 * HO, BLK), BF),
-            pltpu.VMEM((2, BLK + 2 * HO, BLK), BF),
-            pltpu.VMEM((fields * lo, BLK), F32),
-            pltpu.VMEM((fields * lo, BLK), F32),
-            pltpu.VMEM((cells // BLK, fields * lo, BLK), F32),
-            pltpu.SemaphoreType.DMA((cells // BLK,)),
+            pltpu.VMEM((2, fields * lo, HO), F32),
+            pltpu.VMEM((sea_blocks, fields * lo, BLK), F32),
+            pltpu.SemaphoreType.DMA((sea_blocks,)),
+            pltpu.SemaphoreType.DMA((2,)),
+            pltpu.SemaphoreType.DMA((sea_blocks,)),
         ],
-    )(ocean, after_all(sea_before, back), sea_after, ocean_nbr, ocean_nbr_coef, ocean_mix, flux)
+    )(ocean, ocean_mix, after_all(flux, atm_final), wide_before, wide_after, sea_band)
 
     surface_temp = call(
         settle_kernel,

time: 168 us -> 283 us (1.68)
  Pallas kernels: 123 us -> 235 us
  waiting for transfers between devices: 12.5 us -> 26.3 us
  starting transfers between devices: 25.9 us -> 18.7 us
  local copies, waits for them, and re-layouts: 5.5 us -> 2.57 us
    pallas_call x2 -> x3, Pallas kernels: 37 us -> 144 us  [the longest x1 103 us: per_device(): call(band_kernel, (shape((blocks, 2, window, BLK), BF), shape((tall, WIDE...]
    all_to_all x1, waiting for transfers between devices: 0.01 us -> 26.3 us  [per_device(): lax.all_to_all(outgoing, AXES, split_axis=0, concat_axis=0, tiled=True)]
    ppermute x4 -> x2, waiting for transfers between devices: 12.5 us -> 0.01 us  [the longest x1 0.01 us: per_device(): wide_before = lax.ppermute(wide_last, AXES, up)]
    ppermute x4 -> x2, starting transfers between devices: 10.7 us -> 5.39 us  [the longest x1 5.33 us: per_device(): wide_after = lax.ppermute(wide_first, AXES, down)]
    slice x2 -> x0, local copies, waits for them, and re-layouts: 3.44 us -> none  [the longest x1 2.2 us: per_device(): sea_after = lax.ppermute(later_sea[:, :HO], AXES, down)]
    pallas_call x1, Pallas kernels: 31.7 us -> 34.7 us  [per_device(): call(interior_kernel, (shape((blocks, states, BLK)), shape((4 * halo, 2 *...]
  transfers between devices with their start and end apart: 8 -> 6, of which waited for: 1 -> 1; matrix products, arithmetic and copies ran while one was open for 1% -> 0% of each run, Pallas kernels for 66% -> 79%
where the time goes in v5:
time: 283 us
  Pallas kernels  235 us (83%)
  waiting for transfers between devices  26.3 us (9%)
  starting transfers between devices  18.7 us (7%)
    pallas_call x1, Pallas kernels, per_device(): call(band_kernel, (shape((blocks, 2, window, BLK), BF), shape((tall, WIDE...  103 us
    pallas_call x1, Pallas kernels, per_device(): call(interior_kernel, (shape((blocks, states, BLK)), shape((4 * halo, 2 *...  34.7 us
    pallas_call x1, Pallas kernels, per_device(): call(ocean_kernel, shape((fields * lo, cells)), in_specs=[vmem] * 3 + [an...  31.2 us
    pallas_call x1, Pallas kernels, per_device(): call(edge_kernel, shape((rows, columns)), in_specs=[anywhere] * 3 + [vmem...  27.4 us
    all_to_all x1, waiting for transfers between devices, per_device(): lax.all_to_all(outgoing, AXES, split_axis=0, concat_axis=0, tiled=True)  26.3 us
    pallas_call x1, Pallas kernels, per_device(): call(exchange_kernel, (shape((fields, cells)), shape((peers, 2 * parts, l...  12.9 us
    pallas_call x1, Pallas kernels, per_device(): call(band_kernel, shape((sea_blocks, 2, BLK + 2 * HO, BLK), BF), in_specs...  9.27 us
    pallas_call x1, Pallas kernels, per_device(): call(prepare_kernel(fields), (shape((states, columns)), shape((1, columns...  6.07 us
  transfers between devices with their start and end apart: 6, of which 1 were waited for; matrix products, arithmetic and copies ran while one was open for 0% of the time, Pallas kernels for 79%

profile of v5, /device:TPU:0, one launch (start us, length us, event | category | flops | bytes accessed | tf_op | source)
XLA Modules:
  0.0 282.9 jit_solution(5807656779092139540)
XLA Ops:
  0.6 6.1 %shard_map.166 = (f32[16,4096]{1,0:T(8,128)}, f32[1,4096]{1,0:T(1,128)}, f32[40,1024]{1,0:T(8,128)}, f32[40,1024]{1,0:T(8,128)}, f32[16,128]{1,0:T(8,128)}, /*index=5*/bf16[576,304]{1,0:T(8,128)(2,1)}) custom-call(f32[72,72]{1,0:T(8,128)} %mix.1, f32[80,80]{1,0:T(8,128)} %omix.5, f32[288,4096]{1,0:T(8,128)} %bitcast.6, f32[320,4096]{1,0:T(8,128)} %bitcast.10, ...), custom_call_target="tpu_custom_call" | custom-call | flops 1000000 | bytes 10000 | tf_op jit(solution)/shard_map/pallas_call | solution.py:720
  6.7 3.0 %collective-permute-start = (f32[40,1024]{1,0:T(8,128)}, f32[40,1024]{1,0:T(8,128)S(1)}, u32[]{:S(2)}, u32[]{:S(2)}) collective-permute-start(f32[40,1024]{1,0:T(8,128)} %get-tuple-element.28), channel_id=1, source_target_pairs={{0,1},{1,2},{2,3},{3,4},{4,5},{5,6},{6,7},{7,8},{8,9},{9,10},{10,1... | collective-permute-start | bytes 491528 | tf_op jit(solution)/shard_map/ppermute | solution.py:744
  9.7 3.5 %collective-permute-start.1 = (f32[40,1024]{1,0:T(8,128)}, f32[40,1024]{1,0:T(8,128)S(1)}, u32[]{:S(2)}, u32[]{:S(2)}) collective-permute-start(f32[40,1024]{1,0:T(8,128)} %get-tuple-element.29), channel_id=1, source_target_pairs={{1,0},{2,1},{3,2},{4,3},{5,4},{6,5},{7,6},{8,7},{9,8},{10,9},{11,1... | collective-permute-start | bytes 491528 | tf_op jit(solution)/shard_map/ppermute | solution.py:745
  13.2 103.5 %shard_map.167 = (bf16[16,2,768,256]{3,2,1,0:T(8,128)(2,1)}, f32[320,1408]{1,0:T(8,128)}, f32[320,1408]{1,0:T(8,128)}) custom-call(s32[6,4096]{1,0:T(8,128)} %nbr.3, f32[6,4096]{1,0:T(8,128)} %coef.5, f32[288,4096]{1,0:T(8,128)} %bitcast.7, f32[320,4096]{1,0:T(8,128)} %bitcast.11), custom_call_target="tpu_custom_call" | custom-call | flops 1000000 | bytes 10000 | tf_op jit(solution)/shard_map/pallas_call | solution.py:748
  116.7 0.0 collective-permute-done.before
  116.7 0.0 collective-permute-done.1.after
  116.7 0.1 collective-permute-start.2
  116.8 5.3 %collective-permute-start.3 = (f32[320,1408]{1,0:T(8,128)}, f32[320,1408]{1,0:T(8,128)}, u32[]{:S(2)}, u32[]{:S(2)}) collective-permute-start(f32[320,1408]{1,0:T(8,128)} %get-tuple-element.35), channel_id=1, source_target_pairs={{1,0},{2,1},{3,2},{4,3},{5,4},{6,5},{7,6},{8,7},{9,8},{10,9},{11,1... | collective-permute-start | bytes 5406728 | tf_op jit(solution)/shard_map/ppermute | solution.py:764
  122.1 34.7 %shard_map.168 = (f32[16,16,256]{2,1,0:T(8,128)}, bf16[12,576,256]{2,1,0:T(8,128)(2,1)}, bf16[8,576,256]{2,1,0:T(8,128)(2,1)}, bf16[6,2,768,256]{3,2,1,0:T(8,128)(2,1)}) custom-call(f32[16,4096]{1,0:T(8,128)} %get-tuple-element.30.y, f32[40,1024]{1,0:T(8,128)} %copy-done.2, f32[40,1024]{1,0:T(8,128)} %copy-done.3, f32[4,4096]{1,0:T(4,128)} %bulk.3, ...), custom_call_target="tpu_custom_call" | custom-call | flops 1000000 | bytes 10000 | tf_op jit(solution)/shard_map/pallas_call | solution.py:768
  156.8 4.3 %shard_map.169 = f32[32,8,256]{2,1,0:T(8,128)} custom-call(f32[16,16,256]{2,1,0:T(8,128)} %get-tuple-element.47.q, s32[32,512]{1,0:T(8,128)} %bitcast.15), custom_call_target="tpu_custom_call" | custom-call | flops 1000000 | bytes 10000 | tf_op jit(solution)/shard_map/pallas_call | solution.py:794
  161.1 2.8 all-to-all-start
  163.9 9.3 %shard_map.170.band = bf16[16,2,1024,256]{3,2,1,0:T(8,128)(2,1)} custom-call(s32[6,4096]{1,0:T(8,128)} %nbr.5, f32[6,4096]{1,0:T(8,128)} %coef.7), custom_call_target="tpu_custom_call" | custom-call | flops 1000000 | bytes 10000 | tf_op jit(solution)/shard_map/pallas_call | solution.py:803
  173.2 26.3 %all-to-all-done.recv = f32[32,8,256]{2,1,0:T(8,128)S(1)} async-done(((f32[32,8,256]{2,1,0:T(8,128)}), f32[32,8,256]{2,1,0:T(8,128)S(1)}, u32[]{:S(2)}, u32[]{:S(2)}) %all-to-all-start) | async-done | bytes 262176 | tf_op jit(solution)/shard_map/all_to_all | solution.py:800
  199.4 0.7 copy-done.1
  200.1 12.9 %shard_map.171 = (f32[4,4096]{1,0:T(4,128)}, f32[32,4,256]{2,1,0:T(4,128)}) custom-call(f32[32,8,256]{2,1,0:T(8,128)} %copy-done.1, s32[4,4096]{1,0:T(4,128)} %slot.1, f32[4,4096]{1,0:T(4,128)} %weight.1, f32[1,4096]{1,0:T(1,128)} %get-tuple-element.45.yo, f32[40,1024]{1,0:T(8,128)} %copy-done.2, f32[40,1024]{1,0:T(8,128)} %copy-done.3, s32[6,4096]{1,0:T(8,128)} %nbr.5, ...), custom_call_target="tpu_custom_call" | custom-call | flops 1000000 | bytes 10000 | tf_op jit(solution)/shard_map/pallas_call | solution.py:815
  213.1 4.0 %all-to-all-start.1 = ((f32[32,4,256]{2,1,0:T(4,128)}), f32[32,4,256]{2,1,0:T(4,128)S(1)}, u32[]{:S(2)}, u32[]{:S(2)}) async-start(f32[32,4,256]{2,1,0:T(4,128)} %get-tuple-element.46), calls=%async_computation.1 | async-start | bytes 262144 | tf_op jit(solution)/shard_map/all_to_all | solution.py:837
  217.1 0.0 collective-permute-done.2.before
  217.1 0.0 collective-permute-done.3.after
  217.1 1.2 copy-done
  218.3 27.4 %shard_map.172 = f32[288,4096]{1,0:T(8,128)} custom-call(f32[320,1408]{1,0:T(8,128)} %copy-done, f32[320,1408]{1,0:T(8,128)} %collective-permute-done.3.after, f32[288,4096]{1,0:T(8,128)} %bitcast.9, bf16[12,576,256]{2,1,0:T(8,128)(2,1)} %get-tuple-element.40.kept, bf16[8,576,256]{2,1,0:T(8,128)(2,1)} %get-tuple-element.41.mid, ...), custom_call_target="tpu_custom_call" | custom-call | flops 1000000 | bytes 10000 | tf_op jit(solution)/shard_map/pallas_call | solution.py:839
  245.8 31.2 %shard_map.173 = f32[320,4096]{1,0:T(8,128)} custom-call(f32[320,4096]{1,0:T(8,128)} %bitcast.12, f32[80,80]{1,0:T(8,128)} %omix.5, f32[4,4096]{1,0:T(4,128)} %get-tuple-element.51.flux, f32[320,1408]{1,0:T(8,128)} %copy-done, f32[320,1408]{1,0:T(8,128)} %collective-permute-done.3.after, bf16[16,2,1024,256]{3,2,1,0:T(8,128)(2,1)} %shard_map.170.band), custom_call_target="tpu_custom_call" | custom-call | flops 1000000 | bytes 10000 | tf_op jit(solution)/shard_map/pallas_call | solution.py:857
  277.0 0.0 all-to-all-done.1.back
  277.0 0.6 copy-done.4
  277.7 5.2 %shard_map.174 = f32[32,128]{1,0:T(8,128)} custom-call(f32[32,4,256]{2,1,0:T(4,128)} %copy-done.4, s32[32,512]{1,0:T(8,128)} %bitcast.16, f32[4,4096]{1,0:T(4,128)} %surf.5), custom_call_target="tpu_custom_call" | custom-call | flops 1000000 | bytes 10000 | tf_op jit(solution)/shard_map/pallas_call | solution.py:873
  (7 shorter events, 0.0 us)
Async XLA Ops:
  6.7 110.0 %collective-permute-start = (f32[40,1024]{1,0:T(8,128)}, f32[40,1024]{1,0:T(8,128)S(1)}, u32[]{:S(2)}, u32[]{:S(2)}) collective-permute-start(f32[40,1024]{1,0:T(8,128)} %get-tuple-element.28), channel_id=1, source_target_pairs={{0,1},{1,2},{2,3},{3,4},{4,5},{5,6},{6,7},{7,8},{8,9},{9,10},{10,1... | collective-permute-start | bytes 491528 | tf_op jit(solution)/shard_map/ppermute | solution.py:744
  9.7 107.0 %collective-permute-start.1 = (f32[40,1024]{1,0:T(8,128)}, f32[40,1024]{1,0:T(8,128)S(1)}, u32[]{:S(2)}, u32[]{:S(2)}) collective-permute-start(f32[40,1024]{1,0:T(8,128)} %get-tuple-element.29), channel_id=1, source_target_pairs={{1,0},{2,1},{3,2},{4,3},{5,4},{6,5},{7,6},{8,7},{9,8},{10,9},{11,1... | collective-permute-start | bytes 491528 | tf_op jit(solution)/shard_map/ppermute | solution.py:745
  116.7 5.4 %copy-start.2 = (f32[40,1024]{1,0:T(8,128)}, f32[40,1024]{1,0:T(8,128)S(1)}, u32[]{:S(2)}) copy-start(f32[40,1024]{1,0:T(8,128)S(1)} %collective-permute-done.before) | copy-start | bytes 491524
  116.7 5.4 %copy-start.3 = (f32[40,1024]{1,0:T(8,128)}, f32[40,1024]{1,0:T(8,128)S(1)}, u32[]{:S(2)}) copy-start(f32[40,1024]{1,0:T(8,128)S(1)} %collective-permute-done.1.after) | copy-start | bytes 491524
  116.7 100.4 %collective-permute-start.2 = (f32[320,1408]{1,0:T(8,128)}, f32[320,1408]{1,0:T(8,128)S(1)}, u32[]{:S(2)}, u32[]{:S(2)}) collective-permute-start(f32[320,1408]{1,0:T(8,128)} %get-tuple-element.34), channel_id=1, source_target_pairs={{0,1},{1,2},{2,3},{3,4},{4,5},{5,6},{6,7},{7,8},{8,9},{9,10},{10,1... | collective-permute-start | bytes 5406728 | tf_op jit(solution)/shard_map/ppermute | solution.py:763
  116.8 100.3 %collective-permute-start.3 = (f32[320,1408]{1,0:T(8,128)}, f32[320,1408]{1,0:T(8,128)}, u32[]{:S(2)}, u32[]{:S(2)}) collective-permute-start(f32[320,1408]{1,0:T(8,128)} %get-tuple-element.35), channel_id=1, source_target_pairs={{1,0},{2,1},{3,2},{4,3},{5,4},{6,5},{7,6},{8,7},{9,8},{10,9},{11,1... | collective-permute-start | bytes 5406728 | tf_op jit(solution)/shard_map/ppermute | solution.py:764
  161.1 38.3 %all-to-all-start = ((f32[32,8,256]{2,1,0:T(8,128)}), f32[32,8,256]{2,1,0:T(8,128)S(1)}, u32[]{:S(2)}, u32[]{:S(2)}) async-start(f32[32,8,256]{2,1,0:T(8,128)} %shard_map.169), calls=%async_computation | async-start | bytes 524288 | tf_op jit(solution)/shard_map/all_to_all | solution.py:800
  199.4 0.7 copy-start.1
  213.1 63.9 %all-to-all-start.1 = ((f32[32,4,256]{2,1,0:T(4,128)}), f32[32,4,256]{2,1,0:T(4,128)S(1)}, u32[]{:S(2)}, u32[]{:S(2)}) async-start(f32[32,4,256]{2,1,0:T(4,128)} %get-tuple-element.46), calls=%async_computation.1 | async-start | bytes 262144 | tf_op jit(solution)/shard_map/all_to_all | solution.py:837
  217.1 1.2 copy-start
  277.0 0.7 copy-start.4

commit v6 on v4

--- a/solution.py
+++ b/solution.py
@@ -53,10 +53,24 @@
     return lax.dot_general(a, b, (((1,), (1,)), ((), ())), preferred_element_type=F32)
 
 
-def product(x2, w2):
-    rows = x2.shape[0] // 2
-    wide = mm(x2, w2[0])
-    return wide[:rows] + wide[rows:] + mm(x2[:rows], w2[1])
+def products(x2, w2):
+    return mm(x2, w2[0]), mm(x2[: x2.shape[0] // 2], w2[1])
+
+
+def summed(parts):
+    wide, rest = parts
+    rows = rest.shape[0]
+    return wide[:rows] + wide[rows:] + rest
+
+
+def in_turn(works):
+    waiting = None
+    for begin, finish in works:
+        parts = begin()
+        if waiting is not None:
+            waiting[1](summed(waiting[0]))
+        waiting = (parts, finish)
+    waiting[1](summed(waiting[0]))
 
 
 def product_pieces(x2s, w2, result):
@@ -133,7 +147,10 @@
 
 
 def one_hot(ids, rows):
-    return jnp.where(iota((rows, ids.shape[1]), 0) == ids, 1.0, 0.0).astype(BF)
+    lanes = ids.shape[1]
+    wide = jnp.broadcast_to(ids.astype(F32), (rows, lanes)).astype(BF)
+    here = iota((rows, lanes), 0).astype(F32).astype(BF)
+    return jnp.where(here == wide, jnp.ones((rows, lanes), BF), jnp.zeros((rows, lanes), BF))
 
 
 def fold_rows(x, height):
@@ -144,7 +161,7 @@
 
 
 def prepare_kernel(fields):
-    def body(mix, omix, atm, sea, nbr, coef, bulk, surf, spread, code, y, yo, first, last, gains, vertical, top, sem):
+    def body(mix, omix, atm, sea, nbr, coef, bulk, surf, spread, code, sea_spread, y, yo, first, last, gains, vertical, sea_vertical, top, sem):
         la = mix.shape[0]
         columns = atm.shape[1]
         copy = pltpu.make_async_copy(sea.at[: omix.shape[0], :], top, sem)
@@ -179,19 +196,22 @@
             value = jnp.where(lane == s - 1, column, value)
         gains[...] = value
 
-        tall = jnp.concatenate([fourth] * fields, axis=0)
-        spreaded = dot(tall, spread[...])
-        filled = jnp.where(code[...] == 1, spreaded, 0.0)
-        for m in range(ASTEPS):
-            tall = jnp.concatenate([cols_up[ASTEPS - 1 - m]] * fields, axis=0)
-            filled = jnp.where(code[...] == 2 + m, tall, filled)
-        vertical[...] = stacked(filled)
-
-        weights = [jnp.broadcast_to(col(r, eye), (la, 128)) for r in rows_up]
+        spreaded = dot(jnp.concatenate([fourth] * 2, axis=0), spread[...])
+        for p in range(fields // 2):
+            filled = jnp.where(code[p] == 1, spreaded, 0.0)
+            for m in range(ASTEPS):
+                tall = jnp.concatenate([cols_up[ASTEPS - 1 - m]] * 2, axis=0)
+                filled = jnp.where(code[p] == 2 + m, tall, filled)
+            vertical[p] = stacked(filled)
         lo = omix.shape[0]
         sea_eye = iota((lo, lo), 0) == iota((lo, lo), 1)
-        sea_row = omix[0:1, :] + jnp.where(iota((1, lo), 1) == 0, 1.0, 0.0)
-        sea_weight = jnp.broadcast_to(col(sea_row, sea_eye), (lo, 128))
+        sea_step = omix[...] + jnp.where(sea_eye, 1.0, 0.0)
+        spreaded = dot(jnp.concatenate([sea_step] * 2, axis=0), sea_spread[...])
+        blocks = (iota((2 * lo, 2 * lo), 0) >= lo) == (iota((2 * lo, 2 * lo), 1) >= lo)
+        sea_vertical[...] = stacked(jnp.where(blocks, spreaded, 0.0))
+
+        weights = [jnp.broadcast_to(col(r, eye), (la, 128)) for r in rows_up]
+        sea_weight = jnp.broadcast_to(col(sea_step[0:1, :], sea_eye), (lo, 128))
         copy.wait()
         for start in range(0, columns, 128):
             at = slice(start, start + 128)
@@ -215,8 +235,18 @@
     return body
 
 
-def band_kernel(nbr, coef, band, w, sems):
+def band_kernel(nbr, coef, atm, ocean, band, *refs):
+    halos, held, (w, sems, in_sems, out_sems) = refs[:4], refs[4:8], refs[8:]
     blocks = nbr.shape[1] // BLK
+    columns = atm.shape[1]
+    spans = [(atm, 0, WIDE), (atm, columns - WIDE, WIDE), (ocean, 0, HO), (ocean, ocean.shape[1] - HO, HO)]
+    arriving = [
+        pltpu.make_async_copy(source.at[:, first : first + width], held[i], in_sems.at[i])
+        for i, (source, first, width) in enumerate(spans)
+    ]
+    leaving = [pltpu.make_async_copy(held[i], halos[i], out_sems.at[i]) for i in range(len(spans))]
+    for copy in arriving:
+        copy.start()
 
     def copy(b):
         return pltpu.make_async_copy(w.at[b], band.at[b], sems.at[b])
@@ -232,13 +262,19 @@
         copy(b).start()
         return 0
 
-    lax.fori_loop(0, blocks, build, 0)
+    lax.fori_loop(0, blocks // 2, build, 0)
+    for here, there in zip(arriving, leaving):
+        here.wait()
+        there.start()
+    lax.fori_loop(blocks // 2, blocks, build, 0)
 
     def finish(b, _):
         copy(b).wait()
         return 0
 
     lax.fori_loop(0, blocks, finish, 0)
+    for there in leaving:
+        there.wait()
 
 
 def interior_kernel(
@@ -302,42 +338,56 @@
             return moved * keep + gain * jnp.concatenate([flux] * ASTEPS, axis=0)
 
         def edge(e, s=s, zs=zs, zt=zt, advance=advance):
-            x2 = jnp.concatenate([zs[e - 1], zs[e], zs[e + 1]], axis=1)
-            value = advance(product(x2, (w[e - 1, 0], w[e - 1, 1])), e)
-            if s == ASTEPS:
-                q[e - ASTEPS] = value
-            else:
-                zt[e] = stacked(value)
+            def begin():
+                x2 = jnp.concatenate([zs[e - 1], zs[e], zs[e + 1]], axis=1)
+                return products(x2, (w[e - 1, 0], w[e - 1, 1]))
+
+            def finish(moved):
+                value = advance(moved, e)
+                if s == ASTEPS:
+                    q[e - ASTEPS] = value
+                else:
+                    zt[e] = stacked(value)
+
+            return begin, finish
 
         def inner(b, s=s, xs=xs, xt=xt, zt=zt, advance=advance):
-            x2 = jnp.concatenate([xs[b - 1], xs[b], xs[b + 1]], axis=1)
-            moved = product(x2, (w[b + halo, 0], w[b + halo, 1]))
-            value = advance(moved[rows:], b + ASTEPS)
-            if s == ASTEPS:
-                q[b] = value
-                mid[b - ASTEPS] = stacked(moved[:rows])
-            else:
-                high, low = halves(moved[:rows])
-                zh, zl = halves(value)
-                xt[b] = jnp.concatenate([high, zh, low, zl], axis=0)
-                zt[b + ASTEPS] = jnp.concatenate([zh, zl], axis=0)
+            def begin():
+                x2 = jnp.concatenate([xs[b - 1], xs[b], xs[b + 1]], axis=1)
+                return products(x2, (w[b + halo, 0], w[b + halo, 1]))
+
+            def finish(moved):
+                value = advance(moved[rows:], b + ASTEPS)
+                if s == ASTEPS:
+                    q[b] = value
+                    mid[b - ASTEPS] = stacked(moved[:rows])
+                else:
+                    high, low = halves(moved[:rows])
+                    zh, zl = halves(value)
+                    xt[b] = jnp.concatenate([high, zh, low, zl], axis=0)
+                    zt[b + ASTEPS] = jnp.concatenate([zh, zl], axis=0)
+
+            return begin, finish
 
         def together(i, _, s=s, edge=edge, inner=inner):
             if s == 1:
                 arriving(1 + 2 * i).wait()
                 arriving(2 + 2 * i).wait()
-            inner(s + 2 * i)
-            inner(s + 2 * i + 1)
-            edge(s + i)
-            edge(blocks + ASTEPS - s + i)
+            in_turn(
+                [
+                    inner(s + 2 * i),
+                    edge(s + i),
+                    edge(blocks + ASTEPS - s + i),
+                    inner(s + 2 * i + 1),
+                ]
+            )
             return 0
 
         def alone(i, _, s=s, inner=inner):
             if s == 1:
                 arriving(1 + 2 * i).wait()
                 arriving(2 + 2 * i).wait()
-            inner(s + 2 * i)
-            inner(s + 2 * i + 1)
+            in_turn([inner(s + 2 * i), inner(s + 2 * i + 1)])
             return 0
 
         lax.fori_loop(0, ASTEPS, together, 0)
@@ -518,25 +568,31 @@
         at = pl.ds(pl.multiple_of(b * BLK, BLK), BLK)
         return pltpu.make_async_copy(staged.at[b], out.at[:, at], osems.at[b])
 
+    levels = rows // 2
+
     def mixed(source, shift):
-        def one(b):
-            qh, ql = halves(q[b])
-            x2 = source[b - shift]
-            high = jnp.concatenate([x2[:rows], qh], axis=0)
-            low = jnp.concatenate([x2[rows:], ql], axis=0)
-            wide = mm(vertical[...], high)
-            staged[b] = wide[:rows] + wide[rows:] + mm(vertical[:rows], low)
-
-        def pair(i, _):
-            one(2 * i)
-            one(2 * i + 1)
-            leaving(2 * i).start()
-            leaving(2 * i + 1).start()
+        def one(b, p):
+            def begin():
+                qh, ql = halves(q[b])
+                x2 = source[b - shift]
+                high = jnp.concatenate([x2[p * levels : (p + 1) * levels], qh], axis=0)
+                low = jnp.concatenate([x2[rows + p * levels : rows + (p + 1) * levels], ql], axis=0)
+                return mm(vertical[p], high), mm(vertical[p, :levels], low)
+
+            def finish(value):
+                staged[b, p * levels : (p + 1) * levels] = value
+
+            return begin, finish
+
+        def four(i, _):
+            in_turn([one(4 * i + k, p) for k in range(4) for p in range(2)])
+            for k in range(4):
+                leaving(4 * i + k).start()
             return 0
 
-        return pair
-
-    lax.fori_loop(ASTEPS // 2, (blocks - ASTEPS) // 2, mixed(mid, ASTEPS), 0)
+        return four
+
+    lax.fori_loop(1, blocks // 4 - 1, mixed(mid, ASTEPS), 0)
     for copy in arrivals:
         copy.wait()
     for i in range(ASTEPS):
@@ -554,23 +610,27 @@
         for i in needed[s - 1]:
             bands[i].wait()
 
-        def one(i, _, s=s, source=source, target=target, last=last):
-            for side in range(2):
-                base = 6 * side
-                k = s - 1 + i if side == 0 else count + ASTEPS - s + i
+        def one(side, i, s=s, source=source, target=target, last=last):
+            base = 6 * side
+            k = s - 1 + i if side == 0 else count + ASTEPS - s + i
+
+            def begin():
                 x2 = jnp.concatenate([source[base + i + d] for d in range(3)], axis=1)
-                value = stacked(product(x2, (w[k, 0], w[k, 1])))
-                target[base + i + (2 * side if not last else 0)] = value
-            return 0
-
-        lax.fori_loop(0, ASTEPS, one, 0, unroll=2)
+                return products(x2, (w[k, 0], w[k, 1]))
+
+            def finish(moved):
+                target[base + i + (2 * side if not last else 0)] = stacked(moved)
+
+            return begin, finish
+
+        in_turn([one(side, i) for i in range(ASTEPS) for side in range(2)])
         if not last:
             for i in range(2):
                 target[ASTEPS + i] = kept[(s - 1) * 4 + i]
                 target[6 + i] = kept[(s - 1) * 4 + 2 + i]
     final = buffers[ASTEPS % 2]
-    lax.fori_loop(0, ASTEPS // 2, mixed(final, 0), 0)
-    lax.fori_loop((blocks - ASTEPS) // 2, blocks // 2, mixed(final, blocks - ASTEPS - 6), 0)
+    lax.fori_loop(0, 1, mixed(final, 0), 0)
+    lax.fori_loop(blocks // 4 - 1, blocks // 4, mixed(final, blocks - ASTEPS - 6), 0)
 
     def done(b, _):
         leaving(b).wait()
@@ -579,15 +639,13 @@
     lax.fori_loop(0, blocks, done, 0)
 
 
-def ocean_kernel(ocean, before, after, nbr, coef, omix, flux, out, x2, wa, wb, ma, mb, staged, sems):
-    levels = omix.shape[0]
+def ocean_kernel(ocean, before, after, nbr, coef, vertical, top_of, flux, out, x2, wa, wb, ma, mb, laid, staged, sems):
     fields = flux.shape[0]
-    columns = ocean.shape[1]
+    rows, columns = ocean.shape
+    levels = rows // fields
     blocks = columns // BLK
     eye = iota((levels, levels), 0) == iota((levels, levels), 1)
-    step = omix[...] + jnp.where(eye, 1.0, 0.0)
-    top = jnp.broadcast_to(step[:, 0:1], (levels, BLK))
-    mix2 = stacked(step)
+    top = jnp.broadcast_to((top_of[...] + jnp.where(eye, 1.0, 0.0))[:, 0:1], (levels, BLK))
 
     def part(first, width):
         pieces = []
@@ -609,17 +667,8 @@
 
         return band_pieces(store, nbr[:, at] - b * BLK, coef[:, at], HO)
 
-    def finish(b, w, moved):
+    def move(b, w, moved):
         yield from product_pieces([x2[b + d] for d in range(1 + 2 * HO // BLK)], w, moved)
-        at = pl.ds(pl.multiple_of(b * BLK, BLK), BLK)
-        for f in range(fields):
-            rows = slice(f * levels, (f + 1) * levels)
-            high, low = halves(moved[rows])
-            wide = mm(mix2, high)
-            staged[b, rows] = (
-                wide[:levels] + wide[levels:] + mm(mix2[:levels], low) + top * flux[f : f + 1, at]
-            )
-            yield
 
     def leaving(b):
         at = pl.ds(pl.multiple_of(b * BLK, BLK), BLK)
@@ -629,13 +678,39 @@
 
     def one(i, _):
         b = 2 * i
-        interleave(build(b + 1, wb), finish(b, wa, ma))
-        interleave(build(jnp.minimum(b + 2, blocks - 1), wa), finish(b + 1, wb, mb))
-        leaving(b).start()
-        leaving(b + 1).start()
+        interleave(build(b + 1, wb), move(b, wa, ma))
+        interleave(build(jnp.minimum(b + 2, blocks - 1), wa), move(b + 1, wb, mb))
+        laid[b] = stacked(ma[...])
+        laid[b + 1] = stacked(mb[...])
         return 0
 
     lax.fori_loop(0, blocks // 2, one, 0)
+    pair = 2 * levels
+
+    def mixed(b, p):
+        at = pl.ds(pl.multiple_of(b * BLK, BLK), BLK)
+
+        def begin():
+            high = laid[b, p * pair : (p + 1) * pair]
+            low = laid[b, rows + p * pair : rows + (p + 1) * pair]
+            return mm(vertical[...], high), mm(vertical[:pair], low)
+
+        def finish(value):
+            for k in range(2):
+                f = 2 * p + k
+                staged[b, f * levels : (f + 1) * levels] = (
+                    value[k * levels : (k + 1) * levels] + top * flux[f : f + 1, at]
+                )
+
+        return begin, finish
+
+    def four(i, _):
+        in_turn([mixed(4 * i + k, p) for k in range(4) for p in range(fields // 2)])
+        for k in range(4):
+            leaving(4 * i + k).start()
+        return 0
+
+    lax.fori_loop(0, blocks // 4, four, 0)
 
     def done(b, _):
         leaving(b).wait()
@@ -682,15 +757,20 @@
     anywhere = pl.BlockSpec(memory_space=pl.ANY)
 
     depth_k = rows + states
-    r_of, c_of = np.arange(rows)[:, None], np.arange(depth_k)[None, :]
+    half = fields // 2
+    p_of = np.arange(half)[:, None, None]
+    r_of = np.arange(2 * la)[None, :, None]
+    c_of = np.arange(2 * la + states)[None, None, :]
     code = np.where(
-        c_of < rows,
+        c_of < 2 * la,
         (c_of // la == r_of // la) * 1,
-        ((c_of - rows) % fields == r_of // la) * (2 + (c_of - rows) // fields),
-    ).astype(np.int32)
-    spread = ((c_of % la == np.arange(la)[:, None]) & (c_of < rows)).astype(np.float32)
-
-    y, yo, first, last, gains, vertical = call(
+        ((c_of - 2 * la) % fields == 2 * p_of + r_of // la) * (2 + (c_of - 2 * la) // fields),
+    )
+    code = np.broadcast_to(code, (half, 2 * la, 2 * la + states)).astype(np.int32)
+    spread = ((c_of[0] % la == np.arange(la)[:, None]) & (c_of[0] < 2 * la)).astype(np.float32)
+    sea_spread = (np.arange(2 * lo)[None, :] % lo == np.arange(lo)[:, None]).astype(np.float32)
+
+    y, yo, first, last, gains, vertical, sea_vertical = call(
         prepare_kernel(fields),
         (
             shape((states, columns)),
@@ -698,9 +778,10 @@
             shape((40, WIDE)),
             shape((40, WIDE)),
             shape((states, 128)),
-            shape((2 * rows, depth_k), BF),
+            shape((half, 4 * la, 2 * la + states), BF),
+            shape((4 * lo, 2 * lo), BF),
         ),
-        in_specs=[vmem] * 3 + [anywhere] + [vmem] * 6,
+        in_specs=[vmem] * 3 + [anywhere] + [vmem] * 7,
         scratch=[pltpu.VMEM((lo, cells), F32), pltpu.SemaphoreType.DMA(())],
     )(
         atm_mix,
@@ -713,24 +794,31 @@
         atm_surface,
         jnp.asarray(spread),
         jnp.asarray(code),
+        jnp.asarray(sea_spread),
     )
     pack_before = lax.ppermute(last, AXES, up)
     pack_after = lax.ppermute(first, AXES, down)
 
-    band = call(
+    halo_shapes = (shape((rows, WIDE)),) * 2 + (shape((fields * lo, HO)),) * 2
+    band, atm_first, atm_last, sea_first, sea_last = call(
         band_kernel,
-        shape((blocks, 2, window, BLK), BF),
-        in_specs=[vmem] * 2,
-        out_specs=anywhere,
-        scratch=[pltpu.VMEM((blocks, 2, window, BLK), BF), pltpu.SemaphoreType.DMA((blocks,))],
-    )(after_all(atm_nbr, y), atm_nbr_coef)
-
-    pack_before, pack_after = lax.optimization_barrier((pack_before, pack_after, band))[:2]
-    later, later_sea = lax.optimization_barrier((atm, ocean, pack_before, pack_after))[:2]
-    atm_before = lax.ppermute(later[:, columns - WIDE :], AXES, up)
-    atm_after = lax.ppermute(later[:, :WIDE], AXES, down)
-    sea_before = lax.ppermute(later_sea[:, cells - HO :], AXES, up)
-    sea_after = lax.ppermute(later_sea[:, :HO], AXES, down)
+        (shape((blocks, 2, window, BLK), BF),) + halo_shapes,
+        in_specs=[vmem] * 2 + [anywhere] * 2,
+        out_specs=(anywhere,) * 5,
+        scratch=[pltpu.VMEM(h.shape, F32) for h in halo_shapes]
+        + [
+            pltpu.VMEM((blocks, 2, window, BLK), BF),
+            pltpu.SemaphoreType.DMA((blocks,)),
+            pltpu.SemaphoreType.DMA((4,)),
+            pltpu.SemaphoreType.DMA((4,)),
+        ],
+    )(after_all(atm_nbr, y), atm_nbr_coef, atm, ocean)
+
+    pack_before, pack_after, atm_first, atm_last = lax.optimization_barrier(
+        (pack_before, pack_after, atm_first, atm_last)
+    )
+    atm_before = lax.ppermute(atm_last, AXES, up)
+    atm_after = lax.ppermute(atm_first, AXES, down)
 
     total = blocks + 2 * ASTEPS
     halo = ASTEPS - 1
@@ -764,6 +852,12 @@
     )(q, picked)
     received = lax.all_to_all(outgoing, AXES, split_axis=0, concat_axis=0, tiled=True)
 
+    sea_first, sea_last, atm_before, atm_after = lax.optimization_barrier(
+        (sea_first, sea_last, atm_before, atm_after, outgoing)
+    )[:4]
+    sea_before = lax.ppermute(sea_last, AXES, up)
+    sea_after = lax.ppermute(sea_first, AXES, down)
+
     atm_final = call(
         edge_kernel,
         shape((rows, columns)),
@@ -800,7 +894,7 @@
     ocean_final = call(
         ocean_kernel,
         shape((fields * lo, cells)),
-        in_specs=[vmem] * 7,
+        in_specs=[vmem] * 8,
         out_specs=anywhere,
         scratch=[
             pltpu.VMEM(((cells + 2 * HO) // BLK, 2 * fields * lo, BLK), BF),
@@ -808,10 +902,11 @@
             pltpu.VMEM((2, BLK + 2 * HO, BLK), BF),
             pltpu.VMEM((fields * lo, BLK), F32),
             pltpu.VMEM((fields * lo, BLK), F32),
+            pltpu.VMEM((cells // BLK, 2 * fields * lo, BLK), BF),
             pltpu.VMEM((cells // BLK, fields * lo, BLK), F32),
             pltpu.SemaphoreType.DMA((cells // BLK,)),
         ],
-    )(ocean, after_all(sea_before, back), sea_after, ocean_nbr, ocean_nbr_coef, ocean_mix, flux)
+    )(ocean, after_all(sea_before, back), sea_after, ocean_nbr, ocean_nbr_coef, sea_vertical, ocean_mix, flux)
 
     surface_temp = call(
         settle_kernel,

time: 168 us -> 149 us (0.89)
  Pallas kernels: 123 us -> 113 us
  local copies, waits for them, and re-layouts: 5.5 us -> 2.12 us
  starting transfers between devices: 25.9 us -> 23.1 us
  waiting for transfers between devices: 12.5 us -> 9.84 us
    pallas_call x2, Pallas kernels: 37 us -> 29.3 us  [the longest x1 21.1 us: per_device(): call(ocean_kernel, shape((fields * lo, cells)), in_specs=[vmem] * 8, out_...]
    slice x2 -> x0, local copies, waits for them, and re-layouts: 3.44 us -> none  [the longest x1 2.2 us: per_device(): sea_after = lax.ppermute(later_sea[:, :HO], AXES, down)]
    ppermute x4, waiting for transfers between devices: 12.5 us -> 9.83 us  [the longest x1 9.82 us: per_device(): atm_before = lax.ppermute(atm_last, AXES, up)]
    all_to_all x1, starting transfers between devices: 5.41 us -> 3.13 us  [per_device(): lax.all_to_all(back, AXES, split_axis=0, concat_axis=0, tiled=True)]
    pallas_call x1, Pallas kernels: 25.2 us -> 23.1 us  [per_device(): call(edge_kernel, shape((rows, columns)), in_specs=[anywhere] * 3 + [vmem...]
  transfers between devices with their start and end apart: 8 -> 8, of which waited for: 1 -> 1; matrix products, arithmetic and copies ran while one was open for 1% -> 0% of each run, Pallas kernels for 66% -> 68%
where the time goes in v6:
time: 149 us
  Pallas kernels  113 us (76%)
  starting transfers between devices  23.1 us (16%)
  waiting for transfers between devices  9.84 us (7%)
  local copies, waits for them, and re-layouts  2.12 us (1%)
    pallas_call x1, Pallas kernels, per_device(): call(interior_kernel, (shape((blocks, states, BLK)), shape((4 * halo, 2 *...  31.9 us
    pallas_call x1, Pallas kernels, per_device(): call(edge_kernel, shape((rows, columns)), in_specs=[anywhere] * 3 + [vmem...  23.1 us
    pallas_call x1, Pallas kernels, per_device(): call(ocean_kernel, shape((fields * lo, cells)), in_specs=[vmem] * 8, out_...  21.1 us
    pallas_call x1, Pallas kernels, per_device(): call(exchange_kernel, (shape((fields, cells)), shape((peers, 2 * parts, l...  13 us
    ppermute x1, waiting for transfers between devices, per_device(): atm_before = lax.ppermute(atm_last, AXES, up)  9.82 us
    pallas_call x1, Pallas kernels, per_device(): call(band_kernel, (shape((blocks, 2, window, BLK), BF),) + halo_shapes, i...  8.21 us
    pallas_call x1, Pallas kernels, per_device(): call(prepare_kernel(fields), (shape((states, columns)), shape((1, columns...  6.05 us
    ppermute x1, starting transfers between devices, per_device(): atm_after = lax.ppermute(atm_first, AXES, down)  5.33 us
  transfers between devices with their start and end apart: 8, of which 1 were waited for; matrix products, arithmetic and copies ran while one was open for 0% of the time, Pallas kernels for 68%

profile of v6, /device:TPU:0, one launch (start us, length us, event | category | flops | bytes accessed | tf_op | source)
XLA Modules:
  0.0 148.7 jit_solution(5757227854205892078)
XLA Ops:
  0.6 6.1 %shard_map.175 = (f32[16,4096]{1,0:T(8,128)}, f32[1,4096]{1,0:T(1,128)}, f32[40,1024]{1,0:T(8,128)}, f32[40,1024]{1,0:T(8,128)}, f32[16,128]{1,0:T(8,128)}, /*in...) custom-call(f32[72,72]{1,0:T(8,128)} %mix.1, f32[80,80]{1,0:T(8,128)} %top_of.1, f32[288,4096]{1,0:T(8,128)} %bitcast.6, ...), custom_call_target="tpu_custom_call" | custom-call | flops 1000000 | bytes 10000 | tf_op jit(solution)/shard_map/pallas_call | solution.py:773
  6.7 3.0 %collective-permute-start = (f32[40,1024]{1,0:T(8,128)}, f32[40,1024]{1,0:T(8,128)S(1)}, u32[]{:S(2)}, u32[]{:S(2)}) collective-permute-start(f32[40,1024]{1,0:T(8,128)} %get-tuple-element.38), channel_id=1, source_target_pairs={{0,1},{1,2},{2,3},{3,4},{4,5},{5,6},{6,7},{7,8},{8,9},{9,10},{10,1... | collective-permute-start | bytes 491528 | tf_op jit(solution)/shard_map/ppermute | solution.py:799
  9.7 3.5 %collective-permute-start.1 = (f32[40,1024]{1,0:T(8,128)}, f32[40,1024]{1,0:T(8,128)S(1)}, u32[]{:S(2)}, u32[]{:S(2)}) collective-permute-start(f32[40,1024]{1,0:T(8,128)} %get-tuple-element.39), channel_id=1, source_target_pairs={{1,0},{2,1},{3,2},{4,3},{5,4},{6,5},{7,6},{8,7},{9,8},{10,9},{11,1... | collective-permute-start | bytes 491528 | tf_op jit(solution)/shard_map/ppermute | solution.py:800
  13.2 8.2 %shard_map.176 = (bf16[16,2,768,256]{3,2,1,0:T(8,128)(2,1)}, f32[288,1024]{1,0:T(8,128)}, f32[288,1024]{1,0:T(8,128)}, f32[320,384]{1,0:T(8,128)}, f32[320,384]{1,0:T(8,128)}) custom-call(s32[6,4096]{1,0:T(8,128)} %nbr.4, f32[6,4096]{1,0:T(8,128)} %coef.5, f32[288,4096]{1,0:T(8,128)} %bitcast.7, f32[320,4096]{1,0:T(8,128)} %bitcast.11), custom_call_target="tpu_custom_call" | custom-call | flops 1000000 | bytes 10000 | tf_op jit(solution)/shard_map/pallas_call | solution.py:803
  21.4 0.0 collective-permute-done.1.after
  21.4 0.1 collective-permute-start.2
  21.5 5.3 %collective-permute-start.3 = (f32[288,1024]{1,0:T(8,128)}, f32[288,1024]{1,0:T(8,128)S(1)}, u32[]{:S(2)}, u32[]{:S(2)}) collective-permute-start(f32[288,1024]{1,0:T(8,128)} %get-tuple-element.43), channel_id=1, source_target_pairs={{1,0},{2,1},{3,2},{4,3},{5,4},{6,5},{7,6},{8,7},{9,8},{10,9},{11,1... | collective-permute-start | bytes 3538952 | tf_op jit(solution)/shard_map/ppermute | solution.py:821
  26.8 31.9 %shard_map.177 = (f32[16,16,256]{2,1,0:T(8,128)}, bf16[12,576,256]{2,1,0:T(8,128)(2,1)}, bf16[8,576,256]{2,1,0:T(8,128)(2,1)}, bf16[6,2,768,256]{3,2,1,0:T(8,128)(2,1)}) custom-call(f32[288,4096]{1,0:T(8,128)} %bitcast.8, f32[16,4096]{1,0:T(8,128)} %get-tuple-element.34.y, f32[40,1024]{1,0:T(8,128)} %copy-done.3, f32[40,1024]{1,0:T(8,128)} %copy-done.4, ...), custom_call_target="tpu_custom_call" | custom-call | flops 1000000 | bytes 10000 | tf_op jit(solution)/shard_map/pallas_call | solution.py:825
  58.7 4.2 %shard_map.178 = f32[32,8,256]{2,1,0:T(8,128)} custom-call(f32[16,16,256]{2,1,0:T(8,128)} %get-tuple-element.48.q, s32[32,512]{1,0:T(8,128)} %bitcast.15), custom_call_target="tpu_custom_call" | custom-call | flops 1000000 | bytes 10000 | tf_op jit(solution)/shard_map/pallas_call | solution.py:847
  63.0 2.8 %all-to-all-start = ((f32[32,8,256]{2,1,0:T(8,128)}), f32[32,8,256]{2,1,0:T(8,128)S(1)}, u32[]{:S(2)}, u32[]{:S(2)}) async-start(f32[32,8,256]{2,1,0:T(8,128)} %shard_map.178), calls=%async_computation | async-start | bytes 524288 | tf_op jit(solution)/shard_map/all_to_all | solution.py:853
  65.7 9.8 %collective-permute-done.2.before = f32[288,1024]{1,0:T(8,128)S(1)} collective-permute-done((f32[288,1024]{1,0:T(8,128)}, f32[288,1024]{1,0:T(8,128)S(1)}, u32[]{:S(2)}, u32[]{:S(2)}) %collective-permute-start.2) | collective-permute-done | bytes 1179680 | tf_op jit(solution)/shard_map/ppermute | solution.py:820
  75.6 2.4 %collective-permute-start.4 = (f32[320,384]{1,0:T(8,128)}, f32[320,384]{1,0:T(8,128)S(1)}, u32[]{:S(2)}, u32[]{:S(2)}) collective-permute-start(f32[320,384]{1,0:T(8,128)} %get-tuple-element.56), channel_id=1, source_target_pairs={{0,1},{1,2},{2,3},{3,4},{4,5},{5,6},{6,7},{7,8},{8,9},{9,10},{10,1... | collective-permute-start | bytes 1474568 | tf_op jit(solution)/shard_map/ppermute | solution.py:858
  78.0 2.9 %collective-permute-start.5 = (f32[320,384]{1,0:T(8,128)}, f32[320,384]{1,0:T(8,128)}, u32[]{:S(2)}, u32[]{:S(2)}) collective-permute-start(f32[320,384]{1,0:T(8,128)} %get-tuple-element.61), channel_id=1, source_target_pairs={{1,0},{2,1},{3,2},{4,3},{5,4},{6,5},{7,6},{8,7},{9,8},{10,9},{11,1... | collective-permute-start | bytes 1474568 | tf_op jit(solution)/shard_map/ppermute | solution.py:859
  80.9 23.1 %shard_map.179 = f32[288,4096]{1,0:T(8,128)} custom-call(f32[288,1024]{1,0:T(8,128)} %copy-done, f32[288,1024]{1,0:T(8,128)} %copy-done.1, f32[288,4096]{1,0:T(8,128)} %bitcast.9, bf16[12,576,256]{2,1,0:T(8,128)(2,1)} %get-tuple-element.52.kept, bf16[8,576,256]{2,1,0:T(8,128)(2,1)} %get-tuple-element.53.mid, f32[16,16,256]{2,1,0:T(8,128)} %get-tuple-element.48.q, ...), custom_call_target="tpu_custom_call" | custom-call | flops 1000000 | bytes 10000 | tf_op jit(solution)/shard_map/pallas_call | solution.py:861
  104.0 0.0 all-to-all-done.recv
  104.1 0.0 copy-start.2
  104.1 0.7 copy-done.2
  104.8 13.0 %shard_map.180 = (f32[4,4096]{1,0:T(4,128)}, f32[32,4,256]{2,1,0:T(4,128)}) custom-call(f32[32,8,256]{2,1,0:T(8,128)} %copy-done.2, s32[4,4096]{1,0:T(4,128)} %slot.1, f32[4,4096]{1,0:T(4,128)} %weight.1, f32[1,4096]{1,0:T(1,128)} %get-tuple-element.58.yo, f32[40,1024]{1,0:T(8,128)} %copy-done.3, f32[40,1024]{1,0:T(8,128)} %copy-done.4, s32[6,4096]{1,0:T(8,128)} %nbr.6, ...), custom_call_target="tpu_custom_call" | custom-call | flops 1000000 | bytes 10000 | tf_op jit(solution)/shard_map/pallas_call | solution.py:880
  117.7 3.1 %all-to-all-start.1 = ((f32[32,4,256]{2,1,0:T(4,128)}), f32[32,4,256]{2,1,0:T(4,128)S(1)}, u32[]{:S(2)}, u32[]{:S(2)}) async-start(f32[32,4,256]{2,1,0:T(4,128)} %get-tuple-element.59), calls=%async_computation.1 | async-start | bytes 262144 | tf_op jit(solution)/shard_map/all_to_all | solution.py:892
  120.9 0.0 collective-permute-done.4.before
  120.9 0.8 copy-done.6
  121.7 21.1 %shard_map.181 = f32[320,4096]{1,0:T(8,128)} custom-call(f32[320,4096]{1,0:T(8,128)} %bitcast.12, f32[320,384]{1,0:T(8,128)} %copy-done.6, f32[320,384]{1,0:T(8,128)} %collective-permute-done.5.after, s32[6,4096]{1,0:T(8,128)} %nbr.6, f32[6,4096]{1,0:T(8,128)} %coef.7, bf16[320,160]{1,0:T(8,128)(2,1)} %get-tuple-element.62.vertical, f32[80,80]{1,0:T(8,128)} %top_of.1, ...), custom_call_target="tpu_custom_call" | custom-call | flops 1000000 | bytes 10000 | tf_op jit(solution)/shard_map/pallas_call | solution.py:894
  142.8 0.6 copy-done.5
  143.5 5.2 %shard_map.182 = f32[32,128]{1,0:T(8,128)} custom-call(f32[32,4,256]{2,1,0:T(4,128)} %copy-done.5, s32[32,512]{1,0:T(8,128)} %bitcast.16, f32[4,4096]{1,0:T(4,128)} %surf.5), custom_call_target="tpu_custom_call" | custom-call | flops 1000000 | bytes 10000 | tf_op jit(solution)/shard_map/pallas_call | solution.py:911
  (14 shorter events, 0.0 us)
Async XLA Ops:
  6.7 14.7 %collective-permute-start = (f32[40,1024]{1,0:T(8,128)}, f32[40,1024]{1,0:T(8,128)S(1)}, u32[]{:S(2)}, u32[]{:S(2)}) collective-permute-start(f32[40,1024]{1,0:T(8,128)} %get-tuple-element.38), channel_id=1, source_target_pairs={{0,1},{1,2},{2,3},{3,4},{4,5},{5,6},{6,7},{7,8},{8,9},{9,10},{10,1... | collective-permute-start | bytes 491528 | tf_op jit(solution)/shard_map/ppermute | solution.py:799
  9.7 11.7 %collective-permute-start.1 = (f32[40,1024]{1,0:T(8,128)}, f32[40,1024]{1,0:T(8,128)S(1)}, u32[]{:S(2)}, u32[]{:S(2)}) collective-permute-start(f32[40,1024]{1,0:T(8,128)} %get-tuple-element.39), channel_id=1, source_target_pairs={{1,0},{2,1},{3,2},{4,3},{5,4},{6,5},{7,6},{8,7},{9,8},{10,9},{11,1... | collective-permute-start | bytes 491528 | tf_op jit(solution)/shard_map/ppermute | solution.py:800
  21.4 5.4 %copy-start.3 = (f32[40,1024]{1,0:T(8,128)}, f32[40,1024]{1,0:T(8,128)S(1)}, u32[]{:S(2)}) copy-start(f32[40,1024]{1,0:T(8,128)S(1)} %collective-permute-done.before) | copy-start | bytes 491524
  21.4 5.4 %copy-start.4 = (f32[40,1024]{1,0:T(8,128)}, f32[40,1024]{1,0:T(8,128)S(1)}, u32[]{:S(2)}) copy-start(f32[40,1024]{1,0:T(8,128)S(1)} %collective-permute-done.1.after) | copy-start | bytes 491524
  21.4 54.1 %collective-permute-start.2 = (f32[288,1024]{1,0:T(8,128)}, f32[288,1024]{1,0:T(8,128)S(1)}, u32[]{:S(2)}, u32[]{:S(2)}) collective-permute-start(f32[288,1024]{1,0:T(8,128)} %get-tuple-element.42), channel_id=1, source_target_pairs={{0,1},{1,2},{2,3},{3,4},{4,5},{5,6},{6,7},{7,8},{8,9},{9,10},{10,1... | collective-permute-start | bytes 3538952 | tf_op jit(solution)/shard_map/ppermute | solution.py:820
  21.5 54.1 %collective-permute-start.3 = (f32[288,1024]{1,0:T(8,128)}, f32[288,1024]{1,0:T(8,128)S(1)}, u32[]{:S(2)}, u32[]{:S(2)}) collective-permute-start(f32[288,1024]{1,0:T(8,128)} %get-tuple-element.43), channel_id=1, source_target_pairs={{1,0},{2,1},{3,2},{4,3},{5,4},{6,5},{7,6},{8,7},{9,8},{10,9},{11,1... | collective-permute-start | bytes 3538952 | tf_op jit(solution)/shard_map/ppermute | solution.py:821
  63.0 41.1 %all-to-all-start = ((f32[32,8,256]{2,1,0:T(8,128)}), f32[32,8,256]{2,1,0:T(8,128)S(1)}, u32[]{:S(2)}, u32[]{:S(2)}) async-start(f32[32,8,256]{2,1,0:T(8,128)} %shard_map.178), calls=%async_computation | async-start | bytes 524288 | tf_op jit(solution)/shard_map/all_to_all | solution.py:853
  75.6 5.4 %copy-start = (f32[288,1024]{1,0:T(8,128)}, f32[288,1024]{1,0:T(8,128)S(1)}, u32[]{:S(2)}) copy-start(f32[288,1024]{1,0:T(8,128)S(1)} %collective-permute-done.2.before) | copy-start | bytes 3538948
  75.6 5.4 %copy-start.1 = (f32[288,1024]{1,0:T(8,128)}, f32[288,1024]{1,0:T(8,128)S(1)}, u32[]{:S(2)}) copy-start(f32[288,1024]{1,0:T(8,128)S(1)} %collective-permute-done.3.after) | copy-start | bytes 3538948
  75.6 45.3 %collective-permute-start.4 = (f32[320,384]{1,0:T(8,128)}, f32[320,384]{1,0:T(8,128)S(1)}, u32[]{:S(2)}, u32[]{:S(2)}) collective-permute-start(f32[320,384]{1,0:T(8,128)} %get-tuple-element.56), channel_id=1, source_target_pairs={{0,1},{1,2},{2,3},{3,4},{4,5},{5,6},{6,7},{7,8},{8,9},{9,10},{10,1... | collective-permute-start | bytes 1474568 | tf_op jit(solution)/shard_map/ppermute | solution.py:858
  78.0 42.9 %collective-permute-start.5 = (f32[320,384]{1,0:T(8,128)}, f32[320,384]{1,0:T(8,128)}, u32[]{:S(2)}, u32[]{:S(2)}) collective-permute-start(f32[320,384]{1,0:T(8,128)} %get-tuple-element.61), channel_id=1, source_target_pairs={{1,0},{2,1},{3,2},{4,3},{5,4},{6,5},{7,6},{8,7},{9,8},{10,9},{11,1... | collective-permute-start | bytes 1474568 | tf_op jit(solution)/shard_map/ppermute | solution.py:859
  104.1 0.7 copy-start.2
  117.7 25.1 %all-to-all-start.1 = ((f32[32,4,256]{2,1,0:T(4,128)}), f32[32,4,256]{2,1,0:T(4,128)S(1)}, u32[]{:S(2)}, u32[]{:S(2)}) async-start(f32[32,4,256]{2,1,0:T(4,128)} %get-tuple-element.59), calls=%async_computation.1 | async-start | bytes 262144 | tf_op jit(solution)/shard_map/all_to_all | solution.py:892
  120.9 0.8 copy-start.6
  142.8 0.6 copy-start.5

commit v7 on v6

--- a/solution.py
+++ b/solution.py
@@ -1,3 +1,5 @@
+import itertools
+
 import numpy as np
 
 import jax
@@ -278,7 +280,7 @@
 
 
 def interior_kernel(
-    atm, y, before, after, bulk, surf, gains, band, q, kept, mid, far, w, sa, sb, za, zb, bulks, surfs, sems
+    atm, y, before, after, bulk, surf, gains, band, q, kept, mid, far, w, sa, sb, za, zb, bulks, surfs, ma, mb, sems
 ):
     rows, columns = atm.shape
     blocks = columns // BLK
@@ -290,7 +292,7 @@
     def arriving(b):
         return pltpu.make_async_copy(band.at[b], w.at[halo + b], sems.at[b])
 
-    for b in [0, blocks - 1] + list(range(1, blocks - 1)):
+    for b in list(range(1, blocks - 1)) + [0, blocks - 1]:
         arriving(b).start()
 
     leaving = []
@@ -301,19 +303,23 @@
         za[e] = stacked(pack[0:states, at])
         bulks[e] = pack[28:32, at]
         surfs[e] = pack[32:36, at]
-        if e in (0, total - 1):
-            continue
+
+    def build_far(e):
+        pack = before if e < ASTEPS else after
+        local = e if e < ASTEPS else e - ASTEPS - blocks
+        at = slice(local * BLK, (local + 1) * BLK)
         origin = local * BLK + (columns - WIDE if e < ASTEPS else 0)
 
-        def store(first, step, lanes, high, low, e=e):
+        def store(first, step, lanes, high, low):
             w[e - 1, 0, first : first + step, lanes] = high
             w[e - 1, 1, first : first + step, lanes] = low
 
-        build_band(store, pack[16:22, at].astype(jnp.int32) - origin, pack[22:28, at], HA)
+        yield from band_pieces(store, pack[16:22, at].astype(jnp.int32) - origin, pack[22:28, at], HA)
         i = e - 1 if e < ASTEPS else e - 1 - blocks
         copy = pltpu.make_async_copy(w.at[e - 1], far.at[i], sems.at[blocks + i])
         copy.start()
         leaving.append(copy)
+
     for b in range(blocks):
         at = slice(b * BLK, (b + 1) * BLK)
         both = stacked(jnp.concatenate([atm[:, at], y[:, at]], axis=0))
@@ -322,9 +328,6 @@
         za[b + ASTEPS] = jnp.concatenate([both[rows:height], both[height + rows :]], axis=0)
         bulks[b + ASTEPS] = bulk[:, at]
         surfs[b + ASTEPS] = surf[:, at]
-
-    arriving(0).wait()
-    arriving(blocks - 1).wait()
 
     slot = iota((states, BLK), 0) // fields
     for s in range(1, ASTEPS + 1):
@@ -370,9 +373,6 @@
             return begin, finish
 
         def together(i, _, s=s, edge=edge, inner=inner):
-            if s == 1:
-                arriving(1 + 2 * i).wait()
-                arriving(2 + 2 * i).wait()
             in_turn(
                 [
                     inner(s + 2 * i),
@@ -384,15 +384,31 @@
             return 0
 
         def alone(i, _, s=s, inner=inner):
-            if s == 1:
+            in_turn([inner(s + 2 * i), inner(s + 2 * i + 1)])
+            return 0
+
+        if s == 1:
+            builds = [build_far(e) for e in list(range(1, ASTEPS)) + list(range(ASTEPS + blocks, total - 1))]
+
+            def pieces(b, moved):
+                yield from product_pieces([sa[b + d] for d in (-1, 0, 1)], w.at[b + halo], moved)
+
+            for i in range(blocks // 2 - 1):
                 arriving(1 + 2 * i).wait()
                 arriving(2 + 2 * i).wait()
-            in_turn([inner(s + 2 * i), inner(s + 2 * i + 1)])
-            return 0
-
-        lax.fori_loop(0, ASTEPS, together, 0)
-        if blocks // 2 - s > ASTEPS:
-            lax.fori_loop(ASTEPS, blocks // 2 - s, alone, 0)
+                both = itertools.chain(pieces(1 + 2 * i, ma), pieces(2 + 2 * i, mb))
+                interleave(both, *builds[i : i + 1])
+                inner(1 + 2 * i)[1](ma[...])
+                inner(2 + 2 * i)[1](mb[...])
+            for rest in builds[blocks // 2 - 1 :]:
+                interleave(rest)
+            arriving(0).wait()
+            arriving(blocks - 1).wait()
+            in_turn([edge(e) for i in range(ASTEPS) for e in (1 + i, blocks + ASTEPS - 1 + i)])
+        else:
+            lax.fori_loop(0, ASTEPS, together, 0)
+            if blocks // 2 - s > ASTEPS:
+                lax.fori_loop(ASTEPS, blocks // 2 - s, alone, 0)
         if s < ASTEPS:
             height = rows + states
             for i, b in enumerate((s, s + 1, blocks - 2 - s, blocks - 1 - s)):
@@ -476,14 +492,26 @@
 
     def arrive(j, _):
         at = pl.ds(pl.multiple_of(j * BLK, BLK), BLK)
-        flux = jnp.zeros((2 * fields, BLK), F32)
-        for r in range(links):
+        parts = []
+
+        def begin(r):
             ids = slot[r : r + 1, at]
             hot = one_hot(ids & (lanes - 1), lanes)
             hots[j, :, r * BLK : (r + 1) * BLK] = hot
-            got = mm(rows[...], hot)
+            return mm(rows[...], hot)
+
+        def finish(r, got):
+            ids = slot[r : r + 1, at]
             got = jnp.where(high_of_row == ids // lanes, got[:table] + got[table:], 0.0)
-            flux = flux + weight[r : r + 1, at] * fold_rows(got, 2 * fields)
+            parts.append(weight[r : r + 1, at] * fold_rows(got, 2 * fields))
+
+        last = begin(0)
+        for r in range(1, links):
+            got = begin(r)
+            finish(r - 1, last)
+            last = got
+        finish(links - 1, last)
+        flux = sum(parts[1:], parts[0])
         flux = flux[:fields] + flux[fields:]
         flux_out[:, at] = flux
         seas[:, at] += corner * flux[0:1]
@@ -518,9 +546,12 @@
     acc[...] = jnp.zeros_like(acc)
     block_of_row = iota((blocks, lanes), 0)
 
-    def one(d, _):
+    group = 4
+
+    def one(i, _):
         left, hots = [], []
-        for h in range(parts):
+        for k, h in itertools.product(range(group), range(parts)):
+            d = group * i + k
             ids = cols[pl.ds(d, 1), h * lanes : (h + 1) * lanes]
             mask = block_of_row == ids // BLK
             value = jnp.where(mask, back[d, h : h + 1, :], 0.0)
@@ -530,7 +561,7 @@
         acc[...] += mm_t(jnp.concatenate(left, axis=1), jnp.concatenate(hots, axis=1))
         return 0
 
-    lax.fori_loop(0, peers, one, 0, unroll=4)
+    lax.fori_loop(0, peers // group, one, 0)
     sums = acc[: 2 * blocks] + acc[2 * blocks :]
     base = jnp.concatenate([surf[0:1, b * BLK : (b + 1) * BLK] for b in range(blocks)], axis=0)
     value = (base + sums[:blocks]) / (1.0 + sums[blocks:])
@@ -639,53 +670,103 @@
     lax.fori_loop(0, blocks, done, 0)
 
 
-def ocean_kernel(ocean, before, after, nbr, coef, vertical, top_of, flux, out, x2, wa, wb, ma, mb, laid, staged, sems):
+def sea_build(nbr, coef, b, w):
+    at = pl.ds(pl.multiple_of(b * BLK, BLK), BLK)
+
+    def store(first, size, lanes, high, low):
+        w[0, first : first + size, lanes] = high
+        w[1, first : first + size, lanes] = low
+
+    return band_pieces(store, nbr[:, at] - b * BLK, coef[:, at], HO)
+
+
+def sea_inner_kernel(ocean, nbr, coef, laid_out, x2, wa, wb, ma, mb, laid, sems):
+    blocks = ocean.shape[1] // BLK
+    around = 1 + 2 * HO // BLK
+    first = -(-HO // BLK)
+    count = blocks - 2 * first
+    for i in range(count + around - 1):
+        start = (first + i) * BLK - HO
+        x2[i] = stacked(ocean[:, start : start + BLK])
+
+    def leaving(i):
+        return pltpu.make_async_copy(laid.at[i], laid_out.at[i], sems.at[i])
+
+    def move(i, w, moved):
+        yield from product_pieces([x2[i + d] for d in range(around)], w, moved)
+
+    interleave(sea_build(nbr, coef, first, wa))
+
+    def one(k, _):
+        i = 2 * k
+        interleave(sea_build(nbr, coef, first + i + 1, wb), move(i, wa, ma))
+        interleave(sea_build(nbr, coef, jnp.minimum(i + 2, count - 1) + first, wa), move(i + 1, wb, mb))
+        laid[i] = stacked(ma[...])
+        laid[i + 1] = stacked(mb[...])
+        leaving(i).start()
+        leaving(i + 1).start()
+        return 0
+
+    lax.fori_loop(0, count // 2, one, 0)
+
+    def done(i, _):
+        leaving(i).wait()
+        return 0
+
+    lax.fori_loop(0, count, done, 0)
+
+
+def sea_outer_kernel(
+    before, after, nbr, coef, vertical, mix, flux, ocean, laid_in, out, ends, x2, wa, wb, ma, mb, laid, staged, sems, osems
+):
     fields = flux.shape[0]
     rows, columns = ocean.shape
     levels = rows // fields
     blocks = columns // BLK
+    around = 1 + 2 * HO // BLK
+    first = -(-HO // BLK)
+    count = blocks - 2 * first
+    width = ends.shape[2]
+    arriving = [
+        pltpu.make_async_copy(ocean.at[:, :width], ends.at[0], sems.at[0]),
+        pltpu.make_async_copy(ocean.at[:, columns - width :], ends.at[1], sems.at[1]),
+        pltpu.make_async_copy(laid_in, laid.at[first : first + count], sems.at[2]),
+    ]
+    for copy in arriving:
+        copy.start()
     eye = iota((levels, levels), 0) == iota((levels, levels), 1)
-    top = jnp.broadcast_to((top_of[...] + jnp.where(eye, 1.0, 0.0))[:, 0:1], (levels, BLK))
-
-    def part(first, width):
+    top = jnp.broadcast_to((mix[...] + jnp.where(eye, 1.0, 0.0))[:, 0:1], (levels, BLK))
+    outer = list(range(first)) + list(range(blocks - first, blocks))
+    bands, sums = (wa, wb), (ma, mb)
+    interleave(sea_build(nbr, coef, outer[0], wa))
+    arriving[0].wait()
+    arriving[1].wait()
+    spans = ((before, -HO, HO), (ends.at[0], 0, width), (ends.at[1], columns - width, width), (after, columns, HO))
+    held = list(range(first + around - 1)) + list(range(blocks - first, blocks + around - 1))
+    for i, e in enumerate(held):
+        start = e * BLK - HO
         pieces = []
-        for ref, begin, size in ((before, -HO, HO), (ocean, 0, columns), (after, columns, HO)):
-            lo, hi = max(first, begin), min(first + width, begin + size)
+        for ref, begin, size in spans:
+            lo, hi = max(start, begin), min(start + BLK, begin + size)
             if lo < hi:
                 pieces.append(ref[:, lo - begin : hi - begin])
-        return pieces[0] if len(pieces) == 1 else jnp.concatenate(pieces, axis=1)
-
-    for e in range((columns + 2 * HO) // BLK):
-        x2[e] = stacked(part(e * BLK - HO, BLK))
-
-    def build(b, w):
-        at = pl.ds(pl.multiple_of(b * BLK, BLK), BLK)
-
-        def store(first, size, lanes, high, low):
-            w[0, first : first + size, lanes] = high
-            w[1, first : first + size, lanes] = low
-
-        return band_pieces(store, nbr[:, at] - b * BLK, coef[:, at], HO)
+        x2[i] = stacked(pieces[0] if len(pieces) == 1 else jnp.concatenate(pieces, axis=1))
 
     def move(b, w, moved):
-        yield from product_pieces([x2[b + d] for d in range(1 + 2 * HO // BLK)], w, moved)
+        yield from product_pieces([x2[held.index(b + d)] for d in range(around)], w, moved)
+
+    for k, b in enumerate(outer):
+        works = [move(b, bands[k % 2], sums[k % 2])]
+        if k + 1 < len(outer):
+            works.insert(0, sea_build(nbr, coef, outer[k + 1], bands[(k + 1) % 2]))
+        interleave(*works)
+        laid[b] = stacked(sums[k % 2][...])
+    arriving[2].wait()
+    pair = 2 * levels
 
     def leaving(b):
         at = pl.ds(pl.multiple_of(b * BLK, BLK), BLK)
-        return pltpu.make_async_copy(staged.at[b], out.at[:, at], sems.at[b])
-
-    interleave(build(0, wa))
-
-    def one(i, _):
-        b = 2 * i
-        interleave(build(b + 1, wb), move(b, wa, ma))
-        interleave(build(jnp.minimum(b + 2, blocks - 1), wa), move(b + 1, wb, mb))
-        laid[b] = stacked(ma[...])
-        laid[b + 1] = stacked(mb[...])
-        return 0
-
-    lax.fori_loop(0, blocks // 2, one, 0)
-    pair = 2 * levels
+        return pltpu.make_async_copy(staged.at[b], out.at[:, at], osems.at[b])
 
     def mixed(b, p):
         at = pl.ds(pl.multiple_of(b * BLK, BLK), BLK)
@@ -840,6 +921,8 @@
             pltpu.VMEM((total, 2 * states, BLK), BF),
             pltpu.VMEM((total, fields, BLK), F32),
             pltpu.VMEM((total, fields, BLK), F32),
+            pltpu.VMEM((depth_k, BLK), F32),
+            pltpu.VMEM((depth_k, BLK), F32),
             pltpu.SemaphoreType.DMA((blocks + 2 * halo,)),
         ],
     )(atm, y, pack_before, pack_after, bulk_coef, atm_surface, gains, band)
@@ -852,8 +935,30 @@
     )(q, picked)
     received = lax.all_to_all(outgoing, AXES, split_axis=0, concat_axis=0, tiled=True)
 
+    sea_blocks = cells // BLK
+    outer = -(-HO // BLK)
+    around = 1 + 2 * HO // BLK
+    sea_window = BLK + 2 * HO
+    sea_rows = fields * lo
+    inner = sea_blocks - 2 * outer
+    sea_inner = call(
+        sea_inner_kernel,
+        shape((inner, 2 * sea_rows, BLK), BF),
+        in_specs=[vmem] * 3,
+        out_specs=anywhere,
+        scratch=[
+            pltpu.VMEM((inner + around - 1, 2 * sea_rows, BLK), BF),
+            pltpu.VMEM((2, sea_window, BLK), BF),
+            pltpu.VMEM((2, sea_window, BLK), BF),
+            pltpu.VMEM((sea_rows, BLK), F32),
+            pltpu.VMEM((sea_rows, BLK), F32),
+            pltpu.VMEM((inner, 2 * sea_rows, BLK), BF),
+            pltpu.SemaphoreType.DMA((inner,)),
+        ],
+    )(ocean, after_all(ocean_nbr, outgoing), ocean_nbr_coef)
+
     sea_first, sea_last, atm_before, atm_after = lax.optimization_barrier(
-        (sea_first, sea_last, atm_before, atm_after, outgoing)
+        (sea_first, sea_last, atm_before, atm_after, sea_inner)
     )[:4]
     sea_before = lax.ppermute(sea_last, AXES, up)
     sea_after = lax.ppermute(sea_first, AXES, down)
@@ -892,21 +997,33 @@
     returned = lax.all_to_all(back, AXES, split_axis=0, concat_axis=0, tiled=True)
 
     ocean_final = call(
-        ocean_kernel,
-        shape((fields * lo, cells)),
-        in_specs=[vmem] * 8,
+        sea_outer_kernel,
+        shape((sea_rows, cells)),
+        in_specs=[vmem] * 7 + [anywhere] * 2,
         out_specs=anywhere,
         scratch=[
-            pltpu.VMEM(((cells + 2 * HO) // BLK, 2 * fields * lo, BLK), BF),
-            pltpu.VMEM((2, BLK + 2 * HO, BLK), BF),
-            pltpu.VMEM((2, BLK + 2 * HO, BLK), BF),
-            pltpu.VMEM((fields * lo, BLK), F32),
-            pltpu.VMEM((fields * lo, BLK), F32),
-            pltpu.VMEM((cells // BLK, 2 * fields * lo, BLK), BF),
-            pltpu.VMEM((cells // BLK, fields * lo, BLK), F32),
-            pltpu.SemaphoreType.DMA((cells // BLK,)),
+            pltpu.VMEM((2, sea_rows, (outer + around - 1) * BLK - HO), F32),
+            pltpu.VMEM((2 * (outer + around - 1), 2 * sea_rows, BLK), BF),
+            pltpu.VMEM((2, sea_window, BLK), BF),
+            pltpu.VMEM((2, sea_window, BLK), BF),
+            pltpu.VMEM((sea_rows, BLK), F32),
+            pltpu.VMEM((sea_rows, BLK), F32),
+            pltpu.VMEM((sea_blocks, 2 * sea_rows, BLK), BF),
+            pltpu.VMEM((sea_blocks, sea_rows, BLK), F32),
+            pltpu.SemaphoreType.DMA((3,)),
+            pltpu.SemaphoreType.DMA((sea_blocks,)),
         ],
-    )(ocean, after_all(sea_before, back), sea_after, ocean_nbr, ocean_nbr_coef, sea_vertical, ocean_mix, flux)
+    )(
+        after_all(sea_before, back),
+        sea_after,
+        ocean_nbr,
+        ocean_nbr_coef,
+        sea_vertical,
+        ocean_mix,
+        flux,
+        ocean,
+        sea_inner,
+    )
 
     surface_temp = call(
         settle_kernel,

time: 149 us -> 142 us (0.953)
  waiting for transfers between devices: 9.84 us -> 0.02 us
  Pallas kernels: 113 us -> 116 us
    ppermute x1, waiting for transfers between devices: 9.82 us -> 0.01 us  [per_device(): atm_before = lax.ppermute(atm_last, AXES, up)]
    pallas_call x1 -> x2, Pallas kernels: 21.1 us -> 24.2 us  [the longest x1 14.1 us: per_device(): call(sea_inner_kernel, shape((inner, 2 * sea_rows, BLK), BF), in_specs=[v...]
  transfers between devices with their start and end apart: 8 -> 8, of which waited for: 1 -> 0; matrix products, arithmetic and copies ran while one was open for 0% -> 0% of each run, Pallas kernels for 68% -> 74%
where the time goes in v7:
time: 142 us
  Pallas kernels  116 us (82%)
  starting transfers between devices  22.9 us (16%)
  local copies, waits for them, and re-layouts  2.19 us (2%)
    pallas_call x1, Pallas kernels, per_device(): call(interior_kernel, (shape((blocks, states, BLK)), shape((4 * halo, 2 *...  31.9 us
    pallas_call x1, Pallas kernels, per_device(): call(edge_kernel, shape((rows, columns)), in_specs=[anywhere] * 3 + [vmem...  23.1 us
    pallas_call x1, Pallas kernels, per_device(): call(sea_inner_kernel, shape((inner, 2 * sea_rows, BLK), BF), in_specs=[v...  14.1 us
    pallas_call x1, Pallas kernels, per_device(): call(exchange_kernel, (shape((fields, cells)), shape((peers, 2 * parts, l...  13 us
    pallas_call x1, Pallas kernels, per_device(): call(sea_outer_kernel, shape((sea_rows, cells)), in_specs=[vmem] * 7 + [a...  10.1 us
    pallas_call x1, Pallas kernels, per_device(): call(band_kernel, (shape((blocks, 2, window, BLK), BF),) + halo_shapes, i...  8.21 us
    pallas_call x1, Pallas kernels, per_device(): call(prepare_kernel(fields), (shape((states, columns)), shape((1, columns...  6.03 us
    ppermute x1, starting transfers between devices, per_device(): atm_after = lax.ppermute(atm_first, AXES, down)  5.33 us
  transfers between devices with their start and end apart: 8, of which 0 were waited for; matrix products, arithmetic and copies ran while one was open for 0% of the time, Pallas kernels for 74%

profile of v7, /device:TPU:0, one launch (start us, length us, event | category | flops | bytes accessed | tf_op | source)
XLA Modules:
  0.0 141.9 jit_solution(2044742682348480914)
XLA Ops:
  0.6 6.0 %shard_map.175 = (f32[16,4096]{1,0:T(8,128)}, f32[1,4096]{1,0:T(1,128)}, f32[40,1024]{1,0:T(8,128)}, f32[40,1024]{1,0:T(8,128)}, f32[16,128]{1,0:T(8,128)}, /*in...) custom-call(f32[72,72]{1,0:T(8,128)} %mix.2, f32[80,80]{1,0:T(8,128)} %mix.3, f32[288,4096]{1,0:T(8,128)} %bitcast.10, ...), custom_call_target="tpu_custom_call" | custom-call | flops 1000000 | bytes 10000 | tf_op jit(solution)/shard_map/pallas_call | solution.py:854
  6.7 3.0 %collective-permute-start = (f32[40,1024]{1,0:T(8,128)}, f32[40,1024]{1,0:T(8,128)S(1)}, u32[]{:S(2)}, u32[]{:S(2)}) collective-permute-start(f32[40,1024]{1,0:T(8,128)} %get-tuple-element.39), channel_id=1, source_target_pairs={{0,1},{1,2},{2,3},{3,4},{4,5},{5,6},{6,7},{7,8},{8,9},{9,10},{10,1... | collective-permute-start | bytes 491528 | tf_op jit(solution)/shard_map/ppermute | solution.py:880
  9.7 3.5 %collective-permute-start.1 = (f32[40,1024]{1,0:T(8,128)}, f32[40,1024]{1,0:T(8,128)S(1)}, u32[]{:S(2)}, u32[]{:S(2)}) collective-permute-start(f32[40,1024]{1,0:T(8,128)} %get-tuple-element.40), channel_id=1, source_target_pairs={{1,0},{2,1},{3,2},{4,3},{5,4},{6,5},{7,6},{8,7},{9,8},{10,9},{11,1... | collective-permute-start | bytes 491528 | tf_op jit(solution)/shard_map/ppermute | solution.py:881
  13.2 8.2 %shard_map.176 = (bf16[16,2,768,256]{3,2,1,0:T(8,128)(2,1)}, f32[288,1024]{1,0:T(8,128)}, f32[288,1024]{1,0:T(8,128)}, f32[320,384]{1,0:T(8,128)}, f32[320,384]{1,0:T(8,128)}) custom-call(s32[6,4096]{1,0:T(8,128)} %nbr.4, f32[6,4096]{1,0:T(8,128)} %coef.6, f32[288,4096]{1,0:T(8,128)} %bitcast.11, f32[320,4096]{1,0:T(8,128)} %bitcast.7), custom_call_target="tpu_custom_call" | custom-call | flops 1000000 | bytes 10000 | tf_op jit(solution)/shard_map/pallas_call | solution.py:884
  21.4 0.0 collective-permute-done.before
  21.4 0.0 collective-permute-done.1.after
  21.4 0.1 collective-permute-start.2
  21.5 5.3 %collective-permute-start.3 = (f32[288,1024]{1,0:T(8,128)}, f32[288,1024]{1,0:T(8,128)S(1)}, u32[]{:S(2)}, u32[]{:S(2)}) collective-permute-start(f32[288,1024]{1,0:T(8,128)} %get-tuple-element.44), channel_id=1, source_target_pairs={{1,0},{2,1},{3,2},{4,3},{5,4},{6,5},{7,6},{8,7},{9,8},{10,9},{11,1... | collective-permute-start | bytes 3538952 | tf_op jit(solution)/shard_map/ppermute | solution.py:902
  26.8 31.9 %shard_map.177 = (f32[16,16,256]{2,1,0:T(8,128)}, bf16[12,576,256]{2,1,0:T(8,128)(2,1)}, bf16[8,576,256]{2,1,0:T(8,128)(2,1)}, bf16[6,2,768,256]{3,2,1,0:T(8,128)(2,1)}) custom-call(f32[288,4096]{1,0:T(8,128)} %bitcast.12, f32[16,4096]{1,0:T(8,128)} %get-tuple-element.35.y, f32[40,1024]{1,0:T(8,128)} %copy-done.3, f32[40,1024]{1,0:T(8,128)} %copy-done.4, ...), custom_call_target="tpu_custom_call" | custom-call | flops 1000000 | bytes 10000 | tf_op jit(solution)/shard_map/pallas_call | solution.py:906
  58.8 4.3 %shard_map.178 = f32[32,8,256]{2,1,0:T(8,128)} custom-call(f32[16,16,256]{2,1,0:T(8,128)} %get-tuple-element.49.q, s32[32,512]{1,0:T(8,128)} %bitcast.16), custom_call_target="tpu_custom_call" | custom-call | flops 1000000 | bytes 10000 | tf_op jit(solution)/shard_map/pallas_call | solution.py:930
  63.0 2.8 %all-to-all-start = ((f32[32,8,256]{2,1,0:T(8,128)}), f32[32,8,256]{2,1,0:T(8,128)S(1)}, u32[]{:S(2)}, u32[]{:S(2)}) async-start(f32[32,8,256]{2,1,0:T(8,128)} %shard_map.178), calls=%async_computation | async-start | bytes 524288 | tf_op jit(solution)/shard_map/all_to_all | solution.py:936
  65.8 14.1 %shard_map.179.laid_in = bf16[12,640,256]{2,1,0:T(8,128)(2,1)} custom-call(f32[320,4096]{1,0:T(8,128)} %bitcast.8, s32[6,4096]{1,0:T(8,128)} %nbr.7, f32[6,4096]{1,0:T(8,128)} %coef.9), custom_call_target="tpu_custom_call" | custom-call | flops 1000000 | bytes 10000 | tf_op jit(solution)/shard_map/pallas_call | solution.py:944
  80.0 1.5 %collective-permute-start.4 = (f32[320,384]{1,0:T(8,128)}, f32[320,384]{1,0:T(8,128)S(1)}, u32[]{:S(2)}, u32[]{:S(2)}) collective-permute-start(f32[320,384]{1,0:T(8,128)} %get-tuple-element.58), channel_id=1, source_target_pairs={{0,1},{1,2},{2,3},{3,4},{4,5},{5,6},{6,7},{7,8},{8,9},{9,10},{10,1... | collective-permute-start | bytes 1474568 | tf_op jit(solution)/shard_map/ppermute | solution.py:963
  81.5 3.9 %collective-permute-start.5 = (f32[320,384]{1,0:T(8,128)}, f32[320,384]{1,0:T(8,128)}, u32[]{:S(2)}, u32[]{:S(2)}) collective-permute-start(f32[320,384]{1,0:T(8,128)} %get-tuple-element.63), channel_id=1, source_target_pairs={{1,0},{2,1},{3,2},{4,3},{5,4},{6,5},{7,6},{8,7},{9,8},{10,9},{11,1... | collective-permute-start | bytes 1474568 | tf_op jit(solution)/shard_map/ppermute | solution.py:964
  85.4 23.1 %shard_map.180 = f32[288,4096]{1,0:T(8,128)} custom-call(f32[288,1024]{1,0:T(8,128)} %copy-done, f32[288,1024]{1,0:T(8,128)} %copy-done.1, f32[288,4096]{1,0:T(8,128)} %bitcast.13, bf16[12,576,256]{2,1,0:T(8,128)(2,1)} %get-tuple-element.54.kept, bf16[8,576,256]{2,1,0:T(8,128)(2,1)} %get-tuple-element.55.mid, f32[16,16,256]{2,1,0:T(8,128)} %get-tuple-element.49.q, ...), custom_call_target="tpu_custom_call" | custom-call | flops 1000000 | bytes 10000 | tf_op jit(solution)/shard_map/pallas_call | solution.py:966
  108.6 0.0 copy-start.2
  108.6 0.7 copy-done.2
  109.3 13.0 %shard_map.181 = (f32[4,4096]{1,0:T(4,128)}, f32[32,4,256]{2,1,0:T(4,128)}) custom-call(f32[32,8,256]{2,1,0:T(8,128)} %copy-done.2, s32[4,4096]{1,0:T(4,128)} %slot.1, f32[4,4096]{1,0:T(4,128)} %weight.1, f32[1,4096]{1,0:T(1,128)} %get-tuple-element.60.yo, f32[40,1024]{1,0:T(8,128)} %copy-done.3, f32[40,1024]{1,0:T(8,128)} %copy-done.4, s32[6,4096]{1,0:T(8,128)} %nbr.7, ...), custom_call_target="tpu_custom_call" | custom-call | flops 1000000 | bytes 10000 | tf_op jit(solution)/shard_map/pallas_call | solution.py:985
  122.2 2.8 %all-to-all-start.1 = ((f32[32,4,256]{2,1,0:T(4,128)}), f32[32,4,256]{2,1,0:T(4,128)S(1)}, u32[]{:S(2)}, u32[]{:S(2)}) async-start(f32[32,4,256]{2,1,0:T(4,128)} %get-tuple-element.61), calls=%async_computation.1 | async-start | bytes 262144 | tf_op jit(solution)/shard_map/all_to_all | solution.py:997
  125.1 0.0 collective-permute-done.4.before
  125.1 0.8 copy-done.6
  125.9 10.1 %shard_map.182 = f32[320,4096]{1,0:T(8,128)} custom-call(f32[320,384]{1,0:T(8,128)} %copy-done.6, f32[320,384]{1,0:T(8,128)} %collective-permute-done.5.after, s32[6,4096]{1,0:T(8,128)} %nbr.7, f32[6,4096]{1,0:T(8,128)} %coef.9, bf16[320,160]{1,0:T(8,128)(2,1)} %get-tuple-element.64.vertical, f32[80,80]{1,0:T(8,128)} %mix.3, ...), custom_call_target="tpu_custom_call" | custom-call | flops 1000000 | bytes 10000 | tf_op jit(solution)/shard_map/pallas_call | solution.py:999
  136.0 0.6 copy-done.5
  136.7 5.2 %shard_map.183 = f32[32,128]{1,0:T(8,128)} custom-call(f32[32,4,256]{2,1,0:T(4,128)} %copy-done.5, s32[32,512]{1,0:T(8,128)} %bitcast.17, f32[4,4096]{1,0:T(4,128)} %surf.5), custom_call_target="tpu_custom_call" | custom-call | flops 1000000 | bytes 10000 | tf_op jit(solution)/shard_map/pallas_call | solution.py:1028
  (15 shorter events, 0.0 us)
Async XLA Ops:
  6.7 14.7 %collective-permute-start = (f32[40,1024]{1,0:T(8,128)}, f32[40,1024]{1,0:T(8,128)S(1)}, u32[]{:S(2)}, u32[]{:S(2)}) collective-permute-start(f32[40,1024]{1,0:T(8,128)} %get-tuple-element.39), channel_id=1, source_target_pairs={{0,1},{1,2},{2,3},{3,4},{4,5},{5,6},{6,7},{7,8},{8,9},{9,10},{10,1... | collective-permute-start | bytes 491528 | tf_op jit(solution)/shard_map/ppermute | solution.py:880
  9.7 11.7 %collective-permute-start.1 = (f32[40,1024]{1,0:T(8,128)}, f32[40,1024]{1,0:T(8,128)S(1)}, u32[]{:S(2)}, u32[]{:S(2)}) collective-permute-start(f32[40,1024]{1,0:T(8,128)} %get-tuple-element.40), channel_id=1, source_target_pairs={{1,0},{2,1},{3,2},{4,3},{5,4},{6,5},{7,6},{8,7},{9,8},{10,9},{11,1... | collective-permute-start | bytes 491528 | tf_op jit(solution)/shard_map/ppermute | solution.py:881
  21.4 5.4 %copy-start.3 = (f32[40,1024]{1,0:T(8,128)}, f32[40,1024]{1,0:T(8,128)S(1)}, u32[]{:S(2)}) copy-start(f32[40,1024]{1,0:T(8,128)S(1)} %collective-permute-done.before) | copy-start | bytes 491524
  21.4 5.4 %copy-start.4 = (f32[40,1024]{1,0:T(8,128)}, f32[40,1024]{1,0:T(8,128)S(1)}, u32[]{:S(2)}) copy-start(f32[40,1024]{1,0:T(8,128)S(1)} %collective-permute-done.1.after) | copy-start | bytes 491524
  21.4 58.6 %collective-permute-start.2 = (f32[288,1024]{1,0:T(8,128)}, f32[288,1024]{1,0:T(8,128)S(1)}, u32[]{:S(2)}, u32[]{:S(2)}) collective-permute-start(f32[288,1024]{1,0:T(8,128)} %get-tuple-element.43), channel_id=1, source_target_pairs={{0,1},{1,2},{2,3},{3,4},{4,5},{5,6},{6,7},{7,8},{8,9},{9,10},{10,1... | collective-permute-start | bytes 3538952 | tf_op jit(solution)/shard_map/ppermute | solution.py:901
  21.5 58.5 %collective-permute-start.3 = (f32[288,1024]{1,0:T(8,128)}, f32[288,1024]{1,0:T(8,128)S(1)}, u32[]{:S(2)}, u32[]{:S(2)}) collective-permute-start(f32[288,1024]{1,0:T(8,128)} %get-tuple-element.44), channel_id=1, source_target_pairs={{1,0},{2,1},{3,2},{4,3},{5,4},{6,5},{7,6},{8,7},{9,8},{10,9},{11,1... | collective-permute-start | bytes 3538952 | tf_op jit(solution)/shard_map/ppermute | solution.py:902
  63.0 45.5 %all-to-all-start = ((f32[32,8,256]{2,1,0:T(8,128)}), f32[32,8,256]{2,1,0:T(8,128)S(1)}, u32[]{:S(2)}, u32[]{:S(2)}) async-start(f32[32,8,256]{2,1,0:T(8,128)} %shard_map.178), calls=%async_computation | async-start | bytes 524288 | tf_op jit(solution)/shard_map/all_to_all | solution.py:936
  80.0 5.4 %copy-start = (f32[288,1024]{1,0:T(8,128)}, f32[288,1024]{1,0:T(8,128)S(1)}, u32[]{:S(2)}) copy-start(f32[288,1024]{1,0:T(8,128)S(1)} %collective-permute-done.2.before) | copy-start | bytes 3538948
  80.0 5.4 %copy-start.1 = (f32[288,1024]{1,0:T(8,128)}, f32[288,1024]{1,0:T(8,128)S(1)}, u32[]{:S(2)}) copy-start(f32[288,1024]{1,0:T(8,128)S(1)} %collective-permute-done.3.after) | copy-start | bytes 3538948
  80.0 45.1 %collective-permute-start.4 = (f32[320,384]{1,0:T(8,128)}, f32[320,384]{1,0:T(8,128)S(1)}, u32[]{:S(2)}, u32[]{:S(2)}) collective-permute-start(f32[320,384]{1,0:T(8,128)} %get-tuple-element.58), channel_id=1, source_target_pairs={{0,1},{1,2},{2,3},{3,4},{4,5},{5,6},{6,7},{7,8},{8,9},{9,10},{10,1... | collective-permute-start | bytes 1474568 | tf_op jit(solution)/shard_map/ppermute | solution.py:963
  81.5 43.6 %collective-permute-start.5 = (f32[320,384]{1,0:T(8,128)}, f32[320,384]{1,0:T(8,128)}, u32[]{:S(2)}, u32[]{:S(2)}) collective-permute-start(f32[320,384]{1,0:T(8,128)} %get-tuple-element.63), channel_id=1, source_target_pairs={{1,0},{2,1},{3,2},{4,3},{5,4},{6,5},{7,6},{8,7},{9,8},{10,9},{11,1... | collective-permute-start | bytes 1474568 | tf_op jit(solution)/shard_map/ppermute | solution.py:964
  108.6 0.7 copy-start.2
  122.2 13.8 %all-to-all-start.1 = ((f32[32,4,256]{2,1,0:T(4,128)}), f32[32,4,256]{2,1,0:T(4,128)S(1)}, u32[]{:S(2)}, u32[]{:S(2)}) async-start(f32[32,4,256]{2,1,0:T(4,128)} %get-tuple-element.61), calls=%async_computation.1 | async-start | bytes 262144 | tf_op jit(solution)/shard_map/all_to_all | solution.py:997
  125.1 0.9 copy-start.6
  136.0 0.6 copy-start.5

commit v8 on v7

--- a/solution.py
+++ b/solution.py
@@ -163,11 +163,38 @@
 
 
 def prepare_kernel(fields):
-    def body(mix, omix, atm, sea, nbr, coef, bulk, surf, spread, code, sea_spread, y, yo, first, last, gains, vertical, sea_vertical, top, sem):
+    def body(
+        mix, omix, atm, nbr, coef, bulk, surf, spread, code, sea_spread, sea,
+        y, yo, gains, lift, vertical, sea_vertical, wide_first, wide_last, sea_first, sea_last,
+        top, lists, ends, sems,
+    ):
         la = mix.shape[0]
-        columns = atm.shape[1]
-        copy = pltpu.make_async_copy(sea.at[: omix.shape[0], :], top, sem)
+        rows, columns = atm.shape
+        cells = sea.shape[1]
+        copy = pltpu.make_async_copy(sea.at[: omix.shape[0], :], top, sems.at[0])
         copy.start()
+        arriving = [
+            pltpu.make_async_copy(sea.at[:, :HO], ends.at[0], sems.at[1]),
+            pltpu.make_async_copy(sea.at[:, cells - HO :], ends.at[1], sems.at[2]),
+        ]
+        leaving = [
+            pltpu.make_async_copy(atm.at[:, :WIDE], wide_first.at[:rows], sems.at[3]),
+            pltpu.make_async_copy(atm.at[:, columns - WIDE :], wide_last.at[:rows], sems.at[4]),
+            pltpu.make_async_copy(lists.at[0], wide_first.at[rows:], sems.at[5]),
+            pltpu.make_async_copy(lists.at[1], wide_last.at[rows:], sems.at[6]),
+            pltpu.make_async_copy(ends.at[0], sea_first, sems.at[7]),
+            pltpu.make_async_copy(ends.at[1], sea_last, sems.at[8]),
+        ]
+        for i, at in enumerate((slice(0, WIDE), slice(columns - WIDE, columns))):
+            lists[i, 0:6] = nbr[:, at].astype(F32)
+            lists[i, 6:12] = coef[:, at]
+            lists[i, 12:16] = bulk[:, at]
+            lists[i, 16:20] = surf[:, at]
+            lists[i, 20:24] = jnp.zeros((4, WIDE), F32)
+        for here in arriving:
+            here.start()
+        for out in leaving[:4]:
+            out.start()
         eye = iota((la, la), 0) == iota((la, la), 1)
         step = mix[...] + jnp.where(eye, 1.0, 0.0)
 
@@ -213,6 +240,8 @@
         sea_vertical[...] = stacked(jnp.where(blocks, spreaded, 0.0))
 
         weights = [jnp.broadcast_to(col(r, eye), (la, 128)) for r in rows_up]
+        for k, weight in enumerate(weights):
+            lift[k] = weight
         sea_weight = jnp.broadcast_to(col(sea_step[0:1, :], sea_eye), (lo, 128))
         copy.wait()
         for start in range(0, columns, 128):
@@ -225,207 +254,127 @@
                         x * weights[k - 1], axis=0, keepdims=True
                     )
             yo[:, at] = jnp.sum(top[:, at] * sea_weight, axis=0, keepdims=True)
-        for target, at in ((first, slice(0, WIDE)), (last, slice(columns - WIDE, columns))):
-            target[0:16, :] = y[:, at]
-            target[16:22, :] = nbr[:, at].astype(F32)
-            target[22:28, :] = coef[:, at]
-            target[28:32, :] = bulk[:, at]
-            target[32:36, :] = surf[:, at]
-            target[36:37, :] = yo[:, at]
-            target[37:40, :] = jnp.zeros((3, WIDE), F32)
+        for here, out in zip(arriving, leaving[4:]):
+            here.wait()
+            out.start()
+        for out in leaving:
+            out.wait()
 
     return body
 
 
-def band_kernel(nbr, coef, atm, ocean, band, *refs):
-    halos, held, (w, sems, in_sems, out_sems) = refs[:4], refs[4:8], refs[8:]
-    blocks = nbr.shape[1] // BLK
-    columns = atm.shape[1]
-    spans = [(atm, 0, WIDE), (atm, columns - WIDE, WIDE), (ocean, 0, HO), (ocean, ocean.shape[1] - HO, HO)]
-    arriving = [
-        pltpu.make_async_copy(source.at[:, first : first + width], held[i], in_sems.at[i])
-        for i, (source, first, width) in enumerate(spans)
-    ]
-    leaving = [pltpu.make_async_copy(held[i], halos[i], out_sems.at[i]) for i in range(len(spans))]
-    for copy in arriving:
-        copy.start()
-
-    def copy(b):
-        return pltpu.make_async_copy(w.at[b], band.at[b], sems.at[b])
-
-    def build(b, _):
-        at = pl.ds(pl.multiple_of(b * BLK, BLK), BLK)
-
-        def store(first, step, lanes, high, low):
-            w[b, 0, first : first + step, lanes] = high
-            w[b, 1, first : first + step, lanes] = low
-
-        build_band(store, nbr[:, at] - b * BLK, coef[:, at], HA)
-        copy(b).start()
-        return 0
-
-    lax.fori_loop(0, blocks // 2, build, 0)
-    for here, there in zip(arriving, leaving):
-        here.wait()
-        there.start()
-    lax.fori_loop(blocks // 2, blocks, build, 0)
-
-    def finish(b, _):
-        copy(b).wait()
-        return 0
-
-    lax.fori_loop(0, blocks, finish, 0)
-    for there in leaving:
-        there.wait()
+def band_build(ids, coef, w, k):
+    def store(first, step, lanes, high, low):
+        w[k, 0, first : first + step, lanes] = high
+        w[k, 1, first : first + step, lanes] = low
+
+    return band_pieces(store, ids, coef, HA)
+
+
+def advance(moved, s, gains, bulk, surf):
+    fields = bulk.shape[0]
+    states = moved.shape[0]
+    slot = iota((states, BLK), 0) // fields
+    flux = bulk * (surf - moved[(s - 1) * fields : s * fields])
+    kept = jnp.where(slot == s - 1, 0.0, moved)
+    return kept + gains[:, s - 1 : s] * jnp.concatenate([flux] * ASTEPS, axis=0)
 
 
 def interior_kernel(
-    atm, y, before, after, bulk, surf, gains, band, q, kept, mid, far, w, sa, sb, za, zb, bulks, surfs, ma, mb, sems
+    atm, y, nbr, coef, bulk, surf, gains, q, kept_out, mid_out, band, w, sa, sb, ma, mb, kept, mid, sems
 ):
     rows, columns = atm.shape
+    states = y.shape[0]
+    height = rows + states
     blocks = columns // BLK
-    fields = bulk.shape[0]
-    states = fields * ASTEPS
-    total = blocks + 2 * ASTEPS
-    halo = ASTEPS - 1
-
-    def arriving(b):
-        return pltpu.make_async_copy(band.at[b], w.at[halo + b], sems.at[b])
-
-    for b in list(range(1, blocks - 1)) + [0, blocks - 1]:
-        arriving(b).start()
-
+    sent = list(range(ASTEPS)) + list(range(blocks - ASTEPS, blocks))
     leaving = []
-    for e in list(range(ASTEPS)) + list(range(ASTEPS + blocks, total)):
-        pack = before if e < ASTEPS else after
-        local = e if e < ASTEPS else e - ASTEPS - blocks
-        at = slice(local * BLK, (local + 1) * BLK)
-        za[e] = stacked(pack[0:states, at])
-        bulks[e] = pack[28:32, at]
-        surfs[e] = pack[32:36, at]
-
-    def build_far(e):
-        pack = before if e < ASTEPS else after
-        local = e if e < ASTEPS else e - ASTEPS - blocks
-        at = slice(local * BLK, (local + 1) * BLK)
-        origin = local * BLK + (columns - WIDE if e < ASTEPS else 0)
-
-        def store(first, step, lanes, high, low):
-            w[e - 1, 0, first : first + step, lanes] = high
-            w[e - 1, 1, first : first + step, lanes] = low
-
-        yield from band_pieces(store, pack[16:22, at].astype(jnp.int32) - origin, pack[22:28, at], HA)
-        i = e - 1 if e < ASTEPS else e - 1 - blocks
-        copy = pltpu.make_async_copy(w.at[e - 1], far.at[i], sems.at[blocks + i])
+
+    def depart(copy):
         copy.start()
         leaving.append(copy)
 
-    for b in range(blocks):
+    def build(b):
         at = slice(b * BLK, (b + 1) * BLK)
-        both = stacked(jnp.concatenate([atm[:, at], y[:, at]], axis=0))
-        sa[b] = both
-        height = rows + states
-        za[b + ASTEPS] = jnp.concatenate([both[rows:height], both[height + rows :]], axis=0)
-        bulks[b + ASTEPS] = bulk[:, at]
-        surfs[b + ASTEPS] = surf[:, at]
-
-    slot = iota((states, BLK), 0) // fields
+        yield from band_build(nbr[:, at] - b * BLK, coef[:, at], w, b)
+
+    def split(b):
+        at = slice(b * BLK, (b + 1) * BLK)
+        sa[b] = stacked(jnp.concatenate([atm[:, at], y[:, at]], axis=0))
+        yield
+
+    def pieces(b, moved):
+        yield from product_pieces([sa[b + d] for d in (-1, 0, 1)], w.at[b], moved)
+
+    def finish(b, s, moved, target):
+        at = pl.ds(pl.multiple_of(b * BLK, BLK), BLK)
+        value = advance(moved[rows:], s, gains, bulk[:, at], surf[:, at])
+        if s == ASTEPS:
+            q[b - ASTEPS] = value
+            mid[b - ASTEPS] = stacked(moved[:rows])
+        else:
+            high, low = halves(moved[:rows])
+            zh, zl = halves(value)
+            target[b] = jnp.concatenate([high, zh, low, zl], axis=0)
+
+    interleave(itertools.chain(*[split(b) for b in range(4)]))
+    interleave(build(1))
+    interleave(build(2))
+    for i in range(blocks // 2 - 1):
+        b = 2 * i + 1
+        nexts = [b + 2, b + 3] if b + 3 < blocks - 1 else [0, blocks - 1]
+        works = [itertools.chain(pieces(b, ma), pieces(b + 1, mb)), itertools.chain(*[build(k) for k in nexts])]
+        if b + 4 < blocks:
+            works.append(itertools.chain(split(b + 3), split(b + 4)))
+        interleave(*works)
+        finish(b, 1, ma[...], sb)
+        finish(b + 1, 1, mb[...], sb)
+    for i, b in enumerate(sent):
+        depart(pltpu.make_async_copy(w.at[b], band.at[i], sems.at[i]))
+
     for s in range(1, ASTEPS + 1):
         xs, xt = (sa, sb) if s % 2 else (sb, sa)
-        zs, zt = (za, zb) if s % 2 else (zb, za)
-        gain = jnp.broadcast_to(gains[:, s - 1 : s], (states, BLK))
-        keep = jnp.where(slot == s - 1, 0.0, 1.0)
-
-        def advance(moved, e, s=s, gain=gain, keep=keep):
-            flux = bulks[e] * (surfs[e] - moved[(s - 1) * fields : s * fields])
-            return moved * keep + gain * jnp.concatenate([flux] * ASTEPS, axis=0)
-
-        def edge(e, s=s, zs=zs, zt=zt, advance=advance):
-            def begin():
-                x2 = jnp.concatenate([zs[e - 1], zs[e], zs[e + 1]], axis=1)
-                return products(x2, (w[e - 1, 0], w[e - 1, 1]))
-
-            def finish(moved):
-                value = advance(moved, e)
-                if s == ASTEPS:
-                    q[e - ASTEPS] = value
-                else:
-                    zt[e] = stacked(value)
-
-            return begin, finish
-
-        def inner(b, s=s, xs=xs, xt=xt, zt=zt, advance=advance):
+
+        def inner(b, s=s, xs=xs, xt=xt):
             def begin():
                 x2 = jnp.concatenate([xs[b - 1], xs[b], xs[b + 1]], axis=1)
-                return products(x2, (w[b + halo, 0], w[b + halo, 1]))
-
-            def finish(moved):
-                value = advance(moved[rows:], b + ASTEPS)
-                if s == ASTEPS:
-                    q[b] = value
-                    mid[b - ASTEPS] = stacked(moved[:rows])
-                else:
-                    high, low = halves(moved[:rows])
-                    zh, zl = halves(value)
-                    xt[b] = jnp.concatenate([high, zh, low, zl], axis=0)
-                    zt[b + ASTEPS] = jnp.concatenate([zh, zl], axis=0)
-
-            return begin, finish
-
-        def together(i, _, s=s, edge=edge, inner=inner):
-            in_turn(
-                [
-                    inner(s + 2 * i),
-                    edge(s + i),
-                    edge(blocks + ASTEPS - s + i),
-                    inner(s + 2 * i + 1),
-                ]
-            )
-            return 0
-
-        def alone(i, _, s=s, inner=inner):
+                return products(x2, (w[b, 0], w[b, 1]))
+
+            return begin, lambda moved: finish(b, s, moved, xt)
+
+        def pair(i, _, s=s, inner=inner):
             in_turn([inner(s + 2 * i), inner(s + 2 * i + 1)])
             return 0
 
-        if s == 1:
-            builds = [build_far(e) for e in list(range(1, ASTEPS)) + list(range(ASTEPS + blocks, total - 1))]
-
-            def pieces(b, moved):
-                yield from product_pieces([sa[b + d] for d in (-1, 0, 1)], w.at[b + halo], moved)
-
-            for i in range(blocks // 2 - 1):
-                arriving(1 + 2 * i).wait()
-                arriving(2 + 2 * i).wait()
-                both = itertools.chain(pieces(1 + 2 * i, ma), pieces(2 + 2 * i, mb))
-                interleave(both, *builds[i : i + 1])
-                inner(1 + 2 * i)[1](ma[...])
-                inner(2 + 2 * i)[1](mb[...])
-            for rest in builds[blocks // 2 - 1 :]:
-                interleave(rest)
-            arriving(0).wait()
-            arriving(blocks - 1).wait()
-            in_turn([edge(e) for i in range(ASTEPS) for e in (1 + i, blocks + ASTEPS - 1 + i)])
-        else:
-            lax.fori_loop(0, ASTEPS, together, 0)
-            if blocks // 2 - s > ASTEPS:
-                lax.fori_loop(ASTEPS, blocks // 2 - s, alone, 0)
+        if s > 1:
+            lax.fori_loop(0, blocks // 2 - s, pair, 0)
         if s < ASTEPS:
-            height = rows + states
+            at = slice((s - 1) * 4, s * 4)
             for i, b in enumerate((s, s + 1, blocks - 2 - s, blocks - 1 - s)):
-                kept[(s - 1) * 4 + i, :rows] = xt[b, :rows]
-                kept[(s - 1) * 4 + i, rows:] = xt[b, height : height + rows]
+                kept[(s - 1) * 4 + i] = xt[b]
+            depart(pltpu.make_async_copy(kept.at[at], kept_out.at[at], sems.at[len(sent) + s]))
+    depart(pltpu.make_async_copy(mid, mid_out, sems.at[len(sent)]))
     for copy in leaving:
         copy.wait()
 
 
-def send_kernel(q, cols, out, table):
-    fields = q.shape[1] // ASTEPS
+def block_place(b, blocks, ends, middle):
+    if b < ASTEPS:
+        return ends, b
+    if b < blocks - ASTEPS:
+        return middle, b - ASTEPS
+    return ends, b - blocks + 2 * ASTEPS
+
+
+def send_kernel(q_ends, q_mid, cols, out, table):
+    fields = q_mid.shape[1] // ASTEPS
     peers, slots = cols.shape
-    blocks = q.shape[0]
+    blocks = q_ends.shape[0] + q_mid.shape[0]
     lanes = out.shape[2]
     parts = slots // lanes
     for b in range(blocks):
-        table[b * fields : (b + 1) * fields, :] = q[b, (ASTEPS - 1) * fields :, :]
+        ref, i = block_place(b, blocks, q_ends, q_mid)
+        table[b * fields : (b + 1) * fields, :] = ref[i, (ASTEPS - 1) * fields :, :]
     rows = stacked(table[...])
     half = blocks * fields
     block_of_row = iota((half, slots), 0) // fields
@@ -442,26 +391,41 @@
     lax.fori_loop(0, peers, one, 0, unroll=4)
 
 
-def exchange_kernel(recv, slot, weight, yo, before, after, nbr, coef, omix, flux_out, back, rows, tiles, hots, seas, acc):
+def exchange_kernel(
+    recv, slot, weight, yo, nbr, coef, omix, before_in, after_in, flux_out, back, rows, tiles, hots, seas, acc, held, sems
+):
     peers, per_peer, lanes = recv.shape
     links, columns = slot.shape
     fields = flux_out.shape[0]
     parts = per_peer // fields
     highs = peers * parts
     table = highs * fields
-    rows[...] = stacked(recv[...].reshape(table, lanes))
+    arriving = [
+        pltpu.make_async_copy(ref.at[: held.shape[1]], held.at[i], sems.at[i])
+        for i, ref in enumerate((before_in, after_in))
+    ]
+    for copy in arriving:
+        copy.start()
+    rows[...] = jnp.concatenate(halves(recv[...].reshape(table, lanes)), axis=1)
+    levels = omix.shape[0]
+    eye = iota((levels, levels), 0) == iota((levels, levels), 1)
+    corner = omix[0:1, 0:1] + 1.0
+    top = omix[0:1, :] + jnp.where(iota((1, levels), 1) == 0, 1.0, 0.0)
+    top = jnp.sum(jnp.where(eye, top, 0.0), axis=1, keepdims=True)
+    for copy in arriving:
+        copy.wait()
+    before, after = [jnp.sum(held[i] * top, axis=0, keepdims=True) for i in range(2)]
     acc[...] = jnp.zeros_like(acc)
     side = HO // 128
     own_tiles = columns // 128
     for t in range(own_tiles + 2 * side):
         if t < side:
-            line = before[36:37, WIDE - HO + t * 128 : WIDE - HO + (t + 1) * 128]
+            line = before[:, t * 128 : (t + 1) * 128]
         elif t < side + own_tiles:
             line = yo[:, (t - side) * 128 : (t - side + 1) * 128]
         else:
-            line = after[36:37, (t - side - own_tiles) * 128 : (t - side - own_tiles + 1) * 128]
+            line = after[:, (t - side - own_tiles) * 128 : (t - side - own_tiles + 1) * 128]
         tiles[t] = jnp.broadcast_to(line, (8, 128))
-    corner = omix[0:1, 0:1] + 1.0
     high_of_row = iota((table, BLK), 0) // fields
     back_rows = iota((2 * highs, BLK), 0)
     inner = back_rows % (2 * parts)
@@ -498,11 +462,11 @@
             ids = slot[r : r + 1, at]
             hot = one_hot(ids & (lanes - 1), lanes)
             hots[j, :, r * BLK : (r + 1) * BLK] = hot
-            return mm(rows[...], hot)
+            return mm(rows[...], jnp.concatenate([hot, hot], axis=0))
 
         def finish(r, got):
             ids = slot[r : r + 1, at]
-            got = jnp.where(high_of_row == ids // lanes, got[:table] + got[table:], 0.0)
+            got = jnp.where(high_of_row == ids // lanes, got, 0.0)
             parts.append(weight[r : r + 1, at] * fold_rows(got, 2 * fields))
 
         last = begin(0)
@@ -572,102 +536,168 @@
 
 
 def edge_kernel(
-    before, after, atm, kept, mid, q, vertical, band, far, out, w, halos, sides, sa, sb, staged, wsems, sems, osems
+    y, bulk, surf, gains, lift, before, after, atm, kept_in, band, q, ends_out,
+    w, wide, sides, kept, sa, sb, ma, mb, ends, sems,
 ):
     rows = atm.shape[0]
-    blocks = q.shape[0]
+    levels = lift.shape[1]
+    fields = bulk.shape[0]
+    states = y.shape[0]
+    columns = y.shape[1]
+    blocks = columns // BLK
     halo = ASTEPS - 1
     count = halo + ASTEPS
-    arrivals = [
-        pltpu.make_async_copy(before, halos.at[0], sems.at[0]),
-        pltpu.make_async_copy(after, halos.at[1], sems.at[1]),
+    total = blocks + 2 * ASTEPS
+    arriving = [
+        pltpu.make_async_copy(before, wide.at[0], sems.at[0]),
+        pltpu.make_async_copy(after, wide.at[1], sems.at[1]),
         pltpu.make_async_copy(atm.at[:, : 2 * BLK], sides.at[0], sems.at[2]),
-        pltpu.make_async_copy(atm.at[:, (blocks - 2) * BLK :], sides.at[1], sems.at[3]),
+        pltpu.make_async_copy(atm.at[:, columns - 2 * BLK :], sides.at[1], sems.at[3]),
     ]
-    sources = [far.at[i] for i in range(halo)] + [band.at[i] for i in range(ASTEPS)]
-    sources += [band.at[blocks - ASTEPS + i] for i in range(ASTEPS)] + [far.at[halo + i] for i in range(halo)]
-    bands = [pltpu.make_async_copy(source, w.at[i], wsems.at[i]) for i, source in enumerate(sources)]
-    needed = [list(range(ASTEPS)) + list(range(count + halo, 2 * count))]
-    needed += [[ASTEPS - 1 + i, count + halo - i] for i in range(1, ASTEPS)]
-    for copy in arrivals:
+    bands = [pltpu.make_async_copy(band.at[i], w.at[halo + i], sems.at[4 + i]) for i in range(2 * ASTEPS)]
+    keeps = pltpu.make_async_copy(kept_in, kept, sems.at[4 + 2 * ASTEPS])
+    needed = [[0, 2 * ASTEPS - 1]] + [[i, 2 * ASTEPS - 1 - i] for i in range(1, ASTEPS)]
+    for copy in arriving:
         copy.start()
     for group in needed:
         for i in group:
             bands[i].start()
-
-    def leaving(b):
-        at = pl.ds(pl.multiple_of(b * BLK, BLK), BLK)
-        return pltpu.make_async_copy(staged.at[b], out.at[:, at], osems.at[b])
-
-    levels = rows // 2
-
-    def mixed(source, shift):
-        def one(b, p):
-            def begin():
-                qh, ql = halves(q[b])
-                x2 = source[b - shift]
-                high = jnp.concatenate([x2[p * levels : (p + 1) * levels], qh], axis=0)
-                low = jnp.concatenate([x2[rows + p * levels : rows + (p + 1) * levels], ql], axis=0)
-                return mm(vertical[p], high), mm(vertical[p, :levels], low)
-
-            def finish(value):
-                staged[b, p * levels : (p + 1) * levels] = value
-
-            return begin, finish
-
-        def four(i, _):
-            in_turn([one(4 * i + k, p) for k in range(4) for p in range(2)])
-            for k in range(4):
-                leaving(4 * i + k).start()
-            return 0
-
-        return four
-
-    lax.fori_loop(1, blocks // 4 - 1, mixed(mid, ASTEPS), 0)
-    for copy in arrivals:
+    keeps.start()
+
+    def place(e):
+        if e < ASTEPS:
+            return wide.at[0], e
+        if e >= total - ASTEPS:
+            return wide.at[1], e - total + ASTEPS
+        return None, e - ASTEPS
+
+    def coefs(e):
+        ref, local = place(e)
+        at = slice(local * BLK, (local + 1) * BLK)
+        if ref is None:
+            return bulk[:, at], surf[:, at]
+        return ref[rows + 12 : rows + 16, at], ref[rows + 16 : rows + 20, at]
+
+    def build(e):
+        ref, local = place(e)
+        origin = local * BLK + (columns - WIDE if e < ASTEPS else 0)
+        at = slice(local * BLK, (local + 1) * BLK)
+        ids = ref[rows : rows + 6, at].astype(jnp.int32) - origin
+        k = e - 1 if e < ASTEPS else e - (total - 1) + 2 * count
+        yield from band_build(ids, ref[rows + 6 : rows + 12, at], w, k)
+
+    for copy in arriving:
         copy.wait()
     for i in range(ASTEPS):
         at = slice(i * BLK, (i + 1) * BLK)
-        sa[i] = stacked(halos[0, :, at])
-        sa[6 + 2 + i] = stacked(halos[1, :, at])
+        for side in range(2):
+            x = wide[side, :rows, at]
+            lifted = [x[(f + 1) * levels - 1 : (f + 1) * levels] for f in range(fields)]
+            for k in range(ASTEPS - 1):
+                weight = jnp.concatenate([lift[k]] * (BLK // 128), axis=1)
+                for f in range(fields):
+                    lifted.append(jnp.sum(x[f * levels : (f + 1) * levels] * weight, axis=0, keepdims=True))
+            sa[i if side == 0 else 8 + i] = stacked(jnp.concatenate([x] + lifted, axis=0))
     for i in range(2):
         at = slice(i * BLK, (i + 1) * BLK)
-        sa[ASTEPS + i] = stacked(sides[0, :, at])
-        sa[6 + i] = stacked(sides[1, :, at])
+        far = slice(columns - (2 - i) * BLK, columns - (1 - i) * BLK)
+        sa[ASTEPS + i] = stacked(jnp.concatenate([sides[0, :, at], y[:, at]], axis=0))
+        sa[6 + i] = stacked(jnp.concatenate([sides[1, :, at], y[:, far]], axis=0))
+
     buffers = (sa, sb)
+    builds = [itertools.chain(build(1 + i), build(total - 2 - i)) for i in range(halo)]
+    interleave(builds[0])
     for s in range(1, ASTEPS + 1):
         source, target = buffers[(s - 1) % 2], buffers[s % 2]
         last = s == ASTEPS
-        for i in needed[s - 1]:
-            bands[i].wait()
-
-        def one(side, i, s=s, source=source, target=target, last=last):
-            base = 6 * side
-            k = s - 1 + i if side == 0 else count + ASTEPS - s + i
-
+
+        def finish(side, i, moved, s=s, target=target, last=last):
+            e = s + i if side == 0 else total - 1 - s - halo + i
+            value = advance(moved[rows:], s, gains, *coefs(e))
+            if last:
+                q[4 * side + i] = value
+                ends[4 * side + i] = stacked(moved[:rows])
+            else:
+                target[6 * side + i + 2 * side] = stacked(jnp.concatenate([moved[:rows], value], axis=0))
+
+        def band_of(side, i, s=s):
+            return s - 1 + i if side == 0 else count + ASTEPS - s + i
+
+        def one(side, i, source=source, finish=finish, band_of=band_of):
             def begin():
-                x2 = jnp.concatenate([source[base + i + d] for d in range(3)], axis=1)
+                x2 = jnp.concatenate([source[6 * side + i + d] for d in range(3)], axis=1)
+                k = band_of(side, i)
                 return products(x2, (w[k, 0], w[k, 1]))
 
-            def finish(moved):
-                target[base + i + (2 * side if not last else 0)] = stacked(moved)
-
-            return begin, finish
-
-        in_turn([one(side, i) for i in range(ASTEPS) for side in range(2)])
+            return begin, lambda moved: finish(side, i, moved)
+
+        if s == 1:
+            for i in range(halo):
+                pieces = [
+                    product_pieces([source[6 * side + j + d] for d in range(3)], w.at[band_of(side, j)], m)
+                    for side, j, m in ((0, i, ma), (1, halo - i, mb))
+                ]
+                interleave(itertools.chain(*pieces), *builds[i + 1 : i + 2])
+                finish(0, i, ma[...])
+                finish(1, halo - i, mb[...])
+            for k in needed[0]:
+                bands[k].wait()
+            in_turn([one(0, halo), one(1, 0)])
+            keeps.wait()
+        else:
+            for k in needed[s - 1]:
+                bands[k].wait()
+            in_turn([one(side, i) for i in range(ASTEPS) for side in range(2)])
         if not last:
             for i in range(2):
                 target[ASTEPS + i] = kept[(s - 1) * 4 + i]
                 target[6 + i] = kept[(s - 1) * 4 + 2 + i]
-    final = buffers[ASTEPS % 2]
-    lax.fori_loop(0, 1, mixed(final, 0), 0)
-    lax.fori_loop(blocks // 4 - 1, blocks // 4, mixed(final, blocks - ASTEPS - 6), 0)
-
-    def done(b, _):
+    out = pltpu.make_async_copy(ends, ends_out, sems.at[5 + 2 * ASTEPS])
+    out.start()
+    out.wait()
+
+
+def finish_kernel(q_ends, q_mid, vertical, ends_in, mid_in, out, ends, mid, staged, sems, osems):
+    rows = ends.shape[1] // 2
+    levels = rows // 2
+    blocks = staged.shape[0]
+    arriving = [
+        pltpu.make_async_copy(mid_in, mid, sems.at[0]),
+        pltpu.make_async_copy(ends_in, ends, sems.at[1]),
+    ]
+    for copy in arriving:
+        copy.start()
+
+    def leaving(b):
+        at = slice(b * BLK, (b + 1) * BLK)
+        return pltpu.make_async_copy(staged.at[b], out.at[:, at], osems.at[b])
+
+    def one(b, p):
+        ref, i = block_place(b, blocks, ends, mid)
+        share, _ = block_place(b, blocks, q_ends, q_mid)
+
+        def begin():
+            qh, ql = halves(share[i])
+            high = jnp.concatenate([ref[i, p * levels : (p + 1) * levels], qh], axis=0)
+            low = jnp.concatenate([ref[i, rows + p * levels : rows + (p + 1) * levels], ql], axis=0)
+            return mm(vertical[p], high), mm(vertical[p, :levels], low)
+
+        def finish(value):
+            staged[b, p * levels : (p + 1) * levels] = value
+
+        return begin, finish
+
+    middle = list(range(ASTEPS, blocks - ASTEPS))
+    outer = list(range(ASTEPS)) + list(range(blocks - ASTEPS, blocks))
+    for copy, group in zip(arriving, (middle, outer)):
+        copy.wait()
+        for start in range(0, len(group), 4):
+            some = group[start : start + 4]
+            in_turn([one(b, p) for b in some for p in range(2)])
+            for b in some:
+                leaving(b).start()
+    for b in range(blocks):
         leaving(b).wait()
-        return 0
-
-    lax.fori_loop(0, blocks, done, 0)
 
 
 def sea_build(nbr, coef, b, w):
@@ -851,24 +881,33 @@
     spread = ((c_of[0] % la == np.arange(la)[:, None]) & (c_of[0] < 2 * la)).astype(np.float32)
     sea_spread = (np.arange(2 * lo)[None, :] % lo == np.arange(lo)[:, None]).astype(np.float32)
 
-    y, yo, first, last, gains, vertical, sea_vertical = call(
+    wide_rows = rows + 24
+    y, yo, gains, lift, vertical, sea_vertical, wide_first, wide_last, sea_first, sea_last = call(
         prepare_kernel(fields),
         (
             shape((states, columns)),
             shape((1, columns)),
-            shape((40, WIDE)),
-            shape((40, WIDE)),
             shape((states, 128)),
+            shape((ASTEPS - 1, la, 128)),
             shape((half, 4 * la, 2 * la + states), BF),
             shape((4 * lo, 2 * lo), BF),
+            shape((wide_rows, WIDE)),
+            shape((wide_rows, WIDE)),
+            shape((fields * lo, HO)),
+            shape((fields * lo, HO)),
         ),
-        in_specs=[vmem] * 3 + [anywhere] + [vmem] * 7,
-        scratch=[pltpu.VMEM((lo, cells), F32), pltpu.SemaphoreType.DMA(())],
+        in_specs=[vmem] * 10 + [anywhere],
+        out_specs=(vmem,) * 6 + (anywhere,) * 4,
+        scratch=[
+            pltpu.VMEM((lo, cells), F32),
+            pltpu.VMEM((2, 24, WIDE), F32),
+            pltpu.VMEM((2, fields * lo, HO), F32),
+            pltpu.SemaphoreType.DMA((9,)),
+        ],
     )(
         atm_mix,
         ocean_mix,
         atm,
-        ocean,
         atm_nbr,
         atm_nbr_coef,
         bulk_coef,
@@ -876,64 +915,33 @@
         jnp.asarray(spread),
         jnp.asarray(code),
         jnp.asarray(sea_spread),
+        ocean,
     )
-    pack_before = lax.ppermute(last, AXES, up)
-    pack_after = lax.ppermute(first, AXES, down)
-
-    halo_shapes = (shape((rows, WIDE)),) * 2 + (shape((fields * lo, HO)),) * 2
-    band, atm_first, atm_last, sea_first, sea_last = call(
-        band_kernel,
-        (shape((blocks, 2, window, BLK), BF),) + halo_shapes,
-        in_specs=[vmem] * 2 + [anywhere] * 2,
-        out_specs=(anywhere,) * 5,
-        scratch=[pltpu.VMEM(h.shape, F32) for h in halo_shapes]
-        + [
-            pltpu.VMEM((blocks, 2, window, BLK), BF),
-            pltpu.SemaphoreType.DMA((blocks,)),
-            pltpu.SemaphoreType.DMA((4,)),
-            pltpu.SemaphoreType.DMA((4,)),
-        ],
-    )(after_all(atm_nbr, y), atm_nbr_coef, atm, ocean)
-
-    pack_before, pack_after, atm_first, atm_last = lax.optimization_barrier(
-        (pack_before, pack_after, atm_first, atm_last)
-    )
-    atm_before = lax.ppermute(atm_last, AXES, up)
-    atm_after = lax.ppermute(atm_first, AXES, down)
-
-    total = blocks + 2 * ASTEPS
-    halo = ASTEPS - 1
-    q, kept, mid, far = call(
+    wide_before = lax.ppermute(wide_last, AXES, up)
+    wide_after = lax.ppermute(wide_first, AXES, down)
+
+    ends = 2 * ASTEPS
+    q_mid, kept, mid, band = call(
         interior_kernel,
         (
-            shape((blocks, states, BLK)),
-            shape((4 * halo, 2 * rows, BLK), BF),
-            shape((blocks - 2 * ASTEPS, 2 * rows, BLK), BF),
-            shape((2 * halo, 2, window, BLK), BF),
+            shape((blocks - ends, states, BLK)),
+            shape((4 * (ASTEPS - 1), 2 * depth_k, BLK), BF),
+            shape((blocks - ends, 2 * rows, BLK), BF),
+            shape((ends, 2, window, BLK), BF),
         ),
-        in_specs=[vmem] * 7 + [anywhere],
-        out_specs=(vmem, vmem, vmem, anywhere),
+        in_specs=[vmem] * 7,
+        out_specs=(vmem, anywhere, anywhere, anywhere),
         scratch=[
-            pltpu.VMEM((total - 2, 2, window, BLK), BF),
+            pltpu.VMEM((blocks, 2, window, BLK), BF),
             pltpu.VMEM((blocks, 2 * depth_k, BLK), BF),
             pltpu.VMEM((blocks, 2 * depth_k, BLK), BF),
-            pltpu.VMEM((total, 2 * states, BLK), BF),
-            pltpu.VMEM((total, 2 * states, BLK), BF),
-            pltpu.VMEM((total, fields, BLK), F32),
-            pltpu.VMEM((total, fields, BLK), F32),
             pltpu.VMEM((depth_k, BLK), F32),
             pltpu.VMEM((depth_k, BLK), F32),
-            pltpu.SemaphoreType.DMA((blocks + 2 * halo,)),
+            pltpu.VMEM((4 * (ASTEPS - 1), 2 * depth_k, BLK), BF),
+            pltpu.VMEM((blocks - ends, 2 * rows, BLK), BF),
+            pltpu.SemaphoreType.DMA((ends + ASTEPS,)),
         ],
-    )(atm, y, pack_before, pack_after, bulk_coef, atm_surface, gains, band)
-
-    outgoing = call(
-        send_kernel,
-        shape((peers, parts * fields, lanes)),
-        in_specs=[vmem] * 2,
-        scratch=[pltpu.VMEM((blocks * fields, BLK), F32)],
-    )(q, picked)
-    received = lax.all_to_all(outgoing, AXES, split_axis=0, concat_axis=0, tiled=True)
+    )(atm, y, atm_nbr, atm_nbr_coef, bulk_coef, atm_surface, gains)
 
     sea_blocks = cells // BLK
     outer = -(-HO // BLK)
@@ -955,45 +963,79 @@
             pltpu.VMEM((inner, 2 * sea_rows, BLK), BF),
             pltpu.SemaphoreType.DMA((inner,)),
         ],
-    )(ocean, after_all(ocean_nbr, outgoing), ocean_nbr_coef)
-
-    sea_first, sea_last, atm_before, atm_after = lax.optimization_barrier(
-        (sea_first, sea_last, atm_before, atm_after, sea_inner)
+    )(ocean, after_all(ocean_nbr, q_mid), ocean_nbr_coef)
+
+    sea_first, sea_last, wide_before, wide_after = lax.optimization_barrier(
+        (sea_first, sea_last, wide_before, wide_after, sea_inner)
     )[:4]
     sea_before = lax.ppermute(sea_last, AXES, up)
     sea_after = lax.ppermute(sea_first, AXES, down)
 
+    q_ends, tips = call(
+        edge_kernel,
+        (shape((ends, states, BLK)), shape((ends, 2 * rows, BLK), BF)),
+        in_specs=[vmem] * 5 + [anywhere] * 5,
+        out_specs=(vmem, anywhere),
+        scratch=[
+            pltpu.VMEM((2 * (2 * ASTEPS - 1), 2, window, BLK), BF),
+            pltpu.VMEM((2, wide_rows, WIDE), F32),
+            pltpu.VMEM((2, rows, 2 * BLK), F32),
+            pltpu.VMEM((4 * (ASTEPS - 1), 2 * depth_k, BLK), BF),
+            pltpu.VMEM((12, 2 * depth_k, BLK), BF),
+            pltpu.VMEM((12, 2 * depth_k, BLK), BF),
+            pltpu.VMEM((depth_k, BLK), F32),
+            pltpu.VMEM((depth_k, BLK), F32),
+            pltpu.VMEM((ends, 2 * rows, BLK), BF),
+            pltpu.SemaphoreType.DMA((6 + 2 * ASTEPS,)),
+        ],
+    )(y, bulk_coef, atm_surface, gains, lift, wide_before, wide_after, atm, kept, band)
+
+    outgoing = call(
+        send_kernel,
+        shape((peers, parts * fields, lanes)),
+        in_specs=[vmem] * 3,
+        scratch=[pltpu.VMEM((blocks * fields, BLK), F32)],
+    )(q_ends, q_mid, picked)
+    received = lax.all_to_all(outgoing, AXES, split_axis=0, concat_axis=0, tiled=True)
+
     atm_final = call(
-        edge_kernel,
+        finish_kernel,
         shape((rows, columns)),
-        in_specs=[anywhere] * 3 + [vmem] * 4 + [anywhere] * 2,
+        in_specs=[vmem] * 3 + [anywhere] * 2,
         out_specs=anywhere,
         scratch=[
-            pltpu.VMEM((2 * (2 * ASTEPS - 1), 2, window, BLK), BF),
-            pltpu.VMEM((2, rows, WIDE), F32),
-            pltpu.VMEM((2, rows, 2 * BLK), F32),
-            pltpu.VMEM((12, 2 * rows, BLK), BF),
-            pltpu.VMEM((12, 2 * rows, BLK), BF),
+            pltpu.VMEM((ends, 2 * rows, BLK), BF),
+            pltpu.VMEM((blocks - ends, 2 * rows, BLK), BF),
             pltpu.VMEM((blocks, rows, BLK), F32),
-            pltpu.SemaphoreType.DMA((2 * (2 * ASTEPS - 1),)),
-            pltpu.SemaphoreType.DMA((4,)),
+            pltpu.SemaphoreType.DMA((2,)),
             pltpu.SemaphoreType.DMA((blocks,)),
         ],
-    )(after_all(atm_before, outgoing), atm_after, atm, kept, mid, q, vertical, band, far)
-
-    received = after_all(received, atm_final)
+    )(after_all(q_ends, outgoing), q_mid, vertical, tips, mid)
+
     flux, back = call(
         exchange_kernel,
         (shape((fields, cells)), shape((peers, 2 * parts, lanes))),
-        in_specs=[vmem] * 9,
+        in_specs=[vmem] * 7 + [anywhere] * 2,
         scratch=[
-            pltpu.VMEM((2 * peers * parts * fields, lanes), BF),
+            pltpu.VMEM((peers * parts * fields, 2 * lanes), BF),
             pltpu.VMEM((cells // 128 + 2 * HO // 128, 8, 128), F32),
             pltpu.VMEM((cells // BLK, lanes, remap_slot.shape[0] * BLK), BF),
             pltpu.VMEM((1, cells), F32),
             pltpu.VMEM((4 * peers * parts, lanes), F32),
+            pltpu.VMEM((2, lo, HO), F32),
+            pltpu.SemaphoreType.DMA((2,)),
         ],
-    )(received, remap_slot, remap_weight, yo, pack_before, pack_after, ocean_nbr, ocean_nbr_coef, ocean_mix)
+    )(
+        after_all(received, atm_final),
+        remap_slot,
+        remap_weight,
+        yo,
+        ocean_nbr,
+        ocean_nbr_coef,
+        ocean_mix,
+        sea_before,
+        sea_after,
+    )
     returned = lax.all_to_all(back, AXES, split_axis=0, concat_axis=0, tiled=True)
 
     ocean_final = call(

time: 142 us -> 161 us (1.13)
  waiting for transfers between devices: 0.02 us -> 27.2 us
  Pallas kernels: 116 us -> 109 us
  starting transfers between devices: 22.9 us -> 21.2 us
    ppermute x4 -> x2, waiting for transfers between devices: 0.01 us -> 11.8 us  [the longest x1 9.95 us: per_device(): wide_before = lax.ppermute(wide_last, AXES, up)]
    all_to_all x1, waiting for transfers between devices: 0.01 us -> 10.1 us  [per_device(): lax.all_to_all(outgoing, AXES, split_axis=0, concat_axis=0, tiled=True)]
    pallas_call x3, Pallas kernels: 63.2 us -> 53.6 us  [the longest x1 27.5 us: per_device(): call(interior_kernel, (shape((blocks - ends, states, BLK)), shape((4 * (A...]
    ppermute x4 -> x2, starting transfers between devices: 11.9 us -> 6.49 us  [the longest x1 3.5 us: per_device(): wide_after = lax.ppermute(wide_first, AXES, down)]
    ppermute x1, waiting for transfers between devices: 0.01 us -> 3.42 us  [per_device(): sea_before = lax.ppermute(sea_last, AXES, up)]
    all_to_all x1, starting transfers between devices: 2.8 us -> 4.89 us  [per_device(): lax.all_to_all(outgoing, AXES, split_axis=0, concat_axis=0, tiled=True)]
    pallas_call x1, Pallas kernels: 6.03 us -> 7.98 us  [per_device(): call(prepare_kernel(fields), (shape((states, columns)), shape((1, columns...]
    ppermute x1, waiting for transfers between devices: 0.01 us -> 1.86 us  [per_device(): sea_after = lax.ppermute(sea_first, AXES, down)]
  transfers between devices with their start and end apart: 8 -> 6, of which waited for: 0 -> 5; matrix products, arithmetic and copies ran while one was open for 0% -> 0% of each run, Pallas kernels for 74% -> 36%
where the time goes in v8:
time: 161 us
  Pallas kernels  109 us (68%)
  waiting for transfers between devices  27.2 us (17%)
  starting transfers between devices  21.2 us (13%)
  local copies, waits for them, and re-layouts  2.5 us (2%)
    pallas_call x1, Pallas kernels, per_device(): call(interior_kernel, (shape((blocks - ends, states, BLK)), shape((4 * (A...  27.5 us
    pallas_call x1, Pallas kernels, per_device(): call(edge_kernel, (shape((ends, states, BLK)), shape((ends, 2 * rows, BLK...  20.1 us
    pallas_call x1, Pallas kernels, per_device(): call(sea_inner_kernel, shape((inner, 2 * sea_rows, BLK), BF), in_specs=[v...  14.1 us
    pallas_call x1, Pallas kernels, per_device(): call(exchange_kernel, (shape((fields, cells)), shape((peers, 2 * parts, l...  13.9 us
    all_to_all x1, waiting for transfers between devices, per_device(): lax.all_to_all(outgoing, AXES, split_axis=0, concat_axis=0, tiled=True)  10.1 us
    pallas_call x1, Pallas kernels, per_device(): call(sea_outer_kernel, shape((sea_rows, cells)), in_specs=[vmem] * 7 + [a...  10.1 us
    ppermute x1, waiting for transfers between devices, per_device(): wide_before = lax.ppermute(wide_last, AXES, up)  9.95 us
    pallas_call x1, Pallas kernels, per_device(): call(prepare_kernel(fields), (shape((states, columns)), shape((1, columns...  7.98 us
  transfers between devices with their start and end apart: 6, of which 5 were waited for; matrix products, arithmetic and copies ran while one was open for 0% of the time, Pallas kernels for 36%

profile of v8, /device:TPU:0, one launch (start us, length us, event | category | flops | bytes accessed | tf_op | source)
XLA Modules:
  0.0 160.8 jit_solution(5185658082588982724)
XLA Ops:
  0.6 8.0 %shard_map.175 = (f32[16,4096]{1,0:T(8,128)}, f32[1,4096]{1,0:T(1,128)}, f32[16,128]{1,0:T(8,128)}, f32[3,72,128]{2,1,0:T(8,128)}, bf16[2,288,160]{2,1,0:T(8,128...) custom-call(f32[72,72]{1,0:T(8,128)} %mix.2, ...), custom_call_target="tpu_custom_call" | custom-call | flops 1000000 | bytes 10000 | tf_op jit(solution)/shard_map/pallas_call | solution.py:885
  8.6 3.0 %collective-permute-start = (f32[312,1024]{1,0:T(8,128)}, f32[312,1024]{1,0:T(8,128)S(1)}, u32[]{:S(2)}, u32[]{:S(2)}) collective-permute-start(f32[312,1024]{1,0:T(8,128)} %get-tuple-element.35), channel_id=1, source_target_pairs={{0,1},{1,2},{2,3},{3,4},{4,5},{5,6},{6,7},{7,8},{8,9},{9,10},{10,1... | collective-permute-start | bytes 3833864 | tf_op jit(solution)/shard_map/ppermute | solution.py:920
  11.6 3.5 %collective-permute-start.1 = (f32[312,1024]{1,0:T(8,128)}, f32[312,1024]{1,0:T(8,128)S(1)}, u32[]{:S(2)}, u32[]{:S(2)}) collective-permute-start(f32[312,1024]{1,0:T(8,128)} %get-tuple-element.36), channel_id=1, source_target_pairs={{1,0},{2,1},{3,2},{4,3},{5,4},{6,5},{7,6},{8,7},{9,8},{10,9},{11,1... | collective-permute-start | bytes 3833864 | tf_op jit(solution)/shard_map/ppermute | solution.py:921
  15.1 27.5 %shard_map.176 = (f32[8,16,256]{2,1,0:T(8,128)}, bf16[12,608,256]{2,1,0:T(8,128)(2,1)}, bf16[8,576,256]{2,1,0:T(8,128)(2,1)}, bf16[8,2,768,256]{3,2,1,0:T(8,128)(2,1)}) custom-call(f32[288,4096]{1,0:T(8,128)} %bitcast.10, f32[16,4096]{1,0:T(8,128)} %get-tuple-element.30.y, s32[6,4096]{1,0:T(8,128)} %nbr.5, f32[6,4096]{1,0:T(8,128)} %coef.6, f32[4,4096]{1,0:T(4,128)} %bulk.5, ...), custom_call_target="tpu_custom_call" | custom-call | flops 1000000 | bytes 10000 | tf_op jit(solution)/shard_map/pallas_call | solution.py:924
  42.6 14.1 %shard_map.177.laid_in = bf16[12,640,256]{2,1,0:T(8,128)(2,1)} custom-call(f32[320,4096]{1,0:T(8,128)} %bitcast.7, s32[6,4096]{1,0:T(8,128)} %nbr.8, f32[6,4096]{1,0:T(8,128)} %coef.9), custom_call_target="tpu_custom_call" | custom-call | flops 1000000 | bytes 10000 | tf_op jit(solution)/shard_map/pallas_call | solution.py:952
  56.7 9.9 %collective-permute-done.before = f32[312,1024]{1,0:T(8,128)S(1)} collective-permute-done((f32[312,1024]{1,0:T(8,128)}, f32[312,1024]{1,0:T(8,128)S(1)}, u32[]{:S(2)}, u32[]{:S(2)}) %collective-permute-start) | collective-permute-done | bytes 1277984 | tf_op jit(solution)/shard_map/ppermute | solution.py:920
  66.6 1.8 %collective-permute-done.1.after = f32[312,1024]{1,0:T(8,128)S(1)} collective-permute-done((f32[312,1024]{1,0:T(8,128)}, f32[312,1024]{1,0:T(8,128)S(1)}, u32[]{:S(2)}, u32[]{:S(2)}) %collective-permute-start.1) | collective-permute-done | bytes 1277984 | tf_op jit(solution)/shard_map/ppermute | solution.py:921
  68.5 1.1 copy-done.3
  69.5 20.1 %shard_map.178 = (f32[8,16,256]{2,1,0:T(8,128)}, bf16[8,576,256]{2,1,0:T(8,128)(2,1)}) custom-call(f32[16,4096]{1,0:T(8,128)} %get-tuple-element.30.y, f32[4,4096]{1,0:T(4,128)} %bulk.5, f32[4,4096]{1,0:T(4,128)} %surf.7, f32[16,128]{1,0:T(8,128)} %get-tuple-element.31.gains, f32[3,72,128]{2,1,0:T(8,128)} %get-tuple-element.32.lift, f32[312,1024]{1,0:T(8,128)} %copy-done.2, ...), custom_call_target="tpu_custom_call" | custom-call | flops 1000000 | bytes 10000 | tf_op jit(solution)/shard_map/pallas_call | solution.py:974
  89.7 4.3 %shard_map.179 = f32[32,8,256]{2,1,0:T(8,128)} custom-call(f32[8,16,256]{2,1,0:T(8,128)} %get-tuple-element.44.q_ends, f32[8,16,256]{2,1,0:T(8,128)} %get-tuple-element.37.q_mid, s32[32,512]{1,0:T(8,128)} %bitcast.14), custom_call_target="tpu_custom_call" | custom-call | flops 1000000 | bytes 10000 | tf_op jit(solution)/shard_map/pallas_call | solution.py:993
  94.0 4.9 %all-to-all-start = ((f32[32,8,256]{2,1,0:T(8,128)}), f32[32,8,256]{2,1,0:T(8,128)S(1)}, u32[]{:S(2)}, u32[]{:S(2)}) async-start(f32[32,8,256]{2,1,0:T(8,128)} %shard_map.179), calls=%async_computation | async-start | bytes 524288 | tf_op jit(solution)/shard_map/all_to_all | solution.py:999
  98.9 1.8 %collective-permute-start.2 = (f32[320,384]{1,0:T(8,128)S(1)}, f32[320,384]{1,0:T(8,128)S(1)}, u32[]{:S(2)}, u32[]{:S(2)}) collective-permute-start(f32[320,384]{1,0:T(8,128)S(1)} %copy-done.7), channel_id=1, source_target_pairs={{0,1},{1,2},{2,3},{3,4},{4,5},{5,6},{6,7},{7,8},{8,9},{9,10},{10,1... | collective-permute-start | bytes 1474568 | tf_op jit(solution)/shard_map/ppermute | solution.py:971
  100.8 3.7 %collective-permute-start.3 = (f32[320,384]{1,0:T(8,128)S(1)}, f32[320,384]{1,0:T(8,128)S(1)}, u32[]{:S(2)}, u32[]{:S(2)}) collective-permute-start(f32[320,384]{1,0:T(8,128)S(1)} %copy-done.6), channel_id=1, source_target_pairs={{1,0},{2,1},{3,2},{4,3},{5,4},{6,5},{7,6},{8,7},{9,8},{10,9},{11,1... | collective-permute-start | bytes 1474568 | tf_op jit(solution)/shard_map/ppermute | solution.py:972
  104.5 6.1 %shard_map.180 = f32[288,4096]{1,0:T(8,128)} custom-call(f32[8,16,256]{2,1,0:T(8,128)} %get-tuple-element.44.q_ends, f32[8,16,256]{2,1,0:T(8,128)} %get-tuple-element.37.q_mid, bf16[2,288,160]{2,1,0:T(8,128)(2,1)} %get-tuple-element.45.vertical, bf16[8,576,256]{2,1,0:T(8,128)(2,1)} %get-tuple-element.46.ends_in, bf16[8,576,256]{2,1,0:T(8,128)(2,1)} %get-tuple-element.47.mid_in), custom_call_target="tpu_custom_call" | custom-call | flops 1000000 | bytes 10000 | tf_op jit(solution)/shard_map/pallas_call | solution.py:1001
  110.6 10.1 %all-to-all-done.recv = f32[32,8,256]{2,1,0:T(8,128)S(1)} async-done(((f32[32,8,256]{2,1,0:T(8,128)}), f32[32,8,256]{2,1,0:T(8,128)S(1)}, u32[]{:S(2)}, u32[]{:S(2)}) %all-to-all-start) | async-done | bytes 262176 | tf_op jit(solution)/shard_map/all_to_all | solution.py:999
  120.7 3.4 %collective-permute-done.2.before_in.before = f32[320,384]{1,0:T(8,128)S(1)} collective-permute-done((f32[320,384]{1,0:T(8,128)S(1)}, f32[320,384]{1,0:T(8,128)S(1)}, u32[]{:S(2)}, u32[]{:S(2)}) %collective-permute-start.2) | collective-permute-done | bytes 491552 | tf_op jit(solution)/shard_map/ppermute | solution.py:971
  124.1 1.9 %collective-permute-done.3.after_in.after = f32[320,384]{1,0:T(8,128)S(1)} collective-permute-done((f32[320,384]{1,0:T(8,128)S(1)}, f32[320,384]{1,0:T(8,128)S(1)}, u32[]{:S(2)}, u32[]{:S(2)}) %collective-permute-start.3) | collective-permute-done | bytes 491552 | tf_op jit(solution)/shard_map/ppermute | solution.py:972
  126.0 0.8 copy-done.1
  126.7 13.9 %shard_map.181 = (f32[4,4096]{1,0:T(4,128)}, f32[32,4,256]{2,1,0:T(4,128)}) custom-call(f32[32,8,256]{2,1,0:T(8,128)} %copy-done.4, s32[4,4096]{1,0:T(4,128)} %slot.1, f32[4,4096]{1,0:T(4,128)} %weight.1, f32[1,4096]{1,0:T(1,128)} %get-tuple-element.50.yo, s32[6,4096]{1,0:T(8,128)} %nbr.8, f32[6,4096]{1,0:T(8,128)} %coef.9, f32[80,80]{1,0:T(8,128)} %mix.3, ...), custom_call_target="tpu_custom_call" | custom-call | flops 1000000 | bytes 10000 | tf_op jit(solution)/shard_map/pallas_call | solution.py:1015
  140.6 4.2 %all-to-all-start.1 = ((f32[32,4,256]{2,1,0:T(4,128)}), f32[32,4,256]{2,1,0:T(4,128)S(1)}, u32[]{:S(2)}, u32[]{:S(2)}) async-start(f32[32,4,256]{2,1,0:T(4,128)} %get-tuple-element.52), calls=%async_computation.1 | async-start | bytes 262144 | tf_op jit(solution)/shard_map/all_to_all | solution.py:1039
  144.9 10.1 %shard_map.182 = f32[320,4096]{1,0:T(8,128)} custom-call(f32[320,384]{1,0:T(8,128)} %copy-done, f32[320,384]{1,0:T(8,128)} %copy-done.1, s32[6,4096]{1,0:T(8,128)} %nbr.8, f32[6,4096]{1,0:T(8,128)} %coef.9, bf16[320,160]{1,0:T(8,128)(2,1)} %get-tuple-element.54.vertical, f32[80,80]{1,0:T(8,128)} %mix.3, f32[4,4096]{1,0:T(4,128)} %get-tuple-element.55.flux, ...), custom_call_target="tpu_custom_call" | custom-call | flops 1000000 | bytes 10000 | tf_op jit(solution)/shard_map/pallas_call | solution.py:1041
  154.9 0.0 all-to-all-done.1.back
  154.9 0.6 copy-done.5
  155.6 5.2 %shard_map.183 = f32[32,128]{1,0:T(8,128)} custom-call(f32[32,4,256]{2,1,0:T(4,128)} %copy-done.5, s32[32,512]{1,0:T(8,128)} %bitcast.15, f32[4,4096]{1,0:T(4,128)} %surf.7), custom_call_target="tpu_custom_call" | custom-call | flops 1000000 | bytes 10000 | tf_op jit(solution)/shard_map/pallas_call | solution.py:1070
  (13 shorter events, 0.0 us)
Async XLA Ops:
  8.6 58.0 %collective-permute-start = (f32[312,1024]{1,0:T(8,128)}, f32[312,1024]{1,0:T(8,128)S(1)}, u32[]{:S(2)}, u32[]{:S(2)}) collective-permute-start(f32[312,1024]{1,0:T(8,128)} %get-tuple-element.35), channel_id=1, source_target_pairs={{0,1},{1,2},{2,3},{3,4},{4,5},{5,6},{6,7},{7,8},{8,9},{9,10},{10,1... | collective-permute-start | bytes 3833864 | tf_op jit(solution)/shard_map/ppermute | solution.py:920
  11.6 56.9 %collective-permute-start.1 = (f32[312,1024]{1,0:T(8,128)}, f32[312,1024]{1,0:T(8,128)S(1)}, u32[]{:S(2)}, u32[]{:S(2)}) collective-permute-start(f32[312,1024]{1,0:T(8,128)} %get-tuple-element.36), channel_id=1, source_target_pairs={{1,0},{2,1},{3,2},{4,3},{5,4},{6,5},{7,6},{8,7},{9,8},{10,9},{11,1... | collective-permute-start | bytes 3833864 | tf_op jit(solution)/shard_map/ppermute | solution.py:921
  66.6 1.8 %copy-start.2 = (f32[312,1024]{1,0:T(8,128)}, f32[312,1024]{1,0:T(8,128)S(1)}, u32[]{:S(2)}) copy-start(f32[312,1024]{1,0:T(8,128)S(1)} %collective-permute-done.before) | copy-start | bytes 3833860
  68.5 1.1 copy-start.3
  69.5 29.4 %copy-start.7 = (f32[320,384]{1,0:T(8,128)S(1)}, f32[320,384]{1,0:T(8,128)}, u32[]{:S(2)}) copy-start(f32[320,384]{1,0:T(8,128)} %get-tuple-element.48) | copy-start | bytes 1474564
  69.5 31.2 %copy-start.6 = (f32[320,384]{1,0:T(8,128)S(1)}, f32[320,384]{1,0:T(8,128)}, u32[]{:S(2)}) copy-start(f32[320,384]{1,0:T(8,128)} %get-tuple-element.51) | copy-start | bytes 1474564
  94.0 26.6 %all-to-all-start = ((f32[32,8,256]{2,1,0:T(8,128)}), f32[32,8,256]{2,1,0:T(8,128)S(1)}, u32[]{:S(2)}, u32[]{:S(2)}) async-start(f32[32,8,256]{2,1,0:T(8,128)} %shard_map.179), calls=%async_computation | async-start | bytes 524288 | tf_op jit(solution)/shard_map/all_to_all | solution.py:999
  98.9 25.2 %collective-permute-start.2 = (f32[320,384]{1,0:T(8,128)S(1)}, f32[320,384]{1,0:T(8,128)S(1)}, u32[]{:S(2)}, u32[]{:S(2)}) collective-permute-start(f32[320,384]{1,0:T(8,128)S(1)} %copy-done.7), channel_id=1, source_target_pairs={{0,1},{1,2},{2,3},{3,4},{4,5},{5,6},{6,7},{7,8},{8,9},{9,10},{10,1... | collective-permute-start | bytes 1474568 | tf_op jit(solution)/shard_map/ppermute | solution.py:971
  100.8 25.2 %collective-permute-start.3 = (f32[320,384]{1,0:T(8,128)S(1)}, f32[320,384]{1,0:T(8,128)S(1)}, u32[]{:S(2)}, u32[]{:S(2)}) collective-permute-start(f32[320,384]{1,0:T(8,128)S(1)} %copy-done.6), channel_id=1, source_target_pairs={{1,0},{2,1},{3,2},{4,3},{5,4},{6,5},{7,6},{8,7},{9,8},{10,9},{11,1... | collective-permute-start | bytes 1474568 | tf_op jit(solution)/shard_map/ppermute | solution.py:972
  120.7 5.3 %copy-start.4 = (f32[32,8,256]{2,1,0:T(8,128)}, f32[32,8,256]{2,1,0:T(8,128)S(1)}, u32[]{:S(2)}) copy-start(f32[32,8,256]{2,1,0:T(8,128)S(1)} %all-to-all-done.recv) | copy-start | bytes 786436
  124.1 1.9 %copy-start = (f32[320,384]{1,0:T(8,128)}, f32[320,384]{1,0:T(8,128)S(1)}, u32[]{:S(2)}) copy-start(f32[320,384]{1,0:T(8,128)S(1)} %collective-permute-done.2.before_in.before) | copy-start | bytes 1474564
  126.0 0.8 copy-start.1
  140.6 14.3 %all-to-all-start.1 = ((f32[32,4,256]{2,1,0:T(4,128)}), f32[32,4,256]{2,1,0:T(4,128)S(1)}, u32[]{:S(2)}, u32[]{:S(2)}) async-start(f32[32,4,256]{2,1,0:T(4,128)} %get-tuple-element.52), calls=%async_computation.1 | async-start | bytes 262144 | tf_op jit(solution)/shard_map/all_to_all | solution.py:1039
  154.9 0.7 copy-start.5

commit v9 on v8

--- a/solution.py
+++ b/solution.py
@@ -162,39 +162,49 @@
     return total
 
 
+def pack_kernel(nbr, coef, bulk, surf, atm, sea, wide_first, wide_last, sea_first, sea_last, *refs):
+    held, lists, sems = refs[:4], refs[4], refs[5]
+    rows, columns = atm.shape
+    cells = sea.shape[1]
+    sources = (
+        atm.at[:, :WIDE],
+        atm.at[:, columns - WIDE :],
+        sea.at[:, :HO],
+        sea.at[:, cells - HO :],
+    )
+    targets = (wide_first.at[:rows], wide_last.at[:rows], sea_first, sea_last)
+    arriving = [pltpu.make_async_copy(x, held[i], sems.at[i]) for i, x in enumerate(sources)]
+    leaving = [pltpu.make_async_copy(held[i], x, sems.at[4 + i]) for i, x in enumerate(targets)]
+    for copy in arriving:
+        copy.start()
+    need = WIDE - BLK
+    for i, first in enumerate((0, columns - need)):
+        at = slice(first, first + need)
+        lists[i, 0:6, :need] = nbr[:, at].astype(F32)
+        lists[i, 6:12, :need] = coef[:, at]
+        lists[i, 12:16, :need] = bulk[:, at]
+        lists[i, 12:16, need:] = jnp.zeros((4, BLK), F32)
+        for j in range(ASTEPS - 1):
+            lists[i, 4 * j : 4 * j + 4, need:] = surf[:, first + j * BLK : first + (j + 1) * BLK]
+    for i, target in enumerate((wide_first, wide_last)):
+        copy = pltpu.make_async_copy(lists.at[i], target.at[rows:], sems.at[8 + i])
+        copy.start()
+        leaving.append(copy)
+    for here, there in zip(arriving, leaving[:4]):
+        here.wait()
+        there.start()
+    for copy in leaving:
+        copy.wait()
+
+
 def prepare_kernel(fields):
     def body(
-        mix, omix, atm, nbr, coef, bulk, surf, spread, code, sea_spread, sea,
-        y, yo, gains, lift, vertical, sea_vertical, wide_first, wide_last, sea_first, sea_last,
-        top, lists, ends, sems,
+        mix, omix, atm, spread, code, sea_spread, sea, y, yo, gains, lift, vertical, sea_vertical, top, sem
     ):
         la = mix.shape[0]
-        rows, columns = atm.shape
-        cells = sea.shape[1]
-        copy = pltpu.make_async_copy(sea.at[: omix.shape[0], :], top, sems.at[0])
+        columns = atm.shape[1]
+        copy = pltpu.make_async_copy(sea.at[: omix.shape[0], :], top, sem)
         copy.start()
-        arriving = [
-            pltpu.make_async_copy(sea.at[:, :HO], ends.at[0], sems.at[1]),
-            pltpu.make_async_copy(sea.at[:, cells - HO :], ends.at[1], sems.at[2]),
-        ]
-        leaving = [
-            pltpu.make_async_copy(atm.at[:, :WIDE], wide_first.at[:rows], sems.at[3]),
-            pltpu.make_async_copy(atm.at[:, columns - WIDE :], wide_last.at[:rows], sems.at[4]),
-            pltpu.make_async_copy(lists.at[0], wide_first.at[rows:], sems.at[5]),
-            pltpu.make_async_copy(lists.at[1], wide_last.at[rows:], sems.at[6]),
-            pltpu.make_async_copy(ends.at[0], sea_first, sems.at[7]),
-            pltpu.make_async_copy(ends.at[1], sea_last, sems.at[8]),
-        ]
-        for i, at in enumerate((slice(0, WIDE), slice(columns - WIDE, columns))):
-            lists[i, 0:6] = nbr[:, at].astype(F32)
-            lists[i, 6:12] = coef[:, at]
-            lists[i, 12:16] = bulk[:, at]
-            lists[i, 16:20] = surf[:, at]
-            lists[i, 20:24] = jnp.zeros((4, WIDE), F32)
-        for here in arriving:
-            here.start()
-        for out in leaving[:4]:
-            out.start()
         eye = iota((la, la), 0) == iota((la, la), 1)
         step = mix[...] + jnp.where(eye, 1.0, 0.0)
 
@@ -254,11 +264,6 @@
                         x * weights[k - 1], axis=0, keepdims=True
                     )
             yo[:, at] = jnp.sum(top[:, at] * sea_weight, axis=0, keepdims=True)
-        for here, out in zip(arriving, leaving[4:]):
-            here.wait()
-            out.start()
-        for out in leaving:
-            out.wait()
 
     return body
 
@@ -406,7 +411,7 @@
     ]
     for copy in arriving:
         copy.start()
-    rows[...] = jnp.concatenate(halves(recv[...].reshape(table, lanes)), axis=1)
+    rows[...] = stacked(recv[...].reshape(table, lanes))
     levels = omix.shape[0]
     eye = iota((levels, levels), 0) == iota((levels, levels), 1)
     corner = omix[0:1, 0:1] + 1.0
@@ -462,11 +467,11 @@
             ids = slot[r : r + 1, at]
             hot = one_hot(ids & (lanes - 1), lanes)
             hots[j, :, r * BLK : (r + 1) * BLK] = hot
-            return mm(rows[...], jnp.concatenate([hot, hot], axis=0))
+            return mm(rows[...], hot)
 
         def finish(r, got):
             ids = slot[r : r + 1, at]
-            got = jnp.where(high_of_row == ids // lanes, got, 0.0)
+            got = jnp.where(high_of_row == ids // lanes, got[:table] + got[table:], 0.0)
             parts.append(weight[r : r + 1, at] * fold_rows(got, 2 * fields))
 
         last = begin(0)
@@ -576,12 +581,15 @@
         at = slice(local * BLK, (local + 1) * BLK)
         if ref is None:
             return bulk[:, at], surf[:, at]
-        return ref[rows + 12 : rows + 16, at], ref[rows + 16 : rows + 20, at]
+        j = local - 1 if e < ASTEPS else local
+        at = slice(j * BLK, (j + 1) * BLK)
+        return ref[rows + 12 : rows + 16, at], ref[rows + 4 * j : rows + 4 * j + 4, WIDE - BLK :]
 
     def build(e):
         ref, local = place(e)
         origin = local * BLK + (columns - WIDE if e < ASTEPS else 0)
-        at = slice(local * BLK, (local + 1) * BLK)
+        j = local - 1 if e < ASTEPS else local
+        at = slice(j * BLK, (j + 1) * BLK)
         ids = ref[rows : rows + 6, at].astype(jnp.int32) - origin
         k = e - 1 if e < ASTEPS else e - (total - 1) + 2 * count
         yield from band_build(ids, ref[rows + 6 : rows + 12, at], w, k)
@@ -657,47 +665,39 @@
     out.wait()
 
 
-def finish_kernel(q_ends, q_mid, vertical, ends_in, mid_in, out, ends, mid, staged, sems, osems):
-    rows = ends.shape[1] // 2
-    levels = rows // 2
-    blocks = staged.shape[0]
-    arriving = [
-        pltpu.make_async_copy(mid_in, mid, sems.at[0]),
-        pltpu.make_async_copy(ends_in, ends, sems.at[1]),
-    ]
-    for copy in arriving:
-        copy.start()
-
-    def leaving(b):
-        at = slice(b * BLK, (b + 1) * BLK)
-        return pltpu.make_async_copy(staged.at[b], out.at[:, at], osems.at[b])
-
-    def one(b, p):
-        ref, i = block_place(b, blocks, ends, mid)
-        share, _ = block_place(b, blocks, q_ends, q_mid)
-
-        def begin():
-            qh, ql = halves(share[i])
-            high = jnp.concatenate([ref[i, p * levels : (p + 1) * levels], qh], axis=0)
-            low = jnp.concatenate([ref[i, rows + p * levels : rows + (p + 1) * levels], ql], axis=0)
-            return mm(vertical[p], high), mm(vertical[p, :levels], low)
-
-        def finish(value):
-            staged[b, p * levels : (p + 1) * levels] = value
-
-        return begin, finish
-
-    middle = list(range(ASTEPS, blocks - ASTEPS))
-    outer = list(range(ASTEPS)) + list(range(blocks - ASTEPS, blocks))
-    for copy, group in zip(arriving, (middle, outer)):
-        copy.wait()
-        for start in range(0, len(group), 4):
-            some = group[start : start + 4]
-            in_turn([one(b, p) for b in some for p in range(2)])
-            for b in some:
-                leaving(b).start()
-    for b in range(blocks):
-        leaving(b).wait()
+def mix_kernel(blocks):
+    def body(q, vertical, x_in, *refs):
+        out, x, staged, sem, osems = refs[-5:]
+        rows = x.shape[1] // 2
+        levels = rows // 2
+        arriving = pltpu.make_async_copy(x_in, x, sem)
+        arriving.start()
+        arriving.wait()
+
+        def leaving(i):
+            at = slice(blocks[i] * BLK, (blocks[i] + 1) * BLK)
+            return pltpu.make_async_copy(staged.at[i], out.at[:, at], osems.at[i])
+
+        def one(i, p):
+            def begin():
+                qh, ql = halves(q[i])
+                high = jnp.concatenate([x[i, p * levels : (p + 1) * levels], qh], axis=0)
+                low = jnp.concatenate([x[i, rows + p * levels : rows + (p + 1) * levels], ql], axis=0)
+                return mm(vertical[p], high), mm(vertical[p, :levels], low)
+
+            def finish(value):
+                staged[i, p * levels : (p + 1) * levels] = value
+
+            return begin, finish
+
+        for start in range(0, len(blocks), 4):
+            in_turn([one(i, p) for i in range(start, start + 4) for p in range(2)])
+            for i in range(start, start + 4):
+                leaving(i).start()
+        for i in range(len(blocks)):
+            leaving(i).wait()
+
+    return body
 
 
 def sea_build(nbr, coef, b, w):
@@ -746,32 +746,31 @@
     lax.fori_loop(0, count, done, 0)
 
 
-def sea_outer_kernel(
-    before, after, nbr, coef, vertical, mix, flux, ocean, laid_in, out, ends, x2, wa, wb, ma, mb, laid, staged, sems, osems
-):
-    fields = flux.shape[0]
-    rows, columns = ocean.shape
-    levels = rows // fields
+def sea_outer_kernel(nbr, coef, ocean, before_in, after_in, laid_out, ends, halos, x2, wa, wb, ma, mb, laid, sems):
+    columns = ocean.shape[1]
     blocks = columns // BLK
     around = 1 + 2 * HO // BLK
     first = -(-HO // BLK)
-    count = blocks - 2 * first
     width = ends.shape[2]
     arriving = [
         pltpu.make_async_copy(ocean.at[:, :width], ends.at[0], sems.at[0]),
         pltpu.make_async_copy(ocean.at[:, columns - width :], ends.at[1], sems.at[1]),
-        pltpu.make_async_copy(laid_in, laid.at[first : first + count], sems.at[2]),
+        pltpu.make_async_copy(before_in, halos.at[0], sems.at[2]),
+        pltpu.make_async_copy(after_in, halos.at[1], sems.at[3]),
     ]
     for copy in arriving:
         copy.start()
-    eye = iota((levels, levels), 0) == iota((levels, levels), 1)
-    top = jnp.broadcast_to((mix[...] + jnp.where(eye, 1.0, 0.0))[:, 0:1], (levels, BLK))
     outer = list(range(first)) + list(range(blocks - first, blocks))
     bands, sums = (wa, wb), (ma, mb)
     interleave(sea_build(nbr, coef, outer[0], wa))
-    arriving[0].wait()
-    arriving[1].wait()
-    spans = ((before, -HO, HO), (ends.at[0], 0, width), (ends.at[1], columns - width, width), (after, columns, HO))
+    for copy in arriving:
+        copy.wait()
+    spans = (
+        (halos.at[0], -HO, HO),
+        (ends.at[0], 0, width),
+        (ends.at[1], columns - width, width),
+        (halos.at[1], columns, HO),
+    )
     held = list(range(first + around - 1)) + list(range(blocks - first, blocks + around - 1))
     for i, e in enumerate(held):
         start = e * BLK - HO
@@ -790,8 +789,29 @@
         if k + 1 < len(outer):
             works.insert(0, sea_build(nbr, coef, outer[k + 1], bands[(k + 1) % 2]))
         interleave(*works)
-        laid[b] = stacked(sums[k % 2][...])
-    arriving[2].wait()
+        laid[k] = stacked(sums[k % 2][...])
+    out = pltpu.make_async_copy(laid, laid_out, sems.at[4])
+    out.start()
+    out.wait()
+
+
+def sea_mix_kernel(vertical, mix, flux, inner_in, outer_in, out, laid, staged, sems, osems):
+    fields = flux.shape[0]
+    rows = out.shape[0]
+    levels = rows // fields
+    blocks = staged.shape[0]
+    side = outer_in.shape[0] // 2
+    copies = [
+        pltpu.make_async_copy(outer_in.at[:side], laid.at[:side], sems.at[0]),
+        pltpu.make_async_copy(inner_in, laid.at[side : blocks - side], sems.at[1]),
+        pltpu.make_async_copy(outer_in.at[side:], laid.at[blocks - side :], sems.at[2]),
+    ]
+    for copy in copies:
+        copy.start()
+    eye = iota((levels, levels), 0) == iota((levels, levels), 1)
+    top = jnp.broadcast_to((mix[...] + jnp.where(eye, 1.0, 0.0))[:, 0:1], (levels, BLK))
+    for copy in copies:
+        copy.wait()
     pair = 2 * levels
 
     def leaving(b):
@@ -881,8 +901,21 @@
     spread = ((c_of[0] % la == np.arange(la)[:, None]) & (c_of[0] < 2 * la)).astype(np.float32)
     sea_spread = (np.arange(2 * lo)[None, :] % lo == np.arange(lo)[:, None]).astype(np.float32)
 
-    wide_rows = rows + 24
-    y, yo, gains, lift, vertical, sea_vertical, wide_first, wide_last, sea_first, sea_last = call(
+    wide_rows = rows + 16
+    sea_rows = fields * lo
+    halo_shapes = (shape((rows, WIDE)),) * 2 + (shape((sea_rows, HO)),) * 2
+    wide_first, wide_last, sea_first, sea_last = call(
+        pack_kernel,
+        (shape((wide_rows, WIDE)),) * 2 + halo_shapes[2:],
+        in_specs=[vmem] * 4 + [anywhere] * 2,
+        out_specs=(anywhere,) * 4,
+        scratch=[pltpu.VMEM(h.shape, F32) for h in halo_shapes]
+        + [pltpu.VMEM((2, 16, WIDE), F32), pltpu.SemaphoreType.DMA((10,))],
+    )(atm_nbr, atm_nbr_coef, bulk_coef, atm_surface, atm, ocean)
+    wide_before = lax.ppermute(wide_last, AXES, up)
+    wide_after = lax.ppermute(wide_first, AXES, down)
+
+    y, yo, gains, lift, vertical, sea_vertical = call(
         prepare_kernel(fields),
         (
             shape((states, columns)),
@@ -891,34 +924,18 @@
             shape((ASTEPS - 1, la, 128)),
             shape((half, 4 * la, 2 * la + states), BF),
             shape((4 * lo, 2 * lo), BF),
-            shape((wide_rows, WIDE)),
-            shape((wide_rows, WIDE)),
-            shape((fields * lo, HO)),
-            shape((fields * lo, HO)),
         ),
-        in_specs=[vmem] * 10 + [anywhere],
-        out_specs=(vmem,) * 6 + (anywhere,) * 4,
-        scratch=[
-            pltpu.VMEM((lo, cells), F32),
-            pltpu.VMEM((2, 24, WIDE), F32),
-            pltpu.VMEM((2, fields * lo, HO), F32),
-            pltpu.SemaphoreType.DMA((9,)),
-        ],
+        in_specs=[vmem] * 6 + [anywhere],
+        scratch=[pltpu.VMEM((lo, cells), F32), pltpu.SemaphoreType.DMA(())],
     )(
-        atm_mix,
+        after_all(atm_mix, wide_first),
         ocean_mix,
         atm,
-        atm_nbr,
-        atm_nbr_coef,
-        bulk_coef,
-        atm_surface,
         jnp.asarray(spread),
         jnp.asarray(code),
         jnp.asarray(sea_spread),
         ocean,
     )
-    wide_before = lax.ppermute(wide_last, AXES, up)
-    wide_after = lax.ppermute(wide_first, AXES, down)
 
     ends = 2 * ASTEPS
     q_mid, kept, mid, band = call(
@@ -947,7 +964,6 @@
     outer = -(-HO // BLK)
     around = 1 + 2 * HO // BLK
     sea_window = BLK + 2 * HO
-    sea_rows = fields * lo
     inner = sea_blocks - 2 * outer
     sea_inner = call(
         sea_inner_kernel,
@@ -965,9 +981,26 @@
         ],
     )(ocean, after_all(ocean_nbr, q_mid), ocean_nbr_coef)
 
-    sea_first, sea_last, wide_before, wide_after = lax.optimization_barrier(
-        (sea_first, sea_last, wide_before, wide_after, sea_inner)
-    )[:4]
+    middle = list(range(ASTEPS, blocks - ASTEPS))
+    rest = list(range(ASTEPS)) + list(range(blocks - ASTEPS, blocks))
+
+    def mixed(which, *args, aliases=None):
+        return call(
+            mix_kernel(which),
+            shape((rows, columns)),
+            in_specs=[vmem] * 2 + [anywhere] * (len(args) - 2),
+            out_specs=anywhere,
+            scratch=[
+                pltpu.VMEM((len(which), 2 * rows, BLK), BF),
+                pltpu.VMEM((len(which), rows, BLK), F32),
+                pltpu.SemaphoreType.DMA(()),
+                pltpu.SemaphoreType.DMA((len(which),)),
+            ],
+            aliases=aliases,
+        )(*args)
+
+    atm_half = mixed(middle, after_all(q_mid, sea_inner), vertical, mid)
+    sea_first, sea_last = lax.optimization_barrier((sea_first, sea_last, q_mid))[:2]
     sea_before = lax.ppermute(sea_last, AXES, up)
     sea_after = lax.ppermute(sea_first, AXES, down)
 
@@ -988,8 +1021,9 @@
             pltpu.VMEM((ends, 2 * rows, BLK), BF),
             pltpu.SemaphoreType.DMA((6 + 2 * ASTEPS,)),
         ],
-    )(y, bulk_coef, atm_surface, gains, lift, wide_before, wide_after, atm, kept, band)
-
+    )(after_all(y, atm_half), bulk_coef, atm_surface, gains, lift, wide_before, wide_after, atm, kept, band)
+
+    q_ends, sea_before, sea_after = lax.optimization_barrier((q_ends, sea_before, sea_after))
     outgoing = call(
         send_kernel,
         shape((peers, parts * fields, lanes)),
@@ -998,26 +1032,32 @@
     )(q_ends, q_mid, picked)
     received = lax.all_to_all(outgoing, AXES, split_axis=0, concat_axis=0, tiled=True)
 
-    atm_final = call(
-        finish_kernel,
-        shape((rows, columns)),
-        in_specs=[vmem] * 3 + [anywhere] * 2,
+    atm_final = mixed(rest, after_all(q_ends, outgoing), vertical, tips, atm_half, aliases={3: 0})
+
+    sea_outer = call(
+        sea_outer_kernel,
+        shape((2 * outer, 2 * sea_rows, BLK), BF),
+        in_specs=[vmem] * 2 + [anywhere] * 3,
         out_specs=anywhere,
         scratch=[
-            pltpu.VMEM((ends, 2 * rows, BLK), BF),
-            pltpu.VMEM((blocks - ends, 2 * rows, BLK), BF),
-            pltpu.VMEM((blocks, rows, BLK), F32),
-            pltpu.SemaphoreType.DMA((2,)),
-            pltpu.SemaphoreType.DMA((blocks,)),
+            pltpu.VMEM((2, sea_rows, (outer + around - 1) * BLK - HO), F32),
+            pltpu.VMEM((2, sea_rows, HO), F32),
+            pltpu.VMEM((2 * (outer + around - 1), 2 * sea_rows, BLK), BF),
+            pltpu.VMEM((2, sea_window, BLK), BF),
+            pltpu.VMEM((2, sea_window, BLK), BF),
+            pltpu.VMEM((sea_rows, BLK), F32),
+            pltpu.VMEM((sea_rows, BLK), F32),
+            pltpu.VMEM((2 * outer, 2 * sea_rows, BLK), BF),
+            pltpu.SemaphoreType.DMA((5,)),
         ],
-    )(after_all(q_ends, outgoing), q_mid, vertical, tips, mid)
+    )(after_all(ocean_nbr, atm_final), ocean_nbr_coef, ocean, sea_before, sea_after)
 
     flux, back = call(
         exchange_kernel,
         (shape((fields, cells)), shape((peers, 2 * parts, lanes))),
         in_specs=[vmem] * 7 + [anywhere] * 2,
         scratch=[
-            pltpu.VMEM((peers * parts * fields, 2 * lanes), BF),
+            pltpu.VMEM((2 * peers * parts * fields, lanes), BF),
             pltpu.VMEM((cells // 128 + 2 * HO // 128, 8, 128), F32),
             pltpu.VMEM((cells // BLK, lanes, remap_slot.shape[0] * BLK), BF),
             pltpu.VMEM((1, cells), F32),
@@ -1026,7 +1066,7 @@
             pltpu.SemaphoreType.DMA((2,)),
         ],
     )(
-        after_all(received, atm_final),
+        after_all(received, sea_outer),
         remap_slot,
         remap_weight,
         yo,
@@ -1039,33 +1079,17 @@
     returned = lax.all_to_all(back, AXES, split_axis=0, concat_axis=0, tiled=True)
 
     ocean_final = call(
-        sea_outer_kernel,
+        sea_mix_kernel,
         shape((sea_rows, cells)),
-        in_specs=[vmem] * 7 + [anywhere] * 2,
+        in_specs=[vmem] * 3 + [anywhere] * 2,
         out_specs=anywhere,
         scratch=[
-            pltpu.VMEM((2, sea_rows, (outer + around - 1) * BLK - HO), F32),
-            pltpu.VMEM((2 * (outer + around - 1), 2 * sea_rows, BLK), BF),
-            pltpu.VMEM((2, sea_window, BLK), BF),
-            pltpu.VMEM((2, sea_window, BLK), BF),
-            pltpu.VMEM((sea_rows, BLK), F32),
-            pltpu.VMEM((sea_rows, BLK), F32),
             pltpu.VMEM((sea_blocks, 2 * sea_rows, BLK), BF),
             pltpu.VMEM((sea_blocks, sea_rows, BLK), F32),
             pltpu.SemaphoreType.DMA((3,)),
             pltpu.SemaphoreType.DMA((sea_blocks,)),
         ],
-    )(
-        after_all(sea_before, back),
-        sea_after,
-        ocean_nbr,
-        ocean_nbr_coef,
-        sea_vertical,
-        ocean_mix,
-        flux,
-        ocean,
-        sea_inner,
-    )
+    )(sea_vertical, ocean_mix, after_all(flux, back), sea_inner, sea_outer)
 
     surface_temp = call(
         settle_kernel,

time: 161 us -> 152 us (0.944)
  waiting for transfers between devices: 27.2 us -> 4.68 us
  Pallas kernels: 109 us -> 120 us
  starting transfers between devices: 21.2 us -> 23.7 us
    pallas_call x2 -> x5, Pallas kernels: 16.1 us -> 28.3 us  [the longest x2 9.7 us: mixed(): call(mix_kernel(which), shape((rows, columns)), in_specs=[vmem] * 2 + [an...]
    all_to_all x1, waiting for transfers between devices: 10.1 us -> 0.01 us  [per_device(): lax.all_to_all(outgoing, AXES, split_axis=0, concat_axis=0, tiled=True)]
    ppermute x1, waiting for transfers between devices: 9.95 us -> 4.04 us  [per_device(): wide_before = lax.ppermute(wide_last, AXES, up)]
    ppermute x1, waiting for transfers between devices: 3.42 us -> 0.01 us  [per_device(): sea_before = lax.ppermute(sea_last, AXES, up)]
    pallas_call x1, Pallas kernels: 7.98 us -> 5.82 us  [per_device(): call(prepare_kernel(fields), (shape((states, columns)), shape((1, columns...]
    ppermute x1, waiting for transfers between devices: 1.86 us -> 0.01 us  [per_device(): sea_after = lax.ppermute(sea_first, AXES, down)]
    ppermute x1, waiting for transfers between devices: 1.84 us -> 0.01 us  [per_device(): wide_after = lax.ppermute(wide_first, AXES, down)]
  transfers between devices with their start and end apart: 6 -> 6, of which waited for: 5 -> 2; matrix products, arithmetic and copies ran while one was open for 0% -> 0% of each run, Pallas kernels for 36% -> 60%
where the time goes in v9:
time: 152 us
  Pallas kernels  120 us (79%)
  starting transfers between devices  23.7 us (16%)
  waiting for transfers between devices  4.68 us (3%)
  local copies, waits for them, and re-layouts  2.86 us (2%)
    pallas_call x1, Pallas kernels, per_device(): call(interior_kernel, (shape((blocks - ends, states, BLK)), shape((4 * (A...  27.3 us
    pallas_call x1, Pallas kernels, per_device(): call(edge_kernel, (shape((ends, states, BLK)), shape((ends, 2 * rows, BLK...  20 us
    pallas_call x1, Pallas kernels, per_device(): call(sea_inner_kernel, shape((inner, 2 * sea_rows, BLK), BF), in_specs=[v...  14.1 us
    pallas_call x1, Pallas kernels, per_device(): call(exchange_kernel, (shape((fields, cells)), shape((peers, 2 * parts, l...  13.9 us
    pallas_call x2, Pallas kernels, mixed(): call(mix_kernel(which), shape((rows, columns)), in_specs=[vmem] * 2 + [an...  9.7 us
    pallas_call x1, Pallas kernels, per_device(): call(sea_mix_kernel, shape((sea_rows, cells)), in_specs=[vmem] * 3 + [any...  7.27 us
    pallas_call x1, Pallas kernels, per_device(): call(sea_outer_kernel, shape((2 * outer, 2 * sea_rows, BLK), BF), in_spec...  7.21 us
    all_to_all x1, starting transfers between devices, per_device(): lax.all_to_all(back, AXES, split_axis=0, concat_axis=0, tiled=True)  5.84 us
  transfers between devices with their start and end apart: 6, of which 2 were waited for; matrix products, arithmetic and copies ran while one was open for 0% of the time, Pallas kernels for 60%

profile of v9, /device:TPU:0, one launch (start us, length us, event | category | flops | bytes accessed | tf_op | source)
XLA Modules:
  0.0 151.6 jit_solution(7327903094533616154)
XLA Ops:
  0.6 4.1 %shard_map.175 = (f32[304,1024]{1,0:T(8,128)}, f32[304,1024]{1,0:T(8,128)}, f32[320,384]{1,0:T(8,128)}, f32[320,384]{1,0:T(8,128)}) custom-call(s32[6,4096]{1,0:T(8,128)} %nbr.4, f32[6,4096]{1,0:T(8,128)} %coef.6, f32[4,4096]{1,0:T(4,128)} %bulk.5, f32[4,4096]{1,0:T(4,128)} %surf.7, f32[288,4096]{1,0:T(8,128)} %bitcast.10, f32[320,4096]{1,0:T(8,128)} %bitcast.6), custom_call_target="tpu_custom_call" | custom-call | flops 1000000 | bytes 10000 | tf_op jit(solution)/shard_map/pallas_call | solution.py:907
  4.8 3.0 %collective-permute-start = (f32[304,1024]{1,0:T(8,128)}, f32[304,1024]{1,0:T(8,128)S(1)}, u32[]{:S(2)}, u32[]{:S(2)}) collective-permute-start(f32[304,1024]{1,0:T(8,128)} %get-tuple-element.46), channel_id=1, source_target_pairs={{0,1},{1,2},{2,3},{3,4},{4,5},{5,6},{6,7},{7,8},{8,9},{9,10},{10,1... | collective-permute-start | bytes 3735560 | tf_op jit(solution)/shard_map/ppermute | solution.py:915
  7.8 3.5 %collective-permute-start.1 = (f32[304,1024]{1,0:T(8,128)}, f32[304,1024]{1,0:T(8,128)S(1)}, u32[]{:S(2)}, u32[]{:S(2)}) collective-permute-start(f32[304,1024]{1,0:T(8,128)} %get-tuple-element.35), channel_id=1, source_target_pairs={{1,0},{2,1},{3,2},{4,3},{5,4},{6,5},{7,6},{8,7},{9,8},{10,9},{11,1... | collective-permute-start | bytes 3735560 | tf_op jit(solution)/shard_map/ppermute | solution.py:916
  11.3 5.8 %shard_map.176 = (f32[16,4096]{1,0:T(8,128)}, f32[1,4096]{1,0:T(1,128)}, f32[16,128]{1,0:T(8,128)}, f32[3,72,128]{2,1,0:T(8,128)}, bf16[2,288,160]{2,1,0:T(8,128)(2,1)}, /*index=5*/bf16[320,160]{1,0:T(8,128)(2,1)}) custom-call(f32[72,72]{1,0:T(8,128)} %mix.1, f32[80,80]{1,0:T(8,128)} %mix.2, f32[288,4096]{1,0:T(8,128)} %bitcast.11, ...), custom_call_target="tpu_custom_call" | custom-call | flops 1000000 | bytes 10000 | tf_op jit(solution)/shard_map/pallas_call | solution.py:918
  17.1 27.3 %shard_map.177 = (f32[8,16,256]{2,1,0:T(8,128)}, bf16[12,608,256]{2,1,0:T(8,128)(2,1)}, bf16[8,576,256]{2,1,0:T(8,128)(2,1)}, bf16[8,2,768,256]{3,2,1,0:T(8,128)(2,1)}) custom-call(f32[288,4096]{1,0:T(8,128)} %bitcast.12, f32[16,4096]{1,0:T(8,128)} %get-tuple-element.44.y, s32[6,4096]{1,0:T(8,128)} %nbr.4, f32[6,4096]{1,0:T(8,128)} %coef.6, f32[4,4096]{1,0:T(4,128)} %bulk.5, ...), custom_call_target="tpu_custom_call" | custom-call | flops 1000000 | bytes 10000 | tf_op jit(solution)/shard_map/pallas_call | solution.py:941
  44.5 0.2 collective-permute-start.2
  44.7 5.3 %collective-permute-start.3 = (f32[320,384]{1,0:T(8,128)S(1)}, f32[320,384]{1,0:T(8,128)S(1)}, u32[]{:S(2)}, u32[]{:S(2)}) collective-permute-start(f32[320,384]{1,0:T(8,128)S(1)} %copy-done.6), channel_id=1, source_target_pairs={{1,0},{2,1},{3,2},{4,3},{5,4},{6,5},{7,6},{8,7},{9,8},{10,9},{11,1... | collective-permute-start | bytes 1474568 | tf_op jit(solution)/shard_map/ppermute | solution.py:1005
  50.1 14.1 %shard_map.178.inner_in = bf16[12,640,256]{2,1,0:T(8,128)(2,1)} custom-call(f32[320,4096]{1,0:T(8,128)} %bitcast.8, s32[6,4096]{1,0:T(8,128)} %nbr.7, f32[6,4096]{1,0:T(8,128)} %coef.9), custom_call_target="tpu_custom_call" | custom-call | flops 1000000 | bytes 10000 | tf_op jit(solution)/shard_map/pallas_call | solution.py:968
  64.2 4.8 %shard_map.179.refs_0_ = f32[288,4096]{1,0:T(8,128)} custom-call(f32[8,16,256]{2,1,0:T(8,128)} %get-tuple-element.41.q.q_mid, bf16[2,288,160]{2,1,0:T(8,128)(2,1)} %get-tuple-element.42.vertical, bf16[8,576,256]{2,1,0:T(8,128)(2,1)} %get-tuple-element.43.x_in), custom_call_target="tpu_custom_call" | custom-call | flops 1000000 | bytes 10000 | tf_op jit(solution)/shard_map/pallas_call | solution.py:988
  69.0 4.0 %collective-permute-done.before = f32[304,1024]{1,0:T(8,128)S(1)} collective-permute-done((f32[304,1024]{1,0:T(8,128)}, f32[304,1024]{1,0:T(8,128)S(1)}, u32[]{:S(2)}, u32[]{:S(2)}) %collective-permute-start) | collective-permute-done | bytes 1245216 | tf_op jit(solution)/shard_map/ppermute | solution.py:915
  73.1 1.0 copy-done.2
  74.1 0.4 copy-done.3
  74.6 20.0 %shard_map.180 = (f32[8,16,256]{2,1,0:T(8,128)}, bf16[8,576,256]{2,1,0:T(8,128)(2,1)}) custom-call(f32[16,4096]{1,0:T(8,128)} %get-tuple-element.44.y, f32[4,4096]{1,0:T(4,128)} %bulk.5, f32[4,4096]{1,0:T(4,128)} %surf.7, f32[16,128]{1,0:T(8,128)} %get-tuple-element.38.gains, f32[3,72,128]{2,1,0:T(8,128)} %get-tuple-element.45.lift, f32[304,1024]{1,0:T(8,128)} %copy-done.2, ...), custom_call_target="tpu_custom_call" | custom-call | flops 1000000 | bytes 10000 | tf_op jit(solution)/shard_map/pallas_call | solution.py:1007
  94.6 4.8 %shard_map.181 = f32[32,8,256]{2,1,0:T(8,128)} custom-call(f32[8,16,256]{2,1,0:T(8,128)} %get-tuple-element.55.q_ends.q, f32[8,16,256]{2,1,0:T(8,128)} %get-tuple-element.41.q.q_mid, s32[32,512]{1,0:T(8,128)} %bitcast.16), custom_call_target="tpu_custom_call" | custom-call | flops 1000000 | bytes 10000 | tf_op jit(solution)/shard_map/pallas_call | solution.py:1027
  99.5 5.8 %all-to-all-start = ((f32[32,8,256]{2,1,0:T(8,128)}), f32[32,8,256]{2,1,0:T(8,128)S(1)}, u32[]{:S(2)}, u32[]{:S(2)}) async-start(f32[32,8,256]{2,1,0:T(8,128)} %shard_map.181), calls=%async_computation | async-start | bytes 524288 | tf_op jit(solution)/shard_map/all_to_all | solution.py:1033
  105.2 4.9 %shard_map.182 = f32[288,4096]{1,0:T(8,128)} custom-call(f32[8,16,256]{2,1,0:T(8,128)} %get-tuple-element.55.q_ends.q, bf16[2,288,160]{2,1,0:T(8,128)(2,1)} %get-tuple-element.42.vertical, bf16[8,576,256]{2,1,0:T(8,128)(2,1)} %get-tuple-element.56.x_in, f32[288,4096]{1,0:T(8,128)} %shard_map.179.refs_0_), custom_call_target="tpu_custom_call", output_to_operand_aliasing={{}: (3, {})} | custom-call | flops 1000000 | bytes 10000 | tf_op jit(solution)/shard_map/pallas_call | solution.py:988
  110.1 7.2 %shard_map.183.outer_in = bf16[4,640,256]{2,1,0:T(8,128)(2,1)} custom-call(s32[6,4096]{1,0:T(8,128)} %nbr.7, f32[6,4096]{1,0:T(8,128)} %coef.9, f32[320,4096]{1,0:T(8,128)} %bitcast.9, f32[320,384]{1,0:T(8,128)} %copy-done, f32[320,384]{1,0:T(8,128)} %copy-done.1), custom_call_target="tpu_custom_call" | custom-call | flops 1000000 | bytes 10000 | tf_op jit(solution)/shard_map/pallas_call | solution.py:1037
  117.4 0.7 copy-done.4
  118.1 13.9 %shard_map.184 = (f32[4,4096]{1,0:T(4,128)}, f32[32,4,256]{2,1,0:T(4,128)}) custom-call(f32[32,8,256]{2,1,0:T(8,128)} %copy-done.4, s32[4,4096]{1,0:T(4,128)} %slot.1, f32[4,4096]{1,0:T(4,128)} %weight.1, f32[1,4096]{1,0:T(1,128)} %get-tuple-element.62.yo, s32[6,4096]{1,0:T(8,128)} %nbr.7, f32[6,4096]{1,0:T(8,128)} %coef.9, f32[80,80]{1,0:T(8,128)} %mix.2, ...), custom_call_target="tpu_custom_call" | custom-call | flops 1000000 | bytes 10000 | tf_op jit(solution)/shard_map/pallas_call | solution.py:1055
  132.0 5.8 %all-to-all-start.1 = ((f32[32,4,256]{2,1,0:T(4,128)}), f32[32,4,256]{2,1,0:T(4,128)S(1)}, u32[]{:S(2)}, u32[]{:S(2)}) async-start(f32[32,4,256]{2,1,0:T(4,128)} %get-tuple-element.64), calls=%async_computation.1 | async-start | bytes 262144 | tf_op jit(solution)/shard_map/all_to_all | solution.py:1079
  137.8 7.3 %shard_map.185 = f32[320,4096]{1,0:T(8,128)} custom-call(bf16[320,160]{1,0:T(8,128)(2,1)} %get-tuple-element.57.vertical, f32[80,80]{1,0:T(8,128)} %mix.2, f32[4,4096]{1,0:T(4,128)} %get-tuple-element.63.flux, bf16[12,640,256]{2,1,0:T(8,128)(2,1)} %shard_map.178.inner_in, bf16[4,640,256]{2,1,0:T(8,128)(2,1)} %shard_map.183.outer_in), custom_call_target="tpu_custom_call" | custom-call | flops 1000000 | bytes 10000 | tf_op jit(solution)/shard_map/pallas_call | solution.py:1081
  145.1 0.6 all-to-all-done.1.back
  145.7 0.6 copy-done.5
  146.4 5.2 %shard_map.186 = f32[32,128]{1,0:T(8,128)} custom-call(f32[32,4,256]{2,1,0:T(4,128)} %copy-done.5, s32[32,512]{1,0:T(8,128)} %bitcast.17, f32[4,4096]{1,0:T(4,128)} %surf.7), custom_call_target="tpu_custom_call" | custom-call | flops 1000000 | bytes 10000 | tf_op jit(solution)/shard_map/pallas_call | solution.py:1094
  (16 shorter events, 0.0 us)
Async XLA Ops:
  4.8 68.3 %collective-permute-start = (f32[304,1024]{1,0:T(8,128)}, f32[304,1024]{1,0:T(8,128)S(1)}, u32[]{:S(2)}, u32[]{:S(2)}) collective-permute-start(f32[304,1024]{1,0:T(8,128)} %get-tuple-element.46), channel_id=1, source_target_pairs={{0,1},{1,2},{2,3},{3,4},{4,5},{5,6},{6,7},{7,8},{8,9},{9,10},{10,1... | collective-permute-start | bytes 3735560 | tf_op jit(solution)/shard_map/ppermute | solution.py:915
  7.8 65.3 %collective-permute-start.1 = (f32[304,1024]{1,0:T(8,128)}, f32[304,1024]{1,0:T(8,128)S(1)}, u32[]{:S(2)}, u32[]{:S(2)}) collective-permute-start(f32[304,1024]{1,0:T(8,128)} %get-tuple-element.35), channel_id=1, source_target_pairs={{1,0},{2,1},{3,2},{4,3},{5,4},{6,5},{7,6},{8,7},{9,8},{10,9},{11,1... | collective-permute-start | bytes 3735560 | tf_op jit(solution)/shard_map/ppermute | solution.py:916
  17.1 27.4 %copy-start.7 = (f32[320,384]{1,0:T(8,128)S(1)}, f32[320,384]{1,0:T(8,128)}, u32[]{:S(2)}) copy-start(f32[320,384]{1,0:T(8,128)} %get-tuple-element.52) | copy-start | bytes 1474564
  17.1 27.6 %copy-start.6 = (f32[320,384]{1,0:T(8,128)S(1)}, f32[320,384]{1,0:T(8,128)}, u32[]{:S(2)}) copy-start(f32[320,384]{1,0:T(8,128)} %get-tuple-element.53) | copy-start | bytes 1474564
  44.5 50.1 %collective-permute-start.2 = (f32[320,384]{1,0:T(8,128)S(1)}, f32[320,384]{1,0:T(8,128)S(1)}, u32[]{:S(2)}, u32[]{:S(2)}) collective-permute-start(f32[320,384]{1,0:T(8,128)S(1)} %copy-done.7), channel_id=1, source_target_pairs={{0,1},{1,2},{2,3},{3,4},{4,5},{5,6},{6,7},{7,8},{8,9},{9,10},{10,1... | collective-permute-start | bytes 1474568 | tf_op jit(solution)/shard_map/ppermute | solution.py:1004
  44.7 49.9 %collective-permute-start.3 = (f32[320,384]{1,0:T(8,128)S(1)}, f32[320,384]{1,0:T(8,128)S(1)}, u32[]{:S(2)}, u32[]{:S(2)}) collective-permute-start(f32[320,384]{1,0:T(8,128)S(1)} %copy-done.6), channel_id=1, source_target_pairs={{1,0},{2,1},{3,2},{4,3},{5,4},{6,5},{7,6},{8,7},{9,8},{10,9},{11,1... | collective-permute-start | bytes 1474568 | tf_op jit(solution)/shard_map/ppermute | solution.py:1005
  73.1 1.0 copy-start.2
  73.1 1.5 copy-start.3
  94.6 15.5 %copy-start = (f32[320,384]{1,0:T(8,128)}, f32[320,384]{1,0:T(8,128)S(1)}, u32[]{:S(2)}) copy-start(f32[320,384]{1,0:T(8,128)S(1)} %collective-permute-done.2.before_in) | copy-start | bytes 1474564
  94.6 15.5 %copy-start.1 = (f32[320,384]{1,0:T(8,128)}, f32[320,384]{1,0:T(8,128)S(1)}, u32[]{:S(2)}) copy-start(f32[320,384]{1,0:T(8,128)S(1)} %collective-permute-done.3.after_in) | copy-start | bytes 1474564
  99.5 17.9 %all-to-all-start = ((f32[32,8,256]{2,1,0:T(8,128)}), f32[32,8,256]{2,1,0:T(8,128)S(1)}, u32[]{:S(2)}, u32[]{:S(2)}) async-start(f32[32,8,256]{2,1,0:T(8,128)} %shard_map.181), calls=%async_computation | async-start | bytes 524288 | tf_op jit(solution)/shard_map/all_to_all | solution.py:1033
  117.4 0.7 copy-start.4
  132.0 13.8 %all-to-all-start.1 = ((f32[32,4,256]{2,1,0:T(4,128)}), f32[32,4,256]{2,1,0:T(4,128)S(1)}, u32[]{:S(2)}, u32[]{:S(2)}) async-start(f32[32,4,256]{2,1,0:T(4,128)} %get-tuple-element.64), calls=%async_computation.1 | async-start | bytes 262144 | tf_op jit(solution)/shard_map/all_to_all | solution.py:1079
  145.7 0.6 copy-start.5

commit v10 on v8

--- a/solution.py
+++ b/solution.py
@@ -162,39 +162,49 @@
     return total
 
 
+def pack_kernel(nbr, coef, bulk, surf, atm, sea, wide_first, wide_last, sea_first, sea_last, *refs):
+    held, lists, sems = refs[:4], refs[4], refs[5]
+    rows, columns = atm.shape
+    cells = sea.shape[1]
+    sources = (
+        atm.at[:, :WIDE],
+        atm.at[:, columns - WIDE :],
+        sea.at[:, :HO],
+        sea.at[:, cells - HO :],
+    )
+    targets = (wide_first.at[:rows], wide_last.at[:rows], sea_first, sea_last)
+    arriving = [pltpu.make_async_copy(x, held[i], sems.at[i]) for i, x in enumerate(sources)]
+    leaving = [pltpu.make_async_copy(held[i], x, sems.at[4 + i]) for i, x in enumerate(targets)]
+    for copy in arriving:
+        copy.start()
+    need = WIDE - BLK
+    for i, first in enumerate((0, columns - need)):
+        at = slice(first, first + need)
+        lists[i, 0:6, :need] = nbr[:, at].astype(F32)
+        lists[i, 6:12, :need] = coef[:, at]
+        lists[i, 12:16, :need] = bulk[:, at]
+        lists[i, 12:16, need:] = jnp.zeros((4, BLK), F32)
+        for j in range(ASTEPS - 1):
+            lists[i, 4 * j : 4 * j + 4, need:] = surf[:, first + j * BLK : first + (j + 1) * BLK]
+    for i, target in enumerate((wide_first, wide_last)):
+        copy = pltpu.make_async_copy(lists.at[i], target.at[rows:], sems.at[8 + i])
+        copy.start()
+        leaving.append(copy)
+    for here, there in zip(arriving, leaving[:4]):
+        here.wait()
+        there.start()
+    for copy in leaving:
+        copy.wait()
+
+
 def prepare_kernel(fields):
     def body(
-        mix, omix, atm, nbr, coef, bulk, surf, spread, code, sea_spread, sea,
-        y, yo, gains, lift, vertical, sea_vertical, wide_first, wide_last, sea_first, sea_last,
-        top, lists, ends, sems,
+        mix, omix, atm, spread, code, sea_spread, sea, y, yo, gains, lift, vertical, sea_vertical, top, sem
     ):
         la = mix.shape[0]
-        rows, columns = atm.shape
-        cells = sea.shape[1]
-        copy = pltpu.make_async_copy(sea.at[: omix.shape[0], :], top, sems.at[0])
+        columns = atm.shape[1]
+        copy = pltpu.make_async_copy(sea.at[: omix.shape[0], :], top, sem)
         copy.start()
-        arriving = [
-            pltpu.make_async_copy(sea.at[:, :HO], ends.at[0], sems.at[1]),
-            pltpu.make_async_copy(sea.at[:, cells - HO :], ends.at[1], sems.at[2]),
-        ]
-        leaving = [
-            pltpu.make_async_copy(atm.at[:, :WIDE], wide_first.at[:rows], sems.at[3]),
-            pltpu.make_async_copy(atm.at[:, columns - WIDE :], wide_last.at[:rows], sems.at[4]),
-            pltpu.make_async_copy(lists.at[0], wide_first.at[rows:], sems.at[5]),
-            pltpu.make_async_copy(lists.at[1], wide_last.at[rows:], sems.at[6]),
-            pltpu.make_async_copy(ends.at[0], sea_first, sems.at[7]),
-            pltpu.make_async_copy(ends.at[1], sea_last, sems.at[8]),
-        ]
-        for i, at in enumerate((slice(0, WIDE), slice(columns - WIDE, columns))):
-            lists[i, 0:6] = nbr[:, at].astype(F32)
-            lists[i, 6:12] = coef[:, at]
-            lists[i, 12:16] = bulk[:, at]
-            lists[i, 16:20] = surf[:, at]
-            lists[i, 20:24] = jnp.zeros((4, WIDE), F32)
-        for here in arriving:
-            here.start()
-        for out in leaving[:4]:
-            out.start()
         eye = iota((la, la), 0) == iota((la, la), 1)
         step = mix[...] + jnp.where(eye, 1.0, 0.0)
 
@@ -254,11 +264,6 @@
                         x * weights[k - 1], axis=0, keepdims=True
                     )
             yo[:, at] = jnp.sum(top[:, at] * sea_weight, axis=0, keepdims=True)
-        for here, out in zip(arriving, leaving[4:]):
-            here.wait()
-            out.start()
-        for out in leaving:
-            out.wait()
 
     return body
 
@@ -366,7 +371,7 @@
     return ends, b - blocks + 2 * ASTEPS
 
 
-def send_kernel(q_ends, q_mid, cols, out, table):
+def send(q_ends, q_mid, cols, out, table):
     fields = q_mid.shape[1] // ASTEPS
     peers, slots = cols.shape
     blocks = q_ends.shape[0] + q_mid.shape[0]
@@ -406,31 +411,18 @@
     ]
     for copy in arriving:
         copy.start()
-    rows[...] = jnp.concatenate(halves(recv[...].reshape(table, lanes)), axis=1)
+    rows[...] = stacked(recv[...].reshape(table, lanes))
     levels = omix.shape[0]
     eye = iota((levels, levels), 0) == iota((levels, levels), 1)
     corner = omix[0:1, 0:1] + 1.0
     top = omix[0:1, :] + jnp.where(iota((1, levels), 1) == 0, 1.0, 0.0)
     top = jnp.sum(jnp.where(eye, top, 0.0), axis=1, keepdims=True)
-    for copy in arriving:
-        copy.wait()
-    before, after = [jnp.sum(held[i] * top, axis=0, keepdims=True) for i in range(2)]
-    acc[...] = jnp.zeros_like(acc)
-    side = HO // 128
-    own_tiles = columns // 128
-    for t in range(own_tiles + 2 * side):
-        if t < side:
-            line = before[:, t * 128 : (t + 1) * 128]
-        elif t < side + own_tiles:
-            line = yo[:, (t - side) * 128 : (t - side + 1) * 128]
-        else:
-            line = after[:, (t - side - own_tiles) * 128 : (t - side - own_tiles + 1) * 128]
-        tiles[t] = jnp.broadcast_to(line, (8, 128))
     high_of_row = iota((table, BLK), 0) // fields
     back_rows = iota((2 * highs, BLK), 0)
     inner = back_rows % (2 * parts)
     back_high = (back_rows // (2 * parts)) * parts + inner % parts
     pattern = iota((8, BLK), 0) % (2 * parts) // parts
+    side = HO // 128
     window = 1 + 2 * side
     neighbors = nbr.shape[0]
 
@@ -447,13 +439,6 @@
             got = jnp.where(ids // 128 == t, pick, got)
         return middle[0:1] + jnp.sum(cs * (got - middle), axis=0, keepdims=True)
 
-    def base(j, _):
-        at = pl.ds(pl.multiple_of(j * BLK, BLK), BLK)
-        seas[:, at] = jnp.concatenate([surface(j, h) for h in range(BLK // 128)], axis=1)
-        return 0
-
-    lax.fori_loop(0, columns // BLK, base, 0, unroll=2)
-
     def arrive(j, _):
         at = pl.ds(pl.multiple_of(j * BLK, BLK), BLK)
         parts = []
@@ -462,11 +447,11 @@
             ids = slot[r : r + 1, at]
             hot = one_hot(ids & (lanes - 1), lanes)
             hots[j, :, r * BLK : (r + 1) * BLK] = hot
-            return mm(rows[...], jnp.concatenate([hot, hot], axis=0))
+            return mm(rows[...], hot)
 
         def finish(r, got):
             ids = slot[r : r + 1, at]
-            got = jnp.where(high_of_row == ids // lanes, got, 0.0)
+            got = jnp.where(high_of_row == ids // lanes, got[:table] + got[table:], 0.0)
             parts.append(weight[r : r + 1, at] * fold_rows(got, 2 * fields))
 
         last = begin(0)
@@ -478,10 +463,30 @@
         flux = sum(parts[1:], parts[0])
         flux = flux[:fields] + flux[fields:]
         flux_out[:, at] = flux
-        seas[:, at] += corner * flux[0:1]
+        seas[:, at] = corner * flux[0:1]
         return 0
 
     lax.fori_loop(0, columns // BLK, arrive, 0, unroll=2)
+    for copy in arriving:
+        copy.wait()
+    before, after = [jnp.sum(held[i] * top, axis=0, keepdims=True) for i in range(2)]
+    acc[...] = jnp.zeros_like(acc)
+    own_tiles = columns // 128
+    for t in range(own_tiles + 2 * side):
+        if t < side:
+            line = before[:, t * 128 : (t + 1) * 128]
+        elif t < side + own_tiles:
+            line = yo[:, (t - side) * 128 : (t - side + 1) * 128]
+        else:
+            line = after[:, (t - side - own_tiles) * 128 : (t - side - own_tiles + 1) * 128]
+        tiles[t] = jnp.broadcast_to(line, (8, 128))
+
+    def base(j, _):
+        at = pl.ds(pl.multiple_of(j * BLK, BLK), BLK)
+        seas[:, at] += jnp.concatenate([surface(j, h) for h in range(BLK // 128)], axis=1)
+        return 0
+
+    lax.fori_loop(0, columns // BLK, base, 0, unroll=2)
 
     def leave(j, _):
         at = pl.ds(pl.multiple_of(j * BLK, BLK), BLK)
@@ -536,8 +541,8 @@
 
 
 def edge_kernel(
-    y, bulk, surf, gains, lift, before, after, atm, kept_in, band, q, ends_out,
-    w, wide, sides, kept, sa, sb, ma, mb, ends, sems,
+    y, bulk, surf, gains, lift, q_mid, cols, before, after, atm, kept_in, band, q, ends_out, outgoing,
+    w, wide, sides, kept, sa, sb, ma, mb, ends, table, sems,
 ):
     rows = atm.shape[0]
     levels = lift.shape[1]
@@ -576,12 +581,15 @@
         at = slice(local * BLK, (local + 1) * BLK)
         if ref is None:
             return bulk[:, at], surf[:, at]
-        return ref[rows + 12 : rows + 16, at], ref[rows + 16 : rows + 20, at]
+        j = local - 1 if e < ASTEPS else local
+        at = slice(j * BLK, (j + 1) * BLK)
+        return ref[rows + 12 : rows + 16, at], ref[rows + 4 * j : rows + 4 * j + 4, WIDE - BLK :]
 
     def build(e):
         ref, local = place(e)
         origin = local * BLK + (columns - WIDE if e < ASTEPS else 0)
-        at = slice(local * BLK, (local + 1) * BLK)
+        j = local - 1 if e < ASTEPS else local
+        at = slice(j * BLK, (j + 1) * BLK)
         ids = ref[rows : rows + 6, at].astype(jnp.int32) - origin
         k = e - 1 if e < ASTEPS else e - (total - 1) + 2 * count
         yield from band_build(ids, ref[rows + 6 : rows + 12, at], w, k)
@@ -654,6 +662,7 @@
                 target[6 + i] = kept[(s - 1) * 4 + 2 + i]
     out = pltpu.make_async_copy(ends, ends_out, sems.at[5 + 2 * ASTEPS])
     out.start()
+    send(q, q_mid, cols, outgoing, table)
     out.wait()
 
 
@@ -881,8 +890,21 @@
     spread = ((c_of[0] % la == np.arange(la)[:, None]) & (c_of[0] < 2 * la)).astype(np.float32)
     sea_spread = (np.arange(2 * lo)[None, :] % lo == np.arange(lo)[:, None]).astype(np.float32)
 
-    wide_rows = rows + 24
-    y, yo, gains, lift, vertical, sea_vertical, wide_first, wide_last, sea_first, sea_last = call(
+    wide_rows = rows + 16
+    sea_rows = fields * lo
+    halo_shapes = (shape((rows, WIDE)),) * 2 + (shape((sea_rows, HO)),) * 2
+    wide_first, wide_last, sea_first, sea_last = call(
+        pack_kernel,
+        (shape((wide_rows, WIDE)),) * 2 + halo_shapes[2:],
+        in_specs=[vmem] * 4 + [anywhere] * 2,
+        out_specs=(anywhere,) * 4,
+        scratch=[pltpu.VMEM(h.shape, F32) for h in halo_shapes]
+        + [pltpu.VMEM((2, 16, WIDE), F32), pltpu.SemaphoreType.DMA((10,))],
+    )(atm_nbr, atm_nbr_coef, bulk_coef, atm_surface, atm, ocean)
+    wide_before = lax.ppermute(wide_last, AXES, up)
+    wide_after = lax.ppermute(wide_first, AXES, down)
+
+    y, yo, gains, lift, vertical, sea_vertical = call(
         prepare_kernel(fields),
         (
             shape((states, columns)),
@@ -891,34 +913,18 @@
             shape((ASTEPS - 1, la, 128)),
             shape((half, 4 * la, 2 * la + states), BF),
             shape((4 * lo, 2 * lo), BF),
-            shape((wide_rows, WIDE)),
-            shape((wide_rows, WIDE)),
-            shape((fields * lo, HO)),
-            shape((fields * lo, HO)),
         ),
-        in_specs=[vmem] * 10 + [anywhere],
-        out_specs=(vmem,) * 6 + (anywhere,) * 4,
-        scratch=[
-            pltpu.VMEM((lo, cells), F32),
-            pltpu.VMEM((2, 24, WIDE), F32),
-            pltpu.VMEM((2, fields * lo, HO), F32),
-            pltpu.SemaphoreType.DMA((9,)),
-        ],
+        in_specs=[vmem] * 6 + [anywhere],
+        scratch=[pltpu.VMEM((lo, cells), F32), pltpu.SemaphoreType.DMA(())],
     )(
-        atm_mix,
+        after_all(atm_mix, wide_first),
         ocean_mix,
         atm,
-        atm_nbr,
-        atm_nbr_coef,
-        bulk_coef,
-        atm_surface,
         jnp.asarray(spread),
         jnp.asarray(code),
         jnp.asarray(sea_spread),
         ocean,
     )
-    wide_before = lax.ppermute(wide_last, AXES, up)
-    wide_after = lax.ppermute(wide_first, AXES, down)
 
     ends = 2 * ASTEPS
     q_mid, kept, mid, band = call(
@@ -947,7 +953,6 @@
     outer = -(-HO // BLK)
     around = 1 + 2 * HO // BLK
     sea_window = BLK + 2 * HO
-    sea_rows = fields * lo
     inner = sea_blocks - 2 * outer
     sea_inner = call(
         sea_inner_kernel,
@@ -965,17 +970,19 @@
         ],
     )(ocean, after_all(ocean_nbr, q_mid), ocean_nbr_coef)
 
-    sea_first, sea_last, wide_before, wide_after = lax.optimization_barrier(
-        (sea_first, sea_last, wide_before, wide_after, sea_inner)
-    )[:4]
+    sea_first, sea_last = lax.optimization_barrier((sea_first, sea_last, sea_inner))[:2]
     sea_before = lax.ppermute(sea_last, AXES, up)
     sea_after = lax.ppermute(sea_first, AXES, down)
 
-    q_ends, tips = call(
+    q_ends, tips, outgoing = call(
         edge_kernel,
-        (shape((ends, states, BLK)), shape((ends, 2 * rows, BLK), BF)),
-        in_specs=[vmem] * 5 + [anywhere] * 5,
-        out_specs=(vmem, anywhere),
+        (
+            shape((ends, states, BLK)),
+            shape((ends, 2 * rows, BLK), BF),
+            shape((peers, parts * fields, lanes)),
+        ),
+        in_specs=[vmem] * 7 + [anywhere] * 5,
+        out_specs=(vmem, anywhere, vmem),
         scratch=[
             pltpu.VMEM((2 * (2 * ASTEPS - 1), 2, window, BLK), BF),
             pltpu.VMEM((2, wide_rows, WIDE), F32),
@@ -986,16 +993,12 @@
             pltpu.VMEM((depth_k, BLK), F32),
             pltpu.VMEM((depth_k, BLK), F32),
             pltpu.VMEM((ends, 2 * rows, BLK), BF),
+            pltpu.VMEM((blocks * fields, BLK), F32),
             pltpu.SemaphoreType.DMA((6 + 2 * ASTEPS,)),
         ],
-    )(y, bulk_coef, atm_surface, gains, lift, wide_before, wide_after, atm, kept, band)
-
-    outgoing = call(
-        send_kernel,
-        shape((peers, parts * fields, lanes)),
-        in_specs=[vmem] * 3,
-        scratch=[pltpu.VMEM((blocks * fields, BLK), F32)],
-    )(q_ends, q_mid, picked)
+    )(after_all(y, sea_inner), bulk_coef, atm_surface, gains, lift, q_mid, picked, wide_before, wide_after, atm, kept, band)
+
+    sea_before, sea_after, outgoing = lax.optimization_barrier((sea_before, sea_after, outgoing))
     received = lax.all_to_all(outgoing, AXES, split_axis=0, concat_axis=0, tiled=True)
 
     atm_final = call(
@@ -1017,7 +1020,7 @@
         (shape((fields, cells)), shape((peers, 2 * parts, lanes))),
         in_specs=[vmem] * 7 + [anywhere] * 2,
         scratch=[
-            pltpu.VMEM((peers * parts * fields, 2 * lanes), BF),
+            pltpu.VMEM((2 * peers * parts * fields, lanes), BF),
             pltpu.VMEM((cells // 128 + 2 * HO // 128, 8, 128), F32),
             pltpu.VMEM((cells // BLK, lanes, remap_slot.shape[0] * BLK), BF),
             pltpu.VMEM((1, cells), F32),

time: 161 us -> 145 us (0.901)
  waiting for transfers between devices: 27.2 us -> 13.7 us
  Pallas kernels: 109 us -> 107 us
    all_to_all x1, waiting for transfers between devices: 10.1 us -> 4.9 us  [per_device(): lax.all_to_all(outgoing, AXES, split_axis=0, concat_axis=0, tiled=True)]
    ppermute x1, waiting for transfers between devices: 3.42 us -> 0.01 us  [per_device(): sea_before = lax.ppermute(sea_last, AXES, up)]
    pallas_call x1, Pallas kernels: 7.98 us -> 5.82 us  [per_device(): call(prepare_kernel(fields), (shape((states, columns)), shape((1, columns...]
    ppermute x1, waiting for transfers between devices: 1.86 us -> 0.01 us  [per_device(): sea_after = lax.ppermute(sea_first, AXES, down)]
    ppermute x1, waiting for transfers between devices: 1.84 us -> 0.01 us  [per_device(): wide_after = lax.ppermute(wide_first, AXES, down)]
    ppermute x1, starting transfers between devices: 1.82 us -> 0.06 us  [per_device(): sea_before = lax.ppermute(sea_last, AXES, up)]
    all_to_all x1, starting transfers between devices: 4.23 us -> 2.58 us  [per_device(): lax.all_to_all(back, AXES, split_axis=0, concat_axis=0, tiled=True)]
  transfers between devices with their start and end apart: 6 -> 6, of which waited for: 5 -> 2; matrix products, arithmetic and copies ran while one was open for 0% -> 0% of each run, Pallas kernels for 36% -> 59%
where the time goes in v10:
time: 145 us
  Pallas kernels  107 us (74%)
  starting transfers between devices  20 us (14%)
  waiting for transfers between devices  13.7 us (9%)
  local copies, waits for them, and re-layouts  2.79 us (2%)
    pallas_call x1, Pallas kernels, per_device(): call(interior_kernel, (shape((blocks - ends, states, BLK)), shape((4 * (A...  27.5 us
    pallas_call x1, Pallas kernels, per_device(): call(edge_kernel, (shape((ends, states, BLK)), shape((ends, 2 * rows, BLK...  21.4 us
    pallas_call x1, Pallas kernels, per_device(): call(sea_inner_kernel, shape((inner, 2 * sea_rows, BLK), BF), in_specs=[v...  14.2 us
    pallas_call x1, Pallas kernels, per_device(): call(exchange_kernel, (shape((fields, cells)), shape((peers, 2 * parts, l...  12.9 us
    pallas_call x1, Pallas kernels, per_device(): call(sea_outer_kernel, shape((sea_rows, cells)), in_specs=[vmem] * 7 + [a...  10.1 us
    ppermute x1, waiting for transfers between devices, per_device(): wide_before = lax.ppermute(wide_last, AXES, up)  8.75 us
    pallas_call x1, Pallas kernels, per_device(): call(finish_kernel, shape((rows, columns)), in_specs=[vmem] * 3 + [anywhe...  6.06 us
    pallas_call x1, Pallas kernels, per_device(): call(prepare_kernel(fields), (shape((states, columns)), shape((1, columns...  5.82 us
  transfers between devices with their start and end apart: 6, of which 2 were waited for; matrix products, arithmetic and copies ran while one was open for 0% of the time, Pallas kernels for 59%

profile of v10, /device:TPU:0, one launch (start us, length us, event | category | flops | bytes accessed | tf_op | source)
XLA Modules:
  0.0 144.6 jit_solution(308432957644501456)
XLA Ops:
  0.6 4.3 %shard_map.175 = (f32[304,1024]{1,0:T(8,128)}, f32[304,1024]{1,0:T(8,128)}, f32[320,384]{1,0:T(8,128)}, f32[320,384]{1,0:T(8,128)}) custom-call(s32[6,4096]{1,0:T(8,128)} %nbr.5, f32[6,4096]{1,0:T(8,128)} %coef.6, f32[4,4096]{1,0:T(4,128)} %bulk.5, f32[4,4096]{1,0:T(4,128)} %surf.7, f32[288,4096]{1,0:T(8,128)} %bitcast.10, f32[320,4096]{1,0:T(8,128)} %bitcast.6), custom_call_target="tpu_custom_call" | custom-call | flops 1000000 | bytes 10000 | tf_op jit(solution)/shard_map/pallas_call | solution.py:896
  4.9 3.0 %collective-permute-start = (f32[304,1024]{1,0:T(8,128)}, f32[304,1024]{1,0:T(8,128)S(1)}, u32[]{:S(2)}, u32[]{:S(2)}) collective-permute-start(f32[304,1024]{1,0:T(8,128)} %get-tuple-element.42), channel_id=1, source_target_pairs={{0,1},{1,2},{2,3},{3,4},{4,5},{5,6},{6,7},{7,8},{8,9},{9,10},{10,1... | collective-permute-start | bytes 3735560 | tf_op jit(solution)/shard_map/ppermute | solution.py:904
  7.9 3.5 %collective-permute-start.1 = (f32[304,1024]{1,0:T(8,128)}, f32[304,1024]{1,0:T(8,128)S(1)}, u32[]{:S(2)}, u32[]{:S(2)}) collective-permute-start(f32[304,1024]{1,0:T(8,128)} %get-tuple-element.34), channel_id=1, source_target_pairs={{1,0},{2,1},{3,2},{4,3},{5,4},{6,5},{7,6},{8,7},{9,8},{10,9},{11,1... | collective-permute-start | bytes 3735560 | tf_op jit(solution)/shard_map/ppermute | solution.py:905
  11.4 5.8 %shard_map.176 = (f32[16,4096]{1,0:T(8,128)}, f32[1,4096]{1,0:T(1,128)}, f32[16,128]{1,0:T(8,128)}, f32[3,72,128]{2,1,0:T(8,128)}, bf16[2,288,160]{2,1,0:T(8,128)(2,1)}, /*index=5*/bf16[320,160]{1,0:T(8,128)(2,1)}) custom-call(f32[72,72]{1,0:T(8,128)} %mix.1, f32[80,80]{1,0:T(8,128)} %mix.2, f32[288,4096]{1,0:T(8,128)} %bitcast.11, ...), custom_call_target="tpu_custom_call" | custom-call | flops 1000000 | bytes 10000 | tf_op jit(solution)/shard_map/pallas_call | solution.py:907
  17.2 27.5 %shard_map.177 = (f32[8,16,256]{2,1,0:T(8,128)}, bf16[12,608,256]{2,1,0:T(8,128)(2,1)}, bf16[8,576,256]{2,1,0:T(8,128)(2,1)}, bf16[8,2,768,256]{3,2,1,0:T(8,128)(2,1)}) custom-call(f32[288,4096]{1,0:T(8,128)} %bitcast.12, f32[16,4096]{1,0:T(8,128)} %get-tuple-element.40.y, s32[6,4096]{1,0:T(8,128)} %nbr.5, f32[6,4096]{1,0:T(8,128)} %coef.6, f32[4,4096]{1,0:T(4,128)} %bulk.5, ...), custom_call_target="tpu_custom_call" | custom-call | flops 1000000 | bytes 10000 | tf_op jit(solution)/shard_map/pallas_call | solution.py:930
  44.7 14.2 %shard_map.178.laid_in = bf16[12,640,256]{2,1,0:T(8,128)(2,1)} custom-call(f32[320,4096]{1,0:T(8,128)} %bitcast.8, s32[6,4096]{1,0:T(8,128)} %nbr.8, f32[6,4096]{1,0:T(8,128)} %coef.9), custom_call_target="tpu_custom_call" | custom-call | flops 1000000 | bytes 10000 | tf_op jit(solution)/shard_map/pallas_call | solution.py:957
  58.9 0.1 collective-permute-start.2
  59.0 5.3 %collective-permute-start.3 = (f32[320,384]{1,0:T(8,128)S(1)}, f32[320,384]{1,0:T(8,128)S(1)}, u32[]{:S(2)}, u32[]{:S(2)}) collective-permute-start(f32[320,384]{1,0:T(8,128)S(1)} %copy-done.6), channel_id=1, source_target_pairs={{1,0},{2,1},{3,2},{4,3},{5,4},{6,5},{7,6},{8,7},{9,8},{10,9},{11,1... | collective-permute-start | bytes 1474568 | tf_op jit(solution)/shard_map/ppermute | solution.py:975
  64.3 8.8 %collective-permute-done.before = f32[304,1024]{1,0:T(8,128)S(1)} collective-permute-done((f32[304,1024]{1,0:T(8,128)}, f32[304,1024]{1,0:T(8,128)S(1)}, u32[]{:S(2)}, u32[]{:S(2)}) %collective-permute-start) | collective-permute-done | bytes 1245216 | tf_op jit(solution)/shard_map/ppermute | solution.py:904
  73.1 0.0 collective-permute-done.1.after
  73.1 1.1 copy-done.2
  74.2 0.3 copy-done.3
  74.5 21.4 %shard_map.179 = (f32[8,16,256]{2,1,0:T(8,128)}, bf16[8,576,256]{2,1,0:T(8,128)(2,1)}, f32[32,8,256]{2,1,0:T(8,128)}) custom-call(f32[16,4096]{1,0:T(8,128)} %get-tuple-element.40.y, f32[4,4096]{1,0:T(4,128)} %bulk.5, f32[4,4096]{1,0:T(4,128)} %surf.7, f32[16,128]{1,0:T(8,128)} %get-tuple-element.37.gains, f32[3,72,128]{2,1,0:T(8,128)} %get-tuple-element.41.lift, ...), custom_call_target="tpu_custom_call" | custom-call | flops 1000000 | bytes 10000 | tf_op jit(solution)/shard_map/pallas_call | solution.py:977
  95.9 0.0 collective-permute-done.2.before_in.before
  95.9 5.6 %all-to-all-start = ((f32[32,8,256]{2,1,0:T(8,128)}), f32[32,8,256]{2,1,0:T(8,128)S(1)}, u32[]{:S(2)}, u32[]{:S(2)}) async-start(f32[32,8,256]{2,1,0:T(8,128)} %get-tuple-element.51), calls=%async_computation | async-start | bytes 524288 | tf_op jit(solution)/shard_map/all_to_all | solution.py:1002
  101.5 6.1 %shard_map.180 = f32[288,4096]{1,0:T(8,128)} custom-call(f32[8,16,256]{2,1,0:T(8,128)} %get-tuple-element.52.q_ends, f32[8,16,256]{2,1,0:T(8,128)} %get-tuple-element.38.q_mid, bf16[2,288,160]{2,1,0:T(8,128)(2,1)} %get-tuple-element.53.vertical, bf16[8,576,256]{2,1,0:T(8,128)(2,1)} %get-tuple-element.54.ends_in, bf16[8,576,256]{2,1,0:T(8,128)(2,1)} %get-tuple-element.55.mid_in), custom_call_target="tpu_custom_call" | custom-call | flops 1000000 | bytes 10000 | tf_op jit(solution)/shard_map/pallas_call | solution.py:1004
  107.6 4.9 %all-to-all-done.recv = f32[32,8,256]{2,1,0:T(8,128)S(1)} async-done(((f32[32,8,256]{2,1,0:T(8,128)}), f32[32,8,256]{2,1,0:T(8,128)S(1)}, u32[]{:S(2)}, u32[]{:S(2)}) %all-to-all-start) | async-done | bytes 262176 | tf_op jit(solution)/shard_map/all_to_all | solution.py:1002
  112.5 0.7 copy-done.4
  113.2 12.9 %shard_map.181 = (f32[4,4096]{1,0:T(4,128)}, f32[32,4,256]{2,1,0:T(4,128)}) custom-call(f32[32,8,256]{2,1,0:T(8,128)} %copy-done.4, s32[4,4096]{1,0:T(4,128)} %slot.1, f32[4,4096]{1,0:T(4,128)} %weight.1, f32[1,4096]{1,0:T(1,128)} %get-tuple-element.58.yo, s32[6,4096]{1,0:T(8,128)} %nbr.8, f32[6,4096]{1,0:T(8,128)} %coef.9, f32[80,80]{1,0:T(8,128)} %mix.2, ...), custom_call_target="tpu_custom_call" | custom-call | flops 1000000 | bytes 10000 | tf_op jit(solution)/shard_map/pallas_call | solution.py:1018
  126.1 2.6 %all-to-all-start.1 = ((f32[32,4,256]{2,1,0:T(4,128)}), f32[32,4,256]{2,1,0:T(4,128)S(1)}, u32[]{:S(2)}, u32[]{:S(2)}) async-start(f32[32,4,256]{2,1,0:T(4,128)} %get-tuple-element.60), calls=%async_computation.1 | async-start | bytes 262144 | tf_op jit(solution)/shard_map/all_to_all | solution.py:1042
  128.7 10.1 %shard_map.182 = f32[320,4096]{1,0:T(8,128)} custom-call(f32[320,384]{1,0:T(8,128)} %copy-done, f32[320,384]{1,0:T(8,128)} %copy-done.1, s32[6,4096]{1,0:T(8,128)} %nbr.8, f32[6,4096]{1,0:T(8,128)} %coef.9, bf16[320,160]{1,0:T(8,128)(2,1)} %get-tuple-element.62.vertical, f32[80,80]{1,0:T(8,128)} %mix.2, f32[4,4096]{1,0:T(4,128)} %get-tuple-element.63.flux, ...), custom_call_target="tpu_custom_call" | custom-call | flops 1000000 | bytes 10000 | tf_op jit(solution)/shard_map/pallas_call | solution.py:1044
  138.7 0.0 all-to-all-done.1.back
  138.8 0.6 copy-done.5
  139.4 5.2 %shard_map.183 = f32[32,128]{1,0:T(8,128)} custom-call(f32[32,4,256]{2,1,0:T(4,128)} %copy-done.5, s32[32,512]{1,0:T(8,128)} %bitcast.17, f32[4,4096]{1,0:T(4,128)} %surf.7), custom_call_target="tpu_custom_call" | custom-call | flops 1000000 | bytes 10000 | tf_op jit(solution)/shard_map/pallas_call | solution.py:1073
  (13 shorter events, 0.0 us)
Async XLA Ops:
  4.9 68.2 %collective-permute-start = (f32[304,1024]{1,0:T(8,128)}, f32[304,1024]{1,0:T(8,128)S(1)}, u32[]{:S(2)}, u32[]{:S(2)}) collective-permute-start(f32[304,1024]{1,0:T(8,128)} %get-tuple-element.42), channel_id=1, source_target_pairs={{0,1},{1,2},{2,3},{3,4},{4,5},{5,6},{6,7},{7,8},{8,9},{9,10},{10,1... | collective-permute-start | bytes 3735560 | tf_op jit(solution)/shard_map/ppermute | solution.py:904
  7.9 65.2 %collective-permute-start.1 = (f32[304,1024]{1,0:T(8,128)}, f32[304,1024]{1,0:T(8,128)S(1)}, u32[]{:S(2)}, u32[]{:S(2)}) collective-permute-start(f32[304,1024]{1,0:T(8,128)} %get-tuple-element.34), channel_id=1, source_target_pairs={{1,0},{2,1},{3,2},{4,3},{5,4},{6,5},{7,6},{8,7},{9,8},{10,9},{11,1... | collective-permute-start | bytes 3735560 | tf_op jit(solution)/shard_map/ppermute | solution.py:905
  44.7 14.2 %copy-start.7 = (f32[320,384]{1,0:T(8,128)S(1)}, f32[320,384]{1,0:T(8,128)}, u32[]{:S(2)}) copy-start(f32[320,384]{1,0:T(8,128)} %get-tuple-element.48) | copy-start | bytes 1474564
  44.7 14.3 %copy-start.6 = (f32[320,384]{1,0:T(8,128)S(1)}, f32[320,384]{1,0:T(8,128)}, u32[]{:S(2)}) copy-start(f32[320,384]{1,0:T(8,128)} %get-tuple-element.49) | copy-start | bytes 1474564
  58.9 37.0 %collective-permute-start.2 = (f32[320,384]{1,0:T(8,128)S(1)}, f32[320,384]{1,0:T(8,128)S(1)}, u32[]{:S(2)}, u32[]{:S(2)}) collective-permute-start(f32[320,384]{1,0:T(8,128)S(1)} %copy-done.7), channel_id=1, source_target_pairs={{0,1},{1,2},{2,3},{3,4},{4,5},{5,6},{6,7},{7,8},{8,9},{9,10},{10,1... | collective-permute-start | bytes 1474568 | tf_op jit(solution)/shard_map/ppermute | solution.py:974
  59.0 36.9 %collective-permute-start.3 = (f32[320,384]{1,0:T(8,128)S(1)}, f32[320,384]{1,0:T(8,128)S(1)}, u32[]{:S(2)}, u32[]{:S(2)}) collective-permute-start(f32[320,384]{1,0:T(8,128)S(1)} %copy-done.6), channel_id=1, source_target_pairs={{1,0},{2,1},{3,2},{4,3},{5,4},{6,5},{7,6},{8,7},{9,8},{10,9},{11,1... | collective-permute-start | bytes 1474568 | tf_op jit(solution)/shard_map/ppermute | solution.py:975
  73.1 1.1 copy-start.2
  73.1 1.4 copy-start.3
  95.9 11.7 %copy-start = (f32[320,384]{1,0:T(8,128)}, f32[320,384]{1,0:T(8,128)S(1)}, u32[]{:S(2)}) copy-start(f32[320,384]{1,0:T(8,128)S(1)} %collective-permute-done.2.before_in.before) | copy-start | bytes 1474564
  95.9 11.7 %copy-start.1 = (f32[320,384]{1,0:T(8,128)}, f32[320,384]{1,0:T(8,128)S(1)}, u32[]{:S(2)}) copy-start(f32[320,384]{1,0:T(8,128)S(1)} %collective-permute-done.3.after_in.after) | copy-start | bytes 1474564
  95.9 16.6 %all-to-all-start = ((f32[32,8,256]{2,1,0:T(8,128)}), f32[32,8,256]{2,1,0:T(8,128)S(1)}, u32[]{:S(2)}, u32[]{:S(2)}) async-start(f32[32,8,256]{2,1,0:T(8,128)} %get-tuple-element.51), calls=%async_computation | async-start | bytes 524288 | tf_op jit(solution)/shard_map/all_to_all | solution.py:1002
  112.5 0.7 copy-start.4
  126.1 12.7 %all-to-all-start.1 = ((f32[32,4,256]{2,1,0:T(4,128)}), f32[32,4,256]{2,1,0:T(4,128)S(1)}, u32[]{:S(2)}, u32[]{:S(2)}) async-start(f32[32,4,256]{2,1,0:T(4,128)} %get-tuple-element.60), calls=%async_computation.1 | async-start | bytes 262144 | tf_op jit(solution)/shard_map/all_to_all | solution.py:1042
  138.7 0.6 copy-start.5

commit v11 on v10

--- a/solution.py
+++ b/solution.py
@@ -16,7 +16,7 @@
 WIDE = ASTEPS * HA
 BF = jnp.bfloat16
 F32 = jnp.float32
-VMEM_BYTES = 56 * 1024 * 1024
+VMEM_BYTES = 63 * 1024 * 1024
 AXES = ("sec", "blk")
 
 
@@ -970,7 +970,9 @@
         ],
     )(ocean, after_all(ocean_nbr, q_mid), ocean_nbr_coef)
 
-    sea_first, sea_last = lax.optimization_barrier((sea_first, sea_last, sea_inner))[:2]
+    sea_first, sea_last, wide_before, wide_after = lax.optimization_barrier(
+        (sea_first, sea_last, wide_before, wide_after, sea_inner)
+    )[:4]
     sea_before = lax.ppermute(sea_last, AXES, up)
     sea_after = lax.ppermute(sea_first, AXES, down)
 

time: 145 us -> 136 us (0.938)
  waiting for transfers between devices: 13.7 us -> 9.52 us
  local copies, waits for them, and re-layouts: 2.79 us -> 0.66 us
  starting transfers between devices: 20 us -> 18 us
    ppermute x1, waiting for transfers between devices: 8.75 us -> 2.7 us  [per_device(): wide_before = lax.ppermute(wide_last, AXES, up)]
    unnamed x16 -> x6, local copies, waits for them, and re-layouts: 2.79 us -> 0.66 us
    all_to_all x1, starting transfers between devices: 5.57 us -> 3.54 us  [per_device(): lax.all_to_all(outgoing, AXES, split_axis=0, concat_axis=0, tiled=True)]
    ppermute x1, waiting for transfers between devices: 0.01 us -> 1.95 us  [per_device(): wide_after = lax.ppermute(wide_first, AXES, down)]
    ppermute x1, starting transfers between devices: 5.32 us -> 3.85 us  [per_device(): sea_after = lax.ppermute(sea_first, AXES, down)]
  transfers between devices with their start and end apart: 6 -> 6, of which waited for: 2 -> 3; matrix products, arithmetic and copies ran while one was open for 0% -> 0% of each run, Pallas kernels for 59% -> 62%
where the time goes in v11:
time: 136 us
  Pallas kernels  107 us (79%)
  starting transfers between devices  18 us (13%)
  waiting for transfers between devices  9.52 us (7%)
    pallas_call x1, Pallas kernels, per_device(): call(interior_kernel, (shape((blocks - ends, states, BLK)), shape((4 * (A...  27.5 us
    pallas_call x1, Pallas kernels, per_device(): call(edge_kernel, (shape((ends, states, BLK)), shape((ends, 2 * rows, BLK...  21.4 us
    pallas_call x1, Pallas kernels, per_device(): call(sea_inner_kernel, shape((inner, 2 * sea_rows, BLK), BF), in_specs=[v...  14.1 us
    pallas_call x1, Pallas kernels, per_device(): call(exchange_kernel, (shape((fields, cells)), shape((peers, 2 * parts, l...  12.8 us
    pallas_call x1, Pallas kernels, per_device(): call(sea_outer_kernel, shape((sea_rows, cells)), in_specs=[vmem] * 7 + [a...  10.1 us
    pallas_call x1, Pallas kernels, per_device(): call(finish_kernel, shape((rows, columns)), in_specs=[vmem] * 3 + [anywhe...  6.07 us
    pallas_call x1, Pallas kernels, per_device(): call(prepare_kernel(fields), (shape((states, columns)), shape((1, columns...  5.81 us
    pallas_call x1, Pallas kernels, per_device(): call(settle_kernel, shape((columns // 128, 128)), in_specs=[vmem] * 3, sc...  5.21 us
  transfers between devices with their start and end apart: 6, of which 3 were waited for; matrix products, arithmetic and copies ran while one was open for 0% of the time, Pallas kernels for 62%

profile of v11, /device:TPU:0, one launch (start us, length us, event | category | flops | bytes accessed | tf_op | source)
XLA Modules:
  0.0 136.0 jit_solution(18120549315077258808)
XLA Ops:
  0.6 4.1 %shard_map.175 = (f32[304,1024]{1,0:T(8,128)}, f32[304,1024]{1,0:T(8,128)}, f32[320,384]{1,0:T(8,128)}, f32[320,384]{1,0:T(8,128)}) custom-call(s32[6,4096]{1,0:T(8,128)} %nbr.5, f32[6,4096]{1,0:T(8,128)} %coef.6, f32[4,4096]{1,0:T(4,128)} %bulk.5, f32[4,4096]{1,0:T(4,128)} %surf.7, f32[288,4096]{1,0:T(8,128)} %bitcast.10, f32[320,4096]{1,0:T(8,128)} %bitcast.6), custom_call_target="tpu_custom_call" | custom-call | flops 1000000 | bytes 10000 | tf_op jit(solution)/shard_map/pallas_call | solution.py:896
  4.8 3.0 %collective-permute-start = (f32[304,1024]{1,0:T(8,128)}, f32[304,1024]{1,0:T(8,128)}, u32[]{:S(2)}, u32[]{:S(2)}) collective-permute-start(f32[304,1024]{1,0:T(8,128)} %get-tuple-element.46), channel_id=1, source_target_pairs={{0,1},{1,2},{2,3},{3,4},{4,5},{5,6},{6,7},{7,8},{8,9},{9,10},{10,1... | collective-permute-start | bytes 3735560 | tf_op jit(solution)/shard_map/ppermute | solution.py:904
  7.8 3.5 %collective-permute-start.1 = (f32[304,1024]{1,0:T(8,128)}, f32[304,1024]{1,0:T(8,128)}, u32[]{:S(2)}, u32[]{:S(2)}) collective-permute-start(f32[304,1024]{1,0:T(8,128)} %get-tuple-element.36), channel_id=1, source_target_pairs={{1,0},{2,1},{3,2},{4,3},{5,4},{6,5},{7,6},{8,7},{9,8},{10,9},{11,1... | collective-permute-start | bytes 3735560 | tf_op jit(solution)/shard_map/ppermute | solution.py:905
  11.3 5.8 %shard_map.176 = (f32[16,4096]{1,0:T(8,128)}, f32[1,4096]{1,0:T(1,128)}, f32[16,128]{1,0:T(8,128)}, f32[3,72,128]{2,1,0:T(8,128)}, bf16[2,288,160]{2,1,0:T(8,128)(2,1)}, /*index=5*/bf16[320,160]{1,0:T(8,128)(2,1)}) custom-call(f32[72,72]{1,0:T(8,128)} %mix.1, f32[80,80]{1,0:T(8,128)} %mix.2, f32[288,4096]{1,0:T(8,128)} %bitcast.11, ...), custom_call_target="tpu_custom_call" | custom-call | flops 1000000 | bytes 10000 | tf_op jit(solution)/shard_map/pallas_call | solution.py:907
  17.1 27.5 %shard_map.177 = (f32[8,16,256]{2,1,0:T(8,128)}, bf16[12,608,256]{2,1,0:T(8,128)(2,1)}, bf16[8,576,256]{2,1,0:T(8,128)(2,1)}, bf16[8,2,768,256]{3,2,1,0:T(8,128)(2,1)}) custom-call(f32[288,4096]{1,0:T(8,128)} %bitcast.12, f32[16,4096]{1,0:T(8,128)} %get-tuple-element.42.y, s32[6,4096]{1,0:T(8,128)} %nbr.5, f32[6,4096]{1,0:T(8,128)} %coef.6, f32[4,4096]{1,0:T(4,128)} %bulk.5, ...), custom_call_target="tpu_custom_call" | custom-call | flops 1000000 | bytes 10000 | tf_op jit(solution)/shard_map/pallas_call | solution.py:930
  44.6 14.1 %shard_map.178.laid_in = bf16[12,640,256]{2,1,0:T(8,128)(2,1)} custom-call(f32[320,4096]{1,0:T(8,128)} %bitcast.8, s32[6,4096]{1,0:T(8,128)} %nbr.8, f32[6,4096]{1,0:T(8,128)} %coef.9), custom_call_target="tpu_custom_call" | custom-call | flops 1000000 | bytes 10000 | tf_op jit(solution)/shard_map/pallas_call | solution.py:957
  58.7 2.7 %collective-permute-done.before = f32[304,1024]{1,0:T(8,128)} collective-permute-done((f32[304,1024]{1,0:T(8,128)}, f32[304,1024]{1,0:T(8,128)}, u32[]{:S(2)}, u32[]{:S(2)}) %collective-permute-start) | collective-permute-done | bytes 1245216 | tf_op jit(solution)/shard_map/ppermute | solution.py:904
  61.4 1.9 %collective-permute-done.1.after = f32[304,1024]{1,0:T(8,128)} collective-permute-done((f32[304,1024]{1,0:T(8,128)}, f32[304,1024]{1,0:T(8,128)}, u32[]{:S(2)}, u32[]{:S(2)}) %collective-permute-start.1) | collective-permute-done | bytes 1245216 | tf_op jit(solution)/shard_map/ppermute | solution.py:905
  63.4 1.5 %collective-permute-start.2 = (f32[320,384]{1,0:T(8,128)}, f32[320,384]{1,0:T(8,128)S(1)}, u32[]{:S(2)}, u32[]{:S(2)}) collective-permute-start(f32[320,384]{1,0:T(8,128)} %get-tuple-element.52), channel_id=1, source_target_pairs={{0,1},{1,2},{2,3},{3,4},{4,5},{5,6},{6,7},{7,8},{8,9},{9,10},{10,1... | collective-permute-start | bytes 1474568 | tf_op jit(solution)/shard_map/ppermute | solution.py:976
  64.8 3.9 %collective-permute-start.3 = (f32[320,384]{1,0:T(8,128)}, f32[320,384]{1,0:T(8,128)S(1)}, u32[]{:S(2)}, u32[]{:S(2)}) collective-permute-start(f32[320,384]{1,0:T(8,128)} %get-tuple-element.53), channel_id=1, source_target_pairs={{1,0},{2,1},{3,2},{4,3},{5,4},{6,5},{7,6},{8,7},{9,8},{10,9},{11,1... | collective-permute-start | bytes 1474568 | tf_op jit(solution)/shard_map/ppermute | solution.py:977
  68.7 21.4 %shard_map.179 = (f32[8,16,256]{2,1,0:T(8,128)}, bf16[8,576,256]{2,1,0:T(8,128)(2,1)}, f32[32,8,256]{2,1,0:T(8,128)}) custom-call(f32[16,4096]{1,0:T(8,128)} %get-tuple-element.42.y, f32[4,4096]{1,0:T(4,128)} %bulk.5, f32[4,4096]{1,0:T(4,128)} %surf.7, f32[16,128]{1,0:T(8,128)} %get-tuple-element.39.gains, f32[3,72,128]{2,1,0:T(8,128)} %get-tuple-element.43.lift, ...), custom_call_target="tpu_custom_call" | custom-call | flops 1000000 | bytes 10000 | tf_op jit(solution)/shard_map/pallas_call | solution.py:979
  90.1 0.0 collective-permute-done.2.before_in.before
  90.1 0.0 copy-start
  90.1 0.0 collective-permute-done.3.after_in.after
  90.1 3.5 %all-to-all-start = ((f32[32,8,256]{2,1,0:T(8,128)}), f32[32,8,256]{2,1,0:T(8,128)}, u32[]{:S(2)}, u32[]{:S(2)}) async-start(f32[32,8,256]{2,1,0:T(8,128)} %get-tuple-element.55), calls=%async_computation | async-start | bytes 524288 | tf_op jit(solution)/shard_map/all_to_all | solution.py:1004
  93.7 6.1 %shard_map.180 = f32[288,4096]{1,0:T(8,128)} custom-call(f32[8,16,256]{2,1,0:T(8,128)} %get-tuple-element.56.q_ends, f32[8,16,256]{2,1,0:T(8,128)} %get-tuple-element.40.q_mid, bf16[2,288,160]{2,1,0:T(8,128)(2,1)} %get-tuple-element.57.vertical, bf16[8,576,256]{2,1,0:T(8,128)(2,1)} %get-tuple-element.58.ends_in, bf16[8,576,256]{2,1,0:T(8,128)(2,1)} %get-tuple-element.59.mid_in), custom_call_target="tpu_custom_call" | custom-call | flops 1000000 | bytes 10000 | tf_op jit(solution)/shard_map/pallas_call | solution.py:1006
  99.8 0.0 copy-done
  99.8 4.9 %all-to-all-done.recv = f32[32,8,256]{2,1,0:T(8,128)} async-done(((f32[32,8,256]{2,1,0:T(8,128)}), f32[32,8,256]{2,1,0:T(8,128)}, u32[]{:S(2)}, u32[]{:S(2)}) %all-to-all-start) | async-done | bytes 262176 | tf_op jit(solution)/shard_map/all_to_all | solution.py:1004
  104.6 12.8 %shard_map.181 = (f32[4,4096]{1,0:T(4,128)}, f32[32,4,256]{2,1,0:T(4,128)}) custom-call(f32[32,8,256]{2,1,0:T(8,128)} %all-to-all-done.recv, s32[4,4096]{1,0:T(4,128)} %slot.1, f32[4,4096]{1,0:T(4,128)} %weight.1, f32[1,4096]{1,0:T(1,128)} %get-tuple-element.62.yo, s32[6,4096]{1,0:T(8,128)} %nbr.8, f32[6,4096]{1,0:T(8,128)} %coef.9, f32[80,80]{1,0:T(8,128)} %mix.2, ...), custom_call_target="tpu_custom_call" | custom-call | flops 1000000 | bytes 10000 | tf_op jit(solution)/shard_map/pallas_call | solution.py:1020
  117.5 2.6 %all-to-all-start.1 = ((f32[32,4,256]{2,1,0:T(4,128)}), f32[32,4,256]{2,1,0:T(4,128)S(1)}, u32[]{:S(2)}, u32[]{:S(2)}) async-start(f32[32,4,256]{2,1,0:T(4,128)} %get-tuple-element.64), calls=%async_computation.1 | async-start | bytes 262144 | tf_op jit(solution)/shard_map/all_to_all | solution.py:1044
  120.1 10.1 %shard_map.182 = f32[320,4096]{1,0:T(8,128)} custom-call(f32[320,384]{1,0:T(8,128)} %copy-done, f32[320,384]{1,0:T(8,128)} %copy-done.1, s32[6,4096]{1,0:T(8,128)} %nbr.8, f32[6,4096]{1,0:T(8,128)} %coef.9, bf16[320,160]{1,0:T(8,128)(2,1)} %get-tuple-element.66.vertical, f32[80,80]{1,0:T(8,128)} %mix.2, f32[4,4096]{1,0:T(4,128)} %get-tuple-element.67.flux, ...), custom_call_target="tpu_custom_call" | custom-call | flops 1000000 | bytes 10000 | tf_op jit(solution)/shard_map/pallas_call | solution.py:1046
  130.2 0.0 all-to-all-done.1.back
  130.2 0.6 copy-done.2
  130.8 5.2 %shard_map.183 = f32[32,128]{1,0:T(8,128)} custom-call(f32[32,4,256]{2,1,0:T(4,128)} %copy-done.2, s32[32,512]{1,0:T(8,128)} %bitcast.17, f32[4,4096]{1,0:T(4,128)} %surf.7), custom_call_target="tpu_custom_call" | custom-call | flops 1000000 | bytes 10000 | tf_op jit(solution)/shard_map/pallas_call | solution.py:1075
  (3 shorter events, 0.0 us)
Async XLA Ops:
  4.8 56.6 %collective-permute-start = (f32[304,1024]{1,0:T(8,128)}, f32[304,1024]{1,0:T(8,128)}, u32[]{:S(2)}, u32[]{:S(2)}) collective-permute-start(f32[304,1024]{1,0:T(8,128)} %get-tuple-element.46), channel_id=1, source_target_pairs={{0,1},{1,2},{2,3},{3,4},{4,5},{5,6},{6,7},{7,8},{8,9},{9,10},{10,1... | collective-permute-start | bytes 3735560 | tf_op jit(solution)/shard_map/ppermute | solution.py:904
  7.8 55.6 %collective-permute-start.1 = (f32[304,1024]{1,0:T(8,128)}, f32[304,1024]{1,0:T(8,128)}, u32[]{:S(2)}, u32[]{:S(2)}) collective-permute-start(f32[304,1024]{1,0:T(8,128)} %get-tuple-element.36), channel_id=1, source_target_pairs={{1,0},{2,1},{3,2},{4,3},{5,4},{6,5},{7,6},{8,7},{9,8},{10,9},{11,1... | collective-permute-start | bytes 3735560 | tf_op jit(solution)/shard_map/ppermute | solution.py:905
  63.4 26.7 %collective-permute-start.2 = (f32[320,384]{1,0:T(8,128)}, f32[320,384]{1,0:T(8,128)S(1)}, u32[]{:S(2)}, u32[]{:S(2)}) collective-permute-start(f32[320,384]{1,0:T(8,128)} %get-tuple-element.52), channel_id=1, source_target_pairs={{0,1},{1,2},{2,3},{3,4},{4,5},{5,6},{6,7},{7,8},{8,9},{9,10},{10,1... | collective-permute-start | bytes 1474568 | tf_op jit(solution)/shard_map/ppermute | solution.py:976
  64.8 25.3 %collective-permute-start.3 = (f32[320,384]{1,0:T(8,128)}, f32[320,384]{1,0:T(8,128)S(1)}, u32[]{:S(2)}, u32[]{:S(2)}) collective-permute-start(f32[320,384]{1,0:T(8,128)} %get-tuple-element.53), channel_id=1, source_target_pairs={{1,0},{2,1},{3,2},{4,3},{5,4},{6,5},{7,6},{8,7},{9,8},{10,9},{11,1... | collective-permute-start | bytes 1474568 | tf_op jit(solution)/shard_map/ppermute | solution.py:977
  90.1 9.7 %copy-start = (f32[320,384]{1,0:T(8,128)}, f32[320,384]{1,0:T(8,128)S(1)}, u32[]{:S(2)}) copy-start(f32[320,384]{1,0:T(8,128)S(1)} %collective-permute-done.2.before_in.before) | copy-start | bytes 1474564
  90.1 9.7 %copy-start.1 = (f32[320,384]{1,0:T(8,128)}, f32[320,384]{1,0:T(8,128)S(1)}, u32[]{:S(2)}) copy-start(f32[320,384]{1,0:T(8,128)S(1)} %collective-permute-done.3.after_in.after) | copy-start | bytes 1474564
  90.1 14.5 %all-to-all-start = ((f32[32,8,256]{2,1,0:T(8,128)}), f32[32,8,256]{2,1,0:T(8,128)}, u32[]{:S(2)}, u32[]{:S(2)}) async-start(f32[32,8,256]{2,1,0:T(8,128)} %get-tuple-element.55), calls=%async_computation | async-start | bytes 524288 | tf_op jit(solution)/shard_map/all_to_all | solution.py:1004
  117.5 12.7 %all-to-all-start.1 = ((f32[32,4,256]{2,1,0:T(4,128)}), f32[32,4,256]{2,1,0:T(4,128)S(1)}, u32[]{:S(2)}, u32[]{:S(2)}) async-start(f32[32,4,256]{2,1,0:T(4,128)} %get-tuple-element.64), calls=%async_computation.1 | async-start | bytes 262144 | tf_op jit(solution)/shard_map/all_to_all | solution.py:1044
  130.2 0.7 copy-start.2

commit v12 on v11

--- a/solution.py
+++ b/solution.py
@@ -396,35 +396,33 @@
     lax.fori_loop(0, peers, one, 0, unroll=4)
 
 
-def exchange_kernel(
-    recv, slot, weight, yo, nbr, coef, omix, before_in, after_in, flux_out, back, rows, tiles, hots, seas, acc, held, sems
-):
-    peers, per_peer, lanes = recv.shape
-    links, columns = slot.shape
-    fields = flux_out.shape[0]
-    parts = per_peer // fields
-    highs = peers * parts
-    table = highs * fields
+def sea_row_kernel(yo, nbr, coef, omix, before_in, after_in, out, tiles, held, sems):
+    columns = yo.shape[1]
     arriving = [
         pltpu.make_async_copy(ref.at[: held.shape[1]], held.at[i], sems.at[i])
         for i, ref in enumerate((before_in, after_in))
     ]
     for copy in arriving:
         copy.start()
-    rows[...] = stacked(recv[...].reshape(table, lanes))
     levels = omix.shape[0]
     eye = iota((levels, levels), 0) == iota((levels, levels), 1)
-    corner = omix[0:1, 0:1] + 1.0
     top = omix[0:1, :] + jnp.where(iota((1, levels), 1) == 0, 1.0, 0.0)
     top = jnp.sum(jnp.where(eye, top, 0.0), axis=1, keepdims=True)
-    high_of_row = iota((table, BLK), 0) // fields
-    back_rows = iota((2 * highs, BLK), 0)
-    inner = back_rows % (2 * parts)
-    back_high = (back_rows // (2 * parts)) * parts + inner % parts
-    pattern = iota((8, BLK), 0) % (2 * parts) // parts
     side = HO // 128
     window = 1 + 2 * side
     neighbors = nbr.shape[0]
+    for copy in arriving:
+        copy.wait()
+    before, after = [jnp.sum(held[i] * top, axis=0, keepdims=True) for i in range(2)]
+    own_tiles = columns // 128
+    for t in range(own_tiles + 2 * side):
+        if t < side:
+            line = before[:, t * 128 : (t + 1) * 128]
+        elif t < side + own_tiles:
+            line = yo[:, (t - side) * 128 : (t - side + 1) * 128]
+        else:
+            line = after[:, (t - side - own_tiles) * 128 : (t - side - own_tiles + 1) * 128]
+        tiles[t] = jnp.broadcast_to(line, (8, 128))
 
     def surface(j, half):
         t0 = j * (BLK // 128) + half
@@ -439,6 +437,31 @@
             got = jnp.where(ids // 128 == t, pick, got)
         return middle[0:1] + jnp.sum(cs * (got - middle), axis=0, keepdims=True)
 
+    def base(j, _):
+        at = pl.ds(pl.multiple_of(j * BLK, BLK), BLK)
+        out[:, at] = jnp.concatenate([surface(j, h) for h in range(BLK // 128)], axis=1)
+        return 0
+
+    lax.fori_loop(0, columns // BLK, base, 0, unroll=2)
+
+
+def exchange_kernel(
+    recv, slot, weight, base, omix, flux_out, back, rows, hots, seas, acc
+):
+    peers, per_peer, lanes = recv.shape
+    links, columns = slot.shape
+    fields = flux_out.shape[0]
+    parts = per_peer // fields
+    highs = peers * parts
+    table = highs * fields
+    rows[...] = stacked(recv[...].reshape(table, lanes))
+    corner = omix[0:1, 0:1] + 1.0
+    high_of_row = iota((table, BLK), 0) // fields
+    back_rows = iota((2 * highs, BLK), 0)
+    inner = back_rows % (2 * parts)
+    back_high = (back_rows // (2 * parts)) * parts + inner % parts
+    pattern = iota((8, BLK), 0) % (2 * parts) // parts
+
     def arrive(j, _):
         at = pl.ds(pl.multiple_of(j * BLK, BLK), BLK)
         parts = []
@@ -463,31 +486,11 @@
         flux = sum(parts[1:], parts[0])
         flux = flux[:fields] + flux[fields:]
         flux_out[:, at] = flux
-        seas[:, at] = corner * flux[0:1]
+        seas[:, at] = base[:, at] + corner * flux[0:1]
         return 0
 
     lax.fori_loop(0, columns // BLK, arrive, 0, unroll=2)
-    for copy in arriving:
-        copy.wait()
-    before, after = [jnp.sum(held[i] * top, axis=0, keepdims=True) for i in range(2)]
     acc[...] = jnp.zeros_like(acc)
-    own_tiles = columns // 128
-    for t in range(own_tiles + 2 * side):
-        if t < side:
-            line = before[:, t * 128 : (t + 1) * 128]
-        elif t < side + own_tiles:
-            line = yo[:, (t - side) * 128 : (t - side + 1) * 128]
-        else:
-            line = after[:, (t - side - own_tiles) * 128 : (t - side - own_tiles + 1) * 128]
-        tiles[t] = jnp.broadcast_to(line, (8, 128))
-
-    def base(j, _):
-        at = pl.ds(pl.multiple_of(j * BLK, BLK), BLK)
-        seas[:, at] += jnp.concatenate([surface(j, h) for h in range(BLK // 128)], axis=1)
-        return 0
-
-    lax.fori_loop(0, columns // BLK, base, 0, unroll=2)
-
     def leave(j, _):
         at = pl.ds(pl.multiple_of(j * BLK, BLK), BLK)
         sea = seas[:, at]
@@ -1017,30 +1020,28 @@
         ],
     )(after_all(q_ends, outgoing), q_mid, vertical, tips, mid)
 
+    sea_row = call(
+        sea_row_kernel,
+        shape((1, cells)),
+        in_specs=[vmem] * 4 + [anywhere] * 2,
+        scratch=[
+            pltpu.VMEM((cells // 128 + 2 * HO // 128, 8, 128), F32),
+            pltpu.VMEM((2, lo, HO), F32),
+            pltpu.SemaphoreType.DMA((2,)),
+        ],
+    )(after_all(yo, atm_final), ocean_nbr, ocean_nbr_coef, ocean_mix, sea_before, sea_after)
+
     flux, back = call(
         exchange_kernel,
         (shape((fields, cells)), shape((peers, 2 * parts, lanes))),
-        in_specs=[vmem] * 7 + [anywhere] * 2,
+        in_specs=[vmem] * 5,
         scratch=[
             pltpu.VMEM((2 * peers * parts * fields, lanes), BF),
-            pltpu.VMEM((cells // 128 + 2 * HO // 128, 8, 128), F32),
             pltpu.VMEM((cells // BLK, lanes, remap_slot.shape[0] * BLK), BF),
             pltpu.VMEM((1, cells), F32),
             pltpu.VMEM((4 * peers * parts, lanes), F32),
-            pltpu.VMEM((2, lo, HO), F32),
-            pltpu.SemaphoreType.DMA((2,)),
         ],
-    )(
-        after_all(received, atm_final),
-        remap_slot,
-        remap_weight,
-        yo,
-        ocean_nbr,
-        ocean_nbr_coef,
-        ocean_mix,
-        sea_before,
-        sea_after,
-    )
+    )(after_all(received, sea_row), remap_slot, remap_weight, sea_row, ocean_mix)
     returned = lax.all_to_all(back, AXES, split_axis=0, concat_axis=0, tiled=True)
 
     ocean_final = call(

time: 136 us -> 137 us (level)
  waiting for transfers between devices: 9.52 us -> 5.67 us
  Pallas kernels: 107 us -> 110 us
  starting transfers between devices: 18 us -> 19.9 us
    all_to_all x1, waiting for transfers between devices: 4.87 us -> 1.02 us  [per_device(): lax.all_to_all(outgoing, AXES, split_axis=0, concat_axis=0, tiled=True)]
    pallas_call x0 -> x1, Pallas kernels: none -> 3.84 us  [per_device(): call(sea_row_kernel, shape((1, cells)), in_specs=[vmem] * 4 + [anywhere]...]
    all_to_all x1, starting transfers between devices: 2.58 us -> 4.54 us  [per_device(): lax.all_to_all(back, AXES, split_axis=0, concat_axis=0, tiled=True)]
    pallas_call x1, Pallas kernels: 12.8 us -> 11.5 us  [per_device(): call(exchange_kernel, (shape((fields, cells)), shape((peers, 2 * parts, l...]
  transfers between devices with their start and end apart: 6 -> 6, of which waited for: 3 -> 3; matrix products, arithmetic and copies ran while one was open for 0% -> 0% of each run, Pallas kernels for 62% -> 65%
where the time goes in v12:
time: 137 us
  Pallas kernels  110 us (80%)
  starting transfers between devices  19.9 us (15%)
  waiting for transfers between devices  5.67 us (4%)
    pallas_call x1, Pallas kernels, per_device(): call(interior_kernel, (shape((blocks - ends, states, BLK)), shape((4 * (A...  27.5 us
    pallas_call x1, Pallas kernels, per_device(): call(edge_kernel, (shape((ends, states, BLK)), shape((ends, 2 * rows, BLK...  21.4 us
    pallas_call x1, Pallas kernels, per_device(): call(sea_inner_kernel, shape((inner, 2 * sea_rows, BLK), BF), in_specs=[v...  14.1 us
    pallas_call x1, Pallas kernels, per_device(): call(exchange_kernel, (shape((fields, cells)), shape((peers, 2 * parts, l...  11.5 us
    pallas_call x1, Pallas kernels, per_device(): call(sea_outer_kernel, shape((sea_rows, cells)), in_specs=[vmem] * 7 + [a...  10.1 us
    pallas_call x1, Pallas kernels, per_device(): call(finish_kernel, shape((rows, columns)), in_specs=[vmem] * 3 + [anywhe...  6.07 us
    pallas_call x1, Pallas kernels, per_device(): call(prepare_kernel(fields), (shape((states, columns)), shape((1, columns...  5.81 us
    pallas_call x1, Pallas kernels, per_device(): call(settle_kernel, shape((columns // 128, 128)), in_specs=[vmem] * 3, sc...  5.21 us
  transfers between devices with their start and end apart: 6, of which 3 were waited for; matrix products, arithmetic and copies ran while one was open for 0% of the time, Pallas kernels for 65%

profile of v12, /device:TPU:0, one launch (start us, length us, event | category | flops | bytes accessed | tf_op | source)
XLA Modules:
  0.0 136.6 jit_solution(4225328684254992215)
XLA Ops:
  0.6 4.1 %shard_map.175 = (f32[304,1024]{1,0:T(8,128)}, f32[304,1024]{1,0:T(8,128)}, f32[320,384]{1,0:T(8,128)}, f32[320,384]{1,0:T(8,128)}) custom-call(s32[6,4096]{1,0:T(8,128)} %nbr.5, f32[6,4096]{1,0:T(8,128)} %coef.6, f32[4,4096]{1,0:T(4,128)} %bulk.5, f32[4,4096]{1,0:T(4,128)} %surf.7, f32[288,4096]{1,0:T(8,128)} %bitcast.10, f32[320,4096]{1,0:T(8,128)} %bitcast.6), custom_call_target="tpu_custom_call" | custom-call | flops 1000000 | bytes 10000 | tf_op jit(solution)/shard_map/pallas_call | solution.py:899
  4.8 3.0 %collective-permute-start = (f32[304,1024]{1,0:T(8,128)}, f32[304,1024]{1,0:T(8,128)}, u32[]{:S(2)}, u32[]{:S(2)}) collective-permute-start(f32[304,1024]{1,0:T(8,128)} %get-tuple-element.47), channel_id=1, source_target_pairs={{0,1},{1,2},{2,3},{3,4},{4,5},{5,6},{6,7},{7,8},{8,9},{9,10},{10,1... | collective-permute-start | bytes 3735560 | tf_op jit(solution)/shard_map/ppermute | solution.py:907
  7.8 3.5 %collective-permute-start.1 = (f32[304,1024]{1,0:T(8,128)}, f32[304,1024]{1,0:T(8,128)}, u32[]{:S(2)}, u32[]{:S(2)}) collective-permute-start(f32[304,1024]{1,0:T(8,128)} %get-tuple-element.37), channel_id=1, source_target_pairs={{1,0},{2,1},{3,2},{4,3},{5,4},{6,5},{7,6},{8,7},{9,8},{10,9},{11,1... | collective-permute-start | bytes 3735560 | tf_op jit(solution)/shard_map/ppermute | solution.py:908
  11.3 5.8 %shard_map.176 = (f32[16,4096]{1,0:T(8,128)}, f32[1,4096]{1,0:T(1,128)}, f32[16,128]{1,0:T(8,128)}, f32[3,72,128]{2,1,0:T(8,128)}, bf16[2,288,160]{2,1,0:T(8,128)(2,1)}, /*index=5*/bf16[320,160]{1,0:T(8,128)(2,1)}) custom-call(f32[72,72]{1,0:T(8,128)} %mix.1, f32[80,80]{1,0:T(8,128)} %mix.2, f32[288,4096]{1,0:T(8,128)} %bitcast.11, ...), custom_call_target="tpu_custom_call" | custom-call | flops 1000000 | bytes 10000 | tf_op jit(solution)/shard_map/pallas_call | solution.py:910
  17.1 27.5 %shard_map.177 = (f32[8,16,256]{2,1,0:T(8,128)}, bf16[12,608,256]{2,1,0:T(8,128)(2,1)}, bf16[8,576,256]{2,1,0:T(8,128)(2,1)}, bf16[8,2,768,256]{3,2,1,0:T(8,128)(2,1)}) custom-call(f32[288,4096]{1,0:T(8,128)} %bitcast.12, f32[16,4096]{1,0:T(8,128)} %get-tuple-element.43.y, s32[6,4096]{1,0:T(8,128)} %nbr.5, f32[6,4096]{1,0:T(8,128)} %coef.6, f32[4,4096]{1,0:T(4,128)} %bulk.5, ...), custom_call_target="tpu_custom_call" | custom-call | flops 1000000 | bytes 10000 | tf_op jit(solution)/shard_map/pallas_call | solution.py:933
  44.6 14.1 %shard_map.178.laid_in = bf16[12,640,256]{2,1,0:T(8,128)(2,1)} custom-call(f32[320,4096]{1,0:T(8,128)} %bitcast.8, s32[6,4096]{1,0:T(8,128)} %nbr.8, f32[6,4096]{1,0:T(8,128)} %coef.9), custom_call_target="tpu_custom_call" | custom-call | flops 1000000 | bytes 10000 | tf_op jit(solution)/shard_map/pallas_call | solution.py:960
  58.7 2.7 %collective-permute-done.before = f32[304,1024]{1,0:T(8,128)} collective-permute-done((f32[304,1024]{1,0:T(8,128)}, f32[304,1024]{1,0:T(8,128)}, u32[]{:S(2)}, u32[]{:S(2)}) %collective-permute-start) | collective-permute-done | bytes 1245216 | tf_op jit(solution)/shard_map/ppermute | solution.py:907
  61.4 1.9 %collective-permute-done.1.after = f32[304,1024]{1,0:T(8,128)} collective-permute-done((f32[304,1024]{1,0:T(8,128)}, f32[304,1024]{1,0:T(8,128)}, u32[]{:S(2)}, u32[]{:S(2)}) %collective-permute-start.1) | collective-permute-done | bytes 1245216 | tf_op jit(solution)/shard_map/ppermute | solution.py:908
  63.4 1.5 %collective-permute-start.2 = (f32[320,384]{1,0:T(8,128)}, f32[320,384]{1,0:T(8,128)S(1)}, u32[]{:S(2)}, u32[]{:S(2)}) collective-permute-start(f32[320,384]{1,0:T(8,128)} %get-tuple-element.53), channel_id=1, source_target_pairs={{0,1},{1,2},{2,3},{3,4},{4,5},{5,6},{6,7},{7,8},{8,9},{9,10},{10,1... | collective-permute-start | bytes 1474568 | tf_op jit(solution)/shard_map/ppermute | solution.py:979
  64.8 3.9 %collective-permute-start.3 = (f32[320,384]{1,0:T(8,128)}, f32[320,384]{1,0:T(8,128)S(1)}, u32[]{:S(2)}, u32[]{:S(2)}) collective-permute-start(f32[320,384]{1,0:T(8,128)} %get-tuple-element.54), channel_id=1, source_target_pairs={{1,0},{2,1},{3,2},{4,3},{5,4},{6,5},{7,6},{8,7},{9,8},{10,9},{11,1... | collective-permute-start | bytes 1474568 | tf_op jit(solution)/shard_map/ppermute | solution.py:980
  68.7 21.4 %shard_map.179 = (f32[8,16,256]{2,1,0:T(8,128)}, bf16[8,576,256]{2,1,0:T(8,128)(2,1)}, f32[32,8,256]{2,1,0:T(8,128)}) custom-call(f32[16,4096]{1,0:T(8,128)} %get-tuple-element.43.y, f32[4,4096]{1,0:T(4,128)} %bulk.5, f32[4,4096]{1,0:T(4,128)} %surf.7, f32[16,128]{1,0:T(8,128)} %get-tuple-element.40.gains, f32[3,72,128]{2,1,0:T(8,128)} %get-tuple-element.44.lift, ...), custom_call_target="tpu_custom_call" | custom-call | flops 1000000 | bytes 10000 | tf_op jit(solution)/shard_map/pallas_call | solution.py:982
  90.1 0.0 collective-permute-done.2.before_in.before
  90.1 0.0 copy-start
  90.1 0.0 collective-permute-done.3.after_in.after
  90.1 3.5 %all-to-all-start = ((f32[32,8,256]{2,1,0:T(8,128)}), f32[32,8,256]{2,1,0:T(8,128)}, u32[]{:S(2)}, u32[]{:S(2)}) async-start(f32[32,8,256]{2,1,0:T(8,128)} %get-tuple-element.56), calls=%async_computation | async-start | bytes 524288 | tf_op jit(solution)/shard_map/all_to_all | solution.py:1007
  93.7 6.1 %shard_map.180 = f32[288,4096]{1,0:T(8,128)} custom-call(f32[8,16,256]{2,1,0:T(8,128)} %get-tuple-element.57.q_ends, f32[8,16,256]{2,1,0:T(8,128)} %get-tuple-element.41.q_mid, bf16[2,288,160]{2,1,0:T(8,128)(2,1)} %get-tuple-element.58.vertical, bf16[8,576,256]{2,1,0:T(8,128)(2,1)} %get-tuple-element.59.ends_in, bf16[8,576,256]{2,1,0:T(8,128)(2,1)} %get-tuple-element.60.mid_in), custom_call_target="tpu_custom_call" | custom-call | flops 1000000 | bytes 10000 | tf_op jit(solution)/shard_map/pallas_call | solution.py:1009
  99.8 3.8 %shard_map.181.base = f32[1,4096]{1,0:T(1,128)} custom-call(f32[1,4096]{1,0:T(1,128)} %get-tuple-element.63.yo, s32[6,4096]{1,0:T(8,128)} %nbr.8, f32[6,4096]{1,0:T(8,128)} %coef.9, f32[80,80]{1,0:T(8,128)} %mix.2, f32[320,384]{1,0:T(8,128)} %copy-done, f32[320,384]{1,0:T(8,128)} %copy-done.1), custom_call_target="tpu_custom_call" | custom-call | flops 1000000 | bytes 10000 | tf_op jit(solution)/shard_map/pallas_call | solution.py:1023
  103.6 1.0 all-to-all-done.recv
  104.6 11.5 %shard_map.182 = (f32[4,4096]{1,0:T(4,128)}, f32[32,4,256]{2,1,0:T(4,128)}) custom-call(f32[32,8,256]{2,1,0:T(8,128)} %all-to-all-done.recv, s32[4,4096]{1,0:T(4,128)} %slot.1, f32[4,4096]{1,0:T(4,128)} %weight.1, f32[1,4096]{1,0:T(1,128)} %shard_map.181.base, f32[80,80]{1,0:T(8,128)} %mix.2), custom_call_target="tpu_custom_call" | custom-call | flops 1000000 | bytes 10000 | tf_op jit(solution)/shard_map/pallas_call | solution.py:1034
  116.1 4.5 %all-to-all-start.1 = ((f32[32,4,256]{2,1,0:T(4,128)}), f32[32,4,256]{2,1,0:T(4,128)S(1)}, u32[]{:S(2)}, u32[]{:S(2)}) async-start(f32[32,4,256]{2,1,0:T(4,128)} %get-tuple-element.66), calls=%async_computation.1 | async-start | bytes 262144 | tf_op jit(solution)/shard_map/all_to_all | solution.py:1045
  120.7 10.1 %shard_map.183 = f32[320,4096]{1,0:T(8,128)} custom-call(f32[320,384]{1,0:T(8,128)} %copy-done, f32[320,384]{1,0:T(8,128)} %copy-done.1, s32[6,4096]{1,0:T(8,128)} %nbr.8, f32[6,4096]{1,0:T(8,128)} %coef.9, bf16[320,160]{1,0:T(8,128)(2,1)} %get-tuple-element.68.vertical, f32[80,80]{1,0:T(8,128)} %mix.2, f32[4,4096]{1,0:T(4,128)} %get-tuple-element.69.flux, ...), custom_call_target="tpu_custom_call" | custom-call | flops 1000000 | bytes 10000 | tf_op jit(solution)/shard_map/pallas_call | solution.py:1047
  130.7 0.0 all-to-all-done.1.back
  130.8 0.6 copy-done.2
  131.4 5.2 %shard_map.184 = f32[32,128]{1,0:T(8,128)} custom-call(f32[32,4,256]{2,1,0:T(4,128)} %copy-done.2, s32[32,512]{1,0:T(8,128)} %bitcast.17, f32[4,4096]{1,0:T(4,128)} %surf.7), custom_call_target="tpu_custom_call" | custom-call | flops 1000000 | bytes 10000 | tf_op jit(solution)/shard_map/pallas_call | solution.py:1076
  (4 shorter events, 0.0 us)
Async XLA Ops:
  4.8 56.6 %collective-permute-start = (f32[304,1024]{1,0:T(8,128)}, f32[304,1024]{1,0:T(8,128)}, u32[]{:S(2)}, u32[]{:S(2)}) collective-permute-start(f32[304,1024]{1,0:T(8,128)} %get-tuple-element.47), channel_id=1, source_target_pairs={{0,1},{1,2},{2,3},{3,4},{4,5},{5,6},{6,7},{7,8},{8,9},{9,10},{10,1... | collective-permute-start | bytes 3735560 | tf_op jit(solution)/shard_map/ppermute | solution.py:907
  7.8 55.6 %collective-permute-start.1 = (f32[304,1024]{1,0:T(8,128)}, f32[304,1024]{1,0:T(8,128)}, u32[]{:S(2)}, u32[]{:S(2)}) collective-permute-start(f32[304,1024]{1,0:T(8,128)} %get-tuple-element.37), channel_id=1, source_target_pairs={{1,0},{2,1},{3,2},{4,3},{5,4},{6,5},{7,6},{8,7},{9,8},{10,9},{11,1... | collective-permute-start | bytes 3735560 | tf_op jit(solution)/shard_map/ppermute | solution.py:908
  63.4 26.7 %collective-permute-start.2 = (f32[320,384]{1,0:T(8,128)}, f32[320,384]{1,0:T(8,128)S(1)}, u32[]{:S(2)}, u32[]{:S(2)}) collective-permute-start(f32[320,384]{1,0:T(8,128)} %get-tuple-element.53), channel_id=1, source_target_pairs={{0,1},{1,2},{2,3},{3,4},{4,5},{5,6},{6,7},{7,8},{8,9},{9,10},{10,1... | collective-permute-start | bytes 1474568 | tf_op jit(solution)/shard_map/ppermute | solution.py:979
  64.8 25.3 %collective-permute-start.3 = (f32[320,384]{1,0:T(8,128)}, f32[320,384]{1,0:T(8,128)S(1)}, u32[]{:S(2)}, u32[]{:S(2)}) collective-permute-start(f32[320,384]{1,0:T(8,128)} %get-tuple-element.54), channel_id=1, source_target_pairs={{1,0},{2,1},{3,2},{4,3},{5,4},{6,5},{7,6},{8,7},{9,8},{10,9},{11,1... | collective-permute-start | bytes 1474568 | tf_op jit(solution)/shard_map/ppermute | solution.py:980
  90.1 9.7 %copy-start = (f32[320,384]{1,0:T(8,128)}, f32[320,384]{1,0:T(8,128)S(1)}, u32[]{:S(2)}) copy-start(f32[320,384]{1,0:T(8,128)S(1)} %collective-permute-done.2.before_in.before) | copy-start | bytes 1474564
  90.1 9.7 %copy-start.1 = (f32[320,384]{1,0:T(8,128)}, f32[320,384]{1,0:T(8,128)S(1)}, u32[]{:S(2)}) copy-start(f32[320,384]{1,0:T(8,128)S(1)} %collective-permute-done.3.after_in.after) | copy-start | bytes 1474564
  90.1 14.5 %all-to-all-start = ((f32[32,8,256]{2,1,0:T(8,128)}), f32[32,8,256]{2,1,0:T(8,128)}, u32[]{:S(2)}, u32[]{:S(2)}) async-start(f32[32,8,256]{2,1,0:T(8,128)} %get-tuple-element.56), calls=%async_computation | async-start | bytes 524288 | tf_op jit(solution)/shard_map/all_to_all | solution.py:1007
  116.1 14.6 %all-to-all-start.1 = ((f32[32,4,256]{2,1,0:T(4,128)}), f32[32,4,256]{2,1,0:T(4,128)S(1)}, u32[]{:S(2)}, u32[]{:S(2)}) async-start(f32[32,4,256]{2,1,0:T(4,128)} %get-tuple-element.66), calls=%async_computation.1 | async-start | bytes 262144 | tf_op jit(solution)/shard_map/all_to_all | solution.py:1045
  130.7 0.7 copy-start.2
